TPU v7x, 512 devices: a whole 4x4x16 slice. The times are simulated.
512 devices in a mesh: dp: 64 (over z, y_lo, core), tensor: 8 (over y_hi, x).
Axes of the slice: x: 4, y: 4 (y_hi: 2, y_lo: 2; y = y_hi * 2 + y_lo), z: 16, core: 2. Of those that a mesh axis runs over, the one named last changes fastest.
Arguments:
- hidden: bfloat16 [65536, 8192], P(('dp', 'tensor')), may hold values from -6 to 6
- norm_gain: bfloat16 [8192], replicated, may hold values from 0.25 to 1.75
- teacher_k: bfloat16 [8192, 512], P('dp', 'tensor'), may hold values from -0.0625 to 0.0625
- student_k: bfloat16 [8192, 512], P('dp', 'tensor'), may hold values from -0.0625 to 0.0625
- keep_pattern: int32 [2048, 512], P(None, 'tensor'), may hold values from 0 to 5
Outputs:
- grad: float32 [8192, 512], P('dp', 'tensor')
- loss: float32 [], replicated
All inputs are finite; a program needn't handle non-finite values.
Results may differ from a plain program's by a relative error of at most 0.0016.
Values may be sent and summed in bfloat16 or wider, within the bound.
No kernel may reach another device: no remote copies, remote signals or barrier semaphores. Data moves between devices by JAX's collectives and lax.ppermute only.
A program may use at most 128 MiB of HBM per device.

v0:
```python
import jax
import jax.numpy as jnp
from jax import lax
from jax.sharding import PartitionSpec as P


def from_partner(block, axis, bit):
    count = lax.axis_size(axis)
    route = []
    for low in range(count):
        high = low | 1 << bit
        if high != low and high < count:
            route += [(low, high), (high, low)]
    return lax.ppermute(block, axis, route)


def pattern_rows(patterns):
    first = (patterns > 2).astype(jnp.int32) + (patterns > 4).astype(jnp.int32)
    second = jnp.where(patterns < 3, patterns + 1, jnp.where(patterns == 3, 2, 3))
    return (first, second)


def keep_table(patterns):
    first, second = pattern_rows(patterns)
    spots = jnp.arange(4, dtype=jnp.int32)[None, :, None]
    keep = (first[:, None, :] == spots) | (second[:, None, :] == spots)
    return keep.reshape(patterns.shape[0] * 4, patterns.shape[1]).astype(jnp.bfloat16)


def ordered(half, mine, theirs):
    return jnp.where(
        half == 0, jnp.concatenate([mine, theirs], 1), jnp.concatenate([theirs, mine], 1)
    )


def shards(hidden, norm_gain, teacher_k, student_k, keep_pattern):
    tok = hidden.shape[0]
    width = hidden.shape[1]
    tensor_count = lax.axis_size("tensor")
    col_dev = teacher_k.shape[1]
    rows_dev = teacher_k.shape[0]
    groups_dev = rows_dev // 4
    half = lax.axis_index("tensor") % 2
    dp_place = lax.axis_index("dp")
    tokens_all = tok * tensor_count * lax.axis_size("dp")
    x32 = hidden.astype(jnp.float32)
    factor = lax.rsqrt(jnp.mean(x32 * x32, axis=-1, keepdims=True) + 1e-05)
    normed = (x32 * factor * norm_gain.astype(jnp.float32)).astype(jnp.bfloat16)
    rows_all = lax.all_gather(normed, "tensor", axis=0, tiled=True)
    target_all = jnp.dot(
        rows_all,
        lax.all_gather(teacher_k, "dp", axis=0, tiled=True),
        preferred_element_type=jnp.float32,
    ).astype(jnp.bfloat16)
    split_keys = target_all.reshape(tensor_count // 2, 2, tok, col_dev)
    own_keys = lax.dynamic_index_in_dim(split_keys, half, 1, keepdims=False).reshape(-1, col_dev)
    give_keys = lax.dynamic_index_in_dim(split_keys, 1 - half, 1, keepdims=False).reshape(
        -1, col_dev
    )
    got_keys = from_partner(give_keys, "tensor", 0)
    target = ordered(half, own_keys, got_keys)
    split_rows = rows_all.reshape(tensor_count // 2, 2, tok, width)
    student_rows = lax.dynamic_index_in_dim(split_rows, half, 1, keepdims=False).reshape(-1, width)
    own_patterns = lax.dynamic_slice_in_dim(keep_pattern, dp_place * groups_dev, groups_dev, 0)
    own_keep = keep_table(own_patterns)
    masked = student_k * own_keep
    full_cols = lax.all_gather(masked, "dp", axis=0, tiled=True)
    partner_cols = from_partner(full_cols, "tensor", 0)
    weights = ordered(half, full_cols, partner_cols)
    diff = jnp.dot(student_rows, weights, preferred_element_type=jnp.float32) - target.astype(
        jnp.float32
    )
    total = lax.psum(jnp.sum(diff * diff), ("dp", "tensor"))
    loss = total / (tokens_all * col_dev * tensor_count)
    slope = diff.astype(jnp.bfloat16)
    contract = (((0,), (0,)), ((), ()))
    term = lax.dot_general(student_rows, slope, contract, preferred_element_type=jnp.float32)
    own_term = lax.dynamic_slice_in_dim(term, half * col_dev, col_dev, 1)
    give_term = lax.dynamic_slice_in_dim(term, (1 - half) * col_dev, col_dev, 1)
    summed = own_term + from_partner(give_term, "tensor", 0)
    reduced = lax.psum_scatter(summed, "dp", scatter_dimension=0, tiled=True)
    grad = own_keep.astype(jnp.float32) * reduced / jnp.sqrt(jnp.float32(tokens_all))
    return (grad, loss)


def solution(mesh):
    in_specs = (
        P(("dp", "tensor"), None),
        P(),
        P("dp", "tensor"),
        P("dp", "tensor"),
        P(None, "tensor"),
    )
    out_specs = (P("dp", "tensor"), P())
    return jax.shard_map(shards, mesh=mesh, in_specs=in_specs, out_specs=out_specs, check_vma=False)
```

profile of v0, /device:TPU:6, one launch (start us, length us, event | category | flops | bytes accessed | tf_op | source)
XLA Modules:
  0.0 771.0 jit_solution(10613327753333158109)
XLA Ops:
  7.2 0.0 copy-start.2
  7.2 0.0 all-gather.6.cloned.1.call-start
  7.2 1.0 convert_add_fusion
  8.2 0.1 copy.11
  8.3 0.1 copy.12
  8.4 0.1 copy.9
  8.5 0.1 copy.10
  8.6 0.1 eq.52
  8.7 1.3 broadcast_select_fusion
  10.0 0.0 all-gather.6.cloned.1.call-update
  10.0 0.0 all-gather.8.cloned.1.call-start
  10.1 0.7 all-gather.8.cloned.1.call-update
  10.8 0.0 all-gather.4.cloned.1.call-start
  10.8 0.7 convert_element_type.35
  11.6 2.1 fusion
  13.7 0.0 copy-done.2
  13.7 1.9 fusion.2
  15.6 0.0 all-gather.4.cloned.1.call-update
  15.6 0.0 reduce-scatter.2.cloned.1.call-start
  15.7 117.2 %all-gather.6.cloned.1.call-done = bf16[8192,64]{0,1:T(8,128)(2,1)} async-done(((bf16[128,64]{0,1:T(8,128)(2,1)}), bf16[8192,64]{0,1:T(8,128)(2,1)}) %all-gather.6.cloned.1.call-update) | async-done | bytes 1048592 | tf_op jit(solution)/shard_map/all_gather | solution.py:67
  132.8 2.7 collective-permute-start
  135.6 113.3 %all-gather.8.cloned.1.call-done = bf16[8192,64]{0,1:T(8,128)(2,1)} async-done(((bf16[128,64]{0,1:T(8,128)(2,1)}), bf16[8192,64]{0,1:T(8,128)(2,1)}) %all-gather.8.cloned.1.call-update) | async-done | bytes 1048592 | tf_op jit(solution)/shard_map/all_gather | solution.py:52
  248.9 198.9 %all-gather.4.cloned.1.call-done = bf16[1024,8192]{1,0:T(8,128)(2,1)} async-done(((bf16[128,8192]{1,0:T(8,128)(2,1)}), bf16[1024,8192]{1,0:T(8,128)(2,1)}) %all-gather.4.cloned.1.call-update) | async-done | bytes 16777232 | tf_op jit(solution)/shard_map/all_gather | solution.py:49
  447.7 11.2 %convolution_convert_fusion = bf16[1024,64]{0,1:T(8,128)(2,1)S(1)} fusion(bf16[1024,8192]{1,0:T(8,128)(2,1)} %all-gather.4.cloned.1.call-done, bf16[8192,64]{0,1:T(8,128)(2,1)} %all-gather.8.cloned.1.call-done), kind=kOutput, calls=%fused_computation.14 | convolution fusion | flops 1073807360 | bytes 17956864 | tf_op jit(solution)/shard_map/dot_general | solution.py:50
  458.9 0.1 reshape.40
  459.0 0.3 constant_dynamic-slice_fusion.2
  459.3 0.1 copy.16
  459.4 3.1 collective-permute-start.1
  462.6 0.0 copy-start.3
  462.6 7.7 constant_dynamic-slice_fusion.3
  470.3 0.1 copy.15
  470.4 0.0 collective-permute-done
  470.4 0.0 collective-permute-done.1
  470.4 0.0 copy-done.3
  470.4 0.0 copy-start
  470.5 6.5 multiply_reduce_fusion
  477.0 0.0 copy-done
  477.0 1.4 fusion.11
  478.4 0.0 copy-start.1
  478.4 1.9 copy-done.1
  480.3 1.5 constant_dynamic-slice_fusion
  481.8 2.7 collective-permute-start.2
  484.5 46.1 %collective-permute-done.2 = f32[8192,64]{0,1:T(8,128)S(1)} collective-permute-done((f32[8192,64]{0,1:T(8,128)}, f32[8192,64]{0,1:T(8,128)S(1)}, u32[]{:S(2)}, u32[]{:S(2)}) %collective-permute-start.2) | collective-permute-done | bytes 2097184 | tf_op jit(solution)/shard_map/ppermute | solution.py:14
  530.6 3.3 dynamic-slice_add_fusion
  533.9 0.0 reduce-scatter.2.cloned.1.call-update
  533.9 102.5 %psum.7 = f32[]{:T(128)} all-reduce(f32[]{:T(128)} %get-tuple-element.8), channel_id=1, replica_groups=mesh['dp'=64,'tensor'=8] {'dp','tensor'}, use_global_device_ids=true, to_apply=%region_3.4 | all-reduce | flops 1 | bytes 8 | tf_op jit(solution)/shard_map/psum | solution.py:73
  637.0 124.9 %reduce-scatter.2.cloned.1.call-done = f32[128,64]{0,1:T(8,128)} async-done(((f32[8192,64]{0,1:T(8,128)}), f32[128,64]{0,1:T(8,128)}) %reduce-scatter.2.cloned.1.call-update) | async-done | bytes 32784 | tf_op jit(solution)/shard_map/reduce_scatter | solution.py:81
  762.0 1.4 multiply_multiply_fusion
  (4 shorter events, 0.1 us)
Async XLA Ops:
  7.2 6.5 copy-start.2
  7.2 125.7 %all-gather.6.cloned.1.call-start = ((), (), s32[]{:S(2)}) async-start(), calls=%async_computation.2 | async-start | bytes 1064960 | tf_op jit(solution)/shard_map/all_gather | solution.py:67
  10.0 238.8 %all-gather.8.cloned.1.call-start = ((), (), s32[]{:S(2)}) async-start(), calls=%async_computation.3 | async-start | bytes 1064960 | tf_op jit(solution)/shard_map/all_gather | solution.py:52
  10.8 437.0 %all-gather.4.cloned.1.call-start = ((), (), s32[]{:S(2)}) async-start(), calls=%async_computation.1 | async-start | bytes 18874368 | tf_op jit(solution)/shard_map/all_gather | solution.py:49
  15.6 746.4 %reduce-scatter.2.cloned.1.call-start = ((), (), s32[]{:S(2)}) async-start(), calls=%async_computation.4 | async-start | bytes 2129920 | tf_op jit(solution)/shard_map/reduce_scatter | solution.py:81
  132.8 337.6 %collective-permute-start = (bf16[8192,64]{0,1:T(8,128)(2,1)}, bf16[8192,64]{0,1:T(8,128)(2,1)S(1)}, u32[]{:S(2)}, u32[]{:S(2)}) collective-permute-start(bf16[8192,64]{0,1:T(8,128)(2,1)} %all-gather.6.cloned.1.call-done), channel_id=1, source_target_pairs={{0,1},{1,0},{2,3},{3,2},{4,5},{5,4},{6,7},{7,6},{8,9},{9,8},{10,11... | collective-permute-start | bytes 3145736 | tf_op jit(solution)/shard_map/ppermute | solution.py:14
  459.4 11.0 %collective-permute-start.1 = (bf16[512,64]{1,0:T(8,128)(2,1)S(1)}, bf16[512,64]{1,0:T(8,128)(2,1)S(1)}, u32[]{:S(2)}, u32[]{:S(2)}) collective-permute-start(bf16[512,64]{1,0:T(8,128)(2,1)S(1)} %bitcast.19), channel_id=1, source_target_pairs={{0,1},{1,0},{2,3},{3,2},{4,5},{5,4},{6,7},{7,6},{8,9},{9,8},{10,11... | collective-permute-start | bytes 196616 | tf_op jit(solution)/shard_map/ppermute | solution.py:14
  462.6 7.9 %copy-start.3 = (bf16[8192,64]{0,1:T(8,128)(2,1)S(1)}, bf16[8192,64]{0,1:T(8,128)(2,1)}, u32[]{:S(2)}) copy-start(bf16[8192,64]{0,1:T(8,128)(2,1)} %all-gather.6.cloned.1.call-done) | copy-start | bytes 3145732
  470.4 6.5 copy-start
  478.4 2.0 copy-start.1
  481.8 48.8 %collective-permute-start.2 = (f32[8192,64]{0,1:T(8,128)}, f32[8192,64]{0,1:T(8,128)S(1)}, u32[]{:S(2)}, u32[]{:S(2)}) collective-permute-start(f32[8192,64]{0,1:T(8,128)} %constant_dynamic-slice_fusion), channel_id=1, source_target_pairs={{0,1},{1,0},{2,3},{3,2},{4,5},{5,4},{6,7},{7,6},{8,9},{9,8},{10,11... | collective-permute-start | bytes 6291464 | tf_op jit(solution)/shard_map/ppermute | solution.py:14
Sparse Core Ops, SparseCore 0:
  10.6 122.1 all-gather.5
  134.9 113.9 all-gather.7
  252.1 195.6 all-gather.3
  534.0 227.8 reduce-scatter.1
where the time goes:
time: 772 us; the launch traced here: 771 us
  waiting for transfers between devices  601 us (78%)
  blocking collectives  102 us (13%)
  matrix products  19.1 us (2%)
  between operations  15.7 us (2%)
  local copies, waits for them, and re-layouts  12.2 us (2%)
  other arithmetic  11.7 us (2%)
  starting transfers between devices  8.74 us (1%)
    all_gather x1, waiting for transfers between devices, shards(): rows_all = lax.all_gather(normed, 'tensor', axis=0, tiled=True)  199 us
    reduce_scatter x1, waiting for transfers between devices, shards(): reduced = lax.psum_scatter(summed, 'dp', scatter_dimension=0, tiled=True)  125 us
    all_gather x1, waiting for transfers between devices, shards(): full_cols = lax.all_gather(masked, 'dp', axis=0, tiled=True)  117 us
    all_gather x1, waiting for transfers between devices, shards(): lax.all_gather(teacher_k, 'dp', axis=0, tiled=True)  113 us
    psum x1, blocking collectives, shards(): total = lax.psum(jnp.sum(diff * diff), ('dp', 'tensor'))  102 us
    ppermute x3, waiting for transfers between devices, from_partner(): return lax.ppermute(block, axis, route)  46.1 us
  transfers between devices with their start and end apart: 7, of which 5 were waited for; matrix products, arithmetic and copies ran while one was open for 3% of the time, Pallas kernels for 0%

commit v1 on v0

v1 whole, which is shorter than its diff:
```python
import jax
import jax.numpy as jnp
from jax import lax
from jax.experimental import pallas as pl
from jax.experimental.pallas import tpu as pltpu
from jax.sharding import Mesh, PartitionSpec as P

F32 = jnp.float32
BF16 = jnp.bfloat16
NZ, NYL, NC, NYH, NX = 16, 2, 2, 2, 4
AXES = ("z", "yl", "core", "yh", "x")
Y = ("yl", "yh")
ZCX = ("z", "core", "x")
D, KVW, TOKENS = 8192, 512, 65536
SHIFT = 34
VMEM = pl.BlockSpec(memory_space=pltpu.VMEM)


def call(kernel, out_shape, *args, scratch=(), flops=0, name=None):
    size = sum(a.size * a.dtype.itemsize for a in args)
    for o in jax.tree.leaves(out_shape):
        size += o.size * o.dtype.itemsize
    return pl.pallas_call(
        kernel,
        out_shape=out_shape,
        in_specs=[VMEM] * len(args),
        out_specs=jax.tree.map(lambda _: VMEM, out_shape),
        scratch_shapes=list(scratch),
        name=name,
        cost_estimate=pl.CostEstimate(flops=flops, bytes_accessed=size, transcendentals=0),
        compiler_params=pltpu.CompilerParams(vmem_limit_bytes=48 * 1024 * 1024),
    )(*args)


def shape(dims, dtype):
    return jax.ShapeDtypeStruct(dims, dtype)


def lane_group(dims):
    return lax.broadcasted_iota(jnp.int32, dims, len(dims) - 1) // 32


def swap_groups(parts, place):
    total = None
    for b, part in enumerate(parts):
        shift = (b - place) * 32 % 128
        moved = pltpu.roll(part, shift, part.ndim - 1) if shift else part
        here = jnp.where(lane_group(part.shape) == b, moved, 0.0)
        total = here if total is None else total + here
    return total


def keep_of(patterns):
    row = lax.broadcasted_iota(jnp.int32, (128, 32), 0)
    col = lax.broadcasted_iota(jnp.int32, (128, 32), 1)
    spread = jnp.where(row // 4 == col, 1.0, 0.0)
    pat = jnp.dot(spread.astype(BF16), patterns.astype(F32).astype(BF16), preferred_element_type=F32)
    first = jnp.where(pat > 2.5, 1.0, 0.0) + jnp.where(pat > 4.5, 1.0, 0.0)
    second = jnp.where(pat < 2.5, pat + 1.0, jnp.where(pat < 3.5, 2.0, 3.0))
    spot = (lax.broadcasted_iota(jnp.int32, pat.shape, 0) % 4).astype(F32)
    return jnp.where((spot == first) | (spot == second), 1.0, 0.0)


def norm_kernel(x_ref, gain_ref, out_ref, rows_ref):
    total = jnp.zeros((128, 512), F32)
    for g in range(16):
        part = x_ref[:, g * 512 : (g + 1) * 512].astype(F32)
        total += part * part
    factor = lax.rsqrt(jnp.sum(total, axis=1, keepdims=True) / D + 1e-05)
    for yl in range(2):
        for m in range(8):
            for half in range(2):
                at = (8 * m + 4 * half + 2 * yl) * 128
                part = x_ref[:, at : at + 256].astype(F32)
                gain = gain_ref[:, at : at + 256].astype(F32)
                tile = yl * 8 + m
                rows_ref[tile * 128 : (tile + 1) * 128, half * 256 : (half + 1) * 256] = (
                    part * factor * gain
                ).astype(BF16)
    src = lax.broadcasted_iota(jnp.int32, (512, 512), 0)
    dst = lax.broadcasted_iota(jnp.int32, (512, 512), 1)
    goal = (src // 32 % 4) * 128 + src // 128 * 32 + src % 32
    move = jnp.where(goal == dst, 1.0, 0.0).astype(BF16)
    for tile in range(16):
        seg = jnp.dot(
            rows_ref[tile * 128 : (tile + 1) * 128, :], move, preferred_element_type=F32
        ).astype(BF16)
        for x in range(NX):
            out_ref[x, :, tile * 128 : (tile + 1) * 128] = seg[:, x * 128 : (x + 1) * 128]


def pack_kernel(teacher_ref, student_ref, pat_ref, out_ref):
    keep = keep_of(pat_ref[...])
    delta = student_ref[...].astype(F32) * keep - teacher_ref[...].astype(F32)
    delta = delta * 2.0**SHIFT
    delta = (delta * jnp.abs(delta)) * (delta * delta)
    row = lax.broadcasted_iota(jnp.int32, (64, 128), 0)
    col = lax.broadcasted_iota(jnp.int32, (64, 128), 1)
    widen = jnp.where(row == col, 1.0, 0.0).astype(BF16)
    wide = jnp.dot(delta.astype(BF16), widen, preferred_element_type=F32).reshape(4, 4, 8, 128)
    for c in range(NC):
        piece = swap_groups([wide[:, q] for q in range(4)], c).reshape(32, 128).astype(BF16)
        for z in range(NZ):
            out_ref[z, c * 32 : (c + 1) * 32, :] = piece


def spread_kernel(got_ref, out_ref, mid_ref):
    got = got_ref[...].astype(F32).reshape(32, 4, 8, 128)
    for q in range(4):
        mid_ref[:, q] = swap_groups([got[:, x] for x in range(NX)], q)
    rows = mid_ref[...].reshape(1024, 128).astype(BF16)
    for y in range(4):
        out_ref[y] = rows


def forward_kernel(own_ref, pair_ref, w_ref, out_ref, high_ref, low_ref):
    for y in range(4):
        for k in range(4):
            sent = w_ref[y, k * 256 : (k + 1) * 256, :].astype(F32)
            size = jnp.sqrt(jnp.sqrt(jnp.abs(sent))) * 2.0**-SHIFT
            delta = jnp.where(sent < 0, -size, size)
            high = delta.astype(BF16)
            at = (y // 2) * 1024 + k * 256
            lane = (y % 2) * 128
            high_ref[at : at + 256, lane : lane + 128] = high
            low_ref[at : at + 256, lane : lane + 128] = (delta - high.astype(F32)).astype(BF16)
    for x in range(NX):
        for ref, row in ((own_ref, 0), (pair_ref, 128)):
            part = jnp.dot(ref[x], high_ref[...], preferred_element_type=F32)
            part += jnp.dot(ref[x], low_ref[...], preferred_element_type=F32)
            out_ref[x, row : row + 128] = part.astype(BF16)


def slope_kernel(part_ref, out_ref, loss_ref):
    diff = part_ref[0].astype(F32)
    for x in range(1, NX):
        diff = diff + part_ref[x].astype(F32)
    slope = diff.astype(BF16)
    for x in range(NX):
        out_ref[x] = slope
    square = diff * diff
    lanes = square[:, :128] + square[:, 128:]
    loss_ref[...] = jnp.sum(lanes.reshape(32, 8, 128), axis=0)


def grad_kernel(own_ref, pair_ref, slope_ref, out_ref):
    contract = (((0,), (0,)), ((), ()))
    own_s = slope_ref[:, :128, :].reshape(512, 256)
    pair_s = slope_ref[:, 128:, :].reshape(512, 256)
    for k in range(8):
        at = k * 256
        own = own_ref[:, :, at : at + 256].reshape(512, 256)
        pair = pair_ref[:, :, at : at + 256].reshape(512, 256)
        term = lax.dot_general(own, own_s, contract, preferred_element_type=F32)
        term += lax.dot_general(pair, pair_s, contract, preferred_element_type=F32)
        term = term.astype(BF16)
        for yh in range(2):
            out_ref[(k // 4) * 2 + yh, (k % 4) * 256 : (k % 4 + 1) * 256, :] = term[
                :, yh * 128 : (yh + 1) * 128
            ]


def gather_kernel(got_ref, out_ref, mid_ref):
    total = got_ref[0].astype(F32)
    for y in range(1, 4):
        total = total + got_ref[y].astype(F32)
    total = total.reshape(32, 4, 8, 128)
    for x in range(NX):
        mid_ref[:, x] = swap_groups([total[:, q] for q in range(4)], x)
    out_ref[...] = mid_ref[...].reshape(1024, 128).astype(BF16)


def final_kernel(got_ref, pat_ref, out_ref, mid_ref):
    total = got_ref[0].astype(F32)
    for z in range(1, NZ):
        total = total + got_ref[z].astype(F32)
    total = total.reshape(2, 4, 8, 128)
    for q in range(4):
        mid_ref[:, q] = swap_groups([total[0], total[1]], q)
    rows = mid_ref[...].reshape(128, 128)[:, :64]
    out_ref[...] = keep_of(pat_ref[...]) * rows / jnp.sqrt(F32(TOKENS))


def shards(hidden, norm_gain, teacher_k, student_k, keep_pattern):
    z, yl, core = (lax.axis_index(a) for a in ("z", "yl", "core"))
    place = (z * NYL + yl) * NC + core
    pat = lax.dynamic_slice_in_dim(keep_pattern, place * 32, 32, 0)

    packed = call(pack_kernel, shape((NZ, 64, 128), BF16), teacher_k, student_k, pat, name="pack")
    got_w = lax.all_to_all(packed.reshape(128, 8, 128), ZCX, 0, 0, tiled=True)

    split = call(
        norm_kernel,
        shape((NX, 128, 2048), BF16),
        hidden,
        norm_gain.reshape(1, D),
        scratch=[pltpu.VMEM((2048, 512), BF16)],
        flops=2 * 2048 * 512 * 512,
        name="norm",
    )
    own = lax.all_to_all(split, "x", 0, 0, tiled=True)
    pair = lax.ppermute(own, "core", [(0, 1), (1, 0)])

    rows_w = call(
        spread_kernel,
        shape((4, 1024, 128), BF16),
        got_w.reshape(1024, 128),
        scratch=[pltpu.VMEM((32, 4, 8, 128), F32)],
        name="spread",
    )
    all_w = lax.all_to_all(rows_w, Y, 0, 0, tiled=True)

    flops = 2 * 1024 * 2048 * 256
    part = call(
        forward_kernel,
        shape((NX, 256, 256), BF16),
        own,
        pair,
        all_w,
        scratch=[pltpu.VMEM((2048, 256), BF16)] * 2,
        flops=2 * flops,
        name="forward",
    )
    got_part = lax.all_to_all(part, "x", 0, 0, tiled=True)
    slope, loss_part = call(
        slope_kernel, (shape((NX, 256, 256), BF16), shape((8, 128), F32)), got_part, name="slope"
    )
    slopes = lax.all_to_all(slope, "x", 0, 0, tiled=True)
    term = call(
        grad_kernel, shape((4, 1024, 128), BF16), own, pair, slopes, flops=flops, name="grad"
    )
    got_term = lax.all_to_all(term, Y, 0, 0, tiled=True)
    packed_term = call(
        gather_kernel,
        shape((1024, 128), BF16),
        got_term,
        scratch=[pltpu.VMEM((32, 4, 8, 128), F32)],
        name="gather",
    )
    got_sum = lax.all_to_all(packed_term.reshape(128, 8, 128), ZCX, 0, 0, tiled=True)
    grad = call(
        final_kernel,
        shape((128, 64), F32),
        got_sum.reshape(NZ, 64, 128),
        pat,
        scratch=[pltpu.VMEM((4, 4, 8, 128), F32)],
        name="final",
    )

    plane = ("yl", "core", "yh", "x")
    loss_plane = lax.all_to_all(
        jnp.broadcast_to(loss_part, (32, 8, 128)), plane, 0, 0, tiled=True
    ).sum(0)
    loss_all = lax.all_to_all(jnp.broadcast_to(loss_plane, (NZ, 8, 128)), "z", 0, 0, tiled=True)
    loss = jnp.sum(loss_all) / (TOKENS * KVW)
    return grad, loss


def solution(mesh):
    fine = Mesh(mesh.devices.reshape(NZ, NYL, NC, NYH, NX), AXES)
    dp, tensor = ("z", "yl", "core"), ("yh", "x")
    in_specs = (P(AXES, None), P(), P(dp, tensor), P(dp, tensor), P(None, tensor))
    out_specs = (P(dp, tensor), P())
    return jax.shard_map(shards, mesh=fine, in_specs=in_specs, out_specs=out_specs, check_vma=False)
```

time: 772 us -> 209 us (0.27)
  waiting for transfers between devices: 601 us -> 49.7 us
  matrix products: 19.1 us -> 0 us
  starting transfers between devices: 8.74 us -> 22.2 us
  between operations: 15.7 us -> 2.59 us
  Pallas kernels: 0 us -> 12.6 us
  other arithmetic: 11.7 us -> 0.65 us
  blocking collectives: 102 us -> 112 us
    all_gather x3 -> x0, waiting for transfers between devices: 429 us -> none  [the longest x1 199 us: shards(): rows_all = lax.all_gather(normed, 'tensor', axis=0, tiled=True)]
    reduce_scatter x1 -> x0, waiting for transfers between devices: 125 us -> none  [shards(): reduced = lax.psum_scatter(summed, 'dp', scatter_dimension=0, tiled=True)]
    all_to_all x0 -> x5, blocking collectives: none -> 112 us  [the longest x1 41.1 us: shards(): got_w = lax.all_to_all(packed.reshape(128, 8, 128), ZCX, 0, 0, tiled=True)]
    psum x1 -> x0, blocking collectives: 102 us -> none  [shards(): total = lax.psum(jnp.sum(diff * diff), ('dp', 'tensor'))]
    all_to_all x0 -> x4, waiting for transfers between devices: none -> 49.7 us  [the longest x1 21 us: shards(): lax.all_to_all(packed_term.reshape(128, 8, 128), ZCX, 0, 0, tiled=True)]
    ppermute x3 -> x1, waiting for transfers between devices: 46.1 us -> 0.01 us  [shards(): pair = lax.ppermute(own, 'core', [(0, 1), (1, 0)])]
    all_to_all x0 -> x4, starting transfers between devices: none -> 20.3 us  [the longest x1 7.53 us: shards(): lax.all_to_all(packed_term.reshape(128, 8, 128), ZCX, 0, 0, tiled=True)]
    dot_general x3 -> x0, matrix products: 19.1 us -> none  [the longest x1 11.2 us: shards(): jnp.dot(rows_all, lax.all_gather(teacher_k, 'dp', axis=0, tiled=True), pr...]
  transfers between devices with their start and end apart: 7 -> 5, of which waited for: 5 -> 4; matrix products, arithmetic and copies ran while one was open for 3% -> 1% of each run, Pallas kernels for 0% -> 2%
where the time goes in v1:
time: 209 us; the launch traced here: 206 us
  blocking collectives  112 us (54%)
  waiting for transfers between devices  49.7 us (24%)
  starting transfers between devices  22.2 us (11%)
  Pallas kernels  12.6 us (6%)
  local copies, waits for them, and re-layouts  5.72 us (3%)
  between operations  2.59 us (1%)
    all_to_all x1, blocking collectives, shards(): got_w = lax.all_to_all(packed.reshape(128, 8, 128), ZCX, 0, 0, tiled=True)  41.1 us
    all_to_all x1, blocking collectives, shards(): own = lax.all_to_all(split, 'x', 0, 0, tiled=True)  28.8 us
    all_to_all x1, waiting for transfers between devices, shards(): lax.all_to_all(packed_term.reshape(128, 8, 128), ZCX, 0, 0, tiled=True)  21 us
    all_to_all x1, blocking collectives, shards(): all_w = lax.all_to_all(rows_w, Y, 0, 0, tiled=True)  17.5 us
    all_to_all x1, waiting for transfers between devices, shards(): got_term = lax.all_to_all(term, Y, 0, 0, tiled=True)  15 us
    all_to_all x1, blocking collectives, shards(): got_part = lax.all_to_all(part, 'x', 0, 0, tiled=True)  14 us
    pallas_call x8, Pallas kernels, call(): pl.pallas_call(kernel, out_shape=out_shape, in_specs=[VMEM] * len(args),...  12.6 us
    all_to_all x1, waiting for transfers between devices, shards(): lax.all_to_all(jnp.broadcast_to(loss_plane, (NZ, 8, 128)), 'z', 0, 0, til...  11.7 us
  transfers between devices with their start and end apart: 5, of which 4 were waited for; matrix products, arithmetic and copies ran while one was open for 1% of the time, Pallas kernels for 2%

profile of v1, /device:TPU:6, one launch (start us, length us, event | category | flops | bytes accessed | tf_op | source)
XLA Modules:
  0.0 205.7 jit_solution(7341066372917154625)
XLA Ops:
  0.6 0.0 copy-start
  0.6 0.8 reshape.19.gain_ref
  1.4 0.0 copy-start.2
  1.5 1.6 copy-done.2
  3.0 1.9 norm.1
  4.9 0.0 copy-start.3
  4.9 0.0 copy-start.4
  4.9 28.8 %all_to_all.45.own_ref = bf16[4,128,2048]{2,1,0:T(8,128)(2,1)S(1)} all-to-all(bf16[4,128,2048]{2,1,0:T(8,128)(2,1)S(1)} %norm.1), channel_id=1, replica_groups=mesh['z'=16,'yl'=2,'core'=2,'yh'=2,'x'=4] {'x'}, dimensions={0} | all-to-all | bytes 4194304 | tf_op jit(solution)/shard_map/all_to_all | solution.py:201
  33.8 1.9 collective-permute-start
  35.7 0.0 copy-done
  35.7 0.1 constant_dynamic-slice_fusion
  35.8 0.1 copy.15.pat_ref
  35.9 0.0 copy-done.3
  35.9 0.1 copy.12.teacher_ref
  36.0 0.0 copy-done.4
  36.0 0.1 copy.13.student_ref
  36.1 0.4 pack.1
  36.5 41.1 %all_to_all.46 = bf16[128,8,128]{2,1,0:T(8,128)(2,1)S(1)} all-to-all(bf16[128,8,128]{2,1,0:T(8,128)(2,1)S(1)} %bitcast.6), channel_id=1, replica_groups=mesh['z'=16,'yl'=2,'core'=2,'yh'=2,'x'=4] {'z','core','x'}, dimensions={0} | all-to-all | bytes 524288 | tf_op jit(solution)/shard_map/all_to_all | solution.py:190
  77.6 0.3 spread.1
  77.9 17.5 %all_to_all.47.w_ref = bf16[4,1024,128]{2,1,0:T(8,128)(2,1)S(1)} all-to-all(bf16[4,1024,128]{2,1,0:T(8,128)(2,1)S(1)} %spread.1), channel_id=1, replica_groups=mesh['z'=16,'yl'=2,'core'=2,'yh'=2,'x'=4] {'yl','yh'}, dimensions={0} | all-to-all | bytes 2097152 | tf_op jit(solution)/shard_map/all_to_all | solution.py:211
  95.4 0.0 collective-permute-done.pair_ref
  95.4 5.6 %forward.1 = bf16[4,256,256]{2,1,0:T(8,128)(2,1)S(1)} custom-call(bf16[4,128,2048]{2,1,0:T(8,128)(2,1)S(1)} %all_to_all.45.own_ref, bf16[4,128,2048]{2,1,0:T(8,128)(2,1)} %collective-permute-done.pair_ref, bf16[4,1024,128]{2,1,0:T(8,128)(2,1)S(1)} %all_to_all.47.w_ref), custom_call_target="tpu_custom_call" | custom-call | flops 2147483648 | bytes 5767168 | tf_op jit(solution)/shard_map/forward/pallas_call | solution.py:23
  101.0 14.0 %all_to_all.48.part_ref = bf16[4,256,256]{2,1,0:T(8,128)(2,1)S(1)} all-to-all(bf16[4,256,256]{2,1,0:T(8,128)(2,1)S(1)} %forward.1), channel_id=1, replica_groups=mesh['z'=16,'yl'=2,'core'=2,'yh'=2,'x'=4] {'x'}, dimensions={0} | all-to-all | bytes 1048576 | tf_op jit(solution)/shard_map/all_to_all | solution.py:224
  115.0 0.1 slope.1
  115.1 10.9 %all_to_all.49.slope_ref = bf16[4,256,256]{2,1,0:T(8,128)(2,1)S(1)} all-to-all(bf16[4,256,256]{2,1,0:T(8,128)(2,1)S(1)} %get-tuple-element.4), channel_id=1, replica_groups=mesh['z'=16,'yl'=2,'core'=2,'yh'=2,'x'=4] {'x'}, dimensions={0} | all-to-all | bytes 1048576 | tf_op jit(solution)/shard_map/all_to_all | solution.py:228
  126.0 0.7 broadcast_in_dim.6
  126.6 5.8 %all-to-all-start.7 = ((f32[32,8,128]{2,1,0:T(8,128)}), f32[32,8,128]{2,1,0:T(8,128)S(1)}, u32[]{:S(2)}, u32[]{:S(2)}) async-start(f32[32,8,128]{2,1,0:T(8,128)} %broadcast_in_dim.6), calls=%async_computation.7 | async-start | bytes 262144 | tf_op jit(solution)/shard_map/all_to_all | solution.py:251
  132.4 2.9 %grad.1 = bf16[4,1024,128]{2,1,0:T(8,128)(2,1)S(1)} custom-call(bf16[4,128,2048]{2,1,0:T(8,128)(2,1)S(1)} %all_to_all.45.own_ref, bf16[4,128,2048]{2,1,0:T(8,128)(2,1)} %collective-permute-done.pair_ref, bf16[4,256,256]{2,1,0:T(8,128)(2,1)S(1)} %all_to_all.49.slope_ref), custom_call_target="tpu_custom_call" | custom-call | flops 1073741824 | bytes 5767168 | tf_op jit(solution)/shard_map/grad/pallas_call | solution.py:23
  135.3 0.0 copy-start.1
  135.4 1.0 copy-done.1
  136.3 2.1 %all-to-all-done.7 = f32[32,8,128]{2,1,0:T(8,128)S(1)} async-done(((f32[32,8,128]{2,1,0:T(8,128)}), f32[32,8,128]{2,1,0:T(8,128)S(1)}, u32[]{:S(2)}, u32[]{:S(2)}) %all-to-all-start.7) | async-done | bytes 131104 | tf_op jit(solution)/shard_map/all_to_all | solution.py:251
  138.4 3.5 %all-to-all-start.5 = ((bf16[4,1024,128]{2,1,0:T(8,128)(2,1)}), bf16[4,1024,128]{2,1,0:T(8,128)(2,1)S(1)}, u32[]{:S(2)}, u32[]{:S(2)}) async-start(bf16[4,1024,128]{2,1,0:T(8,128)(2,1)} %copy-done.1), calls=%async_computation.5 | async-start | bytes 2097152 | tf_op jit(solution)/shard_map/all_to_all | solution.py:232
  142.0 15.0 %all-to-all-done.5.got_ref = bf16[4,1024,128]{2,1,0:T(8,128)(2,1)S(1)} async-done(((bf16[4,1024,128]{2,1,0:T(8,128)(2,1)}), bf16[4,1024,128]{2,1,0:T(8,128)(2,1)S(1)}, u32[]{:S(2)}, u32[]{:S(2)}) %all-to-all-start.5) | async-done | bytes 1048608 | tf_op jit(solution)/shard_map/all_to_all | solution.py:232
  157.0 0.6 broadcast_in_dim.7
  157.6 3.5 %all-to-all-start.8 = ((f32[16,8,128]{2,1,0:T(8,128)}), f32[16,8,128]{2,1,0:T(8,128)S(1)}, u32[]{:S(2)}, u32[]{:S(2)}) async-start(f32[16,8,128]{2,1,0:T(8,128)} %broadcast_in_dim.7), calls=%async_computation.8 | async-start | bytes 131072 | tf_op jit(solution)/shard_map/all_to_all | solution.py:254
  161.1 1.2 gather.1
  162.3 11.7 %all-to-all-done.8 = f32[16,8,128]{2,1,0:T(8,128)S(1)} async-done(((f32[16,8,128]{2,1,0:T(8,128)}), f32[16,8,128]{2,1,0:T(8,128)S(1)}, u32[]{:S(2)}, u32[]{:S(2)}) %all-to-all-start.8) | async-done | bytes 65568 | tf_op jit(solution)/shard_map/all_to_all | solution.py:254
  173.9 7.5 %all-to-all-start.6 = ((bf16[128,8,128]{2,1,0:T(8,128)(2,1)}), bf16[128,8,128]{2,1,0:T(8,128)(2,1)S(1)}, u32[]{:S(2)}, u32[]{:S(2)}) async-start(bf16[128,8,128]{2,1,0:T(8,128)(2,1)} %bitcast.2), calls=%async_computation.6 | async-start | bytes 524288 | tf_op jit(solution)/shard_map/all_to_all | solution.py:240
  181.5 0.6 reduce_sum.19
  182.8 21.0 %all-to-all-done.6 = bf16[128,8,128]{2,1,0:T(8,128)(2,1)S(1)} async-done(((bf16[128,8,128]{2,1,0:T(8,128)(2,1)}), bf16[128,8,128]{2,1,0:T(8,128)(2,1)S(1)}, u32[]{:S(2)}, u32[]{:S(2)}) %all-to-all-start.6) | async-done | bytes 262176 | tf_op jit(solution)/shard_map/all_to_all | solution.py:240
  203.7 0.2 final.1
  203.9 0.7 copy.14
  (1 shorter events, 0.0 us)
Async XLA Ops:
  0.6 35.1 %copy-start = (s32[2048,64]{0,1:T(8,128)S(1)}, s32[2048,64]{0,1:T(8,128)}, u32[]{:S(2)}) copy-start(s32[2048,64]{0,1:T(8,128)} %param.9) | copy-start | bytes 1572868
  1.4 1.6 copy-start.2
  4.9 30.9 %copy-start.3 = (bf16[128,64]{0,1:T(8,128)(2,1)S(1)}, bf16[128,64]{0,1:T(8,128)(2,1)}, u32[]{:S(2)}) copy-start(bf16[128,64]{0,1:T(8,128)(2,1)} %param.7) | copy-start | bytes 49156
  4.9 31.1 %copy-start.4 = (bf16[128,64]{0,1:T(8,128)(2,1)S(1)}, bf16[128,64]{0,1:T(8,128)(2,1)}, u32[]{:S(2)}) copy-start(bf16[128,64]{0,1:T(8,128)(2,1)} %param.8) | copy-start | bytes 49156
  33.8 61.6 %collective-permute-start = (bf16[4,128,2048]{2,1,0:T(8,128)(2,1)S(1)}, bf16[4,128,2048]{2,1,0:T(8,128)(2,1)}, u32[]{:S(2)}, u32[]{:S(2)}) collective-permute-start(bf16[4,128,2048]{2,1,0:T(8,128)(2,1)S(1)} %all_to_all.45.own_ref), channel_id=1, source_target_pairs={{0,8},{8,0},{1,9},{9,1},{2,10},{10,2},{3,11},{11,3},{4,12},{12,4},... | collective-permute-start | bytes 6291464 | tf_op jit(solution)/shard_map/ppermute | solution.py:202
  126.6 11.7 %all-to-all-start.7 = ((f32[32,8,128]{2,1,0:T(8,128)}), f32[32,8,128]{2,1,0:T(8,128)S(1)}, u32[]{:S(2)}, u32[]{:S(2)}) async-start(f32[32,8,128]{2,1,0:T(8,128)} %broadcast_in_dim.6), calls=%async_computation.7 | async-start | bytes 262144 | tf_op jit(solution)/shard_map/all_to_all | solution.py:251
  135.3 1.0 copy-start.1
  138.4 18.6 %all-to-all-start.5 = ((bf16[4,1024,128]{2,1,0:T(8,128)(2,1)}), bf16[4,1024,128]{2,1,0:T(8,128)(2,1)S(1)}, u32[]{:S(2)}, u32[]{:S(2)}) async-start(bf16[4,1024,128]{2,1,0:T(8,128)(2,1)} %copy-done.1), calls=%async_computation.5 | async-start | bytes 2097152 | tf_op jit(solution)/shard_map/all_to_all | solution.py:232
  157.6 16.4 %all-to-all-start.8 = ((f32[16,8,128]{2,1,0:T(8,128)}), f32[16,8,128]{2,1,0:T(8,128)S(1)}, u32[]{:S(2)}, u32[]{:S(2)}) async-start(f32[16,8,128]{2,1,0:T(8,128)} %broadcast_in_dim.7), calls=%async_computation.8 | async-start | bytes 131072 | tf_op jit(solution)/shard_map/all_to_all | solution.py:254
  173.9 29.8 %all-to-all-start.6 = ((bf16[128,8,128]{2,1,0:T(8,128)(2,1)}), bf16[128,8,128]{2,1,0:T(8,128)(2,1)S(1)}, u32[]{:S(2)}, u32[]{:S(2)}) async-start(bf16[128,8,128]{2,1,0:T(8,128)(2,1)} %bitcast.2), calls=%async_computation.6 | async-start | bytes 524288 | tf_op jit(solution)/shard_map/all_to_all | solution.py:240

commit v2 on v1

--- a/solution.py
+++ b/solution.py
@@ -14,6 +14,8 @@
 D, KVW, TOKENS = 8192, 512, 65536
 SHIFT = 34
 VMEM = pl.BlockSpec(memory_space=pltpu.VMEM)
+SMEM = pl.BlockSpec(memory_space=pltpu.SMEM)
+BACK = (0, 3, 2, 1)
 
 
 def call(kernel, out_shape, *args, scratch=(), flops=0, name=None):
@@ -23,7 +25,7 @@
     return pl.pallas_call(
         kernel,
         out_shape=out_shape,
-        in_specs=[VMEM] * len(args),
+        in_specs=[SMEM if a.shape == (1,) else VMEM for a in args],
         out_specs=jax.tree.map(lambda _: VMEM, out_shape),
         scratch_shapes=list(scratch),
         name=name,
@@ -61,7 +63,8 @@
     return jnp.where((spot == first) | (spot == second), 1.0, 0.0)
 
 
-def norm_kernel(x_ref, gain_ref, out_ref, rows_ref):
+def norm_kernel(x_ref, gain_ref, me_ref, *rest):
+    outs, rows_ref = rest[:NX], rest[NX]
     total = jnp.zeros((128, 512), F32)
     for g in range(16):
         part = x_ref[:, g * 512 : (g + 1) * 512].astype(F32)
@@ -79,14 +82,15 @@
                 ).astype(BF16)
     src = lax.broadcasted_iota(jnp.int32, (512, 512), 0)
     dst = lax.broadcasted_iota(jnp.int32, (512, 512), 1)
-    goal = (src // 32 % 4) * 128 + src // 128 * 32 + src % 32
+    ahead = (src // 32 + NX - me_ref[0]) % NX
+    goal = ahead * 128 + src // 128 * 32 + src % 32
     move = jnp.where(goal == dst, 1.0, 0.0).astype(BF16)
     for tile in range(16):
         seg = jnp.dot(
             rows_ref[tile * 128 : (tile + 1) * 128, :], move, preferred_element_type=F32
         ).astype(BF16)
         for x in range(NX):
-            out_ref[x, :, tile * 128 : (tile + 1) * 128] = seg[:, x * 128 : (x + 1) * 128]
+            outs[x][:, tile * 128 : (tile + 1) * 128] = seg[:, x * 128 : (x + 1) * 128]
 
 
 def pack_kernel(teacher_ref, student_ref, pat_ref, out_ref):
@@ -113,7 +117,8 @@
         out_ref[y] = rows
 
 
-def forward_kernel(own_ref, pair_ref, w_ref, out_ref, high_ref, low_ref):
+def forward_kernel(*refs):
+    pieces, (w_ref, me_ref, out_ref, high_ref, low_ref) = refs[: 2 * NX], refs[2 * NX :]
     for y in range(4):
         for k in range(4):
             sent = w_ref[y, k * 256 : (k + 1) * 256, :].astype(F32)
@@ -124,11 +129,20 @@
             lane = (y % 2) * 128
             high_ref[at : at + 256, lane : lane + 128] = high
             low_ref[at : at + 256, lane : lane + 128] = (delta - high.astype(F32)).astype(BF16)
-    for x in range(NX):
-        for ref, row in ((own_ref, 0), (pair_ref, 128)):
-            part = jnp.dot(ref[x], high_ref[...], preferred_element_type=F32)
-            part += jnp.dot(ref[x], low_ref[...], preferred_element_type=F32)
+    for i in range(NX):
+        x = (me_ref[0] + BACK[i]) % NX
+        for ref, row in ((pieces[i], 0), (pieces[NX + i], 128)):
+            part = jnp.dot(ref[...], high_ref[...], preferred_element_type=F32)
+            part += jnp.dot(ref[...], low_ref[...], preferred_element_type=F32)
             out_ref[x, row : row + 128] = part.astype(BF16)
+
+
+def thirds(value, rows):
+    high = value.astype(BF16).astype(F32)
+    mid = (value - high).astype(BF16).astype(F32)
+    low = value - high - mid
+    row = lax.broadcasted_iota(jnp.int32, (rows, value.shape[1]), 0)
+    return jnp.where(row == 0, high, jnp.where(row == 1, mid, jnp.where(row == 2, low, 0.0)))
 
 
 def slope_kernel(part_ref, out_ref, loss_ref):
@@ -139,51 +153,63 @@
     for x in range(NX):
         out_ref[x] = slope
     square = diff * diff
-    lanes = square[:, :128] + square[:, 128:]
-    loss_ref[...] = jnp.sum(lanes.reshape(32, 8, 128), axis=0)
-
-
-def grad_kernel(own_ref, pair_ref, slope_ref, out_ref):
+    loss_ref[...] = jnp.sum(square[:, :128] + square[:, 128:], axis=0, keepdims=True)
+
+
+def grad_kernel(*refs):
+    pieces, (slope_ref, loss_ref, me_ref, out_ref, s_ref) = refs[: 2 * NX], refs[2 * NX :]
     contract = (((0,), (0,)), ((), ()))
-    own_s = slope_ref[:, :128, :].reshape(512, 256)
-    pair_s = slope_ref[:, 128:, :].reshape(512, 256)
+    for i in range(NX):
+        x = (me_ref[0] + BACK[i]) % NX
+        s_ref[i * 128 : (i + 1) * 128] = slope_ref[x, :128]
+        s_ref[512 + i * 128 : 512 + (i + 1) * 128] = slope_ref[x, 128:]
     for k in range(8):
         at = k * 256
-        own = own_ref[:, :, at : at + 256].reshape(512, 256)
-        pair = pair_ref[:, :, at : at + 256].reshape(512, 256)
-        term = lax.dot_general(own, own_s, contract, preferred_element_type=F32)
-        term += lax.dot_general(pair, pair_s, contract, preferred_element_type=F32)
+        rows = jnp.concatenate([p[:, at : at + 256] for p in pieces], axis=0)
+        term = lax.dot_general(rows, s_ref[...], contract, preferred_element_type=F32)
         term = term.astype(BF16)
         for yh in range(2):
             out_ref[(k // 4) * 2 + yh, (k % 4) * 256 : (k % 4 + 1) * 256, :] = term[
                 :, yh * 128 : (yh + 1) * 128
             ]
+    loss = thirds(loss_ref[...], 16).astype(BF16)
+    for y in range(4):
+        out_ref[y, 1024:, :] = loss
 
 
 def gather_kernel(got_ref, out_ref, mid_ref):
     total = got_ref[0].astype(F32)
     for y in range(1, 4):
         total = total + got_ref[y].astype(F32)
-    total = total.reshape(32, 4, 8, 128)
+    loss = jnp.sum(total[1024:], axis=0, keepdims=True)
+    mid_ref[:, :, 8:, :] = jnp.broadcast_to(thirds(loss, 8), (32, 4, 8, 128))
+    total = total[:1024].reshape(32, 4, 8, 128)
     for x in range(NX):
-        mid_ref[:, x] = swap_groups([total[:, q] for q in range(4)], x)
-    out_ref[...] = mid_ref[...].reshape(1024, 128).astype(BF16)
-
-
-def final_kernel(got_ref, pat_ref, out_ref, mid_ref):
+        mid_ref[:, x, :8, :] = swap_groups([total[:, q] for q in range(4)], x)
+    out_ref[...] = mid_ref[...].reshape(128, 16, 128).astype(BF16)
+
+
+def final_kernel(got_ref, pat_ref, out_ref, loss_ref, mid_ref):
     total = got_ref[0].astype(F32)
     for z in range(1, NZ):
         total = total + got_ref[z].astype(F32)
-    total = total.reshape(2, 4, 8, 128)
+    loss = jnp.sum(jnp.sum(total[:, 8:], axis=0), axis=0, keepdims=True)
+    loss_ref[...] = jnp.sum(loss, axis=1, keepdims=True) / (TOKENS * KVW)
+    total = total[:, :8].reshape(2, 4, 8, 128)
     for q in range(4):
         mid_ref[:, q] = swap_groups([total[0], total[1]], q)
     rows = mid_ref[...].reshape(128, 128)[:, :64]
     out_ref[...] = keep_of(pat_ref[...]) * rows / jnp.sqrt(F32(TOKENS))
 
 
+def ring(step):
+    return [(i, (i + step) % NX) for i in range(NX)]
+
+
 def shards(hidden, norm_gain, teacher_k, student_k, keep_pattern):
-    z, yl, core = (lax.axis_index(a) for a in ("z", "yl", "core"))
+    z, yl, core, x = (lax.axis_index(a) for a in ("z", "yl", "core", "x"))
     place = (z * NYL + yl) * NC + core
+    me = x.reshape(1).astype(jnp.int32)
     pat = lax.dynamic_slice_in_dim(keep_pattern, place * 32, 32, 0)
 
     packed = call(pack_kernel, shape((NZ, 64, 128), BF16), teacher_k, student_k, pat, name="pack")
@@ -191,15 +217,16 @@
 
     split = call(
         norm_kernel,
-        shape((NX, 128, 2048), BF16),
+        (shape((128, 2048), BF16),) * NX,
         hidden,
         norm_gain.reshape(1, D),
+        me,
         scratch=[pltpu.VMEM((2048, 512), BF16)],
         flops=2 * 2048 * 512 * 512,
         name="norm",
     )
-    own = lax.all_to_all(split, "x", 0, 0, tiled=True)
-    pair = lax.ppermute(own, "core", [(0, 1), (1, 0)])
+    own = [split[0]] + [lax.ppermute(split[i], "x", ring(i)) for i in range(1, NX)]
+    pair = [lax.ppermute(piece, "core", [(0, 1), (1, 0)]) for piece in own]
 
     rows_w = call(
         spread_kernel,
@@ -214,46 +241,49 @@
     part = call(
         forward_kernel,
         shape((NX, 256, 256), BF16),
-        own,
-        pair,
+        *own,
+        *pair,
         all_w,
+        me,
         scratch=[pltpu.VMEM((2048, 256), BF16)] * 2,
         flops=2 * flops,
         name="forward",
     )
     got_part = lax.all_to_all(part, "x", 0, 0, tiled=True)
     slope, loss_part = call(
-        slope_kernel, (shape((NX, 256, 256), BF16), shape((8, 128), F32)), got_part, name="slope"
+        slope_kernel, (shape((NX, 256, 256), BF16), shape((1, 128), F32)), got_part, name="slope"
     )
     slopes = lax.all_to_all(slope, "x", 0, 0, tiled=True)
     term = call(
-        grad_kernel, shape((4, 1024, 128), BF16), own, pair, slopes, flops=flops, name="grad"
+        grad_kernel,
+        shape((4, 1040, 128), BF16),
+        *own,
+        *pair,
+        slopes,
+        loss_part,
+        me,
+        scratch=[pltpu.VMEM((1024, 256), BF16)],
+        flops=flops,
+        name="grad",
     )
     got_term = lax.all_to_all(term, Y, 0, 0, tiled=True)
     packed_term = call(
         gather_kernel,
-        shape((1024, 128), BF16),
+        shape((128, 16, 128), BF16),
         got_term,
-        scratch=[pltpu.VMEM((32, 4, 8, 128), F32)],
+        scratch=[pltpu.VMEM((32, 4, 16, 128), F32)],
         name="gather",
     )
-    got_sum = lax.all_to_all(packed_term.reshape(128, 8, 128), ZCX, 0, 0, tiled=True)
-    grad = call(
+    got_sum = lax.all_to_all(packed_term, ZCX, 0, 0, tiled=True)
+    grad, loss = call(
         final_kernel,
-        shape((128, 64), F32),
-        got_sum.reshape(NZ, 64, 128),
+        (shape((128, 64), F32), shape((1, 1), F32)),
+        got_sum.reshape(NZ, 8, 16, 128),
         pat,
         scratch=[pltpu.VMEM((4, 4, 8, 128), F32)],
         name="final",
     )
-
-    plane = ("yl", "core", "yh", "x")
-    loss_plane = lax.all_to_all(
-        jnp.broadcast_to(loss_part, (32, 8, 128)), plane, 0, 0, tiled=True
-    ).sum(0)
-    loss_all = lax.all_to_all(jnp.broadcast_to(loss_plane, (NZ, 8, 128)), "z", 0, 0, tiled=True)
-    loss = jnp.sum(loss_all) / (TOKENS * KVW)
-    return grad, loss
+    return grad, loss.reshape(())
 
 
 def solution(mesh):

time: 209 us -> 173 us (0.83)
  waiting for transfers between devices: 49.7 us -> 10.9 us
  blocking collectives: 112 us -> 90.5 us
  starting transfers between devices: 22.2 us -> 40.7 us
  local copies, waits for them, and re-layouts: 5.72 us -> 12.5 us
    all_to_all x4 -> x2, waiting for transfers between devices: 49.7 us -> 8.72 us  [the longest x1 8.72 us: shards(): got_w = lax.all_to_all(packed.reshape(128, 8, 128), ZCX, 0, 0, tiled=True)]
    all_to_all x3 -> x2, blocking collectives: 87.4 us -> 65.6 us  [the longest x1 47.8 us: shards(): got_sum = lax.all_to_all(packed_term, ZCX, 0, 0, tiled=True)]
    ppermute x1 -> x7, starting transfers between devices: 1.91 us -> 16.8 us  [the longest x3 8.65 us: shards(): lax.ppermute(split[i], 'x', ring(i))]
    unnamed x14 -> x28, local copies, waits for them, and re-layouts: 3.56 us -> 12.4 us
    all_to_all x4 -> x2, starting transfers between devices: 20.3 us -> 23.8 us  [the longest x1 19.4 us: shards(): got_w = lax.all_to_all(packed.reshape(128, 8, 128), ZCX, 0, 0, tiled=True)]
    ppermute x1 -> x7, waiting for transfers between devices: 0.01 us -> 2.2 us  [the longest x3 2.19 us: shards(): lax.ppermute(split[i], 'x', ring(i))]
  transfers between devices with their start and end apart: 5 -> 9, of which waited for: 4 -> 2; matrix products, arithmetic and copies ran while one was open for 1% -> 0% of each run, Pallas kernels for 2% -> 3%
where the time goes in v2:
time: 173 us; the launch traced here: 170 us
  blocking collectives  90.5 us (52%)
  starting transfers between devices  40.7 us (24%)
  Pallas kernels  14.4 us (8%)
  local copies, waits for them, and re-layouts  12.5 us (7%)
  waiting for transfers between devices  10.9 us (6%)
    all_to_all x1, blocking collectives, shards(): got_sum = lax.all_to_all(packed_term, ZCX, 0, 0, tiled=True)  47.8 us
    all_to_all x1, starting transfers between devices, shards(): got_w = lax.all_to_all(packed.reshape(128, 8, 128), ZCX, 0, 0, tiled=True)  19.4 us
    all_to_all x1, blocking collectives, shards(): got_term = lax.all_to_all(term, Y, 0, 0, tiled=True)  17.8 us
    pallas_call x8, Pallas kernels, call(): pl.pallas_call(kernel, out_shape=out_shape, in_specs=[SMEM if a.shape ==...  14.4 us
    all_to_all x1, blocking collectives, shards(): got_part = lax.all_to_all(part, 'x', 0, 0, tiled=True)  13.9 us
    unnamed x28, local copies, waits for them, and re-layouts  12.4 us
    all_to_all x1, blocking collectives, shards(): slopes = lax.all_to_all(slope, 'x', 0, 0, tiled=True)  10.9 us
    all_to_all x1, waiting for transfers between devices, shards(): got_w = lax.all_to_all(packed.reshape(128, 8, 128), ZCX, 0, 0, tiled=True)  8.72 us
  transfers between devices with their start and end apart: 9, of which 2 were waited for; matrix products, arithmetic and copies ran while one was open for 0% of the time, Pallas kernels for 3%

profile of v2, /device:TPU:6, one launch (start us, length us, event | category | flops | bytes accessed | tf_op | source)
XLA Modules:
  0.0 169.8 jit_solution(4384481175826480130)
XLA Ops:
  0.6 0.0 copy-start
  0.7 1.0 copy-done
  1.7 0.1 constant_dynamic-slice_fusion
  1.8 0.1 copy.11.pat_ref
  1.8 0.8 copy.8.teacher_ref
  2.7 0.8 copy.9.student_ref
  3.5 1.1 pack.1
  4.6 19.4 %all-to-all-start = ((bf16[128,8,128]{2,1,0:T(8,128)(2,1)}), bf16[128,8,128]{2,1,0:T(8,128)(2,1)S(1)}, u32[]{:S(2)}, u32[]{:S(2)}) async-start(bf16[128,8,128]{2,1,0:T(8,128)(2,1)} %bitcast.1), calls=%async_computation | async-start | bytes 524288 | tf_op jit(solution)/shard_map/all_to_all | solution.py:216
  24.0 0.0 copy-start.10
  24.0 1.6 copy-done.10
  25.6 3.1 %norm.1 = (bf16[128,2048]{1,0:T(8,128)(2,1)S(1)}, bf16[128,2048]{1,0:T(8,128)(2,1)}, bf16[128,2048]{1,0:T(8,128)(2,1)}, bf16[128,2048]{1,0:T(8,128)(2,1)}) custom-call(bf16[128,8192]{1,0:T(8,128)(2,1)S(1)} %copy-done.10, bf16[1,8192]{1,0:T(2,128)(2,1)S(1)} %reshape.22.gain_ref, s32[1]{0:T(128)} %bitcast.me_ref.refs_9_.refs_10_), custom_call_target="tpu_custom_call" | custom-call | flops 1073741824 | bytes 4210692 | tf_op jit(solution)/shard_map/norm/pallas_call | solution.py:25
  28.7 2.8 %collective-permute-start = (bf16[128,2048]{1,0:T(8,128)(2,1)}, bf16[128,2048]{1,0:T(8,128)(2,1)S(1)}, u32[]{:S(2)}, u32[]{:S(2)}) collective-permute-start(bf16[128,2048]{1,0:T(8,128)(2,1)} %get-tuple-element.11), channel_id=1, source_target_pairs={{0,1},{1,2},{2,3},{3,0},{4,5},{5,6},{6,7},{7,4},{8,9},{9,10},{10,1... | collective-permute-start | bytes 1572872 | tf_op jit(solution)/shard_map/ppermute | solution.py:228
  31.5 3.9 %collective-permute-start.1 = (bf16[128,2048]{1,0:T(8,128)(2,1)}, bf16[128,2048]{1,0:T(8,128)(2,1)S(1)}, u32[]{:S(2)}, u32[]{:S(2)}) collective-permute-start(bf16[128,2048]{1,0:T(8,128)(2,1)} %get-tuple-element.12), channel_id=1, source_target_pairs={{0,2},{1,3},{2,0},{3,1},{4,6},{5,7},{6,4},{7,5},{8,10},{9,11},{10,... | collective-permute-start | bytes 1572872 | tf_op jit(solution)/shard_map/ppermute | solution.py:228
  35.5 1.9 %collective-permute-start.2 = (bf16[128,2048]{1,0:T(8,128)(2,1)}, bf16[128,2048]{1,0:T(8,128)(2,1)}, u32[]{:S(2)}, u32[]{:S(2)}) collective-permute-start(bf16[128,2048]{1,0:T(8,128)(2,1)} %get-tuple-element.13), channel_id=1, source_target_pairs={{0,3},{1,0},{2,1},{3,2},{4,7},{5,4},{6,5},{7,6},{8,11},{9,8},{10,9... | collective-permute-start | bytes 1572872 | tf_op jit(solution)/shard_map/ppermute | solution.py:228
  37.4 8.7 %all-to-all-done = bf16[128,8,128]{2,1,0:T(8,128)(2,1)S(1)} async-done(((bf16[128,8,128]{2,1,0:T(8,128)(2,1)}), bf16[128,8,128]{2,1,0:T(8,128)(2,1)S(1)}, u32[]{:S(2)}, u32[]{:S(2)}) %all-to-all-start) | async-done | bytes 262176 | tf_op jit(solution)/shard_map/all_to_all | solution.py:216
  46.1 1.3 spread.1
  47.4 4.5 %all-to-all-start.1 = ((bf16[4,1024,128]{2,1,0:T(8,128)(2,1)}), bf16[4,1024,128]{2,1,0:T(8,128)(2,1)S(1)}, u32[]{:S(2)}, u32[]{:S(2)}) async-start(bf16[4,1024,128]{2,1,0:T(8,128)(2,1)} %spread.1), calls=%async_computation.1 | async-start | bytes 2097152 | tf_op jit(solution)/shard_map/all_to_all | solution.py:238
  51.9 1.9 %collective-permute-start.3 = (bf16[128,2048]{1,0:T(8,128)(2,1)S(1)}, bf16[128,2048]{1,0:T(8,128)(2,1)S(1)}, u32[]{:S(2)}, u32[]{:S(2)}) collective-permute-start(bf16[128,2048]{1,0:T(8,128)(2,1)S(1)} %get-tuple-element.10.refs_0_), channel_id=1, source_target_pairs={{0,8},{8,0},{1,9},{9,1},{2,10},{10,2},{3,11},{11,3},{4,12},{12,4},... | collective-permute-start | bytes 1572872 | tf_op jit(solution)/shard_map/ppermute | solution.py:229
  53.8 0.0 collective-permute-done.refs_1_
  53.8 2.4 %collective-permute-start.4 = (bf16[128,2048]{1,0:T(8,128)(2,1)S(1)}, bf16[128,2048]{1,0:T(8,128)(2,1)S(1)}, u32[]{:S(2)}, u32[]{:S(2)}) collective-permute-start(bf16[128,2048]{1,0:T(8,128)(2,1)S(1)} %collective-permute-done.refs_1_), channel_id=1, source_target_pairs={{0,8},{8,0},{1,9},{9,1},{2,10},{10,2},{3,11},{11,3},{4,12},{12,4},... | collective-permute-start | bytes 1572872 | tf_op jit(solution)/shard_map/ppermute | solution.py:229
  56.3 0.0 collective-permute-done.1.refs_2_
  56.3 1.9 %collective-permute-start.5 = (bf16[128,2048]{1,0:T(8,128)(2,1)S(1)}, bf16[128,2048]{1,0:T(8,128)(2,1)S(1)}, u32[]{:S(2)}, u32[]{:S(2)}) collective-permute-start(bf16[128,2048]{1,0:T(8,128)(2,1)S(1)} %collective-permute-done.1.refs_2_), channel_id=1, source_target_pairs={{0,8},{8,0},{1,9},{9,1},{2,10},{10,2},{3,11},{11,3},{4,12},{12,4},... | collective-permute-start | bytes 1572872 | tf_op jit(solution)/shard_map/ppermute | solution.py:229
  58.2 2.2 %collective-permute-done.2.refs_3_ = bf16[128,2048]{1,0:T(8,128)(2,1)} collective-permute-done((bf16[128,2048]{1,0:T(8,128)(2,1)}, bf16[128,2048]{1,0:T(8,128)(2,1)}, u32[]{:S(2)}, u32[]{:S(2)}) %collective-permute-start.2) | collective-permute-done | bytes 524320 | tf_op jit(solution)/shard_map/ppermute | solution.py:228
  60.4 2.0 %collective-permute-start.6 = (bf16[128,2048]{1,0:T(8,128)(2,1)}, bf16[128,2048]{1,0:T(8,128)(2,1)S(1)}, u32[]{:S(2)}, u32[]{:S(2)}) collective-permute-start(bf16[128,2048]{1,0:T(8,128)(2,1)} %collective-permute-done.2.refs_3_), channel_id=1, source_target_pairs={{0,8},{8,0},{1,9},{9,1},{2,10},{10,2},{3,11},{11,3},{4,12},{12,4},... | collective-permute-start | bytes 1572872 | tf_op jit(solution)/shard_map/ppermute | solution.py:229
  62.3 0.0 collective-permute-done.3.refs_4_
  62.4 0.0 copy-start.1
  62.4 0.8 copy-done.1
  63.2 0.0 collective-permute-done.4.refs_5_
  63.2 0.8 copy-done.3
  63.9 0.0 collective-permute-done.5.refs_6_
  64.0 0.8 copy-done.5
  64.7 0.0 collective-permute-done.6.refs_7_
  64.8 0.8 copy-done.7
  65.5 0.0 all-to-all-done.1.refs_8_
  65.5 1.0 copy-done.2
  66.6 1.0 copy-done.4
  67.6 1.0 copy-done.6
  68.7 1.0 copy-done.8
  69.7 5.1 %forward.1 = bf16[4,256,256]{2,1,0:T(8,128)(2,1)S(1)} custom-call(bf16[128,2048]{1,0:T(8,128)(2,1)S(1)} %get-tuple-element.10.refs_0_, bf16[128,2048]{1,0:T(8,128)(2,1)S(1)} %collective-permute-done.refs_1_, bf16[128,2048]{1,0:T(8,128)(2,1)S(1)} %collective-permute-done.1.refs_2_, bf16[128,2048]{1,0:T(8,128)(2,1)} %collective-permute-done.2.refs_3_, ...), custom_call_target="tpu_custom_call" | custom-call | flops 2147483648 | bytes 5767172 | tf_op jit(solution)/shard_map/forward/pallas_call | solution.py:25
  74.8 13.9 %all_to_all.30.part_ref = bf16[4,256,256]{2,1,0:T(8,128)(2,1)S(1)} all-to-all(bf16[4,256,256]{2,1,0:T(8,128)(2,1)S(1)} %forward.1), channel_id=1, replica_groups=mesh['z'=16,'yl'=2,'core'=2,'yh'=2,'x'=4] {'x'}, dimensions={0} | all-to-all | bytes 1048576 | tf_op jit(solution)/shard_map/all_to_all | solution.py:252
  88.7 0.1 slope.1
  88.8 10.9 %all_to_all.31.refs_8_ = bf16[4,256,256]{2,1,0:T(8,128)(2,1)S(1)} all-to-all(bf16[4,256,256]{2,1,0:T(8,128)(2,1)S(1)} %get-tuple-element.14), channel_id=1, replica_groups=mesh['z'=16,'yl'=2,'core'=2,'yh'=2,'x'=4] {'x'}, dimensions={0} | all-to-all | bytes 1048576 | tf_op jit(solution)/shard_map/all_to_all | solution.py:256
  99.8 2.4 %grad.1 = bf16[4,1040,128]{2,1,0:T(8,128)(2,1)S(1)} custom-call(bf16[128,2048]{1,0:T(8,128)(2,1)S(1)} %get-tuple-element.10.refs_0_, bf16[128,2048]{1,0:T(8,128)(2,1)S(1)} %collective-permute-done.refs_1_, bf16[128,2048]{1,0:T(8,128)(2,1)S(1)} %collective-permute-done.1.refs_2_, bf16[128,2048]{1,0:T(8,128)(2,1)} %collective-permute-done.2.refs_3_, ...), custom_call_target="tpu_custom_call" | custom-call | flops 1073741824 | bytes 5784068 | tf_op jit(solution)/shard_map/grad/pallas_call | solution.py:25
  102.2 17.8 %all_to_all.32.got_ref = bf16[4,1040,128]{2,1,0:T(8,128)(2,1)S(1)} all-to-all(bf16[4,1040,128]{2,1,0:T(8,128)(2,1)S(1)} %grad.1), channel_id=1, replica_groups=mesh['z'=16,'yl'=2,'core'=2,'yh'=2,'x'=4] {'yl','yh'}, dimensions={0} | all-to-all | bytes 2129920 | tf_op jit(solution)/shard_map/all_to_all | solution.py:269
  120.1 0.5 gather.1
  120.6 47.8 %all_to_all.33 = bf16[128,16,128]{2,1,0:T(8,128)(2,1)S(1)} all-to-all(bf16[128,16,128]{2,1,0:T(8,128)(2,1)S(1)} %gather.1), channel_id=1, replica_groups=mesh['z'=16,'yl'=2,'core'=2,'yh'=2,'x'=4] {'z','core','x'}, dimensions={0} | all-to-all | bytes 1048576 | tf_op jit(solution)/shard_map/all_to_all | solution.py:277
  168.4 0.7 final.1
  169.1 0.7 copy.10
  (12 shorter events, 0.0 us)
Async XLA Ops:
  0.6 1.0 copy-start
  0.6 23.3 %copy-start.11 = (bf16[8192]{0:T(1024)(128)(2,1)S(1)}, bf16[8192]{0:T(1024)(128)(2,1)}, u32[]{:S(2)}) copy-start(bf16[8192]{0:T(1024)(128)(2,1)} %param.6) | copy-start | bytes 49156
  4.6 41.5 %all-to-all-start = ((bf16[128,8,128]{2,1,0:T(8,128)(2,1)}), bf16[128,8,128]{2,1,0:T(8,128)(2,1)S(1)}, u32[]{:S(2)}, u32[]{:S(2)}) async-start(bf16[128,8,128]{2,1,0:T(8,128)(2,1)} %bitcast.1), calls=%async_computation | async-start | bytes 524288 | tf_op jit(solution)/shard_map/all_to_all | solution.py:216
  24.0 1.6 copy-start.10
  28.7 25.1 %collective-permute-start = (bf16[128,2048]{1,0:T(8,128)(2,1)}, bf16[128,2048]{1,0:T(8,128)(2,1)S(1)}, u32[]{:S(2)}, u32[]{:S(2)}) collective-permute-start(bf16[128,2048]{1,0:T(8,128)(2,1)} %get-tuple-element.11), channel_id=1, source_target_pairs={{0,1},{1,2},{2,3},{3,0},{4,5},{5,6},{6,7},{7,4},{8,9},{9,10},{10,1... | collective-permute-start | bytes 1572872 | tf_op jit(solution)/shard_map/ppermute | solution.py:228
  31.5 24.7 %collective-permute-start.1 = (bf16[128,2048]{1,0:T(8,128)(2,1)}, bf16[128,2048]{1,0:T(8,128)(2,1)S(1)}, u32[]{:S(2)}, u32[]{:S(2)}) collective-permute-start(bf16[128,2048]{1,0:T(8,128)(2,1)} %get-tuple-element.12), channel_id=1, source_target_pairs={{0,2},{1,3},{2,0},{3,1},{4,6},{5,7},{6,4},{7,5},{8,10},{9,11},{10,... | collective-permute-start | bytes 1572872 | tf_op jit(solution)/shard_map/ppermute | solution.py:228
  35.5 24.9 %collective-permute-start.2 = (bf16[128,2048]{1,0:T(8,128)(2,1)}, bf16[128,2048]{1,0:T(8,128)(2,1)}, u32[]{:S(2)}, u32[]{:S(2)}) collective-permute-start(bf16[128,2048]{1,0:T(8,128)(2,1)} %get-tuple-element.13), channel_id=1, source_target_pairs={{0,3},{1,0},{2,1},{3,2},{4,7},{5,4},{6,5},{7,6},{8,11},{9,8},{10,9... | collective-permute-start | bytes 1572872 | tf_op jit(solution)/shard_map/ppermute | solution.py:228
  47.4 18.1 %all-to-all-start.1 = ((bf16[4,1024,128]{2,1,0:T(8,128)(2,1)}), bf16[4,1024,128]{2,1,0:T(8,128)(2,1)S(1)}, u32[]{:S(2)}, u32[]{:S(2)}) async-start(bf16[4,1024,128]{2,1,0:T(8,128)(2,1)} %spread.1), calls=%async_computation.1 | async-start | bytes 2097152 | tf_op jit(solution)/shard_map/all_to_all | solution.py:238
  51.9 10.4 %collective-permute-start.3 = (bf16[128,2048]{1,0:T(8,128)(2,1)S(1)}, bf16[128,2048]{1,0:T(8,128)(2,1)S(1)}, u32[]{:S(2)}, u32[]{:S(2)}) collective-permute-start(bf16[128,2048]{1,0:T(8,128)(2,1)S(1)} %get-tuple-element.10.refs_0_), channel_id=1, source_target_pairs={{0,8},{8,0},{1,9},{9,1},{2,10},{10,2},{3,11},{11,3},{4,12},{12,4},... | collective-permute-start | bytes 1572872 | tf_op jit(solution)/shard_map/ppermute | solution.py:229
  53.8 9.3 %collective-permute-start.4 = (bf16[128,2048]{1,0:T(8,128)(2,1)S(1)}, bf16[128,2048]{1,0:T(8,128)(2,1)S(1)}, u32[]{:S(2)}, u32[]{:S(2)}) collective-permute-start(bf16[128,2048]{1,0:T(8,128)(2,1)S(1)} %collective-permute-done.refs_1_), channel_id=1, source_target_pairs={{0,8},{8,0},{1,9},{9,1},{2,10},{10,2},{3,11},{11,3},{4,12},{12,4},... | collective-permute-start | bytes 1572872 | tf_op jit(solution)/shard_map/ppermute | solution.py:229
  56.3 7.7 %collective-permute-start.5 = (bf16[128,2048]{1,0:T(8,128)(2,1)S(1)}, bf16[128,2048]{1,0:T(8,128)(2,1)S(1)}, u32[]{:S(2)}, u32[]{:S(2)}) collective-permute-start(bf16[128,2048]{1,0:T(8,128)(2,1)S(1)} %collective-permute-done.1.refs_2_), channel_id=1, source_target_pairs={{0,8},{8,0},{1,9},{9,1},{2,10},{10,2},{3,11},{11,3},{4,12},{12,4},... | collective-permute-start | bytes 1572872 | tf_op jit(solution)/shard_map/ppermute | solution.py:229
  60.4 4.4 %collective-permute-start.6 = (bf16[128,2048]{1,0:T(8,128)(2,1)}, bf16[128,2048]{1,0:T(8,128)(2,1)S(1)}, u32[]{:S(2)}, u32[]{:S(2)}) collective-permute-start(bf16[128,2048]{1,0:T(8,128)(2,1)} %collective-permute-done.2.refs_3_), channel_id=1, source_target_pairs={{0,8},{8,0},{1,9},{9,1},{2,10},{10,2},{3,11},{11,3},{4,12},{12,4},... | collective-permute-start | bytes 1572872 | tf_op jit(solution)/shard_map/ppermute | solution.py:229
  62.4 0.8 copy-start.1
  63.2 0.8 copy-start.3
  64.0 0.8 copy-start.5
  64.7 0.8 copy-start.7
  65.5 1.0 copy-start.2
  66.6 1.0 copy-start.4
  67.6 1.0 copy-start.6
  68.7 1.0 copy-start.8
  74.8 25.0 %copy-start.9 = (bf16[128,2048]{1,0:T(8,128)(2,1)S(1)}, bf16[128,2048]{1,0:T(8,128)(2,1)}, u32[]{:S(2)}) copy-start(bf16[128,2048]{1,0:T(8,128)(2,1)} %copy-done.7) | copy-start | bytes 1572868

commit v3 on v2

--- a/solution.py
+++ b/solution.py
@@ -25,12 +25,12 @@
     return pl.pallas_call(
         kernel,
         out_shape=out_shape,
-        in_specs=[SMEM if a.shape == (1,) else VMEM for a in args],
+        in_specs=[SMEM if a.shape == (3,) else VMEM for a in args],
         out_specs=jax.tree.map(lambda _: VMEM, out_shape),
         scratch_shapes=list(scratch),
         name=name,
         cost_estimate=pl.CostEstimate(flops=flops, bytes_accessed=size, transcendentals=0),
-        compiler_params=pltpu.CompilerParams(vmem_limit_bytes=48 * 1024 * 1024),
+        compiler_params=pltpu.CompilerParams(vmem_limit_bytes=24 * 1024 * 1024),
     )(*args)
 
 
@@ -52,19 +52,29 @@
     return total
 
 
-def keep_of(patterns):
-    row = lax.broadcasted_iota(jnp.int32, (128, 32), 0)
-    col = lax.broadcasted_iota(jnp.int32, (128, 32), 1)
-    spread = jnp.where(row // 4 == col, 1.0, 0.0)
-    pat = jnp.dot(spread.astype(BF16), patterns.astype(F32).astype(BF16), preferred_element_type=F32)
+def kept_rows(pat):
     first = jnp.where(pat > 2.5, 1.0, 0.0) + jnp.where(pat > 4.5, 1.0, 0.0)
     second = jnp.where(pat < 2.5, pat + 1.0, jnp.where(pat < 3.5, 2.0, 3.0))
-    spot = (lax.broadcasted_iota(jnp.int32, pat.shape, 0) % 4).astype(F32)
-    return jnp.where((spot == first) | (spot == second), 1.0, 0.0)
-
-
-def norm_kernel(x_ref, gain_ref, me_ref, *rest):
-    outs, rows_ref = rest[:NX], rest[NX]
+    return first, second
+
+
+def per_row(patterns):
+    row = lax.broadcasted_iota(jnp.int32, (32, 128), 0)
+    col = lax.broadcasted_iota(jnp.int32, (32, 128), 1)
+    spread = jnp.where(col // 4 == row, 1.0, 0.0).astype(BF16)
+    pat = jnp.dot(patterns.astype(F32).astype(BF16), spread, preferred_element_type=F32)
+    first, second = kept_rows(pat)
+    spot = (lax.broadcasted_iota(jnp.int32, pat.shape, 1) % 4).astype(F32)
+    return first, second, spot
+
+
+def shuffled(place):
+    return place % 4 * 8 + place // 4
+
+
+def norm_kernel(x_ref, gain_ref, pat_ref, at_ref, *rest):
+    outs, rows_ref, pick_ref = rest[:NX], rest[NX], rest[NX + 1]
+    me, core, own_yl = at_ref[0], at_ref[1], at_ref[2]
     total = jnp.zeros((128, 512), F32)
     for g in range(16):
         part = x_ref[:, g * 512 : (g + 1) * 512].astype(F32)
@@ -82,26 +92,47 @@
                 ).astype(BF16)
     src = lax.broadcasted_iota(jnp.int32, (512, 512), 0)
     dst = lax.broadcasted_iota(jnp.int32, (512, 512), 1)
-    ahead = (src // 32 + NX - me_ref[0]) % NX
-    goal = ahead * 128 + src // 128 * 32 + src % 32
+    ahead = (src // 32 + NX - me) % NX
+    goal = ahead * 128 + src // 128 * 32 + shuffled(src % 32)
     move = jnp.where(goal == dst, 1.0, 0.0).astype(BF16)
     for tile in range(16):
         seg = jnp.dot(
             rows_ref[tile * 128 : (tile + 1) * 128, :], move, preferred_element_type=F32
         ).astype(BF16)
         for x in range(NX):
-            outs[x][:, tile * 128 : (tile + 1) * 128] = seg[:, x * 128 : (x + 1) * 128]
+            outs[x][:128, tile * 128 : (tile + 1) * 128] = seg[:, x * 128 : (x + 1) * 128]
+    col = lax.broadcasted_iota(jnp.int32, (64, 128), 0)
+    lane = lax.broadcasted_iota(jnp.int32, (64, 128), 1)
+    pick = jnp.where((col - core * 32 == lane - me * 32) & (lane // 32 == me), 1.0, 0.0)
+    chosen = lax.dot_general(
+        pat_ref[...].astype(F32).astype(BF16),
+        pick.astype(BF16),
+        (((0,), (0,)), ((), ())),
+        preferred_element_type=F32,
+    )
+    pick_ref[...] = chosen.reshape(NZ, NYL, NC, NX, 8, 128)
+    for x in range(NX):
+        rows = pick_ref[:, own_yl, :, (me + x) % NX].reshape(256, 128).astype(BF16)
+        for tile in range(16):
+            outs[x][128:, tile * 128 : (tile + 1) * 128] = rows[tile * 16 : (tile + 1) * 16]
 
 
 def pack_kernel(teacher_ref, student_ref, pat_ref, out_ref):
-    keep = keep_of(pat_ref[...])
+    first, second, spot = per_row(pat_ref[...])
+    keep = jnp.where((spot == first) | (spot == second), 1.0, 0.0)
     delta = student_ref[...].astype(F32) * keep - teacher_ref[...].astype(F32)
     delta = delta * 2.0**SHIFT
-    delta = (delta * jnp.abs(delta)) * (delta * delta)
+    delta = ((delta * jnp.abs(delta)) * (delta * delta)).astype(BF16)
     row = lax.broadcasted_iota(jnp.int32, (64, 128), 0)
     col = lax.broadcasted_iota(jnp.int32, (64, 128), 1)
     widen = jnp.where(row == col, 1.0, 0.0).astype(BF16)
-    wide = jnp.dot(delta.astype(BF16), widen, preferred_element_type=F32).reshape(4, 4, 8, 128)
+    rows = lax.dot_general(
+        delta, widen, (((0,), (0,)), ((), ())), preferred_element_type=F32
+    ).astype(BF16)
+    dst = lax.broadcasted_iota(jnp.int32, (128, 128), 0)
+    src = lax.broadcasted_iota(jnp.int32, (128, 128), 1)
+    move = jnp.where(src // 32 * 32 + shuffled(src % 32) == dst, 1.0, 0.0).astype(BF16)
+    wide = jnp.dot(move, rows, preferred_element_type=F32).reshape(4, 4, 8, 128)
     for c in range(NC):
         piece = swap_groups([wide[:, q] for q in range(4)], c).reshape(32, 128).astype(BF16)
         for z in range(NZ):
@@ -132,8 +163,8 @@
     for i in range(NX):
         x = (me_ref[0] + BACK[i]) % NX
         for ref, row in ((pieces[i], 0), (pieces[NX + i], 128)):
-            part = jnp.dot(ref[...], high_ref[...], preferred_element_type=F32)
-            part += jnp.dot(ref[...], low_ref[...], preferred_element_type=F32)
+            part = jnp.dot(ref[:128, :], high_ref[...], preferred_element_type=F32)
+            part += jnp.dot(ref[:128, :], low_ref[...], preferred_element_type=F32)
             out_ref[x, row : row + 128] = part.astype(BF16)
 
 
@@ -157,7 +188,7 @@
 
 
 def grad_kernel(*refs):
-    pieces, (slope_ref, loss_ref, me_ref, out_ref, s_ref) = refs[: 2 * NX], refs[2 * NX :]
+    pieces, (slope_ref, loss_ref, me_ref, out_ref, pat_ref, s_ref) = refs[: 2 * NX], refs[2 * NX :]
     contract = (((0,), (0,)), ((), ()))
     for i in range(NX):
         x = (me_ref[0] + BACK[i]) % NX
@@ -165,7 +196,7 @@
         s_ref[512 + i * 128 : 512 + (i + 1) * 128] = slope_ref[x, 128:]
     for k in range(8):
         at = k * 256
-        rows = jnp.concatenate([p[:, at : at + 256] for p in pieces], axis=0)
+        rows = jnp.concatenate([p[:128, at : at + 256] for p in pieces], axis=0)
         term = lax.dot_general(rows, s_ref[...], contract, preferred_element_type=F32)
         term = term.astype(BF16)
         for yh in range(2):
@@ -175,31 +206,61 @@
     loss = thirds(loss_ref[...], 16).astype(BF16)
     for y in range(4):
         out_ref[y, 1024:, :] = loss
-
-
-def gather_kernel(got_ref, out_ref, mid_ref):
+    for tile in range(16):
+        pat = pieces[0][128:, tile * 128 : (tile + 1) * 128].astype(F32)
+        for i in range(1, NX):
+            pat += pieces[i][128:, tile * 128 : (tile + 1) * 128].astype(F32)
+        pat_ref[tile * 16 : (tile + 1) * 16, :] = pat.astype(BF16)
+
+
+def gather_kernel(got_ref, pat_ref, out_ref, mid_ref):
     total = got_ref[0].astype(F32)
     for y in range(1, 4):
         total = total + got_ref[y].astype(F32)
     loss = jnp.sum(total[1024:], axis=0, keepdims=True)
-    mid_ref[:, :, 8:, :] = jnp.broadcast_to(thirds(loss, 8), (32, 4, 8, 128))
+    loss = thirds(jnp.broadcast_to(jnp.sum(loss, axis=1, keepdims=True), (1, 128)), 8)
+    row = lax.broadcasted_iota(jnp.int32, (8, 128), 0)
+    lane = lax.broadcasted_iota(jnp.int32, (8, 128), 1)
+    loss = jnp.where(lane == 64 + row, loss, 0.0)
     total = total[:1024].reshape(32, 4, 8, 128)
+    first, second = kept_rows(pat_ref[...].astype(F32).reshape(32, 8, 128))
+    kept = [jnp.zeros_like(first), jnp.zeros_like(first)]
+    for k in range(4):
+        for i, which in enumerate((first, second)):
+            kept[i] += jnp.where(which == k, total[:, k], 0.0)
+    group = lane_group((32, 8, 128))
     for x in range(NX):
-        mid_ref[:, x, :8, :] = swap_groups([total[:, q] for q in range(4)], x)
-    out_ref[...] = mid_ref[...].reshape(128, 16, 128).astype(BF16)
-
-
-def final_kernel(got_ref, pat_ref, out_ref, loss_ref, mid_ref):
+        one = pltpu.roll(kept[0], (4 - x) % 4 * 32, 2)
+        two = pltpu.roll(kept[1], (5 - x) % 4 * 32, 2)
+        mid_ref[:, x] = jnp.where(group == 0, one, jnp.where(group == 1, two, loss[None]))
+    out_ref[...] = mid_ref[...].reshape(1024, 128).astype(BF16)
+
+
+def final_kernel(got_ref, pat_ref, out_ref, loss_ref):
     total = got_ref[0].astype(F32)
     for z in range(1, NZ):
         total = total + got_ref[z].astype(F32)
-    loss = jnp.sum(jnp.sum(total[:, 8:], axis=0), axis=0, keepdims=True)
-    loss_ref[...] = jnp.sum(loss, axis=1, keepdims=True) / (TOKENS * KVW)
-    total = total[:, :8].reshape(2, 4, 8, 128)
-    for q in range(4):
-        mid_ref[:, q] = swap_groups([total[0], total[1]], q)
-    rows = mid_ref[...].reshape(128, 128)[:, :64]
-    out_ref[...] = keep_of(pat_ref[...]) * rows / jnp.sqrt(F32(TOKENS))
+    loss = jnp.where(lane_group(total.shape) == 2, total, 0.0)
+    loss = jnp.sum(jnp.sum(loss, axis=0, keepdims=True), axis=1, keepdims=True)
+    loss_ref[...] = loss / (TOKENS * KVW)
+    one, two = total[:32], total[32:]
+    group = lane_group((32, 128))
+    near = jnp.where(group == 0, one, pltpu.roll(two, 32, 1))
+    far = jnp.where(group == 2, pltpu.roll(one, 32, 1), pltpu.roll(two, 64, 1))
+    kept = jnp.where(group < 2, near, far)
+    row = lax.broadcasted_iota(jnp.int32, (32, 128), 0)
+    col = lax.broadcasted_iota(jnp.int32, (32, 128), 1)
+    spread = jnp.where(col // 4 == row, 1.0, 0.0).astype(BF16)
+    wide = jnp.zeros((128, 128), F32)
+    for _ in range(3):
+        part = kept.astype(BF16)
+        kept = kept - part.astype(F32)
+        wide += lax.dot_general(
+            part, spread, (((0,), (0,)), ((), ())), preferred_element_type=F32
+        )
+    first, second, spot = per_row(pat_ref[...])
+    grad = jnp.where(spot == first, wide[:64], 0.0) + jnp.where(spot == second, wide[64:], 0.0)
+    out_ref[...] = grad / jnp.sqrt(F32(TOKENS))
 
 
 def ring(step):
@@ -209,19 +270,23 @@
 def shards(hidden, norm_gain, teacher_k, student_k, keep_pattern):
     z, yl, core, x = (lax.axis_index(a) for a in ("z", "yl", "core", "x"))
     place = (z * NYL + yl) * NC + core
-    me = x.reshape(1).astype(jnp.int32)
-    pat = lax.dynamic_slice_in_dim(keep_pattern, place * 32, 32, 0)
-
-    packed = call(pack_kernel, shape((NZ, 64, 128), BF16), teacher_k, student_k, pat, name="pack")
+    at = jnp.stack([x, core, yl]).astype(jnp.int32)
+    patterns = keep_pattern.T
+    pat = lax.dynamic_slice_in_dim(patterns, place * 32, 32, 1)
+
+    packed = call(
+        pack_kernel, shape((NZ, 64, 128), BF16), teacher_k.T, student_k.T, pat, name="pack"
+    )
     got_w = lax.all_to_all(packed.reshape(128, 8, 128), ZCX, 0, 0, tiled=True)
 
     split = call(
         norm_kernel,
-        (shape((128, 2048), BF16),) * NX,
+        (shape((144, 2048), BF16),) * NX,
         hidden,
         norm_gain.reshape(1, D),
-        me,
-        scratch=[pltpu.VMEM((2048, 512), BF16)],
+        patterns,
+        at,
+        scratch=[pltpu.VMEM((2048, 512), BF16), pltpu.VMEM((NZ, NYL, NC, NX, 8, 128), F32)],
         flops=2 * 2048 * 512 * 512,
         name="norm",
     )
@@ -244,7 +309,7 @@
         *own,
         *pair,
         all_w,
-        me,
+        at,
         scratch=[pltpu.VMEM((2048, 256), BF16)] * 2,
         flops=2 * flops,
         name="forward",
@@ -254,14 +319,14 @@
         slope_kernel, (shape((NX, 256, 256), BF16), shape((1, 128), F32)), got_part, name="slope"
     )
     slopes = lax.all_to_all(slope, "x", 0, 0, tiled=True)
-    term = call(
+    term, pat_x = call(
         grad_kernel,
-        shape((4, 1040, 128), BF16),
+        (shape((4, 1040, 128), BF16), shape((256, 128), BF16)),
         *own,
         *pair,
         slopes,
         loss_part,
-        me,
+        at,
         scratch=[pltpu.VMEM((1024, 256), BF16)],
         flops=flops,
         name="grad",
@@ -269,21 +334,21 @@
     got_term = lax.all_to_all(term, Y, 0, 0, tiled=True)
     packed_term = call(
         gather_kernel,
-        shape((128, 16, 128), BF16),
+        shape((1024, 128), BF16),
         got_term,
-        scratch=[pltpu.VMEM((32, 4, 16, 128), F32)],
+        pat_x,
+        scratch=[pltpu.VMEM((32, 4, 8, 128), F32)],
         name="gather",
     )
-    got_sum = lax.all_to_all(packed_term, ZCX, 0, 0, tiled=True)
+    got_sum = lax.all_to_all(packed_term.reshape(128, 8, 128), ZCX, 0, 0, tiled=True)
     grad, loss = call(
         final_kernel,
-        (shape((128, 64), F32), shape((1, 1), F32)),
-        got_sum.reshape(NZ, 8, 16, 128),
+        (shape((64, 128), F32), shape((1, 1), F32)),
+        got_sum.reshape(NZ, 64, 128),
         pat,
-        scratch=[pltpu.VMEM((4, 4, 8, 128), F32)],
         name="final",
     )
-    return grad, loss.reshape(())
+    return grad.T, loss.reshape(())
 
 
 def solution(mesh):

time: 173 us -> 166 us (0.960)
  the two profiles are of different devices: /device:TPU:6 before, /device:TPU:1 now
where the time goes in v3:
time: 166 us; the launch traced here: 165 us
  blocking collectives  80.1 us (48%)
  starting transfers between devices  44.4 us (27%)
  Pallas kernels  14.5 us (9%)
  local copies, waits for them, and re-layouts  13.2 us (8%)
  waiting for transfers between devices  12 us (7%)
    all_to_all x1, blocking collectives, shards(): lax.all_to_all(packed_term.reshape(128, 8, 128), ZCX, 0, 0, tiled=True)  40 us
    all_to_all x1, starting transfers between devices, shards(): got_w = lax.all_to_all(packed.reshape(128, 8, 128), ZCX, 0, 0, tiled=True)  20.4 us
    all_to_all x1, blocking collectives, shards(): got_term = lax.all_to_all(term, Y, 0, 0, tiled=True)  16.9 us
    pallas_call x8, Pallas kernels, call(): pl.pallas_call(kernel, out_shape=out_shape, in_specs=[SMEM if a.shape ==...  14.5 us
    all_to_all x1, blocking collectives, shards(): got_part = lax.all_to_all(part, 'x', 0, 0, tiled=True)  12.5 us
    unnamed x32, local copies, waits for them, and re-layouts  11.6 us
    all_to_all x1, blocking collectives, shards(): slopes = lax.all_to_all(slope, 'x', 0, 0, tiled=True)  10.8 us
    ppermute x3, starting transfers between devices, shards(): lax.ppermute(split[i], 'x', ring(i))  10.7 us
  transfers between devices with their start and end apart: 9, of which 2 were waited for; matrix products, arithmetic and copies ran while one was open for 0% of the time, Pallas kernels for 3%

profile of v3, /device:TPU:1, one launch (start us, length us, event | category | flops | bytes accessed | tf_op | source)
XLA Modules:
  0.0 165.1 jit_solution(16295218088565352795)
XLA Ops:
  0.6 0.8 dynamic-slice_bitcast_fusion.pat_ref
  1.5 0.7 copy-done.12
  2.2 0.7 copy-done.13
  2.9 1.3 pack.1
  4.2 20.4 %all-to-all-start = ((bf16[128,8,128]{2,1,0:T(8,128)(2,1)}), bf16[128,8,128]{2,1,0:T(8,128)(2,1)S(1)}, u32[]{:S(2)}, u32[]{:S(2)}) async-start(bf16[128,8,128]{2,1,0:T(8,128)(2,1)} %bitcast.7), calls=%async_computation | async-start | bytes 524288 | tf_op jit(solution)/shard_map/all_to_all | solution.py:280
  24.6 0.7 reshape.22.gain_ref
  25.3 0.1 pad_add_fusion.at_ref.refs_9_.refs_10_
  25.4 1.0 copy-done.14
  26.5 1.6 copy-done.15
  28.0 4.0 %norm.1 = (bf16[144,2048]{1,0:T(8,128)(2,1)S(1)}, bf16[144,2048]{1,0:T(8,128)(2,1)}, bf16[144,2048]{1,0:T(8,128)(2,1)}, bf16[144,2048]{1,0:T(8,128)(2,1)}) custom-call(bf16[128,8192]{1,0:T(8,128)(2,1)S(1)} %copy-done.15, bf16[1,8192]{1,0:T(2,128)(2,1)S(1)} %reshape.22.gain_ref, s32[64,2048]{1,0:T(8,128)S(1)} %bitcast.19, ...), custom_call_target="tpu_custom_call" | custom-call | flops 1073741824 | bytes 4997132 | tf_op jit(solution)/shard_map/norm/pallas_call | solution.py:25
  32.0 3.3 %collective-permute-start = (bf16[144,2048]{1,0:T(8,128)(2,1)}, bf16[144,2048]{1,0:T(8,128)(2,1)S(1)}, u32[]{:S(2)}, u32[]{:S(2)}) collective-permute-start(bf16[144,2048]{1,0:T(8,128)(2,1)} %get-tuple-element.13), channel_id=1, source_target_pairs={{0,1},{1,2},{2,3},{3,0},{4,5},{5,6},{6,7},{7,4},{8,9},{9,10},{10,1... | collective-permute-start | bytes 1769480 | tf_op jit(solution)/shard_map/ppermute | solution.py:293
  35.3 4.3 %collective-permute-start.1 = (bf16[144,2048]{1,0:T(8,128)(2,1)}, bf16[144,2048]{1,0:T(8,128)(2,1)S(1)}, u32[]{:S(2)}, u32[]{:S(2)}) collective-permute-start(bf16[144,2048]{1,0:T(8,128)(2,1)} %get-tuple-element.14), channel_id=1, source_target_pairs={{0,2},{1,3},{2,0},{3,1},{4,6},{5,7},{6,4},{7,5},{8,10},{9,11},{10,... | collective-permute-start | bytes 1769480 | tf_op jit(solution)/shard_map/ppermute | solution.py:293
  39.6 3.1 %collective-permute-start.2 = (bf16[144,2048]{1,0:T(8,128)(2,1)}, bf16[144,2048]{1,0:T(8,128)(2,1)S(1)}, u32[]{:S(2)}, u32[]{:S(2)}) collective-permute-start(bf16[144,2048]{1,0:T(8,128)(2,1)} %get-tuple-element.15), channel_id=1, source_target_pairs={{0,3},{1,0},{2,1},{3,2},{4,7},{5,4},{6,5},{7,6},{8,11},{9,8},{10,9... | collective-permute-start | bytes 1769480 | tf_op jit(solution)/shard_map/ppermute | solution.py:293
  42.7 5.5 %all-to-all-done = bf16[128,8,128]{2,1,0:T(8,128)(2,1)S(1)} async-done(((bf16[128,8,128]{2,1,0:T(8,128)(2,1)}), bf16[128,8,128]{2,1,0:T(8,128)(2,1)S(1)}, u32[]{:S(2)}, u32[]{:S(2)}) %all-to-all-start) | async-done | bytes 262176 | tf_op jit(solution)/shard_map/all_to_all | solution.py:280
  48.2 1.3 spread.1
  49.5 4.2 %all-to-all-start.1 = ((bf16[4,1024,128]{2,1,0:T(8,128)(2,1)}), bf16[4,1024,128]{2,1,0:T(8,128)(2,1)S(1)}, u32[]{:S(2)}, u32[]{:S(2)}) async-start(bf16[4,1024,128]{2,1,0:T(8,128)(2,1)} %spread.1), calls=%async_computation.1 | async-start | bytes 2097152 | tf_op jit(solution)/shard_map/all_to_all | solution.py:303
  53.6 1.9 %collective-permute-start.3 = (bf16[144,2048]{1,0:T(8,128)(2,1)S(1)}, bf16[144,2048]{1,0:T(8,128)(2,1)S(1)}, u32[]{:S(2)}, u32[]{:S(2)}) collective-permute-start(bf16[144,2048]{1,0:T(8,128)(2,1)S(1)} %get-tuple-element.12.refs_0_), channel_id=1, source_target_pairs={{0,8},{8,0},{1,9},{9,1},{2,10},{10,2},{3,11},{11,3},{4,12},{12,4},... | collective-permute-start | bytes 1769480 | tf_op jit(solution)/shard_map/ppermute | solution.py:294
  55.5 0.0 collective-permute-done.refs_1_
  55.6 2.4 %collective-permute-start.4 = (bf16[144,2048]{1,0:T(8,128)(2,1)S(1)}, bf16[144,2048]{1,0:T(8,128)(2,1)S(1)}, u32[]{:S(2)}, u32[]{:S(2)}) collective-permute-start(bf16[144,2048]{1,0:T(8,128)(2,1)S(1)} %collective-permute-done.refs_1_), channel_id=1, source_target_pairs={{0,8},{8,0},{1,9},{9,1},{2,10},{10,2},{3,11},{11,3},{4,12},{12,4},... | collective-permute-start | bytes 1769480 | tf_op jit(solution)/shard_map/ppermute | solution.py:294
  58.0 6.5 %collective-permute-done.1.refs_2_ = bf16[144,2048]{1,0:T(8,128)(2,1)S(1)} collective-permute-done((bf16[144,2048]{1,0:T(8,128)(2,1)}, bf16[144,2048]{1,0:T(8,128)(2,1)S(1)}, u32[]{:S(2)}, u32[]{:S(2)}) %collective-permute-start.1) | collective-permute-done | bytes 589856 | tf_op jit(solution)/shard_map/ppermute | solution.py:293
  64.5 2.9 %collective-permute-start.5 = (bf16[144,2048]{1,0:T(8,128)(2,1)S(1)}, bf16[144,2048]{1,0:T(8,128)(2,1)S(1)}, u32[]{:S(2)}, u32[]{:S(2)}) collective-permute-start(bf16[144,2048]{1,0:T(8,128)(2,1)S(1)} %collective-permute-done.1.refs_2_), channel_id=1, source_target_pairs={{0,8},{8,0},{1,9},{9,1},{2,10},{10,2},{3,11},{11,3},{4,12},{12,4},... | collective-permute-start | bytes 1769480 | tf_op jit(solution)/shard_map/ppermute | solution.py:294
  67.4 0.0 collective-permute-done.2.refs_3_
  67.5 1.9 %collective-permute-start.6 = (bf16[144,2048]{1,0:T(8,128)(2,1)S(1)}, bf16[144,2048]{1,0:T(8,128)(2,1)S(1)}, u32[]{:S(2)}, u32[]{:S(2)}) collective-permute-start(bf16[144,2048]{1,0:T(8,128)(2,1)S(1)} %collective-permute-done.2.refs_3_), channel_id=1, source_target_pairs={{0,8},{8,0},{1,9},{9,1},{2,10},{10,2},{3,11},{11,3},{4,12},{12,4},... | collective-permute-start | bytes 1769480 | tf_op jit(solution)/shard_map/ppermute | solution.py:294
  69.4 0.0 collective-permute-done.3.refs_4_
  69.4 0.0 copy-start
  69.4 0.8 copy-done
  70.2 0.0 collective-permute-done.4.refs_5_
  70.2 0.8 copy-done.3
  71.0 0.0 collective-permute-done.5.refs_6_
  71.0 0.8 copy-done.6
  71.9 0.0 collective-permute-done.6.refs_7_
  71.9 0.8 copy-done.9
  72.7 0.0 all-to-all-done.1.refs_8_
  72.7 1.1 copy-done.1
  73.8 1.1 copy-done.4
  74.8 1.1 copy-done.7
  75.9 1.1 copy-done.10
  77.0 4.6 %forward.1 = bf16[4,256,256]{2,1,0:T(8,128)(2,1)S(1)} custom-call(bf16[144,2048]{1,0:T(8,128)(2,1)S(1)} %get-tuple-element.12.refs_0_, bf16[144,2048]{1,0:T(8,128)(2,1)S(1)} %collective-permute-done.refs_1_, bf16[144,2048]{1,0:T(8,128)(2,1)S(1)} %collective-permute-done.1.refs_2_, bf16[144,2048]{1,0:T(8,128)(2,1)S(1)} %collective-permute-done.2.refs_3_, ...), custom_call_target="tpu_custom_call" | custom-call | flops 2147483648 | bytes 6291468 | tf_op jit(solution)/shard_map/forward/pallas_call | solution.py:25
  81.6 0.0 copy-start.2
  81.6 12.5 %all_to_all.30.part_ref = bf16[4,256,256]{2,1,0:T(8,128)(2,1)S(1)} all-to-all(bf16[4,256,256]{2,1,0:T(8,128)(2,1)S(1)} %forward.1), channel_id=1, replica_groups=mesh['z'=16,'yl'=2,'core'=2,'yh'=2,'x'=4] {'x'}, dimensions={0} | all-to-all | bytes 1048576 | tf_op jit(solution)/shard_map/all_to_all | solution.py:317
  94.1 0.1 slope.1
  94.2 10.8 %all_to_all.31.refs_8_ = bf16[4,256,256]{2,1,0:T(8,128)(2,1)S(1)} all-to-all(bf16[4,256,256]{2,1,0:T(8,128)(2,1)S(1)} %get-tuple-element.16), channel_id=1, replica_groups=mesh['z'=16,'yl'=2,'core'=2,'yh'=2,'x'=4] {'x'}, dimensions={0} | all-to-all | bytes 1048576 | tf_op jit(solution)/shard_map/all_to_all | solution.py:321
  105.0 0.0 copy-done.2
  105.0 1.9 %grad.1 = (bf16[4,1040,128]{2,1,0:T(8,128)(2,1)S(1)}, bf16[256,128]{1,0:T(8,128)(2,1)S(1)}) custom-call(bf16[144,2048]{1,0:T(8,128)(2,1)S(1)} %get-tuple-element.12.refs_0_, bf16[144,2048]{1,0:T(8,128)(2,1)S(1)} %collective-permute-done.refs_1_, bf16[144,2048]{1,0:T(8,128)(2,1)S(1)} %collective-permute-done.1.refs_2_, ...), custom_call_target="tpu_custom_call" | custom-call | flops 1073741824 | bytes 6373900 | tf_op jit(solution)/shard_map/grad/pallas_call | solution.py:25
  106.9 16.9 %all_to_all.32.got_ref = bf16[4,1040,128]{2,1,0:T(8,128)(2,1)S(1)} all-to-all(bf16[4,1040,128]{2,1,0:T(8,128)(2,1)S(1)} %get-tuple-element.18), channel_id=1, replica_groups=mesh['z'=16,'yl'=2,'core'=2,'yh'=2,'x'=4] {'yl','yh'}, dimensions={0} | all-to-all | bytes 2129920 | tf_op jit(solution)/shard_map/all_to_all | solution.py:334
  123.8 0.4 gather.1
  124.2 40.0 %all_to_all.33 = bf16[128,8,128]{2,1,0:T(8,128)(2,1)S(1)} all-to-all(bf16[128,8,128]{2,1,0:T(8,128)(2,1)S(1)} %bitcast.16), channel_id=1, replica_groups=mesh['z'=16,'yl'=2,'core'=2,'yh'=2,'x'=4] {'z','core','x'}, dimensions={0} | all-to-all | bytes 524288 | tf_op jit(solution)/shard_map/all_to_all | solution.py:343
  164.2 1.0 final.1
  (17 shorter events, 0.0 us)
Async XLA Ops:
  1.5 0.7 copy-start.12
  2.2 0.7 copy-start.13
  4.2 44.0 %all-to-all-start = ((bf16[128,8,128]{2,1,0:T(8,128)(2,1)}), bf16[128,8,128]{2,1,0:T(8,128)(2,1)S(1)}, u32[]{:S(2)}, u32[]{:S(2)}) async-start(bf16[128,8,128]{2,1,0:T(8,128)(2,1)} %bitcast.7), calls=%async_computation | async-start | bytes 524288 | tf_op jit(solution)/shard_map/all_to_all | solution.py:280
  25.4 1.0 copy-start.14
  26.5 1.6 copy-start.15
  32.0 23.5 %collective-permute-start = (bf16[144,2048]{1,0:T(8,128)(2,1)}, bf16[144,2048]{1,0:T(8,128)(2,1)S(1)}, u32[]{:S(2)}, u32[]{:S(2)}) collective-permute-start(bf16[144,2048]{1,0:T(8,128)(2,1)} %get-tuple-element.13), channel_id=1, source_target_pairs={{0,1},{1,2},{2,3},{3,0},{4,5},{5,6},{6,7},{7,4},{8,9},{9,10},{10,1... | collective-permute-start | bytes 1769480 | tf_op jit(solution)/shard_map/ppermute | solution.py:293
  35.3 29.2 %collective-permute-start.1 = (bf16[144,2048]{1,0:T(8,128)(2,1)}, bf16[144,2048]{1,0:T(8,128)(2,1)S(1)}, u32[]{:S(2)}, u32[]{:S(2)}) collective-permute-start(bf16[144,2048]{1,0:T(8,128)(2,1)} %get-tuple-element.14), channel_id=1, source_target_pairs={{0,2},{1,3},{2,0},{3,1},{4,6},{5,7},{6,4},{7,5},{8,10},{9,11},{10,... | collective-permute-start | bytes 1769480 | tf_op jit(solution)/shard_map/ppermute | solution.py:293
  39.6 27.8 %collective-permute-start.2 = (bf16[144,2048]{1,0:T(8,128)(2,1)}, bf16[144,2048]{1,0:T(8,128)(2,1)S(1)}, u32[]{:S(2)}, u32[]{:S(2)}) collective-permute-start(bf16[144,2048]{1,0:T(8,128)(2,1)} %get-tuple-element.15), channel_id=1, source_target_pairs={{0,3},{1,0},{2,1},{3,2},{4,7},{5,4},{6,5},{7,6},{8,11},{9,8},{10,9... | collective-permute-start | bytes 1769480 | tf_op jit(solution)/shard_map/ppermute | solution.py:293
  49.5 23.2 %all-to-all-start.1 = ((bf16[4,1024,128]{2,1,0:T(8,128)(2,1)}), bf16[4,1024,128]{2,1,0:T(8,128)(2,1)S(1)}, u32[]{:S(2)}, u32[]{:S(2)}) async-start(bf16[4,1024,128]{2,1,0:T(8,128)(2,1)} %spread.1), calls=%async_computation.1 | async-start | bytes 2097152 | tf_op jit(solution)/shard_map/all_to_all | solution.py:303
  53.6 15.7 %collective-permute-start.3 = (bf16[144,2048]{1,0:T(8,128)(2,1)S(1)}, bf16[144,2048]{1,0:T(8,128)(2,1)S(1)}, u32[]{:S(2)}, u32[]{:S(2)}) collective-permute-start(bf16[144,2048]{1,0:T(8,128)(2,1)S(1)} %get-tuple-element.12.refs_0_), channel_id=1, source_target_pairs={{0,8},{8,0},{1,9},{9,1},{2,10},{10,2},{3,11},{11,3},{4,12},{12,4},... | collective-permute-start | bytes 1769480 | tf_op jit(solution)/shard_map/ppermute | solution.py:294
  55.6 14.7 %collective-permute-start.4 = (bf16[144,2048]{1,0:T(8,128)(2,1)S(1)}, bf16[144,2048]{1,0:T(8,128)(2,1)S(1)}, u32[]{:S(2)}, u32[]{:S(2)}) collective-permute-start(bf16[144,2048]{1,0:T(8,128)(2,1)S(1)} %collective-permute-done.refs_1_), channel_id=1, source_target_pairs={{0,8},{8,0},{1,9},{9,1},{2,10},{10,2},{3,11},{11,3},{4,12},{12,4},... | collective-permute-start | bytes 1769480 | tf_op jit(solution)/shard_map/ppermute | solution.py:294
  64.5 6.5 %collective-permute-start.5 = (bf16[144,2048]{1,0:T(8,128)(2,1)S(1)}, bf16[144,2048]{1,0:T(8,128)(2,1)S(1)}, u32[]{:S(2)}, u32[]{:S(2)}) collective-permute-start(bf16[144,2048]{1,0:T(8,128)(2,1)S(1)} %collective-permute-done.1.refs_2_), channel_id=1, source_target_pairs={{0,8},{8,0},{1,9},{9,1},{2,10},{10,2},{3,11},{11,3},{4,12},{12,4},... | collective-permute-start | bytes 1769480 | tf_op jit(solution)/shard_map/ppermute | solution.py:294
  67.5 4.4 %collective-permute-start.6 = (bf16[144,2048]{1,0:T(8,128)(2,1)S(1)}, bf16[144,2048]{1,0:T(8,128)(2,1)S(1)}, u32[]{:S(2)}, u32[]{:S(2)}) collective-permute-start(bf16[144,2048]{1,0:T(8,128)(2,1)S(1)} %collective-permute-done.2.refs_3_), channel_id=1, source_target_pairs={{0,8},{8,0},{1,9},{9,1},{2,10},{10,2},{3,11},{11,3},{4,12},{12,4},... | collective-permute-start | bytes 1769480 | tf_op jit(solution)/shard_map/ppermute | solution.py:294
  69.4 0.8 copy-start
  70.2 0.8 copy-start.3
  71.0 0.8 copy-start.6
  71.9 0.8 copy-start.9
  72.7 1.1 copy-start.1
  73.8 1.1 copy-start.4
  74.8 1.1 copy-start.7
  75.9 1.1 copy-start.10
  81.6 23.4 %copy-start.2 = (bf16[144,2048]{1,0:T(8,128)(2,1)S(1)}, bf16[144,2048]{1,0:T(8,128)(2,1)}, u32[]{:S(2)}) copy-start(bf16[144,2048]{1,0:T(8,128)(2,1)} %copy-done) | copy-start | bytes 1769476
  81.6 23.4 %copy-start.5 = (bf16[144,2048]{1,0:T(8,128)(2,1)S(1)}, bf16[144,2048]{1,0:T(8,128)(2,1)}, u32[]{:S(2)}) copy-start(bf16[144,2048]{1,0:T(8,128)(2,1)} %copy-done.3) | copy-start | bytes 1769476
  81.6 23.4 %copy-start.8 = (bf16[144,2048]{1,0:T(8,128)(2,1)S(1)}, bf16[144,2048]{1,0:T(8,128)(2,1)}, u32[]{:S(2)}) copy-start(bf16[144,2048]{1,0:T(8,128)(2,1)} %copy-done.6) | copy-start | bytes 1769476
  81.6 23.4 %copy-start.11 = (bf16[144,2048]{1,0:T(8,128)(2,1)S(1)}, bf16[144,2048]{1,0:T(8,128)(2,1)}, u32[]{:S(2)}) copy-start(bf16[144,2048]{1,0:T(8,128)(2,1)} %copy-done.9) | copy-start | bytes 1769476

commit v4 on v3

--- a/solution.py
+++ b/solution.py
@@ -15,22 +15,26 @@
 SHIFT = 34
 VMEM = pl.BlockSpec(memory_space=pltpu.VMEM)
 SMEM = pl.BlockSpec(memory_space=pltpu.SMEM)
-BACK = (0, 3, 2, 1)
-
-
-def call(kernel, out_shape, *args, scratch=(), flops=0, name=None):
+STEP = (0, 2, 1, 3)
+BACK = (0, 2, 3, 1)
+
+
+def call(kernel, out_shape, *args, scratch=(), flops=0, name=None, far=(), space=pltpu.HBM, held=True, grant=24):
     size = sum(a.size * a.dtype.itemsize for a in args)
     for o in jax.tree.leaves(out_shape):
         size += o.size * o.dtype.itemsize
+    specs = [SMEM if a.shape == (4,) else VMEM for a in args]
+    for i in far:
+        specs[i] = pl.BlockSpec(memory_space=space)
     return pl.pallas_call(
         kernel,
-        out_shape=out_shape,
-        in_specs=[SMEM if a.shape == (3,) else VMEM for a in args],
+        out_shape=jax.tree.map(lambda o: pltpu.VMEM(o.shape, o.dtype), out_shape) if held else out_shape,
+        in_specs=specs,
         out_specs=jax.tree.map(lambda _: VMEM, out_shape),
         scratch_shapes=list(scratch),
         name=name,
         cost_estimate=pl.CostEstimate(flops=flops, bytes_accessed=size, transcendentals=0),
-        compiler_params=pltpu.CompilerParams(vmem_limit_bytes=24 * 1024 * 1024),
+        compiler_params=pltpu.CompilerParams(vmem_limit_bytes=grant * 1024 * 1024),
     )(*args)
 
 
@@ -58,37 +62,41 @@
     return first, second
 
 
-def per_row(patterns):
-    row = lax.broadcasted_iota(jnp.int32, (32, 128), 0)
-    col = lax.broadcasted_iota(jnp.int32, (32, 128), 1)
-    spread = jnp.where(col // 4 == row, 1.0, 0.0).astype(BF16)
-    pat = jnp.dot(patterns.astype(F32).astype(BF16), spread, preferred_element_type=F32)
-    first, second = kept_rows(pat)
-    spot = (lax.broadcasted_iota(jnp.int32, pat.shape, 1) % 4).astype(F32)
-    return first, second, spot
+def row_of_four(dims):
+    return (lax.broadcasted_iota(jnp.int32, dims, 1) % 4).astype(F32)
 
 
 def shuffled(place):
     return place % 4 * 8 + place // 4
 
 
-def norm_kernel(x_ref, gain_ref, pat_ref, at_ref, *rest):
-    outs, rows_ref, pick_ref = rest[:NX], rest[NX], rest[NX + 1]
+def norm_kernel(x_hbm, gain_ref, pat_hbm, at_ref, *rest):
+    outs, (rows_ref, pick_ref, x_ref, pat_ref, sems) = rest[:NX], rest[NX:]
     me, core, own_yl = at_ref[0], at_ref[1], at_ref[2]
+    cuts = [pl.ds(i * 2048, 2048) for i in range(4)]
+    loads = [
+        pltpu.make_async_copy(x_hbm.at[:, cut], x_ref.at[:, cut], sems.at[i])
+        for i, cut in enumerate(cuts)
+    ]
+    loads.append(pltpu.make_async_copy(pat_hbm, pat_ref, sems.at[4]))
+    for load in loads:
+        load.start()
     total = jnp.zeros((128, 512), F32)
     for g in range(16):
+        if g % 4 == 0:
+            loads[g // 4].wait()
         part = x_ref[:, g * 512 : (g + 1) * 512].astype(F32)
         total += part * part
     factor = lax.rsqrt(jnp.sum(total, axis=1, keepdims=True) / D + 1e-05)
+    gain = gain_ref[...].astype(F32)
     for yl in range(2):
         for m in range(8):
-            for half in range(2):
-                at = (8 * m + 4 * half + 2 * yl) * 128
-                part = x_ref[:, at : at + 256].astype(F32)
-                gain = gain_ref[:, at : at + 256].astype(F32)
-                tile = yl * 8 + m
-                rows_ref[tile * 128 : (tile + 1) * 128, half * 256 : (half + 1) * 256] = (
-                    part * factor * gain
+            tile = yl * 8 + m
+            for b in range(4):
+                block = 8 * m + 4 * (b // 2) + 2 * yl + b % 2
+                part = x_ref[:, block * 128 : (block + 1) * 128].astype(F32)
+                rows_ref[tile * 128 : (tile + 1) * 128, b * 128 : (b + 1) * 128] = (
+                    part * factor * gain[block : block + 1, :]
                 ).astype(BF16)
     src = lax.broadcasted_iota(jnp.int32, (512, 512), 0)
     dst = lax.broadcasted_iota(jnp.int32, (512, 512), 1)
@@ -99,10 +107,11 @@
         seg = jnp.dot(
             rows_ref[tile * 128 : (tile + 1) * 128, :], move, preferred_element_type=F32
         ).astype(BF16)
-        for x in range(NX):
-            outs[x][:128, tile * 128 : (tile + 1) * 128] = seg[:, x * 128 : (x + 1) * 128]
+        for i, x in enumerate(STEP):
+            outs[i][:128, tile * 128 : (tile + 1) * 128] = seg[:, x * 128 : (x + 1) * 128]
     col = lax.broadcasted_iota(jnp.int32, (64, 128), 0)
     lane = lax.broadcasted_iota(jnp.int32, (64, 128), 1)
+    loads[4].wait()
     pick = jnp.where((col - core * 32 == lane - me * 32) & (lane // 32 == me), 1.0, 0.0)
     chosen = lax.dot_general(
         pat_ref[...].astype(F32).astype(BF16),
@@ -111,14 +120,32 @@
         preferred_element_type=F32,
     )
     pick_ref[...] = chosen.reshape(NZ, NYL, NC, NX, 8, 128)
-    for x in range(NX):
+    for i, x in enumerate(STEP):
         rows = pick_ref[:, own_yl, :, (me + x) % NX].reshape(256, 128).astype(BF16)
         for tile in range(16):
-            outs[x][128:, tile * 128 : (tile + 1) * 128] = rows[tile * 16 : (tile + 1) * 16]
-
-
-def pack_kernel(teacher_ref, student_ref, pat_ref, out_ref):
-    first, second, spot = per_row(pat_ref[...])
+            outs[i][128:, tile * 128 : (tile + 1) * 128] = rows[tile * 16 : (tile + 1) * 16]
+
+
+def pack_kernel(teacher_hbm, student_hbm, pat_hbm, at_ref, out_ref, rows_ref, *scratch):
+    teacher_ref, student_ref, pat_ref, sems = scratch
+    place = at_ref[3]
+    window = pl.ds(pl.multiple_of(place // 4 * 128, 128), 128)
+    loads = [
+        pltpu.make_async_copy(pat_hbm.at[:, window], pat_ref, sems.at[0]),
+        pltpu.make_async_copy(teacher_hbm, teacher_ref, sems.at[1]),
+        pltpu.make_async_copy(student_hbm, student_ref, sems.at[2]),
+    ]
+    for load in loads:
+        load.start()
+    for load in loads:
+        load.wait()
+    row = lax.broadcasted_iota(jnp.int32, (128, 128), 0)
+    col = lax.broadcasted_iota(jnp.int32, (128, 128), 1)
+    spread = jnp.where(col // 4 + place % 4 * 32 == row, 1.0, 0.0).astype(BF16)
+    pat = jnp.dot(pat_ref[...].astype(F32).astype(BF16), spread, preferred_element_type=F32)
+    rows_ref[...] = pat
+    first, second = kept_rows(pat)
+    spot = row_of_four(pat.shape)
     keep = jnp.where((spot == first) | (spot == second), 1.0, 0.0)
     delta = student_ref[...].astype(F32) * keep - teacher_ref[...].astype(F32)
     delta = delta * 2.0**SHIFT
@@ -149,7 +176,13 @@
 
 
 def forward_kernel(*refs):
-    pieces, (w_ref, me_ref, out_ref, high_ref, low_ref) = refs[: 2 * NX], refs[2 * NX :]
+    pieces, (w_ref, me_ref, out_ref, high_ref, low_ref, held_ref, sems) = refs[: 2 * NX], refs[2 * NX :]
+    loads = [
+        pltpu.make_async_copy(p.at[pl.ds(0, 128)], held_ref.at[i], sems.at[i])
+        for i, p in enumerate(pieces)
+    ]
+    for load in loads:
+        load.start()
     for y in range(4):
         for k in range(4):
             sent = w_ref[y, k * 256 : (k + 1) * 256, :].astype(F32)
@@ -162,9 +195,10 @@
             low_ref[at : at + 256, lane : lane + 128] = (delta - high.astype(F32)).astype(BF16)
     for i in range(NX):
         x = (me_ref[0] + BACK[i]) % NX
-        for ref, row in ((pieces[i], 0), (pieces[NX + i], 128)):
-            part = jnp.dot(ref[:128, :], high_ref[...], preferred_element_type=F32)
-            part += jnp.dot(ref[:128, :], low_ref[...], preferred_element_type=F32)
+        for piece, row in ((i, 0), (NX + i, 128)):
+            loads[piece].wait()
+            part = jnp.dot(held_ref[piece], high_ref[...], preferred_element_type=F32)
+            part += jnp.dot(held_ref[piece], low_ref[...], preferred_element_type=F32)
             out_ref[x, row : row + 128] = part.astype(BF16)
 
 
@@ -258,7 +292,8 @@
         wide += lax.dot_general(
             part, spread, (((0,), (0,)), ((), ())), preferred_element_type=F32
         )
-    first, second, spot = per_row(pat_ref[...])
+    first, second = kept_rows(pat_ref[...])
+    spot = row_of_four(wide[:64].shape)
     grad = jnp.where(spot == first, wide[:64], 0.0) + jnp.where(spot == second, wide[64:], 0.0)
     out_ref[...] = grad / jnp.sqrt(F32(TOKENS))
 
@@ -270,12 +305,25 @@
 def shards(hidden, norm_gain, teacher_k, student_k, keep_pattern):
     z, yl, core, x = (lax.axis_index(a) for a in ("z", "yl", "core", "x"))
     place = (z * NYL + yl) * NC + core
-    at = jnp.stack([x, core, yl]).astype(jnp.int32)
+    at = jnp.stack([x, core, yl, place]).astype(jnp.int32)
     patterns = keep_pattern.T
-    pat = lax.dynamic_slice_in_dim(patterns, place * 32, 32, 1)
-
-    packed = call(
-        pack_kernel, shape((NZ, 64, 128), BF16), teacher_k.T, student_k.T, pat, name="pack"
+
+    packed, pat = call(
+        pack_kernel,
+        (shape((NZ, 64, 128), BF16), shape((64, 128), F32)),
+        teacher_k.T,
+        student_k.T,
+        patterns,
+        at,
+        scratch=[
+            pltpu.VMEM((64, 128), BF16),
+            pltpu.VMEM((64, 128), BF16),
+            pltpu.VMEM((64, 128), jnp.int32),
+            pltpu.SemaphoreType.DMA((3,)),
+        ],
+        far=(0, 1, 2),
+        grant=60,
+        name="pack",
     )
     got_w = lax.all_to_all(packed.reshape(128, 8, 128), ZCX, 0, 0, tiled=True)
 
@@ -283,14 +331,22 @@
         norm_kernel,
         (shape((144, 2048), BF16),) * NX,
         hidden,
-        norm_gain.reshape(1, D),
+        norm_gain.reshape(64, 128),
         patterns,
         at,
-        scratch=[pltpu.VMEM((2048, 512), BF16), pltpu.VMEM((NZ, NYL, NC, NX, 8, 128), F32)],
+        scratch=[
+            pltpu.VMEM((2048, 512), BF16),
+            pltpu.VMEM((NZ, NYL, NC, NX, 8, 128), F32),
+            pltpu.VMEM((128, D), BF16),
+            pltpu.VMEM((64, 2048), jnp.int32),
+            pltpu.SemaphoreType.DMA((5,)),
+        ],
+        far=(0, 2),
+        grant=60,
         flops=2 * 2048 * 512 * 512,
         name="norm",
     )
-    own = [split[0]] + [lax.ppermute(split[i], "x", ring(i)) for i in range(1, NX)]
+    own = [split[0]] + [lax.ppermute(split[i], "x", ring(STEP[i])) for i in range(1, NX)]
     pair = [lax.ppermute(piece, "core", [(0, 1), (1, 0)]) for piece in own]
 
     rows_w = call(
@@ -310,7 +366,15 @@
         *pair,
         all_w,
         at,
-        scratch=[pltpu.VMEM((2048, 256), BF16)] * 2,
+        scratch=[
+            pltpu.VMEM((2048, 256), BF16),
+            pltpu.VMEM((2048, 256), BF16),
+            pltpu.VMEM((2 * NX, 128, 2048), BF16),
+            pltpu.SemaphoreType.DMA((2 * NX,)),
+        ],
+        far=range(2 * NX),
+        grant=60,
+        space=pl.ANY,
         flops=2 * flops,
         name="forward",
     )
@@ -346,6 +410,7 @@
         (shape((64, 128), F32), shape((1, 1), F32)),
         got_sum.reshape(NZ, 64, 128),
         pat,
+        held=False,
         name="final",
     )
     return grad.T, loss.reshape(())

time: 166 us -> 165 us (level)
  local copies, waits for them, and re-layouts: 13.2 us -> 3.85 us
  Pallas kernels: 14.5 us -> 22.4 us
    pallas_call x8, Pallas kernels: 14.5 us -> 22.4 us  [call(): pl.pallas_call(kernel, out_shape=jax.tree.map(lambda o: pltpu.VMEM(o.shap...]
    unnamed x32 -> x30, local copies, waits for them, and re-layouts: 11.6 us -> 3.85 us
  transfers between devices with their start and end apart: 9 -> 9, of which waited for: 2 -> 3; matrix products, arithmetic and copies ran while one was open for 0% -> 0% of each run, Pallas kernels for 3% -> 4%
where the time goes in v4:
time: 165 us; the launch traced here: 164 us
  blocking collectives  79.4 us (48%)
  starting transfers between devices  44.6 us (27%)
  Pallas kernels  22.4 us (14%)
  waiting for transfers between devices  12 us (7%)
  local copies, waits for them, and re-layouts  3.85 us (2%)
    all_to_all x1, blocking collectives, shards(): lax.all_to_all(packed_term.reshape(128, 8, 128), ZCX, 0, 0, tiled=True)  40 us
    pallas_call x8, Pallas kernels, call(): pl.pallas_call(kernel, out_shape=jax.tree.map(lambda o: pltpu.VMEM(o.shap...  22.4 us
    all_to_all x1, starting transfers between devices, shards(): got_w = lax.all_to_all(packed.reshape(128, 8, 128), ZCX, 0, 0, tiled=True)  20.4 us
    all_to_all x1, blocking collectives, shards(): got_term = lax.all_to_all(term, Y, 0, 0, tiled=True)  16.4 us
    all_to_all x1, blocking collectives, shards(): got_part = lax.all_to_all(part, 'x', 0, 0, tiled=True)  12.6 us
    ppermute x3, starting transfers between devices, shards(): lax.ppermute(split[i], 'x', ring(STEP[i]))  11.3 us
    all_to_all x1, blocking collectives, shards(): slopes = lax.all_to_all(slope, 'x', 0, 0, tiled=True)  10.3 us
    ppermute x4, starting transfers between devices, shards(): pair = [lax.ppermute(piece, 'core', [(0, 1), (1, 0)]) for piece in own]  8.64 us
  transfers between devices with their start and end apart: 9, of which 3 were waited for; matrix products, arithmetic and copies ran while one was open for 0% of the time, Pallas kernels for 4%

profile of v4, /device:TPU:1, one launch (start us, length us, event | category | flops | bytes accessed | tf_op | source)
XLA Modules:
  0.0 163.7 jit_solution(17210871963855019726)
XLA Ops:
  0.6 0.6 pad_add_fusion.at_ref.refs_9_.refs_10_
  1.2 2.7 %pack.1 = (bf16[16,64,128]{2,1,0:T(8,128)(2,1)}, f32[64,128]{1,0:T(8,128)S(1)}) custom-call(bf16[64,128]{1,0:T(8,128)(2,1)} %bitcast.19, bf16[64,128]{1,0:T(8,128)(2,1)} %bitcast.20, s32[64,2048]{1,0:T(8,128)} %bitcast.17, s32[4]{0:T(128)} %pad_add_fusion.at_ref.refs_9_.refs_10_), custom_call_target="tpu_custom_call" | custom-call | bytes 851984 | tf_op jit(solution)/shard_map/pack/pallas_call | solution.py:29
  3.9 20.4 %all-to-all-start = ((bf16[128,8,128]{2,1,0:T(8,128)(2,1)}), bf16[128,8,128]{2,1,0:T(8,128)(2,1)S(1)}, u32[]{:S(2)}, u32[]{:S(2)}) async-start(bf16[128,8,128]{2,1,0:T(8,128)(2,1)} %bitcast.8), calls=%async_computation | async-start | bytes 524288 | tf_op jit(solution)/shard_map/all_to_all | solution.py:328
  24.4 5.9 %norm.1 = (bf16[144,2048]{1,0:T(8,128)(2,1)S(1)}, bf16[144,2048]{1,0:T(8,128)(2,1)}, bf16[144,2048]{1,0:T(8,128)(2,1)}, bf16[144,2048]{1,0:T(8,128)(2,1)}) custom-call(bf16[128,8192]{1,0:T(8,128)(2,1)} %x_hbm.1, bf16[64,128]{1,0:T(8,128)(2,1)} %bitcast.22, s32[64,2048]{1,0:T(8,128)} %bitcast.18, s32[4]{0:T(128)} %pad_add_fusion.at_ref.refs_9_.refs_10_), custom_call_target="tpu_custom_call" | custom-call | flops 1073741824 | bytes 4997136 | tf_op jit(solution)/shard_map/norm/pallas_call | solution.py:29
  30.2 0.0 copy-start
  30.3 4.8 %collective-permute-start = (bf16[144,2048]{1,0:T(8,128)(2,1)}, bf16[144,2048]{1,0:T(8,128)(2,1)S(1)}, u32[]{:S(2)}, u32[]{:S(2)}) collective-permute-start(bf16[144,2048]{1,0:T(8,128)(2,1)} %get-tuple-element.15), channel_id=1, source_target_pairs={{0,2},{1,3},{2,0},{3,1},{4,6},{5,7},{6,4},{7,5},{8,10},{9,11},{10,... | collective-permute-start | bytes 1769480 | tf_op jit(solution)/shard_map/ppermute | solution.py:349
  35.1 2.2 %collective-permute-start.1 = (bf16[144,2048]{1,0:T(8,128)(2,1)}, bf16[144,2048]{1,0:T(8,128)(2,1)S(1)}, u32[]{:S(2)}, u32[]{:S(2)}) collective-permute-start(bf16[144,2048]{1,0:T(8,128)(2,1)} %get-tuple-element.16), channel_id=1, source_target_pairs={{0,1},{1,2},{2,3},{3,0},{4,5},{5,6},{6,7},{7,4},{8,9},{9,10},{10,1... | collective-permute-start | bytes 1769480 | tf_op jit(solution)/shard_map/ppermute | solution.py:349
  37.3 4.3 %collective-permute-start.2 = (bf16[144,2048]{1,0:T(8,128)(2,1)}, bf16[144,2048]{1,0:T(8,128)(2,1)S(1)}, u32[]{:S(2)}, u32[]{:S(2)}) collective-permute-start(bf16[144,2048]{1,0:T(8,128)(2,1)} %get-tuple-element.17), channel_id=1, source_target_pairs={{0,3},{1,0},{2,1},{3,2},{4,7},{5,4},{6,5},{7,6},{8,11},{9,8},{10,9... | collective-permute-start | bytes 1769480 | tf_op jit(solution)/shard_map/ppermute | solution.py:349
  41.6 6.4 %all-to-all-done = bf16[128,8,128]{2,1,0:T(8,128)(2,1)S(1)} async-done(((bf16[128,8,128]{2,1,0:T(8,128)(2,1)}), bf16[128,8,128]{2,1,0:T(8,128)(2,1)S(1)}, u32[]{:S(2)}, u32[]{:S(2)}) %all-to-all-start) | async-done | bytes 262176 | tf_op jit(solution)/shard_map/all_to_all | solution.py:328
  48.0 1.3 spread.1
  49.2 4.2 %all-to-all-start.1 = ((bf16[4,1024,128]{2,1,0:T(8,128)(2,1)}), bf16[4,1024,128]{2,1,0:T(8,128)(2,1)}, u32[]{:S(2)}, u32[]{:S(2)}) async-start(bf16[4,1024,128]{2,1,0:T(8,128)(2,1)} %spread.1), calls=%async_computation.1 | async-start | bytes 2097152 | tf_op jit(solution)/shard_map/all_to_all | solution.py:359
  53.5 0.0 copy-done
  53.5 1.9 %collective-permute-start.3 = (bf16[144,2048]{1,0:T(8,128)(2,1)S(1)}, bf16[144,2048]{1,0:T(8,128)(2,1)S(1)}, u32[]{:S(2)}, u32[]{:S(2)}) collective-permute-start(bf16[144,2048]{1,0:T(8,128)(2,1)S(1)} %get-tuple-element.14.refs_0_), channel_id=1, source_target_pairs={{0,8},{8,0},{1,9},{9,1},{2,10},{10,2},{3,11},{11,3},{4,12},{12,4},... | collective-permute-start | bytes 1769480 | tf_op jit(solution)/shard_map/ppermute | solution.py:350
  55.4 0.0 collective-permute-done.refs_1_
  55.5 0.0 copy-start.2
  55.5 2.4 %collective-permute-start.4 = (bf16[144,2048]{1,0:T(8,128)(2,1)S(1)}, bf16[144,2048]{1,0:T(8,128)(2,1)S(1)}, u32[]{:S(2)}, u32[]{:S(2)}) collective-permute-start(bf16[144,2048]{1,0:T(8,128)(2,1)S(1)} %collective-permute-done.refs_1_), channel_id=1, source_target_pairs={{0,8},{8,0},{1,9},{9,1},{2,10},{10,2},{3,11},{11,3},{4,12},{12,4},... | collective-permute-start | bytes 1769480 | tf_op jit(solution)/shard_map/ppermute | solution.py:350
  57.9 5.3 %collective-permute-done.1.refs_2_ = bf16[144,2048]{1,0:T(8,128)(2,1)S(1)} collective-permute-done((bf16[144,2048]{1,0:T(8,128)(2,1)}, bf16[144,2048]{1,0:T(8,128)(2,1)S(1)}, u32[]{:S(2)}, u32[]{:S(2)}) %collective-permute-start.1) | collective-permute-done | bytes 589856 | tf_op jit(solution)/shard_map/ppermute | solution.py:349
  63.2 2.3 %collective-permute-start.5 = (bf16[144,2048]{1,0:T(8,128)(2,1)S(1)}, bf16[144,2048]{1,0:T(8,128)(2,1)S(1)}, u32[]{:S(2)}, u32[]{:S(2)}) collective-permute-start(bf16[144,2048]{1,0:T(8,128)(2,1)S(1)} %collective-permute-done.1.refs_2_), channel_id=1, source_target_pairs={{0,8},{8,0},{1,9},{9,1},{2,10},{10,2},{3,11},{11,3},{4,12},{12,4},... | collective-permute-start | bytes 1769480 | tf_op jit(solution)/shard_map/ppermute | solution.py:350
  65.5 0.0 collective-permute-done.2.refs_3_
  65.5 0.0 copy-start.6
  65.5 2.0 %collective-permute-start.6 = (bf16[144,2048]{1,0:T(8,128)(2,1)S(1)}, bf16[144,2048]{1,0:T(8,128)(2,1)}, u32[]{:S(2)}, u32[]{:S(2)}) collective-permute-start(bf16[144,2048]{1,0:T(8,128)(2,1)S(1)} %collective-permute-done.2.refs_3_), channel_id=1, source_target_pairs={{0,8},{8,0},{1,9},{9,1},{2,10},{10,2},{3,11},{11,3},{4,12},{12,4},... | collective-permute-start | bytes 1769480 | tf_op jit(solution)/shard_map/ppermute | solution.py:350
  67.5 0.0 collective-permute-done.3.refs_4_
  67.6 0.0 copy-start.8
  67.6 0.0 collective-permute-done.4.refs_5_
  67.6 0.0 copy-start.10
  67.6 0.0 collective-permute-done.5.refs_6_
  67.6 0.9 copy-done.10
  68.5 0.8 copy-done.12
  69.3 0.3 collective-permute-done.6.refs_7_
  69.5 0.0 all-to-all-done.1.refs_8_
  69.5 0.0 copy-done.2
  69.5 0.0 copy-done.4
  69.6 0.0 copy-done.6
  69.6 0.0 copy-done.8
  69.6 0.0 copy-start.11
  69.6 8.6 %forward.1 = bf16[4,256,256]{2,1,0:T(8,128)(2,1)S(1)} custom-call(bf16[144,2048]{1,0:T(8,128)(2,1)} %copy-done, bf16[144,2048]{1,0:T(8,128)(2,1)} %copy-done.2, bf16[144,2048]{1,0:T(8,128)(2,1)} %copy-done.4, bf16[144,2048]{1,0:T(8,128)(2,1)} %copy-done.6, bf16[144,2048]{1,0:T(8,128)(2,1)} %copy-done.8, bf16[144,2048]{1,0:T(8,128)(2,1)} %copy-done.10, ...), custom_call_target="tpu_custom_call" | custom-call | flops 2147483648 | bytes 6291472 | tf_op jit(solution)/shard_map/forward/pallas_call | solution.py:29
  78.1 0.0 copy-start.1
  78.2 12.6 %all_to_all.30.part_ref = bf16[4,256,256]{2,1,0:T(8,128)(2,1)S(1)} all-to-all(bf16[4,256,256]{2,1,0:T(8,128)(2,1)S(1)} %forward.1), channel_id=1, replica_groups=mesh['z'=16,'yl'=2,'core'=2,'yh'=2,'x'=4] {'x'}, dimensions={0} | all-to-all | bytes 1048576 | tf_op jit(solution)/shard_map/all_to_all | solution.py:381
  90.8 0.1 slope.1
  90.9 10.3 %all_to_all.31.refs_8_ = bf16[4,256,256]{2,1,0:T(8,128)(2,1)S(1)} all-to-all(bf16[4,256,256]{2,1,0:T(8,128)(2,1)S(1)} %get-tuple-element.19), channel_id=1, replica_groups=mesh['z'=16,'yl'=2,'core'=2,'yh'=2,'x'=4] {'x'}, dimensions={0} | all-to-all | bytes 1048576 | tf_op jit(solution)/shard_map/all_to_all | solution.py:385
  101.3 0.0 copy-done.3
  101.3 1.1 copy-done.9
  102.4 1.1 copy-done.13
  103.4 2.5 %grad.1 = (bf16[4,1040,128]{2,1,0:T(8,128)(2,1)S(1)}, bf16[256,128]{1,0:T(8,128)(2,1)S(1)}) custom-call(bf16[144,2048]{1,0:T(8,128)(2,1)S(1)} %copy-done.1, bf16[144,2048]{1,0:T(8,128)(2,1)S(1)} %copy-done.3, bf16[144,2048]{1,0:T(8,128)(2,1)S(1)} %copy-done.5, bf16[144,2048]{1,0:T(8,128)(2,1)S(1)} %copy-done.7, bf16[144,2048]{1,0:T(8,128)(2,1)S(1)} %copy-done.9, ...), custom_call_target="tpu_custom_call" | custom-call | flops 1073741824 | bytes 6373904 | tf_op jit(solution)/shard_map/grad/pallas_call | solution.py:29
  105.9 16.4 %all_to_all.32.got_ref = bf16[4,1040,128]{2,1,0:T(8,128)(2,1)S(1)} all-to-all(bf16[4,1040,128]{2,1,0:T(8,128)(2,1)S(1)} %get-tuple-element.21), channel_id=1, replica_groups=mesh['z'=16,'yl'=2,'core'=2,'yh'=2,'x'=4] {'yl','yh'}, dimensions={0} | all-to-all | bytes 2129920 | tf_op jit(solution)/shard_map/all_to_all | solution.py:398
  122.3 0.4 gather.1
  122.7 40.0 %all_to_all.33 = bf16[128,8,128]{2,1,0:T(8,128)(2,1)S(1)} all-to-all(bf16[128,8,128]{2,1,0:T(8,128)(2,1)S(1)} %bitcast.16), channel_id=1, replica_groups=mesh['z'=16,'yl'=2,'core'=2,'yh'=2,'x'=4] {'z','core','x'}, dimensions={0} | all-to-all | bytes 524288 | tf_op jit(solution)/shard_map/all_to_all | solution.py:407
  162.8 0.9 final.1
  (13 shorter events, 0.0 us)
Async XLA Ops:
  3.9 44.0 %all-to-all-start = ((bf16[128,8,128]{2,1,0:T(8,128)(2,1)}), bf16[128,8,128]{2,1,0:T(8,128)(2,1)S(1)}, u32[]{:S(2)}, u32[]{:S(2)}) async-start(bf16[128,8,128]{2,1,0:T(8,128)(2,1)} %bitcast.8), calls=%async_computation | async-start | bytes 524288 | tf_op jit(solution)/shard_map/all_to_all | solution.py:328
  30.2 23.3 %copy-start = (bf16[144,2048]{1,0:T(8,128)(2,1)}, bf16[144,2048]{1,0:T(8,128)(2,1)S(1)}, u32[]{:S(2)}) copy-start(bf16[144,2048]{1,0:T(8,128)(2,1)S(1)} %get-tuple-element.14.refs_0_) | copy-start | bytes 1769476
  30.3 25.2 %collective-permute-start = (bf16[144,2048]{1,0:T(8,128)(2,1)}, bf16[144,2048]{1,0:T(8,128)(2,1)S(1)}, u32[]{:S(2)}, u32[]{:S(2)}) collective-permute-start(bf16[144,2048]{1,0:T(8,128)(2,1)} %get-tuple-element.15), channel_id=1, source_target_pairs={{0,2},{1,3},{2,0},{3,1},{4,6},{5,7},{6,4},{7,5},{8,10},{9,11},{10,... | collective-permute-start | bytes 1769480 | tf_op jit(solution)/shard_map/ppermute | solution.py:349
  35.1 28.1 %collective-permute-start.1 = (bf16[144,2048]{1,0:T(8,128)(2,1)}, bf16[144,2048]{1,0:T(8,128)(2,1)S(1)}, u32[]{:S(2)}, u32[]{:S(2)}) collective-permute-start(bf16[144,2048]{1,0:T(8,128)(2,1)} %get-tuple-element.16), channel_id=1, source_target_pairs={{0,1},{1,2},{2,3},{3,0},{4,5},{5,6},{6,7},{7,4},{8,9},{9,10},{10,1... | collective-permute-start | bytes 1769480 | tf_op jit(solution)/shard_map/ppermute | solution.py:349
  37.3 28.2 %collective-permute-start.2 = (bf16[144,2048]{1,0:T(8,128)(2,1)}, bf16[144,2048]{1,0:T(8,128)(2,1)S(1)}, u32[]{:S(2)}, u32[]{:S(2)}) collective-permute-start(bf16[144,2048]{1,0:T(8,128)(2,1)} %get-tuple-element.17), channel_id=1, source_target_pairs={{0,3},{1,0},{2,1},{3,2},{4,7},{5,4},{6,5},{7,6},{8,11},{9,8},{10,9... | collective-permute-start | bytes 1769480 | tf_op jit(solution)/shard_map/ppermute | solution.py:349
  49.2 20.3 %all-to-all-start.1 = ((bf16[4,1024,128]{2,1,0:T(8,128)(2,1)}), bf16[4,1024,128]{2,1,0:T(8,128)(2,1)}, u32[]{:S(2)}, u32[]{:S(2)}) async-start(bf16[4,1024,128]{2,1,0:T(8,128)(2,1)} %spread.1), calls=%async_computation.1 | async-start | bytes 2097152 | tf_op jit(solution)/shard_map/all_to_all | solution.py:359
  53.5 14.0 %collective-permute-start.3 = (bf16[144,2048]{1,0:T(8,128)(2,1)S(1)}, bf16[144,2048]{1,0:T(8,128)(2,1)S(1)}, u32[]{:S(2)}, u32[]{:S(2)}) collective-permute-start(bf16[144,2048]{1,0:T(8,128)(2,1)S(1)} %get-tuple-element.14.refs_0_), channel_id=1, source_target_pairs={{0,8},{8,0},{1,9},{9,1},{2,10},{10,2},{3,11},{11,3},{4,12},{12,4},... | collective-permute-start | bytes 1769480 | tf_op jit(solution)/shard_map/ppermute | solution.py:350
  55.5 14.1 %copy-start.2 = (bf16[144,2048]{1,0:T(8,128)(2,1)}, bf16[144,2048]{1,0:T(8,128)(2,1)S(1)}, u32[]{:S(2)}) copy-start(bf16[144,2048]{1,0:T(8,128)(2,1)S(1)} %collective-permute-done.refs_1_) | copy-start | bytes 1769476
  55.5 12.1 %collective-permute-start.4 = (bf16[144,2048]{1,0:T(8,128)(2,1)S(1)}, bf16[144,2048]{1,0:T(8,128)(2,1)S(1)}, u32[]{:S(2)}, u32[]{:S(2)}) collective-permute-start(bf16[144,2048]{1,0:T(8,128)(2,1)S(1)} %collective-permute-done.refs_1_), channel_id=1, source_target_pairs={{0,8},{8,0},{1,9},{9,1},{2,10},{10,2},{3,11},{11,3},{4,12},{12,4},... | collective-permute-start | bytes 1769480 | tf_op jit(solution)/shard_map/ppermute | solution.py:350
  63.2 6.4 %copy-start.4 = (bf16[144,2048]{1,0:T(8,128)(2,1)}, bf16[144,2048]{1,0:T(8,128)(2,1)S(1)}, u32[]{:S(2)}) copy-start(bf16[144,2048]{1,0:T(8,128)(2,1)S(1)} %collective-permute-done.1.refs_2_) | copy-start | bytes 1769476
  63.2 4.4 %collective-permute-start.5 = (bf16[144,2048]{1,0:T(8,128)(2,1)S(1)}, bf16[144,2048]{1,0:T(8,128)(2,1)S(1)}, u32[]{:S(2)}, u32[]{:S(2)}) collective-permute-start(bf16[144,2048]{1,0:T(8,128)(2,1)S(1)} %collective-permute-done.1.refs_2_), channel_id=1, source_target_pairs={{0,8},{8,0},{1,9},{9,1},{2,10},{10,2},{3,11},{11,3},{4,12},{12,4},... | collective-permute-start | bytes 1769480 | tf_op jit(solution)/shard_map/ppermute | solution.py:350
  65.5 4.1 %copy-start.6 = (bf16[144,2048]{1,0:T(8,128)(2,1)}, bf16[144,2048]{1,0:T(8,128)(2,1)S(1)}, u32[]{:S(2)}) copy-start(bf16[144,2048]{1,0:T(8,128)(2,1)S(1)} %collective-permute-done.2.refs_3_) | copy-start | bytes 1769476
  65.5 4.0 %collective-permute-start.6 = (bf16[144,2048]{1,0:T(8,128)(2,1)S(1)}, bf16[144,2048]{1,0:T(8,128)(2,1)}, u32[]{:S(2)}, u32[]{:S(2)}) collective-permute-start(bf16[144,2048]{1,0:T(8,128)(2,1)S(1)} %collective-permute-done.2.refs_3_), channel_id=1, source_target_pairs={{0,8},{8,0},{1,9},{9,1},{2,10},{10,2},{3,11},{11,3},{4,12},{12,4},... | collective-permute-start | bytes 1769480 | tf_op jit(solution)/shard_map/ppermute | solution.py:350
  67.6 2.0 %copy-start.8 = (bf16[144,2048]{1,0:T(8,128)(2,1)}, bf16[144,2048]{1,0:T(8,128)(2,1)S(1)}, u32[]{:S(2)}) copy-start(bf16[144,2048]{1,0:T(8,128)(2,1)S(1)} %collective-permute-done.3.refs_4_) | copy-start | bytes 1769476
  67.6 0.9 copy-start.10
  68.5 0.8 copy-start.12
  69.6 31.7 %copy-start.11 = (bf16[144,2048]{1,0:T(8,128)(2,1)S(1)}, bf16[144,2048]{1,0:T(8,128)(2,1)}, u32[]{:S(2)}) copy-start(bf16[144,2048]{1,0:T(8,128)(2,1)} %copy-done.10) | copy-start | bytes 1769476
  78.1 23.1 %copy-start.1 = (bf16[144,2048]{1,0:T(8,128)(2,1)S(1)}, bf16[144,2048]{1,0:T(8,128)(2,1)}, u32[]{:S(2)}) copy-start(bf16[144,2048]{1,0:T(8,128)(2,1)} %copy-done) | copy-start | bytes 1769476
  78.2 23.1 %copy-start.3 = (bf16[144,2048]{1,0:T(8,128)(2,1)S(1)}, bf16[144,2048]{1,0:T(8,128)(2,1)}, u32[]{:S(2)}) copy-start(bf16[144,2048]{1,0:T(8,128)(2,1)} %copy-done.2) | copy-start | bytes 1769476
  78.2 23.1 %copy-start.5 = (bf16[144,2048]{1,0:T(8,128)(2,1)S(1)}, bf16[144,2048]{1,0:T(8,128)(2,1)}, u32[]{:S(2)}) copy-start(bf16[144,2048]{1,0:T(8,128)(2,1)} %copy-done.4) | copy-start | bytes 1769476
  78.2 23.1 %copy-start.7 = (bf16[144,2048]{1,0:T(8,128)(2,1)S(1)}, bf16[144,2048]{1,0:T(8,128)(2,1)}, u32[]{:S(2)}) copy-start(bf16[144,2048]{1,0:T(8,128)(2,1)} %copy-done.6) | copy-start | bytes 1769476
  78.2 23.1 %copy-start.14 = (s32[4]{0:T(128)S(1)}, s32[4]{0:T(128)}, u32[]{:S(2)}) copy-start(s32[4]{0:T(128)} %pad_add_fusion.at_ref.refs_9_.refs_10_) | copy-start | bytes 52
  101.3 1.1 copy-start.9
  102.4 1.1 copy-start.13

commit v5 on v4

--- a/solution.py
+++ b/solution.py
@@ -19,16 +19,16 @@
 BACK = (0, 2, 3, 1)
 
 
-def call(kernel, out_shape, *args, scratch=(), flops=0, name=None, far=(), space=pltpu.HBM, held=True, grant=24):
+def call(kernel, out_shape, *args, scratch=(), flops=0, name=None, far=(), grant=24):
     size = sum(a.size * a.dtype.itemsize for a in args)
     for o in jax.tree.leaves(out_shape):
         size += o.size * o.dtype.itemsize
-    specs = [SMEM if a.shape == (4,) else VMEM for a in args]
+    specs = [SMEM if a.shape == (5,) else VMEM for a in args]
     for i in far:
-        specs[i] = pl.BlockSpec(memory_space=space)
+        specs[i] = pl.BlockSpec(memory_space=pl.ANY)
     return pl.pallas_call(
         kernel,
-        out_shape=jax.tree.map(lambda o: pltpu.VMEM(o.shape, o.dtype), out_shape) if held else out_shape,
+        out_shape=out_shape,
         in_specs=specs,
         out_specs=jax.tree.map(lambda _: VMEM, out_shape),
         scratch_shapes=list(scratch),
@@ -70,15 +70,14 @@
     return place % 4 * 8 + place // 4
 
 
-def norm_kernel(x_hbm, gain_ref, pat_hbm, at_ref, *rest):
-    outs, (rows_ref, pick_ref, x_ref, pat_ref, sems) = rest[:NX], rest[NX:]
-    me, core, own_yl = at_ref[0], at_ref[1], at_ref[2]
+def norm_kernel(x_hbm, gain_ref, at_ref, *rest):
+    outs, (rows_ref, x_ref, sems) = rest[:NX], rest[NX:]
+    me = at_ref[0]
     cuts = [pl.ds(i * 2048, 2048) for i in range(4)]
     loads = [
         pltpu.make_async_copy(x_hbm.at[:, cut], x_ref.at[:, cut], sems.at[i])
         for i, cut in enumerate(cuts)
     ]
-    loads.append(pltpu.make_async_copy(pat_hbm, pat_ref, sems.at[4]))
     for load in loads:
         load.start()
     total = jnp.zeros((128, 512), F32)
@@ -108,10 +107,14 @@
             rows_ref[tile * 128 : (tile + 1) * 128, :], move, preferred_element_type=F32
         ).astype(BF16)
         for i, x in enumerate(STEP):
-            outs[i][:128, tile * 128 : (tile + 1) * 128] = seg[:, x * 128 : (x + 1) * 128]
+            outs[i][:, tile * 128 : (tile + 1) * 128] = seg[:, x * 128 : (x + 1) * 128]
+
+
+def choose_kernel(pat_ref, at_ref, *outs):
+    me, core, own_yl = at_ref[0], at_ref[1], at_ref[2]
+    outs, pick_ref = outs[:NX], outs[NX]
     col = lax.broadcasted_iota(jnp.int32, (64, 128), 0)
     lane = lax.broadcasted_iota(jnp.int32, (64, 128), 1)
-    loads[4].wait()
     pick = jnp.where((col - core * 32 == lane - me * 32) & (lane // 32 == me), 1.0, 0.0)
     chosen = lax.dot_general(
         pat_ref[...].astype(F32).astype(BF16),
@@ -121,9 +124,14 @@
     )
     pick_ref[...] = chosen.reshape(NZ, NYL, NC, NX, 8, 128)
     for i, x in enumerate(STEP):
-        rows = pick_ref[:, own_yl, :, (me + x) % NX].reshape(256, 128).astype(BF16)
-        for tile in range(16):
-            outs[i][128:, tile * 128 : (tile + 1) * 128] = rows[tile * 16 : (tile + 1) * 16]
+        outs[i][...] = pick_ref[:, own_yl, :, (me + x) % NX].reshape(256, 128).astype(BF16)
+
+
+def join_kernel(*refs):
+    total = refs[0][...].astype(F32)
+    for ref in refs[1:NX]:
+        total += ref[...].astype(F32)
+    refs[NX][...] = total.astype(BF16)
 
 
 def pack_kernel(teacher_hbm, student_hbm, pat_hbm, at_ref, out_ref, rows_ref, *scratch):
@@ -175,14 +183,7 @@
         out_ref[y] = rows
 
 
-def forward_kernel(*refs):
-    pieces, (w_ref, me_ref, out_ref, high_ref, low_ref, held_ref, sems) = refs[: 2 * NX], refs[2 * NX :]
-    loads = [
-        pltpu.make_async_copy(p.at[pl.ds(0, 128)], held_ref.at[i], sems.at[i])
-        for i, p in enumerate(pieces)
-    ]
-    for load in loads:
-        load.start()
+def decode_kernel(w_ref, high_ref, low_ref):
     for y in range(4):
         for k in range(4):
             sent = w_ref[y, k * 256 : (k + 1) * 256, :].astype(F32)
@@ -193,12 +194,15 @@
             lane = (y % 2) * 128
             high_ref[at : at + 256, lane : lane + 128] = high
             low_ref[at : at + 256, lane : lane + 128] = (delta - high.astype(F32)).astype(BF16)
+
+
+def forward_kernel(*refs):
+    pieces, (high_ref, low_ref, at_ref, out_ref) = refs[: 2 * NX], refs[2 * NX :]
     for i in range(NX):
-        x = (me_ref[0] + BACK[i]) % NX
-        for piece, row in ((i, 0), (NX + i, 128)):
-            loads[piece].wait()
-            part = jnp.dot(held_ref[piece], high_ref[...], preferred_element_type=F32)
-            part += jnp.dot(held_ref[piece], low_ref[...], preferred_element_type=F32)
+        x = (at_ref[0] + BACK[i]) % NX
+        for ref, row in ((pieces[i], 0), (pieces[NX + i], 128)):
+            part = jnp.dot(ref[...], high_ref[...], preferred_element_type=F32)
+            part += jnp.dot(ref[...], low_ref[...], preferred_element_type=F32)
             out_ref[x, row : row + 128] = part.astype(BF16)
 
 
@@ -222,46 +226,43 @@
 
 
 def grad_kernel(*refs):
-    pieces, (slope_ref, loss_ref, me_ref, out_ref, pat_ref, s_ref) = refs[: 2 * NX], refs[2 * NX :]
+    pieces, pats, rest = refs[: 2 * NX], refs[2 * NX : 2 * NX + 4], refs[2 * NX + 4 :]
+    slope_ref, loss_ref, at_ref, out_ref, s_ref, term_ref = rest
     contract = (((0,), (0,)), ((), ()))
     for i in range(NX):
-        x = (me_ref[0] + BACK[i]) % NX
+        x = (at_ref[0] + BACK[i]) % NX
         s_ref[i * 128 : (i + 1) * 128] = slope_ref[x, :128]
         s_ref[512 + i * 128 : 512 + (i + 1) * 128] = slope_ref[x, 128:]
     for k in range(8):
         at = k * 256
-        rows = jnp.concatenate([p[:128, at : at + 256] for p in pieces], axis=0)
+        rows = jnp.concatenate([p[:, at : at + 256] for p in pieces], axis=0)
         term = lax.dot_general(rows, s_ref[...], contract, preferred_element_type=F32)
-        term = term.astype(BF16)
         for yh in range(2):
-            out_ref[(k // 4) * 2 + yh, (k % 4) * 256 : (k % 4 + 1) * 256, :] = term[
+            term_ref[(k // 4) * 2 + yh, (k % 4) * 8 : (k % 4 + 1) * 8] = term[
                 :, yh * 128 : (yh + 1) * 128
-            ]
+            ].reshape(8, 4, 8, 128)
     loss = thirds(loss_ref[...], 16).astype(BF16)
-    for y in range(4):
-        out_ref[y, 1024:, :] = loss
-    for tile in range(16):
-        pat = pieces[0][128:, tile * 128 : (tile + 1) * 128].astype(F32)
-        for i in range(1, NX):
-            pat += pieces[i][128:, tile * 128 : (tile + 1) * 128].astype(F32)
-        pat_ref[tile * 16 : (tile + 1) * 16, :] = pat.astype(BF16)
-
-
-def gather_kernel(got_ref, pat_ref, out_ref, mid_ref):
+    for i in range(4):
+        y = at_ref[4] ^ i
+        first, second = kept_rows(pats[i][...].astype(F32).reshape(32, 8, 128))
+        for row, which in ((0, first), (256, second)):
+            kept = jnp.zeros_like(which)
+            for k in range(4):
+                kept += jnp.where(which == k, term_ref[y, :, k], 0.0)
+            out_ref[y, row : row + 256] = kept.reshape(256, 128).astype(BF16)
+        out_ref[y, 512:] = loss
+
+
+def gather_kernel(got_ref, out_ref, mid_ref):
     total = got_ref[0].astype(F32)
     for y in range(1, 4):
         total = total + got_ref[y].astype(F32)
-    loss = jnp.sum(total[1024:], axis=0, keepdims=True)
+    loss = jnp.sum(total[512:], axis=0, keepdims=True)
     loss = thirds(jnp.broadcast_to(jnp.sum(loss, axis=1, keepdims=True), (1, 128)), 8)
     row = lax.broadcasted_iota(jnp.int32, (8, 128), 0)
     lane = lax.broadcasted_iota(jnp.int32, (8, 128), 1)
     loss = jnp.where(lane == 64 + row, loss, 0.0)
-    total = total[:1024].reshape(32, 4, 8, 128)
-    first, second = kept_rows(pat_ref[...].astype(F32).reshape(32, 8, 128))
-    kept = [jnp.zeros_like(first), jnp.zeros_like(first)]
-    for k in range(4):
-        for i, which in enumerate((first, second)):
-            kept[i] += jnp.where(which == k, total[:, k], 0.0)
+    kept = [total[:256].reshape(32, 8, 128), total[256:512].reshape(32, 8, 128)]
     group = lane_group((32, 8, 128))
     for x in range(NX):
         one = pltpu.roll(kept[0], (4 - x) % 4 * 32, 2)
@@ -303,9 +304,9 @@
 
 
 def shards(hidden, norm_gain, teacher_k, student_k, keep_pattern):
-    z, yl, core, x = (lax.axis_index(a) for a in ("z", "yl", "core", "x"))
+    z, yl, core, yh, x = (lax.axis_index(a) for a in AXES)
     place = (z * NYL + yl) * NC + core
-    at = jnp.stack([x, core, yl, place]).astype(jnp.int32)
+    at = jnp.stack([x, core, yl, place, yl * NYH + yh]).astype(jnp.int32)
     patterns = keep_pattern.T
 
     packed, pat = call(
@@ -329,21 +330,18 @@
 
     split = call(
         norm_kernel,
-        (shape((144, 2048), BF16),) * NX,
+        (shape((128, 2048), BF16),) * NX,
         hidden,
         norm_gain.reshape(64, 128),
-        patterns,
         at,
         scratch=[
             pltpu.VMEM((2048, 512), BF16),
-            pltpu.VMEM((NZ, NYL, NC, NX, 8, 128), F32),
             pltpu.VMEM((128, D), BF16),
-            pltpu.VMEM((64, 2048), jnp.int32),
-            pltpu.SemaphoreType.DMA((5,)),
+            pltpu.SemaphoreType.DMA((4,)),
         ],
-        far=(0, 2),
+        flops=2 * 2048 * 512 * 512,
+        far=(0,),
         grant=60,
-        flops=2 * 2048 * 512 * 512,
         name="norm",
     )
     own = [split[0]] + [lax.ppermute(split[i], "x", ring(STEP[i])) for i in range(1, NX)]
@@ -357,6 +355,17 @@
         name="spread",
     )
     all_w = lax.all_to_all(rows_w, Y, 0, 0, tiled=True)
+    high, low = call(decode_kernel, (shape((2048, 256), BF16),) * 2, all_w, name="decode")
+
+    late, _ = lax.optimization_barrier((patterns, rows_w))
+    chosen = call(
+        choose_kernel,
+        (shape((256, 128), BF16),) * NX,
+        late,
+        at,
+        scratch=[pltpu.VMEM((NZ, NYL, NC, NX, 8, 128), F32)],
+        name="choose",
+    )
 
     flops = 2 * 1024 * 2048 * 256
     part = call(
@@ -364,34 +373,33 @@
         shape((NX, 256, 256), BF16),
         *own,
         *pair,
-        all_w,
+        high,
+        low,
         at,
-        scratch=[
-            pltpu.VMEM((2048, 256), BF16),
-            pltpu.VMEM((2048, 256), BF16),
-            pltpu.VMEM((2 * NX, 128, 2048), BF16),
-            pltpu.SemaphoreType.DMA((2 * NX,)),
-        ],
-        far=range(2 * NX),
-        grant=60,
-        space=pl.ANY,
         flops=2 * flops,
         name="forward",
     )
+    part, chosen = lax.optimization_barrier((part, chosen))
     got_part = lax.all_to_all(part, "x", 0, 0, tiled=True)
+    line = [chosen[0]] + [lax.ppermute(chosen[i], "x", ring(STEP[i])) for i in range(1, NX)]
     slope, loss_part = call(
         slope_kernel, (shape((NX, 256, 256), BF16), shape((1, 128), F32)), got_part, name="slope"
     )
+    slope, line = lax.optimization_barrier((slope, line))
     slopes = lax.all_to_all(slope, "x", 0, 0, tiled=True)
-    term, pat_x = call(
+    joined = call(join_kernel, shape((256, 128), BF16), *line, name="join")
+    pats = [joined] + [lax.ppermute(joined, Y, [(y, y ^ i) for y in range(4)]) for i in range(1, 4)]
+
+    term = call(
         grad_kernel,
-        (shape((4, 1040, 128), BF16), shape((256, 128), BF16)),
+        shape((4, 528, 128), BF16),
         *own,
         *pair,
+        *pats,
         slopes,
         loss_part,
         at,
-        scratch=[pltpu.VMEM((1024, 256), BF16)],
+        scratch=[pltpu.VMEM((1024, 256), BF16), pltpu.VMEM((4, 32, 4, 8, 128), F32)],
         flops=flops,
         name="grad",
     )
@@ -400,7 +408,6 @@
         gather_kernel,
         shape((1024, 128), BF16),
         got_term,
-        pat_x,
         scratch=[pltpu.VMEM((32, 4, 8, 128), F32)],
         name="gather",
     )
@@ -410,7 +417,6 @@
         (shape((64, 128), F32), shape((1, 1), F32)),
         got_sum.reshape(NZ, 64, 128),
         pat,
-        held=False,
         name="final",
     )
     return grad.T, loss.reshape(())

time: 165 us -> 166 us (level)
  starting transfers between devices: 44.6 us -> 74.1 us
  blocking collectives: 79.4 us -> 53.7 us
  local copies, waits for them, and re-layouts: 3.85 us -> 0.62 us
    all_to_all x2 -> x0, blocking collectives: 23 us -> none  [the longest x1 12.6 us: shards(): got_part = lax.all_to_all(part, 'x', 0, 0, tiled=True)]
    ppermute x0 -> x6, starting transfers between devices: none -> 21.1 us  [the longest x3 11.4 us: shards(): lax.ppermute(chosen[i], 'x', ring(STEP[i]))]
    all_to_all x0 -> x2, starting transfers between devices: none -> 8.29 us  [the longest x1 4.26 us: shards(): slopes = lax.all_to_all(slope, 'x', 0, 0, tiled=True)]
    all_to_all x1, blocking collectives: 16.4 us -> 11 us  [shards(): got_term = lax.all_to_all(term, Y, 0, 0, tiled=True)]
    unnamed x30 -> x8, local copies, waits for them, and re-layouts: 3.85 us -> 0.02 us
    ppermute x3, waiting for transfers between devices: 5.32 us -> 2.42 us  [shards(): lax.ppermute(split[i], 'x', ring(STEP[i]))]
    all_to_all x1, blocking collectives: 40 us -> 42.7 us  [shards(): lax.all_to_all(packed_term.reshape(128, 8, 128), ZCX, 0, 0, tiled=True)]
    all_to_all x1, waiting for transfers between devices: 0.01 us -> 1.92 us  [shards(): all_w = lax.all_to_all(rows_w, Y, 0, 0, tiled=True)]
  transfers between devices with their start and end apart: 9 -> 17, of which waited for: 3 -> 5; matrix products, arithmetic and copies ran while one was open for 0% -> 0% of each run, Pallas kernels for 4% -> 6%
where the time goes in v5:
time: 166 us; the launch traced here: 165 us
  starting transfers between devices  74.1 us (45%)
  blocking collectives  53.7 us (32%)
  Pallas kernels  23.2 us (14%)
  waiting for transfers between devices  12.7 us (8%)
    all_to_all x1, blocking collectives, shards(): lax.all_to_all(packed_term.reshape(128, 8, 128), ZCX, 0, 0, tiled=True)  42.7 us
    pallas_call x11, Pallas kernels, call(): pl.pallas_call(kernel, out_shape=out_shape, in_specs=specs, out_specs=jax...  23.2 us
    all_to_all x1, starting transfers between devices, shards(): got_w = lax.all_to_all(packed.reshape(128, 8, 128), ZCX, 0, 0, tiled=True)  20.4 us
    ppermute x3, starting transfers between devices, shards(): lax.ppermute(split[i], 'x', ring(STEP[i]))  11.4 us
    ppermute x3, starting transfers between devices, shards(): lax.ppermute(chosen[i], 'x', ring(STEP[i]))  11.4 us
    all_to_all x1, blocking collectives, shards(): got_term = lax.all_to_all(term, Y, 0, 0, tiled=True)  11 us
    ppermute x3, starting transfers between devices, shards(): lax.ppermute(joined, Y, [(y, y ^ i) for y in range(4)])  9.76 us
    ppermute x4, starting transfers between devices, shards(): pair = [lax.ppermute(piece, 'core', [(0, 1), (1, 0)]) for piece in own]  8.63 us
  transfers between devices with their start and end apart: 17, of which 5 were waited for; matrix products, arithmetic and copies ran while one was open for 0% of the time, Pallas kernels for 6%

profile of v5, /device:TPU:1, one launch (start us, length us, event | category | flops | bytes accessed | tf_op | source)
XLA Modules:
  0.0 165.2 jit_solution(6118702001742620611)
XLA Ops:
  0.6 0.6 stack.23.at_ref.refs_10_.refs_14_
  1.2 2.7 %pack.1 = (bf16[16,64,128]{2,1,0:T(8,128)(2,1)}, f32[64,128]{1,0:T(8,128)}) custom-call(bf16[64,128]{1,0:T(8,128)(2,1)} %bitcast.21, bf16[64,128]{1,0:T(8,128)(2,1)} %bitcast.22, s32[64,2048]{1,0:T(8,128)} %bitcast.15, s32[5]{0:T(128)} %stack.23.at_ref.refs_10_.refs_14_), custom_call_target="tpu_custom_call" | custom-call | bytes 851988 | tf_op jit(solution)/shard_map/pack/pallas_call | solution.py:29
  4.0 20.4 %all-to-all-start = ((bf16[128,8,128]{2,1,0:T(8,128)(2,1)}), bf16[128,8,128]{2,1,0:T(8,128)(2,1)S(1)}, u32[]{:S(2)}, u32[]{:S(2)}) async-start(bf16[128,8,128]{2,1,0:T(8,128)(2,1)} %bitcast.20), calls=%async_computation | async-start | bytes 524288 | tf_op jit(solution)/shard_map/all_to_all | solution.py:329
  24.4 5.6 %norm.1 = (bf16[128,2048]{1,0:T(8,128)(2,1)}, bf16[128,2048]{1,0:T(8,128)(2,1)}, bf16[128,2048]{1,0:T(8,128)(2,1)}, bf16[128,2048]{1,0:T(8,128)(2,1)}) custom-call(bf16[128,8192]{1,0:T(8,128)(2,1)} %x_hbm.1, bf16[64,128]{1,0:T(8,128)(2,1)} %bitcast.24, s32[5]{0:T(128)} %stack.23.at_ref.refs_10_.refs_14_), custom_call_target="tpu_custom_call" | custom-call | flops 1073741824 | bytes 4210708 | tf_op jit(solution)/shard_map/norm/pallas_call | solution.py:29
  30.0 0.0 copy-start
  30.0 4.9 %collective-permute-start = (bf16[128,2048]{1,0:T(8,128)(2,1)}, bf16[128,2048]{1,0:T(8,128)(2,1)S(1)}, u32[]{:S(2)}, u32[]{:S(2)}) collective-permute-start(bf16[128,2048]{1,0:T(8,128)(2,1)} %get-tuple-element.30), channel_id=1, source_target_pairs={{0,2},{1,3},{2,0},{3,1},{4,6},{5,7},{6,4},{7,5},{8,10},{9,11},{10,... | collective-permute-start | bytes 1572872 | tf_op jit(solution)/shard_map/ppermute | solution.py:347
  35.0 2.2 %collective-permute-start.1 = (bf16[128,2048]{1,0:T(8,128)(2,1)}, bf16[128,2048]{1,0:T(8,128)(2,1)S(1)}, u32[]{:S(2)}, u32[]{:S(2)}) collective-permute-start(bf16[128,2048]{1,0:T(8,128)(2,1)} %get-tuple-element.31), channel_id=1, source_target_pairs={{0,1},{1,2},{2,3},{3,0},{4,5},{5,6},{6,7},{7,4},{8,9},{9,10},{10,1... | collective-permute-start | bytes 1572872 | tf_op jit(solution)/shard_map/ppermute | solution.py:347
  37.2 4.3 %collective-permute-start.2 = (bf16[128,2048]{1,0:T(8,128)(2,1)}, bf16[128,2048]{1,0:T(8,128)(2,1)}, u32[]{:S(2)}, u32[]{:S(2)}) collective-permute-start(bf16[128,2048]{1,0:T(8,128)(2,1)} %get-tuple-element.32), channel_id=1, source_target_pairs={{0,3},{1,0},{2,1},{3,2},{4,7},{5,4},{6,5},{7,6},{8,11},{9,8},{10,9... | collective-permute-start | bytes 1572872 | tf_op jit(solution)/shard_map/ppermute | solution.py:347
  41.5 6.5 %all-to-all-done = bf16[128,8,128]{2,1,0:T(8,128)(2,1)S(1)} async-done(((bf16[128,8,128]{2,1,0:T(8,128)(2,1)}), bf16[128,8,128]{2,1,0:T(8,128)(2,1)S(1)}, u32[]{:S(2)}, u32[]{:S(2)}) %all-to-all-start) | async-done | bytes 262176 | tf_op jit(solution)/shard_map/all_to_all | solution.py:329
  48.0 1.3 spread.1
  49.3 4.2 %all-to-all-start.1 = ((bf16[4,1024,128]{2,1,0:T(8,128)(2,1)}), bf16[4,1024,128]{2,1,0:T(8,128)(2,1)S(1)}, u32[]{:S(2)}, u32[]{:S(2)}) async-start(bf16[4,1024,128]{2,1,0:T(8,128)(2,1)} %spread.1), calls=%async_computation.1 | async-start | bytes 2097152 | tf_op jit(solution)/shard_map/all_to_all | solution.py:357
  53.5 1.9 %collective-permute-start.3 = (bf16[128,2048]{1,0:T(8,128)(2,1)S(1)}, bf16[128,2048]{1,0:T(8,128)(2,1)}, u32[]{:S(2)}, u32[]{:S(2)}) collective-permute-start(bf16[128,2048]{1,0:T(8,128)(2,1)S(1)} %copy-done.1), channel_id=1, source_target_pairs={{0,8},{8,0},{1,9},{9,1},{2,10},{10,2},{3,11},{11,3},{4,12},{12,4},... | collective-permute-start | bytes 1572872 | tf_op jit(solution)/shard_map/ppermute | solution.py:348
  55.4 0.0 collective-permute-done.refs_1_
  55.4 2.4 %collective-permute-start.4 = (bf16[128,2048]{1,0:T(8,128)(2,1)S(1)}, bf16[128,2048]{1,0:T(8,128)(2,1)}, u32[]{:S(2)}, u32[]{:S(2)}) collective-permute-start(bf16[128,2048]{1,0:T(8,128)(2,1)S(1)} %collective-permute-done.refs_1_), channel_id=1, source_target_pairs={{0,8},{8,0},{1,9},{9,1},{2,10},{10,2},{3,11},{11,3},{4,12},{12,4},... | collective-permute-start | bytes 1572872 | tf_op jit(solution)/shard_map/ppermute | solution.py:348
  57.8 2.4 %collective-permute-done.1.refs_2_ = bf16[128,2048]{1,0:T(8,128)(2,1)S(1)} collective-permute-done((bf16[128,2048]{1,0:T(8,128)(2,1)}, bf16[128,2048]{1,0:T(8,128)(2,1)S(1)}, u32[]{:S(2)}, u32[]{:S(2)}) %collective-permute-start.1) | collective-permute-done | bytes 524320 | tf_op jit(solution)/shard_map/ppermute | solution.py:347
  60.2 2.4 %collective-permute-start.5 = (bf16[128,2048]{1,0:T(8,128)(2,1)S(1)}, bf16[128,2048]{1,0:T(8,128)(2,1)}, u32[]{:S(2)}, u32[]{:S(2)}) collective-permute-start(bf16[128,2048]{1,0:T(8,128)(2,1)S(1)} %collective-permute-done.1.refs_2_), channel_id=1, source_target_pairs={{0,8},{8,0},{1,9},{9,1},{2,10},{10,2},{3,11},{11,3},{4,12},{12,4},... | collective-permute-start | bytes 1572872 | tf_op jit(solution)/shard_map/ppermute | solution.py:348
  62.6 0.0 collective-permute-done.2.refs_3_
  62.6 1.9 %collective-permute-start.6 = (bf16[128,2048]{1,0:T(8,128)(2,1)}, bf16[128,2048]{1,0:T(8,128)(2,1)}, u32[]{:S(2)}, u32[]{:S(2)}) collective-permute-start(bf16[128,2048]{1,0:T(8,128)(2,1)} %collective-permute-done.2.refs_3_), channel_id=1, source_target_pairs={{0,8},{8,0},{1,9},{9,1},{2,10},{10,2},{3,11},{11,3},{4,12},{12,4},... | collective-permute-start | bytes 1572872 | tf_op jit(solution)/shard_map/ppermute | solution.py:348
  64.6 0.9 choose.1
  65.5 1.9 %all-to-all-done.1.w_ref = bf16[4,1024,128]{2,1,0:T(8,128)(2,1)S(1)} async-done(((bf16[4,1024,128]{2,1,0:T(8,128)(2,1)}), bf16[4,1024,128]{2,1,0:T(8,128)(2,1)S(1)}, u32[]{:S(2)}, u32[]{:S(2)}) %all-to-all-start.1) | async-done | bytes 1048608 | tf_op jit(solution)/shard_map/all_to_all | solution.py:357
  67.5 1.7 %decode.1 = (bf16[2048,256]{1,0:T(8,128)(2,1)S(1)}, bf16[2048,256]{1,0:T(8,128)(2,1)S(1)}) custom-call(bf16[4,1024,128]{2,1,0:T(8,128)(2,1)S(1)} %all-to-all-done.1.w_ref), custom_call_target="tpu_custom_call" | custom-call | bytes 3145728 | tf_op jit(solution)/shard_map/decode/pallas_call | solution.py:29
  69.1 0.0 collective-permute-done.3.refs_4_
  69.2 0.0 collective-permute-done.4.refs_5_
  69.2 0.0 collective-permute-done.5.refs_6_
  69.2 0.0 collective-permute-done.6.refs_7_
  69.2 4.9 %forward.1 = bf16[4,256,256]{2,1,0:T(8,128)(2,1)} custom-call(bf16[128,2048]{1,0:T(8,128)(2,1)S(1)} %copy-done.1, bf16[128,2048]{1,0:T(8,128)(2,1)S(1)} %collective-permute-done.refs_1_, bf16[128,2048]{1,0:T(8,128)(2,1)S(1)} %collective-permute-done.1.refs_2_, bf16[128,2048]{1,0:T(8,128)(2,1)} %collective-permute-done.2.refs_3_, ...), custom_call_target="tpu_custom_call" | custom-call | flops 2147483648 | bytes 6815764 | tf_op jit(solution)/shard_map/forward/pallas_call | solution.py:29
  74.1 4.0 %all-to-all-start.2 = ((bf16[4,256,256]{2,1,0:T(8,128)(2,1)}), bf16[4,256,256]{2,1,0:T(8,128)(2,1)S(1)}, u32[]{:S(2)}, u32[]{:S(2)}) async-start(bf16[4,256,256]{2,1,0:T(8,128)(2,1)} %forward.1), calls=%async_computation.2 | async-start | bytes 1048576 | tf_op jit(solution)/shard_map/all_to_all | solution.py:383
  78.1 4.9 %collective-permute-start.7 = (bf16[256,128]{1,0:T(8,128)(2,1)S(1)}, bf16[256,128]{1,0:T(8,128)(2,1)S(1)}, u32[]{:S(2)}, u32[]{:S(2)}) collective-permute-start(bf16[256,128]{1,0:T(8,128)(2,1)S(1)} %get-tuple-element.44), channel_id=1, source_target_pairs={{0,2},{1,3},{2,0},{3,1},{4,6},{5,7},{6,4},{7,5},{8,10},{9,11},{10,... | collective-permute-start | bytes 196616 | tf_op jit(solution)/shard_map/ppermute | solution.py:384
  83.0 2.2 %collective-permute-start.8 = (bf16[256,128]{1,0:T(8,128)(2,1)S(1)}, bf16[256,128]{1,0:T(8,128)(2,1)S(1)}, u32[]{:S(2)}, u32[]{:S(2)}) collective-permute-start(bf16[256,128]{1,0:T(8,128)(2,1)S(1)} %get-tuple-element.45), channel_id=1, source_target_pairs={{0,1},{1,2},{2,3},{3,0},{4,5},{5,6},{6,7},{7,4},{8,9},{9,10},{10,1... | collective-permute-start | bytes 196616 | tf_op jit(solution)/shard_map/ppermute | solution.py:384
  85.2 4.3 %collective-permute-start.9 = (bf16[256,128]{1,0:T(8,128)(2,1)S(1)}, bf16[256,128]{1,0:T(8,128)(2,1)S(1)}, u32[]{:S(2)}, u32[]{:S(2)}) collective-permute-start(bf16[256,128]{1,0:T(8,128)(2,1)S(1)} %get-tuple-element.46), channel_id=1, source_target_pairs={{0,3},{1,0},{2,1},{3,2},{4,7},{5,4},{6,5},{7,6},{8,11},{9,8},{10,9... | collective-permute-start | bytes 196616 | tf_op jit(solution)/shard_map/ppermute | solution.py:384
  89.5 0.0 all-to-all-done.2.part_ref
  89.5 0.9 slope.1
  90.4 0.0 collective-permute-done.7.refs_1_
  90.4 0.0 collective-permute-done.8.refs_2_
  90.4 0.4 collective-permute-done.9.refs_3_
  90.8 4.3 %all-to-all-start.3 = ((bf16[4,256,256]{2,1,0:T(8,128)(2,1)}), bf16[4,256,256]{2,1,0:T(8,128)(2,1)S(1)}, u32[]{:S(2)}, u32[]{:S(2)}) async-start(bf16[4,256,256]{2,1,0:T(8,128)(2,1)} %get-tuple-element.51), calls=%async_computation.3 | async-start | bytes 1048576 | tf_op jit(solution)/shard_map/all_to_all | solution.py:389
  95.1 2.5 %collective-permute-start.12 = (bf16[256,128]{1,0:T(8,128)(2,1)S(1)}, bf16[256,128]{1,0:T(8,128)(2,1)S(1)}, u32[]{:S(2)}, u32[]{:S(2)}) collective-permute-start(bf16[256,128]{1,0:T(8,128)(2,1)S(1)} %join.1.refs_8_), channel_id=1, source_target_pairs={{0,20},{4,16},{16,4},{20,0},{1,21},{5,17},{17,5},{21,1},{2,22},{6,... | collective-permute-start | bytes 196616 | tf_op jit(solution)/shard_map/ppermute | solution.py:391
  97.6 2.2 %collective-permute-start.11 = (bf16[256,128]{1,0:T(8,128)(2,1)S(1)}, bf16[256,128]{1,0:T(8,128)(2,1)S(1)}, u32[]{:S(2)}, u32[]{:S(2)}) collective-permute-start(bf16[256,128]{1,0:T(8,128)(2,1)S(1)} %join.1.refs_8_), channel_id=1, source_target_pairs={{0,16},{4,20},{16,0},{20,4},{1,17},{5,21},{17,1},{21,5},{2,18},{6,... | collective-permute-start | bytes 196616 | tf_op jit(solution)/shard_map/ppermute | solution.py:391
  99.8 5.0 %collective-permute-start.10 = (bf16[256,128]{1,0:T(8,128)(2,1)S(1)}, bf16[256,128]{1,0:T(8,128)(2,1)S(1)}, u32[]{:S(2)}, u32[]{:S(2)}) collective-permute-start(bf16[256,128]{1,0:T(8,128)(2,1)S(1)} %join.1.refs_8_), channel_id=1, source_target_pairs={{0,4},{4,0},{16,20},{20,16},{1,5},{5,1},{17,21},{21,17},{2,6},{6,2... | collective-permute-start | bytes 196616 | tf_op jit(solution)/shard_map/ppermute | solution.py:391
  104.9 0.0 collective-permute-done.11.refs_10_
  104.9 1.4 collective-permute-done.10.refs_9_
  106.4 0.0 all-to-all-done.3.refs_12_
  106.4 4.0 %grad.1 = bf16[4,528,128]{2,1,0:T(8,128)(2,1)S(1)} custom-call(bf16[128,2048]{1,0:T(8,128)(2,1)S(1)} %copy-done.1, bf16[128,2048]{1,0:T(8,128)(2,1)S(1)} %collective-permute-done.refs_1_, bf16[128,2048]{1,0:T(8,128)(2,1)S(1)} %collective-permute-done.1.refs_2_, bf16[128,2048]{1,0:T(8,128)(2,1)} %collective-permute-done.2.refs_3_, ...), custom_call_target="tpu_custom_call" | custom-call | flops 1073741824 | bytes 5521940 | tf_op jit(solution)/shard_map/grad/pallas_call | solution.py:29
  110.3 0.0 copy-start.2
  110.4 11.0 %all_to_all.30.got_ref = bf16[4,528,128]{2,1,0:T(8,128)(2,1)S(1)} all-to-all(bf16[4,528,128]{2,1,0:T(8,128)(2,1)S(1)} %grad.1), channel_id=1, replica_groups=mesh['z'=16,'yl'=2,'core'=2,'yh'=2,'x'=4] {'yl','yh'}, dimensions={0} | all-to-all | bytes 1081344 | tf_op jit(solution)/shard_map/all_to_all | solution.py:406
  121.4 0.2 gather.1
  121.6 42.7 %all_to_all.31 = bf16[128,8,128]{2,1,0:T(8,128)(2,1)S(1)} all-to-all(bf16[128,8,128]{2,1,0:T(8,128)(2,1)S(1)} %bitcast.18), channel_id=1, replica_groups=mesh['z'=16,'yl'=2,'core'=2,'yh'=2,'x'=4] {'z','core','x'}, dimensions={0} | all-to-all | bytes 524288 | tf_op jit(solution)/shard_map/all_to_all | solution.py:414
  164.3 0.9 final.1
  (8 shorter events, 0.1 us)
Async XLA Ops:
  4.0 44.0 %all-to-all-start = ((bf16[128,8,128]{2,1,0:T(8,128)(2,1)}), bf16[128,8,128]{2,1,0:T(8,128)(2,1)S(1)}, u32[]{:S(2)}, u32[]{:S(2)}) async-start(bf16[128,8,128]{2,1,0:T(8,128)(2,1)} %bitcast.20), calls=%async_computation | async-start | bytes 524288 | tf_op jit(solution)/shard_map/all_to_all | solution.py:329
  30.0 23.5 %copy-start.1 = (bf16[128,2048]{1,0:T(8,128)(2,1)S(1)}, bf16[128,2048]{1,0:T(8,128)(2,1)}, u32[]{:S(2)}) copy-start(bf16[128,2048]{1,0:T(8,128)(2,1)} %get-tuple-element.29.refs_0_) | copy-start | bytes 1572868
  30.0 34.6 %copy-start = (s32[2048,64]{0,1:T(8,128)S(1)}, s32[2048,64]{0,1:T(8,128)}, u32[]{:S(2)}) copy-start(s32[2048,64]{0,1:T(8,128)} %param.9) | copy-start | bytes 1572868
  30.0 34.6 %copy-start.3 = (s32[5]{0:T(128)S(1)}, s32[5]{0:T(128)}, u32[]{:S(2)}) copy-start(s32[5]{0:T(128)} %stack.23.at_ref.refs_10_.refs_14_) | copy-start | bytes 64
  30.0 25.4 %collective-permute-start = (bf16[128,2048]{1,0:T(8,128)(2,1)}, bf16[128,2048]{1,0:T(8,128)(2,1)S(1)}, u32[]{:S(2)}, u32[]{:S(2)}) collective-permute-start(bf16[128,2048]{1,0:T(8,128)(2,1)} %get-tuple-element.30), channel_id=1, source_target_pairs={{0,2},{1,3},{2,0},{3,1},{4,6},{5,7},{6,4},{7,5},{8,10},{9,11},{10,... | collective-permute-start | bytes 1572872 | tf_op jit(solution)/shard_map/ppermute | solution.py:347
  35.0 25.3 %collective-permute-start.1 = (bf16[128,2048]{1,0:T(8,128)(2,1)}, bf16[128,2048]{1,0:T(8,128)(2,1)S(1)}, u32[]{:S(2)}, u32[]{:S(2)}) collective-permute-start(bf16[128,2048]{1,0:T(8,128)(2,1)} %get-tuple-element.31), channel_id=1, source_target_pairs={{0,1},{1,2},{2,3},{3,0},{4,5},{5,6},{6,7},{7,4},{8,9},{9,10},{10,1... | collective-permute-start | bytes 1572872 | tf_op jit(solution)/shard_map/ppermute | solution.py:347
  37.2 25.5 %collective-permute-start.2 = (bf16[128,2048]{1,0:T(8,128)(2,1)}, bf16[128,2048]{1,0:T(8,128)(2,1)}, u32[]{:S(2)}, u32[]{:S(2)}) collective-permute-start(bf16[128,2048]{1,0:T(8,128)(2,1)} %get-tuple-element.32), channel_id=1, source_target_pairs={{0,3},{1,0},{2,1},{3,2},{4,7},{5,4},{6,5},{7,6},{8,11},{9,8},{10,9... | collective-permute-start | bytes 1572872 | tf_op jit(solution)/shard_map/ppermute | solution.py:347
  49.3 18.2 %all-to-all-start.1 = ((bf16[4,1024,128]{2,1,0:T(8,128)(2,1)}), bf16[4,1024,128]{2,1,0:T(8,128)(2,1)S(1)}, u32[]{:S(2)}, u32[]{:S(2)}) async-start(bf16[4,1024,128]{2,1,0:T(8,128)(2,1)} %spread.1), calls=%async_computation.1 | async-start | bytes 2097152 | tf_op jit(solution)/shard_map/all_to_all | solution.py:357
  53.5 15.7 %collective-permute-start.3 = (bf16[128,2048]{1,0:T(8,128)(2,1)S(1)}, bf16[128,2048]{1,0:T(8,128)(2,1)}, u32[]{:S(2)}, u32[]{:S(2)}) collective-permute-start(bf16[128,2048]{1,0:T(8,128)(2,1)S(1)} %copy-done.1), channel_id=1, source_target_pairs={{0,8},{8,0},{1,9},{9,1},{2,10},{10,2},{3,11},{11,3},{4,12},{12,4},... | collective-permute-start | bytes 1572872 | tf_op jit(solution)/shard_map/ppermute | solution.py:348
  55.4 13.8 %collective-permute-start.4 = (bf16[128,2048]{1,0:T(8,128)(2,1)S(1)}, bf16[128,2048]{1,0:T(8,128)(2,1)}, u32[]{:S(2)}, u32[]{:S(2)}) collective-permute-start(bf16[128,2048]{1,0:T(8,128)(2,1)S(1)} %collective-permute-done.refs_1_), channel_id=1, source_target_pairs={{0,8},{8,0},{1,9},{9,1},{2,10},{10,2},{3,11},{11,3},{4,12},{12,4},... | collective-permute-start | bytes 1572872 | tf_op jit(solution)/shard_map/ppermute | solution.py:348
  60.2 8.9 %collective-permute-start.5 = (bf16[128,2048]{1,0:T(8,128)(2,1)S(1)}, bf16[128,2048]{1,0:T(8,128)(2,1)}, u32[]{:S(2)}, u32[]{:S(2)}) collective-permute-start(bf16[128,2048]{1,0:T(8,128)(2,1)S(1)} %collective-permute-done.1.refs_2_), channel_id=1, source_target_pairs={{0,8},{8,0},{1,9},{9,1},{2,10},{10,2},{3,11},{11,3},{4,12},{12,4},... | collective-permute-start | bytes 1572872 | tf_op jit(solution)/shard_map/ppermute | solution.py:348
  62.6 6.5 %collective-permute-start.6 = (bf16[128,2048]{1,0:T(8,128)(2,1)}, bf16[128,2048]{1,0:T(8,128)(2,1)}, u32[]{:S(2)}, u32[]{:S(2)}) collective-permute-start(bf16[128,2048]{1,0:T(8,128)(2,1)} %collective-permute-done.2.refs_3_), channel_id=1, source_target_pairs={{0,8},{8,0},{1,9},{9,1},{2,10},{10,2},{3,11},{11,3},{4,12},{12,4},... | collective-permute-start | bytes 1572872 | tf_op jit(solution)/shard_map/ppermute | solution.py:348
  74.1 15.4 %all-to-all-start.2 = ((bf16[4,256,256]{2,1,0:T(8,128)(2,1)}), bf16[4,256,256]{2,1,0:T(8,128)(2,1)S(1)}, u32[]{:S(2)}, u32[]{:S(2)}) async-start(bf16[4,256,256]{2,1,0:T(8,128)(2,1)} %forward.1), calls=%async_computation.2 | async-start | bytes 1048576 | tf_op jit(solution)/shard_map/all_to_all | solution.py:383
  78.1 12.3 %collective-permute-start.7 = (bf16[256,128]{1,0:T(8,128)(2,1)S(1)}, bf16[256,128]{1,0:T(8,128)(2,1)S(1)}, u32[]{:S(2)}, u32[]{:S(2)}) collective-permute-start(bf16[256,128]{1,0:T(8,128)(2,1)S(1)} %get-tuple-element.44), channel_id=1, source_target_pairs={{0,2},{1,3},{2,0},{3,1},{4,6},{5,7},{6,4},{7,5},{8,10},{9,11},{10,... | collective-permute-start | bytes 196616 | tf_op jit(solution)/shard_map/ppermute | solution.py:384
  83.0 7.4 %collective-permute-start.8 = (bf16[256,128]{1,0:T(8,128)(2,1)S(1)}, bf16[256,128]{1,0:T(8,128)(2,1)S(1)}, u32[]{:S(2)}, u32[]{:S(2)}) collective-permute-start(bf16[256,128]{1,0:T(8,128)(2,1)S(1)} %get-tuple-element.45), channel_id=1, source_target_pairs={{0,1},{1,2},{2,3},{3,0},{4,5},{5,6},{6,7},{7,4},{8,9},{9,10},{10,1... | collective-permute-start | bytes 196616 | tf_op jit(solution)/shard_map/ppermute | solution.py:384
  85.2 5.6 %collective-permute-start.9 = (bf16[256,128]{1,0:T(8,128)(2,1)S(1)}, bf16[256,128]{1,0:T(8,128)(2,1)S(1)}, u32[]{:S(2)}, u32[]{:S(2)}) collective-permute-start(bf16[256,128]{1,0:T(8,128)(2,1)S(1)} %get-tuple-element.46), channel_id=1, source_target_pairs={{0,3},{1,0},{2,1},{3,2},{4,7},{5,4},{6,5},{7,6},{8,11},{9,8},{10,9... | collective-permute-start | bytes 196616 | tf_op jit(solution)/shard_map/ppermute | solution.py:384
  90.8 15.6 %all-to-all-start.3 = ((bf16[4,256,256]{2,1,0:T(8,128)(2,1)}), bf16[4,256,256]{2,1,0:T(8,128)(2,1)S(1)}, u32[]{:S(2)}, u32[]{:S(2)}) async-start(bf16[4,256,256]{2,1,0:T(8,128)(2,1)} %get-tuple-element.51), calls=%async_computation.3 | async-start | bytes 1048576 | tf_op jit(solution)/shard_map/all_to_all | solution.py:389
  95.1 9.8 %collective-permute-start.12 = (bf16[256,128]{1,0:T(8,128)(2,1)S(1)}, bf16[256,128]{1,0:T(8,128)(2,1)S(1)}, u32[]{:S(2)}, u32[]{:S(2)}) collective-permute-start(bf16[256,128]{1,0:T(8,128)(2,1)S(1)} %join.1.refs_8_), channel_id=1, source_target_pairs={{0,20},{4,16},{16,4},{20,0},{1,21},{5,17},{17,5},{21,1},{2,22},{6,... | collective-permute-start | bytes 196616 | tf_op jit(solution)/shard_map/ppermute | solution.py:391
  97.6 7.3 %collective-permute-start.11 = (bf16[256,128]{1,0:T(8,128)(2,1)S(1)}, bf16[256,128]{1,0:T(8,128)(2,1)S(1)}, u32[]{:S(2)}, u32[]{:S(2)}) collective-permute-start(bf16[256,128]{1,0:T(8,128)(2,1)S(1)} %join.1.refs_8_), channel_id=1, source_target_pairs={{0,16},{4,20},{16,0},{20,4},{1,17},{5,21},{17,1},{21,5},{2,18},{6,... | collective-permute-start | bytes 196616 | tf_op jit(solution)/shard_map/ppermute | solution.py:391
  99.8 6.5 %collective-permute-start.10 = (bf16[256,128]{1,0:T(8,128)(2,1)S(1)}, bf16[256,128]{1,0:T(8,128)(2,1)S(1)}, u32[]{:S(2)}, u32[]{:S(2)}) collective-permute-start(bf16[256,128]{1,0:T(8,128)(2,1)S(1)} %join.1.refs_8_), channel_id=1, source_target_pairs={{0,4},{4,0},{16,20},{20,16},{1,5},{5,1},{17,21},{21,17},{2,6},{6,2... | collective-permute-start | bytes 196616 | tf_op jit(solution)/shard_map/ppermute | solution.py:391
  110.3 53.9 %copy-start.2 = (f32[64,128]{1,0:T(8,128)S(1)}, f32[64,128]{1,0:T(8,128)}, u32[]{:S(2)}) copy-start(f32[64,128]{1,0:T(8,128)} %get-tuple-element.53.pat_ref) | copy-start | bytes 98308

commit v6 on v5

--- a/solution.py
+++ b/solution.py
@@ -110,28 +110,26 @@
             outs[i][:, tile * 128 : (tile + 1) * 128] = seg[:, x * 128 : (x + 1) * 128]
 
 
-def choose_kernel(pat_ref, at_ref, *outs):
-    me, core, own_yl = at_ref[0], at_ref[1], at_ref[2]
-    outs, pick_ref = outs[:NX], outs[NX]
+def choose_kernel(pat_ref, at_ref, out_ref, pick_ref):
     col = lax.broadcasted_iota(jnp.int32, (64, 128), 0)
     lane = lax.broadcasted_iota(jnp.int32, (64, 128), 1)
-    pick = jnp.where((col - core * 32 == lane - me * 32) & (lane // 32 == me), 1.0, 0.0)
+    pick = jnp.where(col - at_ref[1] * 32 == lane % 32, 1.0, 0.0).astype(BF16)
     chosen = lax.dot_general(
         pat_ref[...].astype(F32).astype(BF16),
-        pick.astype(BF16),
+        pick,
         (((0,), (0,)), ((), ())),
         preferred_element_type=F32,
     )
     pick_ref[...] = chosen.reshape(NZ, NYL, NC, NX, 8, 128)
-    for i, x in enumerate(STEP):
-        outs[i][...] = pick_ref[:, own_yl, :, (me + x) % NX].reshape(256, 128).astype(BF16)
-
-
-def join_kernel(*refs):
-    total = refs[0][...].astype(F32)
-    for ref in refs[1:NX]:
-        total += ref[...].astype(F32)
-    refs[NX][...] = total.astype(BF16)
+    group = lane_group((32, 128))
+    for x in range(NX):
+        for yl in range(NYL):
+            rows = pick_ref[:, yl, :, x].reshape(8, 32, 128)
+            for tile in range(2):
+                total = jnp.zeros((32, 128), F32)
+                for b in range(4):
+                    total = jnp.where(group == b, rows[tile * 4 + b], total)
+                out_ref[x, yl * 32 : (yl + 1) * 32, tile * 128 : (tile + 1) * 128] = total.astype(BF16)
 
 
 def pack_kernel(teacher_hbm, student_hbm, pat_hbm, at_ref, out_ref, rows_ref, *scratch):
@@ -197,13 +195,22 @@
 
 
 def forward_kernel(*refs):
-    pieces, (high_ref, low_ref, at_ref, out_ref) = refs[: 2 * NX], refs[2 * NX :]
-    for i in range(NX):
-        x = (at_ref[0] + BACK[i]) % NX
-        for ref, row in ((pieces[i], 0), (pieces[NX + i], 128)):
-            part = jnp.dot(ref[...], high_ref[...], preferred_element_type=F32)
-            part += jnp.dot(ref[...], low_ref[...], preferred_element_type=F32)
-            out_ref[x, row : row + 128] = part.astype(BF16)
+    own, pair, rest = refs[:NX], refs[NX : 2 * NX], refs[2 * NX :]
+    high_ref, low_ref, own_pat, other_pat, at_ref, out_ref, held_ref, sems = rest
+    loads = [pltpu.make_async_copy(pair[i], held_ref.at[i], sems.at[i]) for i in range(NX)]
+    for load in loads:
+        load.start()
+    for x in range(NX):
+        out_ref[x, 256:320] = own_pat[x]
+        out_ref[x, 320:] = other_pat[x]
+    for row in (0, 128):
+        for i in range(NX):
+            if row:
+                loads[i].wait()
+            rows = held_ref[i] if row else own[i][...]
+            part = jnp.dot(rows, high_ref[...], preferred_element_type=F32)
+            part += jnp.dot(rows, low_ref[...], preferred_element_type=F32)
+            out_ref[(at_ref[0] + BACK[i]) % NX, row : row + 128] = part.astype(BF16)
 
 
 def thirds(value, rows):
@@ -214,20 +221,31 @@
     return jnp.where(row == 0, high, jnp.where(row == 1, mid, jnp.where(row == 2, low, 0.0)))
 
 
-def slope_kernel(part_ref, out_ref, loss_ref):
-    diff = part_ref[0].astype(F32)
+def slope_kernel(part_ref, out_ref, loss_ref, pat_ref):
+    diff = part_ref[0, :256].astype(F32)
     for x in range(1, NX):
-        diff = diff + part_ref[x].astype(F32)
+        diff = diff + part_ref[x, :256].astype(F32)
     slope = diff.astype(BF16)
     for x in range(NX):
         out_ref[x] = slope
     square = diff * diff
     loss_ref[...] = jnp.sum(square[:, :128] + square[:, 128:], axis=0, keepdims=True)
+    group = lane_group((32, 128))
+    for part in range(4):
+        for b in range(8):
+            total = jnp.zeros((32, 128), F32)
+            for x in range(NX):
+                sent = part_ref[x, 256 + part * 32 : 288 + part * 32, b // 4 * 128 : b // 4 * 128 + 128]
+                shift = (x - b) % 4 * 32
+                sent = sent.astype(F32)
+                sent = pltpu.roll(sent, shift, 1) if shift else sent
+                total = jnp.where(group == x, sent, total)
+            pat_ref[part, b * 32 : (b + 1) * 32, :] = total.astype(BF16)
 
 
 def grad_kernel(*refs):
-    pieces, pats, rest = refs[: 2 * NX], refs[2 * NX : 2 * NX + 4], refs[2 * NX + 4 :]
-    slope_ref, loss_ref, at_ref, out_ref, s_ref, term_ref = rest
+    own, (held_ref, *rest) = refs[:NX], refs[NX:]
+    pat_ref, slope_ref, loss_ref, at_ref, out_ref, s_ref, term_ref = rest
     contract = (((0,), (0,)), ((), ()))
     for i in range(NX):
         x = (at_ref[0] + BACK[i]) % NX
@@ -235,7 +253,9 @@
         s_ref[512 + i * 128 : 512 + (i + 1) * 128] = slope_ref[x, 128:]
     for k in range(8):
         at = k * 256
-        rows = jnp.concatenate([p[:, at : at + 256] for p in pieces], axis=0)
+        rows = [ref[:, at : at + 256] for ref in own]
+        rows += [held_ref[i, :, at : at + 256] for i in range(NX)]
+        rows = jnp.concatenate(rows, axis=0)
         term = lax.dot_general(rows, s_ref[...], contract, preferred_element_type=F32)
         for yh in range(2):
             term_ref[(k // 4) * 2 + yh, (k % 4) * 8 : (k % 4 + 1) * 8] = term[
@@ -243,8 +263,8 @@
             ].reshape(8, 4, 8, 128)
     loss = thirds(loss_ref[...], 16).astype(BF16)
     for i in range(4):
-        y = at_ref[4] ^ i
-        first, second = kept_rows(pats[i][...].astype(F32).reshape(32, 8, 128))
+        y = i % 2 * 2 + jnp.where(i < 2, at_ref[4], 1 - at_ref[4])
+        first, second = kept_rows(pat_ref[i].astype(F32).reshape(32, 8, 128))
         for row, which in ((0, first), (256, second)):
             kept = jnp.zeros_like(which)
             for k in range(4):
@@ -306,7 +326,7 @@
 def shards(hidden, norm_gain, teacher_k, student_k, keep_pattern):
     z, yl, core, yh, x = (lax.axis_index(a) for a in AXES)
     place = (z * NYL + yl) * NC + core
-    at = jnp.stack([x, core, yl, place, yl * NYH + yh]).astype(jnp.int32)
+    at = jnp.stack([x, core, yl, place, yh]).astype(jnp.int32)
     patterns = keep_pattern.T
 
     packed, pat = call(
@@ -358,44 +378,47 @@
     high, low = call(decode_kernel, (shape((2048, 256), BF16),) * 2, all_w, name="decode")
 
     late, _ = lax.optimization_barrier((patterns, rows_w))
-    chosen = call(
+    own_pat = call(
         choose_kernel,
-        (shape((256, 128), BF16),) * NX,
+        shape((NX, 64, 256), BF16),
         late,
         at,
         scratch=[pltpu.VMEM((NZ, NYL, NC, NX, 8, 128), F32)],
         name="choose",
     )
+    other_pat = lax.ppermute(own_pat, "yh", [(0, 1), (1, 0)])
 
     flops = 2 * 1024 * 2048 * 256
-    part = call(
+    part, held = call(
         forward_kernel,
-        shape((NX, 256, 256), BF16),
+        (shape((NX, 384, 256), BF16), shape((NX, 128, 2048), BF16)),
         *own,
         *pair,
         high,
         low,
+        own_pat,
+        other_pat,
         at,
+        scratch=[pltpu.SemaphoreType.DMA((NX,))],
         flops=2 * flops,
+        far=range(NX, 2 * NX),
         name="forward",
     )
-    part, chosen = lax.optimization_barrier((part, chosen))
     got_part = lax.all_to_all(part, "x", 0, 0, tiled=True)
-    line = [chosen[0]] + [lax.ppermute(chosen[i], "x", ring(STEP[i])) for i in range(1, NX)]
-    slope, loss_part = call(
-        slope_kernel, (shape((NX, 256, 256), BF16), shape((1, 128), F32)), got_part, name="slope"
-    )
-    slope, line = lax.optimization_barrier((slope, line))
+    slope, loss_part, pats = call(
+        slope_kernel,
+        (shape((NX, 256, 256), BF16), shape((1, 128), F32), shape((4, 256, 128), BF16)),
+        got_part,
+        name="slope",
+    )
     slopes = lax.all_to_all(slope, "x", 0, 0, tiled=True)
-    joined = call(join_kernel, shape((256, 128), BF16), *line, name="join")
-    pats = [joined] + [lax.ppermute(joined, Y, [(y, y ^ i) for y in range(4)]) for i in range(1, 4)]
 
     term = call(
         grad_kernel,
         shape((4, 528, 128), BF16),
         *own,
-        *pair,
-        *pats,
+        held,
+        pats,
         slopes,
         loss_part,
         at,

time: 166 us -> 160 us (0.964)
  starting transfers between devices: 74.1 us -> 49.5 us
  blocking collectives: 53.7 us -> 75.8 us
  waiting for transfers between devices: 12.7 us -> 10.4 us
    all_to_all x0 -> x2, blocking collectives: none -> 23.3 us  [the longest x1 14 us: shards(): got_part = lax.all_to_all(part, 'x', 0, 0, tiled=True)]
    ppermute x6 -> x1, starting transfers between devices: 21.1 us -> 4.83 us  [shards(): other_pat = lax.ppermute(own_pat, 'yh', [(0, 1), (1, 0)])]
    all_to_all x2 -> x0, starting transfers between devices: 8.29 us -> none  [the longest x1 4.26 us: shards(): slopes = lax.all_to_all(slope, 'x', 0, 0, tiled=True)]
    all_to_all x1, waiting for transfers between devices: 1.92 us -> 0.01 us  [shards(): all_w = lax.all_to_all(rows_w, Y, 0, 0, tiled=True)]
    pallas_call x11 -> x10, Pallas kernels: 23.2 us -> 22 us  [call(): pl.pallas_call(kernel, out_shape=out_shape, in_specs=specs, out_specs=jax...]
  transfers between devices with their start and end apart: 17 -> 10, of which waited for: 5 -> 3; matrix products, arithmetic and copies ran while one was open for 0% -> 0% of each run, Pallas kernels for 6% -> 6%
where the time goes in v6:
time: 160 us; the launch traced here: 159 us
  blocking collectives  75.8 us (47%)
  starting transfers between devices  49.5 us (31%)
  Pallas kernels  22 us (14%)
  waiting for transfers between devices  10.4 us (6%)
    all_to_all x1, blocking collectives, shards(): lax.all_to_all(packed_term.reshape(128, 8, 128), ZCX, 0, 0, tiled=True)  41.5 us
    pallas_call x10, Pallas kernels, call(): pl.pallas_call(kernel, out_shape=out_shape, in_specs=specs, out_specs=jax...  22 us
    all_to_all x1, starting transfers between devices, shards(): got_w = lax.all_to_all(packed.reshape(128, 8, 128), ZCX, 0, 0, tiled=True)  20.4 us
    all_to_all x1, blocking collectives, shards(): got_part = lax.all_to_all(part, 'x', 0, 0, tiled=True)  14 us
    ppermute x3, starting transfers between devices, shards(): lax.ppermute(split[i], 'x', ring(STEP[i]))  11.4 us
    all_to_all x1, blocking collectives, shards(): got_term = lax.all_to_all(term, Y, 0, 0, tiled=True)  11 us
    all_to_all x1, blocking collectives, shards(): slopes = lax.all_to_all(slope, 'x', 0, 0, tiled=True)  9.34 us
    ppermute x4, starting transfers between devices, shards(): pair = [lax.ppermute(piece, 'core', [(0, 1), (1, 0)]) for piece in own]  8.63 us
  transfers between devices with their start and end apart: 10, of which 3 were waited for; matrix products, arithmetic and copies ran while one was open for 0% of the time, Pallas kernels for 6%

profile of v6, /device:TPU:1, one launch (start us, length us, event | category | flops | bytes accessed | tf_op | source)
XLA Modules:
  0.0 159.2 jit_solution(15680759876496503082)
XLA Ops:
  0.6 0.7 stack.23.at_ref.refs_12_.refs_8_
  1.3 2.7 %pack.1 = (bf16[16,64,128]{2,1,0:T(8,128)(2,1)}, f32[64,128]{1,0:T(8,128)}) custom-call(bf16[64,128]{1,0:T(8,128)(2,1)} %bitcast.21, bf16[64,128]{1,0:T(8,128)(2,1)} %bitcast.22, s32[64,2048]{1,0:T(8,128)} %bitcast.15, s32[5]{0:T(128)} %stack.23.at_ref.refs_12_.refs_8_), custom_call_target="tpu_custom_call" | custom-call | bytes 851988 | tf_op jit(solution)/shard_map/pack/pallas_call | solution.py:29
  4.0 20.4 %all-to-all-start = ((bf16[128,8,128]{2,1,0:T(8,128)(2,1)}), bf16[128,8,128]{2,1,0:T(8,128)(2,1)S(1)}, u32[]{:S(2)}, u32[]{:S(2)}) async-start(bf16[128,8,128]{2,1,0:T(8,128)(2,1)} %bitcast.20), calls=%async_computation | async-start | bytes 524288 | tf_op jit(solution)/shard_map/all_to_all | solution.py:349
  24.5 5.6 %norm.1 = (bf16[128,2048]{1,0:T(8,128)(2,1)}, bf16[128,2048]{1,0:T(8,128)(2,1)}, bf16[128,2048]{1,0:T(8,128)(2,1)}, bf16[128,2048]{1,0:T(8,128)(2,1)}) custom-call(bf16[128,8192]{1,0:T(8,128)(2,1)} %x_hbm.1, bf16[64,128]{1,0:T(8,128)(2,1)} %bitcast.24, s32[5]{0:T(128)} %stack.23.at_ref.refs_12_.refs_8_), custom_call_target="tpu_custom_call" | custom-call | flops 1073741824 | bytes 4210708 | tf_op jit(solution)/shard_map/norm/pallas_call | solution.py:29
  30.0 0.0 copy-start.1
  30.1 0.0 copy-start
  30.1 0.0 copy-start.3
  30.1 4.9 %collective-permute-start = (bf16[128,2048]{1,0:T(8,128)(2,1)}, bf16[128,2048]{1,0:T(8,128)(2,1)S(1)}, u32[]{:S(2)}, u32[]{:S(2)}) collective-permute-start(bf16[128,2048]{1,0:T(8,128)(2,1)} %get-tuple-element.19), channel_id=1, source_target_pairs={{0,2},{1,3},{2,0},{3,1},{4,6},{5,7},{6,4},{7,5},{8,10},{9,11},{10,... | collective-permute-start | bytes 1572872 | tf_op jit(solution)/shard_map/ppermute | solution.py:367
  35.0 2.2 %collective-permute-start.1 = (bf16[128,2048]{1,0:T(8,128)(2,1)}, bf16[128,2048]{1,0:T(8,128)(2,1)S(1)}, u32[]{:S(2)}, u32[]{:S(2)}) collective-permute-start(bf16[128,2048]{1,0:T(8,128)(2,1)} %get-tuple-element.20), channel_id=1, source_target_pairs={{0,1},{1,2},{2,3},{3,0},{4,5},{5,6},{6,7},{7,4},{8,9},{9,10},{10,1... | collective-permute-start | bytes 1572872 | tf_op jit(solution)/shard_map/ppermute | solution.py:367
  37.2 4.3 %collective-permute-start.2 = (bf16[128,2048]{1,0:T(8,128)(2,1)}, bf16[128,2048]{1,0:T(8,128)(2,1)}, u32[]{:S(2)}, u32[]{:S(2)}) collective-permute-start(bf16[128,2048]{1,0:T(8,128)(2,1)} %get-tuple-element.21), channel_id=1, source_target_pairs={{0,3},{1,0},{2,1},{3,2},{4,7},{5,4},{6,5},{7,6},{8,11},{9,8},{10,9... | collective-permute-start | bytes 1572872 | tf_op jit(solution)/shard_map/ppermute | solution.py:367
  41.5 6.5 %all-to-all-done = bf16[128,8,128]{2,1,0:T(8,128)(2,1)S(1)} async-done(((bf16[128,8,128]{2,1,0:T(8,128)(2,1)}), bf16[128,8,128]{2,1,0:T(8,128)(2,1)S(1)}, u32[]{:S(2)}, u32[]{:S(2)}) %all-to-all-start) | async-done | bytes 262176 | tf_op jit(solution)/shard_map/all_to_all | solution.py:349
  48.0 1.3 spread.1
  49.3 4.2 %all-to-all-start.1 = ((bf16[4,1024,128]{2,1,0:T(8,128)(2,1)}), bf16[4,1024,128]{2,1,0:T(8,128)(2,1)S(1)}, u32[]{:S(2)}, u32[]{:S(2)}) async-start(bf16[4,1024,128]{2,1,0:T(8,128)(2,1)} %spread.1), calls=%async_computation.1 | async-start | bytes 2097152 | tf_op jit(solution)/shard_map/all_to_all | solution.py:377
  53.5 0.0 copy-done.1
  53.5 1.9 %collective-permute-start.3 = (bf16[128,2048]{1,0:T(8,128)(2,1)S(1)}, bf16[128,2048]{1,0:T(8,128)(2,1)}, u32[]{:S(2)}, u32[]{:S(2)}) collective-permute-start(bf16[128,2048]{1,0:T(8,128)(2,1)S(1)} %copy-done.1), channel_id=1, source_target_pairs={{0,8},{8,0},{1,9},{9,1},{2,10},{10,2},{3,11},{11,3},{4,12},{12,4},... | collective-permute-start | bytes 1572872 | tf_op jit(solution)/shard_map/ppermute | solution.py:368
  55.4 0.0 collective-permute-done.refs_1_
  55.5 2.4 %collective-permute-start.4 = (bf16[128,2048]{1,0:T(8,128)(2,1)S(1)}, bf16[128,2048]{1,0:T(8,128)(2,1)}, u32[]{:S(2)}, u32[]{:S(2)}) collective-permute-start(bf16[128,2048]{1,0:T(8,128)(2,1)S(1)} %collective-permute-done.refs_1_), channel_id=1, source_target_pairs={{0,8},{8,0},{1,9},{9,1},{2,10},{10,2},{3,11},{11,3},{4,12},{12,4},... | collective-permute-start | bytes 1572872 | tf_op jit(solution)/shard_map/ppermute | solution.py:368
  57.9 2.4 %collective-permute-done.1.refs_2_ = bf16[128,2048]{1,0:T(8,128)(2,1)S(1)} collective-permute-done((bf16[128,2048]{1,0:T(8,128)(2,1)}, bf16[128,2048]{1,0:T(8,128)(2,1)S(1)}, u32[]{:S(2)}, u32[]{:S(2)}) %collective-permute-start.1) | collective-permute-done | bytes 524320 | tf_op jit(solution)/shard_map/ppermute | solution.py:367
  60.3 2.4 %collective-permute-start.5 = (bf16[128,2048]{1,0:T(8,128)(2,1)S(1)}, bf16[128,2048]{1,0:T(8,128)(2,1)}, u32[]{:S(2)}, u32[]{:S(2)}) collective-permute-start(bf16[128,2048]{1,0:T(8,128)(2,1)S(1)} %collective-permute-done.1.refs_2_), channel_id=1, source_target_pairs={{0,8},{8,0},{1,9},{9,1},{2,10},{10,2},{3,11},{11,3},{4,12},{12,4},... | collective-permute-start | bytes 1572872 | tf_op jit(solution)/shard_map/ppermute | solution.py:368
  62.7 0.0 collective-permute-done.2.refs_3_
  62.7 1.9 %collective-permute-start.6 = (bf16[128,2048]{1,0:T(8,128)(2,1)}, bf16[128,2048]{1,0:T(8,128)(2,1)}, u32[]{:S(2)}, u32[]{:S(2)}) collective-permute-start(bf16[128,2048]{1,0:T(8,128)(2,1)} %collective-permute-done.2.refs_3_), channel_id=1, source_target_pairs={{0,8},{8,0},{1,9},{9,1},{2,10},{10,2},{3,11},{11,3},{4,12},{12,4},... | collective-permute-start | bytes 1572872 | tf_op jit(solution)/shard_map/ppermute | solution.py:368
  64.6 0.0 copy-done
  64.6 0.0 copy-done.3
  64.6 0.9 choose.1.refs_10_
  65.5 4.8 %collective-permute-start.7 = (bf16[4,64,256]{2,1,0:T(8,128)(2,1)S(1)}, bf16[4,64,256]{2,1,0:T(8,128)(2,1)S(1)}, u32[]{:S(2)}, u32[]{:S(2)}) collective-permute-start(bf16[4,64,256]{2,1,0:T(8,128)(2,1)S(1)} %choose.1.refs_10_), channel_id=1, source_target_pairs={{0,4},{4,0},{1,5},{5,1},{2,6},{6,2},{3,7},{7,3},{8,12},{12,8},{9,1... | collective-permute-start | bytes 393224 | tf_op jit(solution)/shard_map/ppermute | solution.py:389
  70.4 0.0 all-to-all-done.1.w_ref
  70.4 1.7 %decode.1 = (bf16[2048,256]{1,0:T(8,128)(2,1)S(1)}, bf16[2048,256]{1,0:T(8,128)(2,1)S(1)}) custom-call(bf16[4,1024,128]{2,1,0:T(8,128)(2,1)S(1)} %all-to-all-done.1.w_ref), custom_call_target="tpu_custom_call" | custom-call | bytes 3145728 | tf_op jit(solution)/shard_map/decode/pallas_call | solution.py:29
  72.1 0.0 collective-permute-done.3.refs_4_
  72.1 0.0 collective-permute-done.4.refs_5_
  72.1 0.0 collective-permute-done.5.refs_6_
  72.1 0.0 collective-permute-done.6.refs_7_
  72.1 1.4 collective-permute-done.7.refs_11_
  73.5 5.1 %forward.1 = (bf16[4,384,256]{2,1,0:T(8,128)(2,1)S(1)}, bf16[4,128,2048]{2,1,0:T(8,128)(2,1)S(1)}) custom-call(bf16[128,2048]{1,0:T(8,128)(2,1)S(1)} %copy-done.1, bf16[128,2048]{1,0:T(8,128)(2,1)S(1)} %collective-permute-done.refs_1_, bf16[128,2048]{1,0:T(8,128)(2,1)S(1)} %collective-permute-done.1.refs_2_, ...), custom_call_target="tpu_custom_call" | custom-call | flops 2147483648 | bytes 9437204 | tf_op jit(solution)/shard_map/forward/pallas_call | solution.py:29
  78.6 14.0 %all_to_all.30.part_ref = bf16[4,384,256]{2,1,0:T(8,128)(2,1)S(1)} all-to-all(bf16[4,384,256]{2,1,0:T(8,128)(2,1)S(1)} %get-tuple-element.27), channel_id=1, replica_groups=mesh['z'=16,'yl'=2,'core'=2,'yh'=2,'x'=4] {'x'}, dimensions={0} | all-to-all | bytes 1572864 | tf_op jit(solution)/shard_map/all_to_all | solution.py:407
  92.6 0.4 slope.1
  93.0 9.3 %all_to_all.31.refs_6_ = bf16[4,256,256]{2,1,0:T(8,128)(2,1)S(1)} all-to-all(bf16[4,256,256]{2,1,0:T(8,128)(2,1)S(1)} %get-tuple-element.29), channel_id=1, replica_groups=mesh['z'=16,'yl'=2,'core'=2,'yh'=2,'x'=4] {'x'}, dimensions={0} | all-to-all | bytes 1048576 | tf_op jit(solution)/shard_map/all_to_all | solution.py:414
  102.4 3.2 %grad.1 = bf16[4,528,128]{2,1,0:T(8,128)(2,1)S(1)} custom-call(bf16[128,2048]{1,0:T(8,128)(2,1)S(1)} %copy-done.1, bf16[128,2048]{1,0:T(8,128)(2,1)S(1)} %collective-permute-done.refs_1_, bf16[128,2048]{1,0:T(8,128)(2,1)S(1)} %collective-permute-done.1.refs_2_, bf16[128,2048]{1,0:T(8,128)(2,1)} %collective-permute-done.2.refs_3_, ...), custom_call_target="tpu_custom_call" | custom-call | flops 1073741824 | bytes 5521940 | tf_op jit(solution)/shard_map/grad/pallas_call | solution.py:29
  105.6 0.0 copy-start.2
  105.6 11.0 %all_to_all.32.got_ref = bf16[4,528,128]{2,1,0:T(8,128)(2,1)S(1)} all-to-all(bf16[4,528,128]{2,1,0:T(8,128)(2,1)S(1)} %grad.1), channel_id=1, replica_groups=mesh['z'=16,'yl'=2,'core'=2,'yh'=2,'x'=4] {'yl','yh'}, dimensions={0} | all-to-all | bytes 1081344 | tf_op jit(solution)/shard_map/all_to_all | solution.py:429
  116.6 0.2 gather.1
  116.8 41.5 %all_to_all.33 = bf16[128,8,128]{2,1,0:T(8,128)(2,1)S(1)} all-to-all(bf16[128,8,128]{2,1,0:T(8,128)(2,1)S(1)} %bitcast.18), channel_id=1, replica_groups=mesh['z'=16,'yl'=2,'core'=2,'yh'=2,'x'=4] {'z','core','x'}, dimensions={0} | all-to-all | bytes 524288 | tf_op jit(solution)/shard_map/all_to_all | solution.py:437
  158.3 0.0 copy-done.2
  158.3 0.9 final.1
Async XLA Ops:
  4.0 44.0 %all-to-all-start = ((bf16[128,8,128]{2,1,0:T(8,128)(2,1)}), bf16[128,8,128]{2,1,0:T(8,128)(2,1)S(1)}, u32[]{:S(2)}, u32[]{:S(2)}) async-start(bf16[128,8,128]{2,1,0:T(8,128)(2,1)} %bitcast.20), calls=%async_computation | async-start | bytes 524288 | tf_op jit(solution)/shard_map/all_to_all | solution.py:349
  30.0 23.5 %copy-start.1 = (bf16[128,2048]{1,0:T(8,128)(2,1)S(1)}, bf16[128,2048]{1,0:T(8,128)(2,1)}, u32[]{:S(2)}) copy-start(bf16[128,2048]{1,0:T(8,128)(2,1)} %get-tuple-element.18.refs_0_) | copy-start | bytes 1572868
  30.1 34.6 %copy-start = (s32[2048,64]{0,1:T(8,128)S(1)}, s32[2048,64]{0,1:T(8,128)}, u32[]{:S(2)}) copy-start(s32[2048,64]{0,1:T(8,128)} %param.9) | copy-start | bytes 1572868
  30.1 34.6 %copy-start.3 = (s32[5]{0:T(128)S(1)}, s32[5]{0:T(128)}, u32[]{:S(2)}) copy-start(s32[5]{0:T(128)} %stack.23.at_ref.refs_12_.refs_8_) | copy-start | bytes 64
  30.1 25.4 %collective-permute-start = (bf16[128,2048]{1,0:T(8,128)(2,1)}, bf16[128,2048]{1,0:T(8,128)(2,1)S(1)}, u32[]{:S(2)}, u32[]{:S(2)}) collective-permute-start(bf16[128,2048]{1,0:T(8,128)(2,1)} %get-tuple-element.19), channel_id=1, source_target_pairs={{0,2},{1,3},{2,0},{3,1},{4,6},{5,7},{6,4},{7,5},{8,10},{9,11},{10,... | collective-permute-start | bytes 1572872 | tf_op jit(solution)/shard_map/ppermute | solution.py:367
  35.0 25.3 %collective-permute-start.1 = (bf16[128,2048]{1,0:T(8,128)(2,1)}, bf16[128,2048]{1,0:T(8,128)(2,1)S(1)}, u32[]{:S(2)}, u32[]{:S(2)}) collective-permute-start(bf16[128,2048]{1,0:T(8,128)(2,1)} %get-tuple-element.20), channel_id=1, source_target_pairs={{0,1},{1,2},{2,3},{3,0},{4,5},{5,6},{6,7},{7,4},{8,9},{9,10},{10,1... | collective-permute-start | bytes 1572872 | tf_op jit(solution)/shard_map/ppermute | solution.py:367
  37.2 25.5 %collective-permute-start.2 = (bf16[128,2048]{1,0:T(8,128)(2,1)}, bf16[128,2048]{1,0:T(8,128)(2,1)}, u32[]{:S(2)}, u32[]{:S(2)}) collective-permute-start(bf16[128,2048]{1,0:T(8,128)(2,1)} %get-tuple-element.21), channel_id=1, source_target_pairs={{0,3},{1,0},{2,1},{3,2},{4,7},{5,4},{6,5},{7,6},{8,11},{9,8},{10,9... | collective-permute-start | bytes 1572872 | tf_op jit(solution)/shard_map/ppermute | solution.py:367
  49.3 21.0 %all-to-all-start.1 = ((bf16[4,1024,128]{2,1,0:T(8,128)(2,1)}), bf16[4,1024,128]{2,1,0:T(8,128)(2,1)S(1)}, u32[]{:S(2)}, u32[]{:S(2)}) async-start(bf16[4,1024,128]{2,1,0:T(8,128)(2,1)} %spread.1), calls=%async_computation.1 | async-start | bytes 2097152 | tf_op jit(solution)/shard_map/all_to_all | solution.py:377
  53.5 18.5 %collective-permute-start.3 = (bf16[128,2048]{1,0:T(8,128)(2,1)S(1)}, bf16[128,2048]{1,0:T(8,128)(2,1)}, u32[]{:S(2)}, u32[]{:S(2)}) collective-permute-start(bf16[128,2048]{1,0:T(8,128)(2,1)S(1)} %copy-done.1), channel_id=1, source_target_pairs={{0,8},{8,0},{1,9},{9,1},{2,10},{10,2},{3,11},{11,3},{4,12},{12,4},... | collective-permute-start | bytes 1572872 | tf_op jit(solution)/shard_map/ppermute | solution.py:368
  55.5 16.6 %collective-permute-start.4 = (bf16[128,2048]{1,0:T(8,128)(2,1)S(1)}, bf16[128,2048]{1,0:T(8,128)(2,1)}, u32[]{:S(2)}, u32[]{:S(2)}) collective-permute-start(bf16[128,2048]{1,0:T(8,128)(2,1)S(1)} %collective-permute-done.refs_1_), channel_id=1, source_target_pairs={{0,8},{8,0},{1,9},{9,1},{2,10},{10,2},{3,11},{11,3},{4,12},{12,4},... | collective-permute-start | bytes 1572872 | tf_op jit(solution)/shard_map/ppermute | solution.py:368
  60.3 11.8 %collective-permute-start.5 = (bf16[128,2048]{1,0:T(8,128)(2,1)S(1)}, bf16[128,2048]{1,0:T(8,128)(2,1)}, u32[]{:S(2)}, u32[]{:S(2)}) collective-permute-start(bf16[128,2048]{1,0:T(8,128)(2,1)S(1)} %collective-permute-done.1.refs_2_), channel_id=1, source_target_pairs={{0,8},{8,0},{1,9},{9,1},{2,10},{10,2},{3,11},{11,3},{4,12},{12,4},... | collective-permute-start | bytes 1572872 | tf_op jit(solution)/shard_map/ppermute | solution.py:368
  62.7 9.4 %collective-permute-start.6 = (bf16[128,2048]{1,0:T(8,128)(2,1)}, bf16[128,2048]{1,0:T(8,128)(2,1)}, u32[]{:S(2)}, u32[]{:S(2)}) collective-permute-start(bf16[128,2048]{1,0:T(8,128)(2,1)} %collective-permute-done.2.refs_3_), channel_id=1, source_target_pairs={{0,8},{8,0},{1,9},{9,1},{2,10},{10,2},{3,11},{11,3},{4,12},{12,4},... | collective-permute-start | bytes 1572872 | tf_op jit(solution)/shard_map/ppermute | solution.py:368
  65.5 8.0 %collective-permute-start.7 = (bf16[4,64,256]{2,1,0:T(8,128)(2,1)S(1)}, bf16[4,64,256]{2,1,0:T(8,128)(2,1)S(1)}, u32[]{:S(2)}, u32[]{:S(2)}) collective-permute-start(bf16[4,64,256]{2,1,0:T(8,128)(2,1)S(1)} %choose.1.refs_10_), channel_id=1, source_target_pairs={{0,4},{4,0},{1,5},{5,1},{2,6},{6,2},{3,7},{7,3},{8,12},{12,8},{9,1... | collective-permute-start | bytes 393224 | tf_op jit(solution)/shard_map/ppermute | solution.py:389
  105.6 52.7 %copy-start.2 = (f32[64,128]{1,0:T(8,128)S(1)}, f32[64,128]{1,0:T(8,128)}, u32[]{:S(2)}) copy-start(f32[64,128]{1,0:T(8,128)} %get-tuple-element.31.pat_ref) | copy-start | bytes 98308

commit v7 on v6

--- a/solution.py
+++ b/solution.py
@@ -9,8 +9,7 @@
 BF16 = jnp.bfloat16
 NZ, NYL, NC, NYH, NX = 16, 2, 2, 2, 4
 AXES = ("z", "yl", "core", "yh", "x")
-Y = ("yl", "yh")
-ZCX = ("z", "core", "x")
+PLANE = ("yl", "core", "yh", "x")
 D, KVW, TOKENS = 8192, 512, 65536
 SHIFT = 34
 VMEM = pl.BlockSpec(memory_space=pltpu.VMEM)
@@ -44,6 +43,10 @@
 
 def lane_group(dims):
     return lax.broadcasted_iota(jnp.int32, dims, len(dims) - 1) // 32
+
+
+def place_in_plane(yl, c, yh, x):
+    return ((yl * NC + c) * NYH + yh) * NX + x
 
 
 def swap_groups(parts, place):
@@ -111,25 +114,20 @@
 
 
 def choose_kernel(pat_ref, at_ref, out_ref, pick_ref):
+    pats = pat_ref[...].astype(F32).astype(BF16)
     col = lax.broadcasted_iota(jnp.int32, (64, 128), 0)
     lane = lax.broadcasted_iota(jnp.int32, (64, 128), 1)
-    pick = jnp.where(col - at_ref[1] * 32 == lane % 32, 1.0, 0.0).astype(BF16)
-    chosen = lax.dot_general(
-        pat_ref[...].astype(F32).astype(BF16),
-        pick,
-        (((0,), (0,)), ((), ())),
-        preferred_element_type=F32,
-    )
-    pick_ref[...] = chosen.reshape(NZ, NYL, NC, NX, 8, 128)
     group = lane_group((32, 128))
-    for x in range(NX):
-        for yl in range(NYL):
-            rows = pick_ref[:, yl, :, x].reshape(8, 32, 128)
-            for tile in range(2):
-                total = jnp.zeros((32, 128), F32)
-                for b in range(4):
-                    total = jnp.where(group == b, rows[tile * 4 + b], total)
-                out_ref[x, yl * 32 : (yl + 1) * 32, tile * 128 : (tile + 1) * 128] = total.astype(BF16)
+    for c in range(NC):
+        pick = jnp.where(col - c * 32 == lane % 32, 1.0, 0.0).astype(BF16)
+        chosen = lax.dot_general(pats, pick, (((0,), (0,)), ((), ())), preferred_element_type=F32)
+        pick_ref[...] = chosen.reshape(NZ, NYL, NC, NX, 8, 128)
+        for x in range(NX):
+            rows = pick_ref[:, at_ref[2], at_ref[1], x].reshape(4, 32, 128)
+            total = rows[0]
+            for b in range(1, 4):
+                total = jnp.where(group == b, rows[b], total)
+            out_ref[c * NX + x] = total.astype(BF16)
 
 
 def pack_kernel(teacher_hbm, student_hbm, pat_hbm, at_ref, out_ref, rows_ref, *scratch):
@@ -172,45 +170,60 @@
             out_ref[z, c * 32 : (c + 1) * 32, :] = piece
 
 
-def spread_kernel(got_ref, out_ref, mid_ref):
-    got = got_ref[...].astype(F32).reshape(32, 4, 8, 128)
-    for q in range(4):
-        mid_ref[:, q] = swap_groups([got[:, x] for x in range(NX)], q)
-    rows = mid_ref[...].reshape(1024, 128).astype(BF16)
-    for y in range(4):
-        out_ref[y] = rows
-
-
-def decode_kernel(w_ref, high_ref, low_ref):
-    for y in range(4):
+def spread_kernel(got_ref, pat_ref, out_ref):
+    got = got_ref[...].astype(F32).reshape(NZ, 8, 8, 128)
+    for c in range(NC):
+        for x in range(NX):
+            rows = got[:, c * NX + x].reshape(128, 128).astype(BF16)
+            for y in range(4):
+                at = place_in_plane(y // 2, c, y % 2, x)
+                out_ref[at, :128, :] = rows
+                out_ref[at, 128:, :] = pat_ref[c * NX + x]
+
+
+def decode_kernel(got_ref, high_ref, low_ref, pat_ref, w_ref):
+    for yl in range(NYL):
+        for c in range(NC):
+            for yh in range(NYH):
+                at = [place_in_plane(yl, c, yh, x) for x in range(NX)]
+                parts = [got_ref[i, :128, :].astype(F32).reshape(NZ, 8, 128) for i in at]
+                for q in range(4):
+                    sent = swap_groups(parts, q)
+                    size = jnp.sqrt(jnp.sqrt(jnp.abs(sent))) * 2.0**-SHIFT
+                    delta = jnp.where(sent < 0, -size, size)
+                    w_ref[yl, :, c, q, :, yh * 128 : (yh + 1) * 128] = delta
+                parts = [got_ref[i, 128:, :].astype(F32) for i in at]
+                for b in range(4):
+                    rows = swap_groups(parts, b).reshape(4, 8, 128)
+                    pat_ref[yl * NYH + yh, b * 4 : (b + 1) * 4, c] = rows
+    for yl in range(NYL):
         for k in range(4):
-            sent = w_ref[y, k * 256 : (k + 1) * 256, :].astype(F32)
-            size = jnp.sqrt(jnp.sqrt(jnp.abs(sent))) * 2.0**-SHIFT
-            delta = jnp.where(sent < 0, -size, size)
+            delta = w_ref[yl, k * 4 : (k + 1) * 4].reshape(256, 256)
             high = delta.astype(BF16)
-            at = (y // 2) * 1024 + k * 256
-            lane = (y % 2) * 128
-            high_ref[at : at + 256, lane : lane + 128] = high
-            low_ref[at : at + 256, lane : lane + 128] = (delta - high.astype(F32)).astype(BF16)
+            at = yl * 1024 + k * 256
+            high_ref[at : at + 256, :] = high
+            low_ref[at : at + 256, :] = (delta - high.astype(F32)).astype(BF16)
 
 
 def forward_kernel(*refs):
     own, pair, rest = refs[:NX], refs[NX : 2 * NX], refs[2 * NX :]
-    high_ref, low_ref, own_pat, other_pat, at_ref, out_ref, held_ref, sems = rest
+    high_ref, low_ref, at_ref, out_ref, held_ref, sems = rest
     loads = [pltpu.make_async_copy(pair[i], held_ref.at[i], sems.at[i]) for i in range(NX)]
     for load in loads:
         load.start()
-    for x in range(NX):
-        out_ref[x, 256:320] = own_pat[x]
-        out_ref[x, 320:] = other_pat[x]
     for row in (0, 128):
+        if row:
+            for load in loads:
+                load.wait()
+            rows = held_ref[...].reshape(512, 2048)
+        else:
+            rows = jnp.concatenate([ref[...] for ref in own], axis=0)
+        part = jnp.dot(rows, high_ref[...], preferred_element_type=F32)
+        part += jnp.dot(rows, low_ref[...], preferred_element_type=F32)
+        part = part.astype(BF16)
         for i in range(NX):
-            if row:
-                loads[i].wait()
-            rows = held_ref[i] if row else own[i][...]
-            part = jnp.dot(rows, high_ref[...], preferred_element_type=F32)
-            part += jnp.dot(rows, low_ref[...], preferred_element_type=F32)
-            out_ref[(at_ref[0] + BACK[i]) % NX, row : row + 128] = part.astype(BF16)
+            x = (at_ref[0] + BACK[i]) % NX
+            out_ref[x, row : row + 128] = part[i * 128 : (i + 1) * 128]
 
 
 def thirds(value, rows):
@@ -221,26 +234,15 @@
     return jnp.where(row == 0, high, jnp.where(row == 1, mid, jnp.where(row == 2, low, 0.0)))
 
 
-def slope_kernel(part_ref, out_ref, loss_ref, pat_ref):
-    diff = part_ref[0, :256].astype(F32)
+def slope_kernel(part_ref, out_ref, loss_ref):
+    diff = part_ref[0].astype(F32)
     for x in range(1, NX):
-        diff = diff + part_ref[x, :256].astype(F32)
+        diff = diff + part_ref[x].astype(F32)
     slope = diff.astype(BF16)
     for x in range(NX):
         out_ref[x] = slope
     square = diff * diff
     loss_ref[...] = jnp.sum(square[:, :128] + square[:, 128:], axis=0, keepdims=True)
-    group = lane_group((32, 128))
-    for part in range(4):
-        for b in range(8):
-            total = jnp.zeros((32, 128), F32)
-            for x in range(NX):
-                sent = part_ref[x, 256 + part * 32 : 288 + part * 32, b // 4 * 128 : b // 4 * 128 + 128]
-                shift = (x - b) % 4 * 32
-                sent = sent.astype(F32)
-                sent = pltpu.roll(sent, shift, 1) if shift else sent
-                total = jnp.where(group == x, sent, total)
-            pat_ref[part, b * 32 : (b + 1) * 32, :] = total.astype(BF16)
 
 
 def grad_kernel(*refs):
@@ -262,47 +264,56 @@
                 :, yh * 128 : (yh + 1) * 128
             ].reshape(8, 4, 8, 128)
     loss = thirds(loss_ref[...], 16).astype(BF16)
-    for i in range(4):
-        y = i % 2 * 2 + jnp.where(i < 2, at_ref[4], 1 - at_ref[4])
-        first, second = kept_rows(pat_ref[i].astype(F32).reshape(32, 8, 128))
-        for row, which in ((0, first), (256, second)):
-            kept = jnp.zeros_like(which)
-            for k in range(4):
-                kept += jnp.where(which == k, term_ref[y, :, k], 0.0)
-            out_ref[y, row : row + 256] = kept.reshape(256, 128).astype(BF16)
-        out_ref[y, 512:] = loss
+    for y in range(4):
+        which = kept_rows(pat_ref[y].reshape(32, 8, 128))
+        kept = [jnp.zeros((32, 8, 128), F32) for _ in which]
+        for k in range(4):
+            for i in range(2):
+                kept[i] += jnp.where(which[i] == k, term_ref[y, :, k], 0.0)
+        kept = [part.reshape(2, 8, NC, 8, 128) for part in kept]
+        for c in range(NC):
+            parts = [kept[i][half, :, c] for half in range(2) for i in range(2)]
+            for x in range(NX):
+                at = place_in_plane(y // 2, c, y % 2, x)
+                out_ref[at, :64, :] = swap_groups(parts, x).reshape(64, 128).astype(BF16)
+                out_ref[at, 64:, :] = loss
 
 
 def gather_kernel(got_ref, out_ref, mid_ref):
-    total = got_ref[0].astype(F32)
-    for y in range(1, 4):
-        total = total + got_ref[y].astype(F32)
-    loss = jnp.sum(total[512:], axis=0, keepdims=True)
-    loss = thirds(jnp.broadcast_to(jnp.sum(loss, axis=1, keepdims=True), (1, 128)), 8)
-    row = lax.broadcasted_iota(jnp.int32, (8, 128), 0)
-    lane = lax.broadcasted_iota(jnp.int32, (8, 128), 1)
-    loss = jnp.where(lane == 64 + row, loss, 0.0)
-    kept = [total[:256].reshape(32, 8, 128), total[256:512].reshape(32, 8, 128)]
-    group = lane_group((32, 8, 128))
+    loss = got_ref[0, 64:, :].astype(F32)
+    for i in range(1, 32):
+        loss = loss + got_ref[i, 64:, :].astype(F32)
+    loss = jnp.sum(jnp.sum(loss, axis=0, keepdims=True), axis=1, keepdims=True)
+    loss = thirds(jnp.broadcast_to(loss, (1, 128)), 16)
+    lane = lax.broadcasted_iota(jnp.int32, (16, 128), 1)
+    mid_ref[:, 32:, :] = jnp.broadcast_to(jnp.where(lane == 0, loss, 0.0), (NZ, 16, 128))
+    group = lane_group((8, 8, 128))
     for x in range(NX):
-        one = pltpu.roll(kept[0], (4 - x) % 4 * 32, 2)
-        two = pltpu.roll(kept[1], (5 - x) % 4 * 32, 2)
-        mid_ref[:, x] = jnp.where(group == 0, one, jnp.where(group == 1, two, loss[None]))
-    out_ref[...] = mid_ref[...].reshape(1024, 128).astype(BF16)
+        sums = []
+        for c in range(NC):
+            total = jnp.zeros((64, 128), F32)
+            for y in range(4):
+                total += got_ref[place_in_plane(y // 2, c, y % 2, x), :64, :].astype(F32)
+            sums.append(total.reshape(8, 8, 128))
+        for half in range(2):
+            rows = jnp.zeros((8, 8, 128), F32)
+            for kept in range(2):
+                for c in range(NC):
+                    goal = kept * 2 + c
+                    shift = (goal - half * 2 - kept) % 4 * 32
+                    moved = pltpu.roll(sums[c], shift, 2) if shift else sums[c]
+                    rows = jnp.where(group == goal, moved, rows)
+            mid_ref[half * 8 : (half + 1) * 8, x * 8 : (x + 1) * 8, :] = rows
+    out_ref[...] = mid_ref[...].astype(BF16)
 
 
 def final_kernel(got_ref, pat_ref, out_ref, loss_ref):
     total = got_ref[0].astype(F32)
     for z in range(1, NZ):
         total = total + got_ref[z].astype(F32)
-    loss = jnp.where(lane_group(total.shape) == 2, total, 0.0)
-    loss = jnp.sum(jnp.sum(loss, axis=0, keepdims=True), axis=1, keepdims=True)
+    loss = jnp.sum(jnp.sum(total[32:], axis=0, keepdims=True), axis=1, keepdims=True)
     loss_ref[...] = loss / (TOKENS * KVW)
-    one, two = total[:32], total[32:]
-    group = lane_group((32, 128))
-    near = jnp.where(group == 0, one, pltpu.roll(two, 32, 1))
-    far = jnp.where(group == 2, pltpu.roll(one, 32, 1), pltpu.roll(two, 64, 1))
-    kept = jnp.where(group < 2, near, far)
+    kept = total[:32]
     row = lax.broadcasted_iota(jnp.int32, (32, 128), 0)
     col = lax.broadcasted_iota(jnp.int32, (32, 128), 1)
     spread = jnp.where(col // 4 == row, 1.0, 0.0).astype(BF16)
@@ -346,7 +357,7 @@
         grant=60,
         name="pack",
     )
-    got_w = lax.all_to_all(packed.reshape(128, 8, 128), ZCX, 0, 0, tiled=True)
+    got_w = lax.all_to_all(packed, "z", 0, 0, tiled=True)
 
     split = call(
         norm_kernel,
@@ -367,37 +378,32 @@
     own = [split[0]] + [lax.ppermute(split[i], "x", ring(STEP[i])) for i in range(1, NX)]
     pair = [lax.ppermute(piece, "core", [(0, 1), (1, 0)]) for piece in own]
 
-    rows_w = call(
-        spread_kernel,
-        shape((4, 1024, 128), BF16),
-        got_w.reshape(1024, 128),
-        scratch=[pltpu.VMEM((32, 4, 8, 128), F32)],
-        name="spread",
-    )
-    all_w = lax.all_to_all(rows_w, Y, 0, 0, tiled=True)
-    high, low = call(decode_kernel, (shape((2048, 256), BF16),) * 2, all_w, name="decode")
-
-    late, _ = lax.optimization_barrier((patterns, rows_w))
     own_pat = call(
         choose_kernel,
-        shape((NX, 64, 256), BF16),
-        late,
+        shape((8, 32, 128), BF16),
+        patterns,
         at,
         scratch=[pltpu.VMEM((NZ, NYL, NC, NX, 8, 128), F32)],
         name="choose",
     )
-    other_pat = lax.ppermute(own_pat, "yh", [(0, 1), (1, 0)])
+    rows_w = call(spread_kernel, shape((32, 160, 128), BF16), got_w, own_pat, name="spread")
+    all_w = lax.all_to_all(rows_w, PLANE, 0, 0, tiled=True)
+    high, low, pats = call(
+        decode_kernel,
+        (shape((2048, 256), BF16),) * 2 + (shape((4, NZ, NC, 8, 128), F32),),
+        all_w,
+        scratch=[pltpu.VMEM((NYL, NZ, NC, 4, 8, 256), F32)],
+        name="decode",
+    )
 
     flops = 2 * 1024 * 2048 * 256
     part, held = call(
         forward_kernel,
-        (shape((NX, 384, 256), BF16), shape((NX, 128, 2048), BF16)),
+        (shape((NX, 256, 256), BF16), shape((NX, 128, 2048), BF16)),
         *own,
         *pair,
         high,
         low,
-        own_pat,
-        other_pat,
         at,
         scratch=[pltpu.SemaphoreType.DMA((NX,))],
         flops=2 * flops,
@@ -405,17 +411,14 @@
         name="forward",
     )
     got_part = lax.all_to_all(part, "x", 0, 0, tiled=True)
-    slope, loss_part, pats = call(
-        slope_kernel,
-        (shape((NX, 256, 256), BF16), shape((1, 128), F32), shape((4, 256, 128), BF16)),
-        got_part,
-        name="slope",
+    slope, loss_part = call(
+        slope_kernel, (shape((NX, 256, 256), BF16), shape((1, 128), F32)), got_part, name="slope"
     )
     slopes = lax.all_to_all(slope, "x", 0, 0, tiled=True)
 
     term = call(
         grad_kernel,
-        shape((4, 528, 128), BF16),
+        shape((32, 80, 128), BF16),
         *own,
         held,
         pats,
@@ -426,19 +429,19 @@
         flops=flops,
         name="grad",
     )
-    got_term = lax.all_to_all(term, Y, 0, 0, tiled=True)
+    got_term = lax.all_to_all(term, PLANE, 0, 0, tiled=True)
     packed_term = call(
         gather_kernel,
-        shape((1024, 128), BF16),
+        shape((NZ, 48, 128), BF16),
         got_term,
-        scratch=[pltpu.VMEM((32, 4, 8, 128), F32)],
+        scratch=[pltpu.VMEM((NZ, 48, 128), F32)],
         name="gather",
     )
-    got_sum = lax.all_to_all(packed_term.reshape(128, 8, 128), ZCX, 0, 0, tiled=True)
+    got_sum = lax.all_to_all(packed_term, "z", 0, 0, tiled=True)
     grad, loss = call(
         final_kernel,
         (shape((64, 128), F32), shape((1, 1), F32)),
-        got_sum.reshape(NZ, 64, 128),
+        got_sum,
         pat,
         name="final",
     )

time: 160 us -> 169 us (1.056)
  the two profiles are of different devices: /device:TPU:1 before, /device:TPU:32 now
where the time goes in v7:
time: 169 us; the launch traced here: 168 us
  blocking collectives  64.7 us (38%)
  starting transfers between devices  42.9 us (25%)
  waiting for transfers between devices  34 us (20%)
  Pallas kernels  22.6 us (13%)
  local copies, waits for them, and re-layouts  3.3 us (2%)
    pallas_call x10, Pallas kernels, call(): pl.pallas_call(kernel, out_shape=out_shape, in_specs=specs, out_specs=jax...  22.6 us
    all_to_all x1, blocking collectives, shards(): got_sum = lax.all_to_all(packed_term, 'z', 0, 0, tiled=True)  22.1 us
    ppermute x3, waiting for transfers between devices, shards(): lax.ppermute(split[i], 'x', ring(STEP[i]))  18.9 us
    all_to_all x1, blocking collectives, shards(): got_term = lax.all_to_all(term, PLANE, 0, 0, tiled=True)  18.6 us
    all_to_all x1, starting transfers between devices, shards(): got_w = lax.all_to_all(packed, 'z', 0, 0, tiled=True)  15.2 us
    all_to_all x1, waiting for transfers between devices, shards(): got_w = lax.all_to_all(packed, 'z', 0, 0, tiled=True)  15.1 us
    all_to_all x1, blocking collectives, shards(): got_part = lax.all_to_all(part, 'x', 0, 0, tiled=True)  12.5 us
    ppermute x3, starting transfers between devices, shards(): lax.ppermute(split[i], 'x', ring(STEP[i]))  12.3 us
  transfers between devices with their start and end apart: 9, of which 3 were waited for; matrix products, arithmetic and copies ran while one was open for 0% of the time, Pallas kernels for 6%

profile of v7, /device:TPU:32, one launch (start us, length us, event | category | flops | bytes accessed | tf_op | source)
XLA Modules:
  0.0 168.4 jit_solution(1478852640649787744)
XLA Ops:
  0.6 0.6 stack.23.at_ref.refs_10_.refs_8_
  1.2 2.7 %pack.1 = (bf16[16,64,128]{2,1,0:T(8,128)(2,1)}, f32[64,128]{1,0:T(8,128)}) custom-call(bf16[64,128]{1,0:T(8,128)(2,1)} %bitcast.13, bf16[64,128]{1,0:T(8,128)(2,1)} %bitcast.14, s32[64,2048]{1,0:T(8,128)} %bitcast.11, s32[5]{0:T(128)} %stack.23.at_ref.refs_10_.refs_8_), custom_call_target="tpu_custom_call" | custom-call | bytes 851988 | tf_op jit(solution)/shard_map/pack/pallas_call | solution.py:28
  4.0 15.2 %all-to-all-start = ((bf16[16,64,128]{2,1,0:T(8,128)(2,1)}), bf16[16,64,128]{2,1,0:T(8,128)(2,1)S(1)}, u32[]{:S(2)}, u32[]{:S(2)}) async-start(bf16[16,64,128]{2,1,0:T(8,128)(2,1)} %get-tuple-element.21), calls=%async_computation | async-start | bytes 524288 | tf_op jit(solution)/shard_map/all_to_all | solution.py:360
  19.2 0.0 copy-start
  19.2 1.0 copy-done
  20.3 0.0 copy-start.4
  20.3 0.6 copy-done.4
  20.9 1.1 choose.1.pat_ref
  22.0 15.1 %all-to-all-done.got_ref = bf16[16,64,128]{2,1,0:T(8,128)(2,1)S(1)} async-done(((bf16[16,64,128]{2,1,0:T(8,128)(2,1)}), bf16[16,64,128]{2,1,0:T(8,128)(2,1)S(1)}, u32[]{:S(2)}, u32[]{:S(2)}) %all-to-all-start) | async-done | bytes 262176 | tf_op jit(solution)/shard_map/all_to_all | solution.py:360
  37.1 1.2 spread.1
  38.4 7.3 %all-to-all-start.1 = ((bf16[32,160,128]{2,1,0:T(8,128)(2,1)}), bf16[32,160,128]{2,1,0:T(8,128)(2,1)S(1)}, u32[]{:S(2)}, u32[]{:S(2)}) async-start(bf16[32,160,128]{2,1,0:T(8,128)(2,1)} %spread.1), calls=%async_computation.1 | async-start | bytes 2621440 | tf_op jit(solution)/shard_map/all_to_all | solution.py:390
  45.7 0.0 copy-start.5
  45.7 5.6 %norm.1 = (bf16[128,2048]{1,0:T(8,128)(2,1)}, bf16[128,2048]{1,0:T(8,128)(2,1)}, bf16[128,2048]{1,0:T(8,128)(2,1)}, bf16[128,2048]{1,0:T(8,128)(2,1)}) custom-call(bf16[128,8192]{1,0:T(8,128)(2,1)} %x_hbm.1, bf16[64,128]{1,0:T(8,128)(2,1)} %bitcast.16, s32[5]{0:T(128)} %stack.23.at_ref.refs_10_.refs_8_), custom_call_target="tpu_custom_call" | custom-call | flops 1073741824 | bytes 4210708 | tf_op jit(solution)/shard_map/norm/pallas_call | solution.py:28
  51.3 5.2 %collective-permute-start = (bf16[128,2048]{1,0:T(8,128)(2,1)}, bf16[128,2048]{1,0:T(8,128)(2,1)S(1)}, u32[]{:S(2)}, u32[]{:S(2)}) collective-permute-start(bf16[128,2048]{1,0:T(8,128)(2,1)} %get-tuple-element.18), channel_id=1, source_target_pairs={{0,2},{1,3},{2,0},{3,1},{4,6},{5,7},{6,4},{7,5},{8,10},{9,11},{10,... | collective-permute-start | bytes 1572872 | tf_op jit(solution)/shard_map/ppermute | solution.py:378
  56.5 2.5 %collective-permute-start.1 = (bf16[128,2048]{1,0:T(8,128)(2,1)}, bf16[128,2048]{1,0:T(8,128)(2,1)S(1)}, u32[]{:S(2)}, u32[]{:S(2)}) collective-permute-start(bf16[128,2048]{1,0:T(8,128)(2,1)} %get-tuple-element.19), channel_id=1, source_target_pairs={{0,1},{1,2},{2,3},{3,0},{4,5},{5,6},{6,7},{7,4},{8,9},{9,10},{10,1... | collective-permute-start | bytes 1572872 | tf_op jit(solution)/shard_map/ppermute | solution.py:378
  59.0 4.6 %collective-permute-start.2 = (bf16[128,2048]{1,0:T(8,128)(2,1)}, bf16[128,2048]{1,0:T(8,128)(2,1)S(1)}, u32[]{:S(2)}, u32[]{:S(2)}) collective-permute-start(bf16[128,2048]{1,0:T(8,128)(2,1)} %get-tuple-element.20), channel_id=1, source_target_pairs={{0,3},{1,0},{2,1},{3,2},{4,7},{5,4},{6,5},{7,6},{8,11},{9,8},{10,9... | collective-permute-start | bytes 1572872 | tf_op jit(solution)/shard_map/ppermute | solution.py:378
  63.6 1.9 %collective-permute-start.3 = (bf16[128,2048]{1,0:T(8,128)(2,1)}, bf16[128,2048]{1,0:T(8,128)(2,1)S(1)}, u32[]{:S(2)}, u32[]{:S(2)}) collective-permute-start(bf16[128,2048]{1,0:T(8,128)(2,1)} %get-tuple-element.17.refs_0_), channel_id=1, source_target_pairs={{0,8},{8,0},{1,9},{9,1},{2,10},{10,2},{3,11},{11,3},{4,12},{12,4},... | collective-permute-start | bytes 1572872 | tf_op jit(solution)/shard_map/ppermute | solution.py:379
  65.5 10.3 %collective-permute-done.refs_1_ = bf16[128,2048]{1,0:T(8,128)(2,1)S(1)} collective-permute-done((bf16[128,2048]{1,0:T(8,128)(2,1)}, bf16[128,2048]{1,0:T(8,128)(2,1)S(1)}, u32[]{:S(2)}, u32[]{:S(2)}) %collective-permute-start) | collective-permute-done | bytes 524320 | tf_op jit(solution)/shard_map/ppermute | solution.py:378
  75.8 1.9 %collective-permute-start.4 = (bf16[128,2048]{1,0:T(8,128)(2,1)S(1)}, bf16[128,2048]{1,0:T(8,128)(2,1)}, u32[]{:S(2)}, u32[]{:S(2)}) collective-permute-start(bf16[128,2048]{1,0:T(8,128)(2,1)S(1)} %collective-permute-done.refs_1_), channel_id=1, source_target_pairs={{0,8},{8,0},{1,9},{9,1},{2,10},{10,2},{3,11},{11,3},{4,12},{12,4},... | collective-permute-start | bytes 1572872 | tf_op jit(solution)/shard_map/ppermute | solution.py:379
  77.7 8.5 %collective-permute-done.1.refs_2_ = bf16[128,2048]{1,0:T(8,128)(2,1)S(1)} collective-permute-done((bf16[128,2048]{1,0:T(8,128)(2,1)}, bf16[128,2048]{1,0:T(8,128)(2,1)S(1)}, u32[]{:S(2)}, u32[]{:S(2)}) %collective-permute-start.1) | collective-permute-done | bytes 524320 | tf_op jit(solution)/shard_map/ppermute | solution.py:378
  86.3 1.9 %collective-permute-start.5 = (bf16[128,2048]{1,0:T(8,128)(2,1)S(1)}, bf16[128,2048]{1,0:T(8,128)(2,1)}, u32[]{:S(2)}, u32[]{:S(2)}) collective-permute-start(bf16[128,2048]{1,0:T(8,128)(2,1)S(1)} %collective-permute-done.1.refs_2_), channel_id=1, source_target_pairs={{0,8},{8,0},{1,9},{9,1},{2,10},{10,2},{3,11},{11,3},{4,12},{12,4},... | collective-permute-start | bytes 1572872 | tf_op jit(solution)/shard_map/ppermute | solution.py:379
  88.2 0.0 collective-permute-done.2.refs_3_
  88.2 2.4 %collective-permute-start.6 = (bf16[128,2048]{1,0:T(8,128)(2,1)S(1)}, bf16[128,2048]{1,0:T(8,128)(2,1)}, u32[]{:S(2)}, u32[]{:S(2)}) collective-permute-start(bf16[128,2048]{1,0:T(8,128)(2,1)S(1)} %collective-permute-done.2.refs_3_), channel_id=1, source_target_pairs={{0,8},{8,0},{1,9},{9,1},{2,10},{10,2},{3,11},{11,3},{4,12},{12,4},... | collective-permute-start | bytes 1572872 | tf_op jit(solution)/shard_map/ppermute | solution.py:379
  90.6 0.0 all-to-all-done.1.got_ref
  90.6 2.8 %decode.1 = (bf16[2048,256]{1,0:T(8,128)(2,1)S(1)}, bf16[2048,256]{1,0:T(8,128)(2,1)S(1)}, f32[4,16,2,8,128]{4,3,2,1,0:T(8,128)S(1)}) custom-call(bf16[32,160,128]{2,1,0:T(8,128)(2,1)S(1)} %all-to-all-done.1.got_ref), custom_call_target="tpu_custom_call" | custom-call | bytes 3932160 | tf_op jit(solution)/shard_map/decode/pallas_call | solution.py:28
  93.4 0.0 collective-permute-done.3.refs_4_
  93.4 0.0 collective-permute-done.4.refs_5_
  93.4 0.0 collective-permute-done.5.refs_6_
  93.4 0.0 collective-permute-done.6.refs_7_
  93.4 0.0 copy-done.5
  93.5 0.0 copy-start.1
  93.5 1.0 copy-done.1
  94.5 5.3 %forward.1 = (bf16[4,256,256]{2,1,0:T(8,128)(2,1)S(1)}, bf16[4,128,2048]{2,1,0:T(8,128)(2,1)S(1)}) custom-call(bf16[128,2048]{1,0:T(8,128)(2,1)S(1)} %copy-done.1, bf16[128,2048]{1,0:T(8,128)(2,1)S(1)} %collective-permute-done.refs_1_, bf16[128,2048]{1,0:T(8,128)(2,1)S(1)} %collective-permute-done.1.refs_2_, ...), custom_call_target="tpu_custom_call" | custom-call | flops 2147483648 | bytes 8912916 | tf_op jit(solution)/shard_map/forward/pallas_call | solution.py:28
  99.8 0.0 copy-start.2
  99.9 12.5 %all_to_all.30.part_ref = bf16[4,256,256]{2,1,0:T(8,128)(2,1)S(1)} all-to-all(bf16[4,256,256]{2,1,0:T(8,128)(2,1)S(1)} %get-tuple-element.26), channel_id=1, replica_groups=mesh['z'=16,'yl'=2,'core'=2,'yh'=2,'x'=4] {'x'}, dimensions={0} | all-to-all | bytes 1048576 | tf_op jit(solution)/shard_map/all_to_all | solution.py:413
  112.3 0.1 slope.1
  112.4 11.5 %all_to_all.31.refs_6_ = bf16[4,256,256]{2,1,0:T(8,128)(2,1)S(1)} all-to-all(bf16[4,256,256]{2,1,0:T(8,128)(2,1)S(1)} %get-tuple-element.27), channel_id=1, replica_groups=mesh['z'=16,'yl'=2,'core'=2,'yh'=2,'x'=4] {'x'}, dimensions={0} | all-to-all | bytes 1048576 | tf_op jit(solution)/shard_map/all_to_all | solution.py:417
  123.9 0.0 copy-done.2
  123.9 2.6 %grad.1 = bf16[32,80,128]{2,1,0:T(8,128)(2,1)S(1)} custom-call(bf16[128,2048]{1,0:T(8,128)(2,1)S(1)} %copy-done.2, bf16[128,2048]{1,0:T(8,128)(2,1)S(1)} %collective-permute-done.refs_1_, bf16[128,2048]{1,0:T(8,128)(2,1)S(1)} %collective-permute-done.1.refs_2_, bf16[128,2048]{1,0:T(8,128)(2,1)S(1)} %collective-permute-done.2.refs_3_, ...), custom_call_target="tpu_custom_call" | custom-call | flops 1073741824 | bytes 5898772 | tf_op jit(solution)/shard_map/grad/pallas_call | solution.py:28
  126.5 0.0 copy-start.3
  126.6 18.6 %all_to_all.32.got_ref = bf16[32,80,128]{2,1,0:T(8,128)(2,1)S(1)} all-to-all(bf16[32,80,128]{2,1,0:T(8,128)(2,1)S(1)} %grad.1), channel_id=1, replica_groups=mesh['z'=16,'yl'=2,'core'=2,'yh'=2,'x'=4] {'yl','core','yh','x'}, dimensions={0} | all-to-all | bytes 1310720 | tf_op jit(solution)/shard_map/all_to_all | solution.py:432
  145.2 0.2 gather.1
  145.4 22.1 %all_to_all.33.got_ref = bf16[16,48,128]{2,1,0:T(8,128)(2,1)S(1)} all-to-all(bf16[16,48,128]{2,1,0:T(8,128)(2,1)S(1)} %gather.1), channel_id=1, replica_groups=mesh['z'=16,'yl'=2,'core'=2,'yh'=2,'x'=4] {'z'}, dimensions={0} | all-to-all | bytes 393216 | tf_op jit(solution)/shard_map/all_to_all | solution.py:440
  167.5 0.0 copy-done.3
  167.5 0.9 final.1
Async XLA Ops:
  4.0 33.1 %all-to-all-start = ((bf16[16,64,128]{2,1,0:T(8,128)(2,1)}), bf16[16,64,128]{2,1,0:T(8,128)(2,1)S(1)}, u32[]{:S(2)}, u32[]{:S(2)}) async-start(bf16[16,64,128]{2,1,0:T(8,128)(2,1)} %get-tuple-element.21), calls=%async_computation | async-start | bytes 524288 | tf_op jit(solution)/shard_map/all_to_all | solution.py:360
  19.2 1.0 copy-start
  20.3 0.6 copy-start.4
  38.4 52.3 %all-to-all-start.1 = ((bf16[32,160,128]{2,1,0:T(8,128)(2,1)}), bf16[32,160,128]{2,1,0:T(8,128)(2,1)S(1)}, u32[]{:S(2)}, u32[]{:S(2)}) async-start(bf16[32,160,128]{2,1,0:T(8,128)(2,1)} %spread.1), calls=%async_computation.1 | async-start | bytes 2621440 | tf_op jit(solution)/shard_map/all_to_all | solution.py:390
  45.7 47.8 %copy-start.5 = (s32[5]{0:T(128)S(1)}, s32[5]{0:T(128)}, u32[]{:S(2)}) copy-start(s32[5]{0:T(128)} %stack.23.at_ref.refs_10_.refs_8_) | copy-start | bytes 64
  51.3 24.5 %collective-permute-start = (bf16[128,2048]{1,0:T(8,128)(2,1)}, bf16[128,2048]{1,0:T(8,128)(2,1)S(1)}, u32[]{:S(2)}, u32[]{:S(2)}) collective-permute-start(bf16[128,2048]{1,0:T(8,128)(2,1)} %get-tuple-element.18), channel_id=1, source_target_pairs={{0,2},{1,3},{2,0},{3,1},{4,6},{5,7},{6,4},{7,5},{8,10},{9,11},{10,... | collective-permute-start | bytes 1572872 | tf_op jit(solution)/shard_map/ppermute | solution.py:378
  56.5 29.8 %collective-permute-start.1 = (bf16[128,2048]{1,0:T(8,128)(2,1)}, bf16[128,2048]{1,0:T(8,128)(2,1)S(1)}, u32[]{:S(2)}, u32[]{:S(2)}) collective-permute-start(bf16[128,2048]{1,0:T(8,128)(2,1)} %get-tuple-element.19), channel_id=1, source_target_pairs={{0,1},{1,2},{2,3},{3,0},{4,5},{5,6},{6,7},{7,4},{8,9},{9,10},{10,1... | collective-permute-start | bytes 1572872 | tf_op jit(solution)/shard_map/ppermute | solution.py:378
  59.0 29.2 %collective-permute-start.2 = (bf16[128,2048]{1,0:T(8,128)(2,1)}, bf16[128,2048]{1,0:T(8,128)(2,1)S(1)}, u32[]{:S(2)}, u32[]{:S(2)}) collective-permute-start(bf16[128,2048]{1,0:T(8,128)(2,1)} %get-tuple-element.20), channel_id=1, source_target_pairs={{0,3},{1,0},{2,1},{3,2},{4,7},{5,4},{6,5},{7,6},{8,11},{9,8},{10,9... | collective-permute-start | bytes 1572872 | tf_op jit(solution)/shard_map/ppermute | solution.py:378
  63.6 29.8 %collective-permute-start.3 = (bf16[128,2048]{1,0:T(8,128)(2,1)}, bf16[128,2048]{1,0:T(8,128)(2,1)S(1)}, u32[]{:S(2)}, u32[]{:S(2)}) collective-permute-start(bf16[128,2048]{1,0:T(8,128)(2,1)} %get-tuple-element.17.refs_0_), channel_id=1, source_target_pairs={{0,8},{8,0},{1,9},{9,1},{2,10},{10,2},{3,11},{11,3},{4,12},{12,4},... | collective-permute-start | bytes 1572872 | tf_op jit(solution)/shard_map/ppermute | solution.py:379
  75.8 17.6 %collective-permute-start.4 = (bf16[128,2048]{1,0:T(8,128)(2,1)S(1)}, bf16[128,2048]{1,0:T(8,128)(2,1)}, u32[]{:S(2)}, u32[]{:S(2)}) collective-permute-start(bf16[128,2048]{1,0:T(8,128)(2,1)S(1)} %collective-permute-done.refs_1_), channel_id=1, source_target_pairs={{0,8},{8,0},{1,9},{9,1},{2,10},{10,2},{3,11},{11,3},{4,12},{12,4},... | collective-permute-start | bytes 1572872 | tf_op jit(solution)/shard_map/ppermute | solution.py:379
  86.3 7.1 %collective-permute-start.5 = (bf16[128,2048]{1,0:T(8,128)(2,1)S(1)}, bf16[128,2048]{1,0:T(8,128)(2,1)}, u32[]{:S(2)}, u32[]{:S(2)}) collective-permute-start(bf16[128,2048]{1,0:T(8,128)(2,1)S(1)} %collective-permute-done.1.refs_2_), channel_id=1, source_target_pairs={{0,8},{8,0},{1,9},{9,1},{2,10},{10,2},{3,11},{11,3},{4,12},{12,4},... | collective-permute-start | bytes 1572872 | tf_op jit(solution)/shard_map/ppermute | solution.py:379
  88.2 5.2 %collective-permute-start.6 = (bf16[128,2048]{1,0:T(8,128)(2,1)S(1)}, bf16[128,2048]{1,0:T(8,128)(2,1)}, u32[]{:S(2)}, u32[]{:S(2)}) collective-permute-start(bf16[128,2048]{1,0:T(8,128)(2,1)S(1)} %collective-permute-done.2.refs_3_), channel_id=1, source_target_pairs={{0,8},{8,0},{1,9},{9,1},{2,10},{10,2},{3,11},{11,3},{4,12},{12,4},... | collective-permute-start | bytes 1572872 | tf_op jit(solution)/shard_map/ppermute | solution.py:379
  93.5 1.0 copy-start.1
  99.8 24.1 %copy-start.2 = (bf16[128,2048]{1,0:T(8,128)(2,1)S(1)}, bf16[128,2048]{1,0:T(8,128)(2,1)}, u32[]{:S(2)}) copy-start(bf16[128,2048]{1,0:T(8,128)(2,1)} %get-tuple-element.17.refs_0_) | copy-start | bytes 1572868
  126.5 41.0 %copy-start.3 = (f32[64,128]{1,0:T(8,128)S(1)}, f32[64,128]{1,0:T(8,128)}, u32[]{:S(2)}) copy-start(f32[64,128]{1,0:T(8,128)} %get-tuple-element.29.pat_ref) | copy-start | bytes 98308

commit v8 on v7

--- a/solution.py
+++ b/solution.py
@@ -9,6 +9,8 @@
 BF16 = jnp.bfloat16
 NZ, NYL, NC, NYH, NX = 16, 2, 2, 2, 4
 AXES = ("z", "yl", "core", "yh", "x")
+Y = ("yl", "yh")
+ZCX = ("z", "core", "x")
 PLANE = ("yl", "core", "yh", "x")
 D, KVW, TOKENS = 8192, 512, 65536
 SHIFT = 34
@@ -117,17 +119,11 @@
     pats = pat_ref[...].astype(F32).astype(BF16)
     col = lax.broadcasted_iota(jnp.int32, (64, 128), 0)
     lane = lax.broadcasted_iota(jnp.int32, (64, 128), 1)
-    group = lane_group((32, 128))
     for c in range(NC):
         pick = jnp.where(col - c * 32 == lane % 32, 1.0, 0.0).astype(BF16)
         chosen = lax.dot_general(pats, pick, (((0,), (0,)), ((), ())), preferred_element_type=F32)
         pick_ref[...] = chosen.reshape(NZ, NYL, NC, NX, 8, 128)
-        for x in range(NX):
-            rows = pick_ref[:, at_ref[2], at_ref[1], x].reshape(4, 32, 128)
-            total = rows[0]
-            for b in range(1, 4):
-                total = jnp.where(group == b, rows[b], total)
-            out_ref[c * NX + x] = total.astype(BF16)
+        out_ref[c] = pick_ref[:, at_ref[2], at_ref[1]]
 
 
 def pack_kernel(teacher_hbm, student_hbm, pat_hbm, at_ref, out_ref, rows_ref, *scratch):
@@ -170,39 +166,26 @@
             out_ref[z, c * 32 : (c + 1) * 32, :] = piece
 
 
-def spread_kernel(got_ref, pat_ref, out_ref):
-    got = got_ref[...].astype(F32).reshape(NZ, 8, 8, 128)
-    for c in range(NC):
-        for x in range(NX):
-            rows = got[:, c * NX + x].reshape(128, 128).astype(BF16)
-            for y in range(4):
-                at = place_in_plane(y // 2, c, y % 2, x)
-                out_ref[at, :128, :] = rows
-                out_ref[at, 128:, :] = pat_ref[c * NX + x]
-
-
-def decode_kernel(got_ref, high_ref, low_ref, pat_ref, w_ref):
-    for yl in range(NYL):
-        for c in range(NC):
-            for yh in range(NYH):
-                at = [place_in_plane(yl, c, yh, x) for x in range(NX)]
-                parts = [got_ref[i, :128, :].astype(F32).reshape(NZ, 8, 128) for i in at]
-                for q in range(4):
-                    sent = swap_groups(parts, q)
-                    size = jnp.sqrt(jnp.sqrt(jnp.abs(sent))) * 2.0**-SHIFT
-                    delta = jnp.where(sent < 0, -size, size)
-                    w_ref[yl, :, c, q, :, yh * 128 : (yh + 1) * 128] = delta
-                parts = [got_ref[i, 128:, :].astype(F32) for i in at]
-                for b in range(4):
-                    rows = swap_groups(parts, b).reshape(4, 8, 128)
-                    pat_ref[yl * NYH + yh, b * 4 : (b + 1) * 4, c] = rows
-    for yl in range(NYL):
+def spread_kernel(got_ref, out_ref, mid_ref):
+    got = got_ref[...].astype(F32).reshape(32, 4, 8, 128)
+    for q in range(4):
+        mid_ref[:, q] = swap_groups([got[:, x] for x in range(NX)], q)
+    rows = mid_ref[...].reshape(1024, 128).astype(BF16)
+    for y in range(4):
+        out_ref[y] = rows
+
+
+def decode_kernel(w_ref, high_ref, low_ref):
+    for y in range(4):
         for k in range(4):
-            delta = w_ref[yl, k * 4 : (k + 1) * 4].reshape(256, 256)
+            sent = w_ref[y, k * 256 : (k + 1) * 256, :].astype(F32)
+            size = jnp.sqrt(jnp.sqrt(jnp.abs(sent))) * 2.0**-SHIFT
+            delta = jnp.where(sent < 0, -size, size)
             high = delta.astype(BF16)
-            at = yl * 1024 + k * 256
-            high_ref[at : at + 256, :] = high
-            low_ref[at : at + 256, :] = (delta - high.astype(F32)).astype(BF16)
+            at = (y // 2) * 1024 + k * 256
+            lane = (y % 2) * 128
+            high_ref[at : at + 256, lane : lane + 128] = high
+            low_ref[at : at + 256, lane : lane + 128] = (delta - high.astype(F32)).astype(BF16)
 
 
 def forward_kernel(*refs):
@@ -247,7 +230,7 @@
 
 def grad_kernel(*refs):
     own, (held_ref, *rest) = refs[:NX], refs[NX:]
-    pat_ref, slope_ref, loss_ref, at_ref, out_ref, s_ref, term_ref = rest
+    slope_ref, loss_ref, at_ref, out_ref, s_ref, term_ref = rest
     contract = (((0,), (0,)), ((), ()))
     for i in range(NX):
         x = (at_ref[0] + BACK[i]) % NX
@@ -265,45 +248,37 @@
             ].reshape(8, 4, 8, 128)
     loss = thirds(loss_ref[...], 16).astype(BF16)
     for y in range(4):
-        which = kept_rows(pat_ref[y].reshape(32, 8, 128))
-        kept = [jnp.zeros((32, 8, 128), F32) for _ in which]
-        for k in range(4):
-            for i in range(2):
-                kept[i] += jnp.where(which[i] == k, term_ref[y, :, k], 0.0)
-        kept = [part.reshape(2, 8, NC, 8, 128) for part in kept]
+        term = term_ref[y].reshape(NZ, NC, 4, 8, 128)
         for c in range(NC):
-            parts = [kept[i][half, :, c] for half in range(2) for i in range(2)]
+            parts = [term[:, c, q] for q in range(4)]
             for x in range(NX):
                 at = place_in_plane(y // 2, c, y % 2, x)
-                out_ref[at, :64, :] = swap_groups(parts, x).reshape(64, 128).astype(BF16)
-                out_ref[at, 64:, :] = loss
-
-
-def gather_kernel(got_ref, out_ref, mid_ref):
-    loss = got_ref[0, 64:, :].astype(F32)
+                out_ref[at, :128, :] = swap_groups(parts, x).reshape(128, 128).astype(BF16)
+                out_ref[at, 128:, :] = loss
+
+
+def gather_kernel(got_ref, pat_ref, out_ref, mid_ref):
+    loss = got_ref[0, 128:, :].astype(F32)
     for i in range(1, 32):
-        loss = loss + got_ref[i, 64:, :].astype(F32)
+        loss = loss + got_ref[i, 128:, :].astype(F32)
     loss = jnp.sum(jnp.sum(loss, axis=0, keepdims=True), axis=1, keepdims=True)
     loss = thirds(jnp.broadcast_to(loss, (1, 128)), 16)
     lane = lax.broadcasted_iota(jnp.int32, (16, 128), 1)
     mid_ref[:, 32:, :] = jnp.broadcast_to(jnp.where(lane == 0, loss, 0.0), (NZ, 16, 128))
-    group = lane_group((8, 8, 128))
+    group = lane_group((NZ, 8, 128))
     for x in range(NX):
-        sums = []
+        rows = jnp.zeros((NZ, 8, 128), F32)
         for c in range(NC):
-            total = jnp.zeros((64, 128), F32)
+            total = jnp.zeros((128, 128), F32)
             for y in range(4):
-                total += got_ref[place_in_plane(y // 2, c, y % 2, x), :64, :].astype(F32)
-            sums.append(total.reshape(8, 8, 128))
-        for half in range(2):
-            rows = jnp.zeros((8, 8, 128), F32)
-            for kept in range(2):
-                for c in range(NC):
-                    goal = kept * 2 + c
-                    shift = (goal - half * 2 - kept) % 4 * 32
-                    moved = pltpu.roll(sums[c], shift, 2) if shift else sums[c]
-                    rows = jnp.where(group == goal, moved, rows)
-            mid_ref[half * 8 : (half + 1) * 8, x * 8 : (x + 1) * 8, :] = rows
+                total += got_ref[place_in_plane(y // 2, c, y % 2, x), :128, :].astype(F32)
+            total = total.reshape(NZ, 8, 128)
+            for i, which in enumerate(kept_rows(pat_ref[c, :, x])):
+                kept = jnp.where(which == group.astype(F32), total, 0.0)
+                kept += pltpu.roll(kept, 64, 2)
+                kept += pltpu.roll(kept, 32, 2)
+                rows = jnp.where(group == i * 2 + c, kept, rows)
+        mid_ref[:, x * 8 : (x + 1) * 8, :] = rows
     out_ref[...] = mid_ref[...].astype(BF16)
 
 
@@ -357,7 +332,7 @@
         grant=60,
         name="pack",
     )
-    got_w = lax.all_to_all(packed, "z", 0, 0, tiled=True)
+    got_w = lax.all_to_all(packed.reshape(128, 8, 128), ZCX, 0, 0, tiled=True)
 
     split = call(
         norm_kernel,
@@ -378,22 +353,24 @@
     own = [split[0]] + [lax.ppermute(split[i], "x", ring(STEP[i])) for i in range(1, NX)]
     pair = [lax.ppermute(piece, "core", [(0, 1), (1, 0)]) for piece in own]
 
+    rows_w = call(
+        spread_kernel,
+        shape((4, 1024, 128), BF16),
+        got_w.reshape(1024, 128),
+        scratch=[pltpu.VMEM((32, 4, 8, 128), F32)],
+        name="spread",
+    )
+    all_w = lax.all_to_all(rows_w, Y, 0, 0, tiled=True)
+    high, low = call(decode_kernel, (shape((2048, 256), BF16),) * 2, all_w, name="decode")
+
+    late, _ = lax.optimization_barrier((patterns, rows_w))
     own_pat = call(
         choose_kernel,
-        shape((8, 32, 128), BF16),
-        patterns,
+        shape((NC, NZ, NX, 8, 128), F32),
+        late,
         at,
         scratch=[pltpu.VMEM((NZ, NYL, NC, NX, 8, 128), F32)],
         name="choose",
-    )
-    rows_w = call(spread_kernel, shape((32, 160, 128), BF16), got_w, own_pat, name="spread")
-    all_w = lax.all_to_all(rows_w, PLANE, 0, 0, tiled=True)
-    high, low, pats = call(
-        decode_kernel,
-        (shape((2048, 256), BF16),) * 2 + (shape((4, NZ, NC, 8, 128), F32),),
-        all_w,
-        scratch=[pltpu.VMEM((NYL, NZ, NC, 4, 8, 256), F32)],
-        name="decode",
     )
 
     flops = 2 * 1024 * 2048 * 256
@@ -418,10 +395,9 @@
 
     term = call(
         grad_kernel,
-        shape((32, 80, 128), BF16),
+        shape((32, 144, 128), BF16),
         *own,
         held,
-        pats,
         slopes,
         loss_part,
         at,
@@ -434,6 +410,7 @@
         gather_kernel,
         shape((NZ, 48, 128), BF16),
         got_term,
+        own_pat,
         scratch=[pltpu.VMEM((NZ, 48, 128), F32)],
         name="gather",
     )

time: 169 us -> 155 us (0.917)
  the two profiles are of different devices: /device:TPU:32 before, /device:TPU:6 now
where the time goes in v8:
time: 155 us; the launch traced here: 152 us
  blocking collectives  51.2 us (33%)
  starting transfers between devices  47.7 us (31%)
  waiting for transfers between devices  27.1 us (17%)
  Pallas kernels  24.3 us (16%)
    all_to_all x1, blocking collectives, shards(): got_sum = lax.all_to_all(packed_term, 'z', 0, 0, tiled=True)  26.1 us
    pallas_call x10, Pallas kernels, call(): pl.pallas_call(kernel, out_shape=out_shape, in_specs=specs, out_specs=jax...  24.3 us
    all_to_all x1, starting transfers between devices, shards(): got_w = lax.all_to_all(packed.reshape(128, 8, 128), ZCX, 0, 0, tiled=True)  19.4 us
    all_to_all x1, waiting for transfers between devices, shards(): got_term = lax.all_to_all(term, PLANE, 0, 0, tiled=True)  15.5 us
    all_to_all x1, blocking collectives, shards(): got_part = lax.all_to_all(part, 'x', 0, 0, tiled=True)  14.2 us
    all_to_all x1, blocking collectives, shards(): slopes = lax.all_to_all(slope, 'x', 0, 0, tiled=True)  11 us
    ppermute x3, starting transfers between devices, shards(): lax.ppermute(split[i], 'x', ring(STEP[i]))  9.4 us
    ppermute x4, starting transfers between devices, shards(): pair = [lax.ppermute(piece, 'core', [(0, 1), (1, 0)]) for piece in own]  8.63 us
  transfers between devices with their start and end apart: 10, of which 4 were waited for; matrix products, arithmetic and copies ran while one was open for 0% of the time, Pallas kernels for 6%

profile of v8, /device:TPU:6, one launch (start us, length us, event | category | flops | bytes accessed | tf_op | source)
XLA Modules:
  0.0 151.9 jit_solution(17257084374560501646)
XLA Ops:
  0.6 0.6 stack.23.at_ref.refs_10_.refs_7_
  1.3 2.7 %pack.1 = (bf16[16,64,128]{2,1,0:T(8,128)(2,1)}, f32[64,128]{1,0:T(8,128)}) custom-call(bf16[64,128]{1,0:T(8,128)(2,1)} %bitcast.17, bf16[64,128]{1,0:T(8,128)(2,1)} %bitcast.18, s32[64,2048]{1,0:T(8,128)} %bitcast.13, s32[5]{0:T(128)} %stack.23.at_ref.refs_10_.refs_7_), custom_call_target="tpu_custom_call" | custom-call | bytes 851988 | tf_op jit(solution)/shard_map/pack/pallas_call | solution.py:30
  4.0 19.4 %all-to-all-start = ((bf16[128,8,128]{2,1,0:T(8,128)(2,1)}), bf16[128,8,128]{2,1,0:T(8,128)(2,1)S(1)}, u32[]{:S(2)}, u32[]{:S(2)}) async-start(bf16[128,8,128]{2,1,0:T(8,128)(2,1)} %bitcast.16), calls=%async_computation | async-start | bytes 524288 | tf_op jit(solution)/shard_map/all_to_all | solution.py:335
  23.4 5.6 %norm.1 = (bf16[128,2048]{1,0:T(8,128)(2,1)}, bf16[128,2048]{1,0:T(8,128)(2,1)}, bf16[128,2048]{1,0:T(8,128)(2,1)}, bf16[128,2048]{1,0:T(8,128)(2,1)}) custom-call(bf16[128,8192]{1,0:T(8,128)(2,1)} %x_hbm.1, bf16[64,128]{1,0:T(8,128)(2,1)} %bitcast.20, s32[5]{0:T(128)} %stack.23.at_ref.refs_10_.refs_7_), custom_call_target="tpu_custom_call" | custom-call | flops 1073741824 | bytes 4210708 | tf_op jit(solution)/shard_map/norm/pallas_call | solution.py:30
  29.0 0.0 copy-start.1
  29.0 3.5 %collective-permute-start = (bf16[128,2048]{1,0:T(8,128)(2,1)}, bf16[128,2048]{1,0:T(8,128)(2,1)S(1)}, u32[]{:S(2)}, u32[]{:S(2)}) collective-permute-start(bf16[128,2048]{1,0:T(8,128)(2,1)} %get-tuple-element.18), channel_id=1, source_target_pairs={{0,2},{1,3},{2,0},{3,1},{4,6},{5,7},{6,4},{7,5},{8,10},{9,11},{10,... | collective-permute-start | bytes 1572872 | tf_op jit(solution)/shard_map/ppermute | solution.py:353
  32.5 4.0 %collective-permute-start.1 = (bf16[128,2048]{1,0:T(8,128)(2,1)}, bf16[128,2048]{1,0:T(8,128)(2,1)S(1)}, u32[]{:S(2)}, u32[]{:S(2)}) collective-permute-start(bf16[128,2048]{1,0:T(8,128)(2,1)} %get-tuple-element.19), channel_id=1, source_target_pairs={{0,1},{1,2},{2,3},{3,0},{4,5},{5,6},{6,7},{7,4},{8,9},{9,10},{10,1... | collective-permute-start | bytes 1572872 | tf_op jit(solution)/shard_map/ppermute | solution.py:353
  36.5 1.9 %collective-permute-start.2 = (bf16[128,2048]{1,0:T(8,128)(2,1)}, bf16[128,2048]{1,0:T(8,128)(2,1)S(1)}, u32[]{:S(2)}, u32[]{:S(2)}) collective-permute-start(bf16[128,2048]{1,0:T(8,128)(2,1)} %get-tuple-element.20), channel_id=1, source_target_pairs={{0,3},{1,0},{2,1},{3,2},{4,7},{5,4},{6,5},{7,6},{8,11},{9,8},{10,9... | collective-permute-start | bytes 1572872 | tf_op jit(solution)/shard_map/ppermute | solution.py:353
  38.4 7.1 %all-to-all-done = bf16[128,8,128]{2,1,0:T(8,128)(2,1)S(1)} async-done(((bf16[128,8,128]{2,1,0:T(8,128)(2,1)}), bf16[128,8,128]{2,1,0:T(8,128)(2,1)S(1)}, u32[]{:S(2)}, u32[]{:S(2)}) %all-to-all-start) | async-done | bytes 262176 | tf_op jit(solution)/shard_map/all_to_all | solution.py:335
  45.5 0.0 copy-start.3
  45.5 1.3 spread.1
  46.9 4.5 %all-to-all-start.1 = ((bf16[4,1024,128]{2,1,0:T(8,128)(2,1)}), bf16[4,1024,128]{2,1,0:T(8,128)(2,1)S(1)}, u32[]{:S(2)}, u32[]{:S(2)}) async-start(bf16[4,1024,128]{2,1,0:T(8,128)(2,1)} %spread.1), calls=%async_computation.1 | async-start | bytes 2097152 | tf_op jit(solution)/shard_map/all_to_all | solution.py:363
  51.3 0.0 copy-done.1
  51.3 1.9 %collective-permute-start.3 = (bf16[128,2048]{1,0:T(8,128)(2,1)S(1)}, bf16[128,2048]{1,0:T(8,128)(2,1)}, u32[]{:S(2)}, u32[]{:S(2)}) collective-permute-start(bf16[128,2048]{1,0:T(8,128)(2,1)S(1)} %copy-done.1), channel_id=1, source_target_pairs={{0,8},{8,0},{1,9},{9,1},{2,10},{10,2},{3,11},{11,3},{4,12},{12,4},... | collective-permute-start | bytes 1572872 | tf_op jit(solution)/shard_map/ppermute | solution.py:354
  53.2 0.0 collective-permute-done.refs_1_
  53.3 2.4 %collective-permute-start.4 = (bf16[128,2048]{1,0:T(8,128)(2,1)S(1)}, bf16[128,2048]{1,0:T(8,128)(2,1)}, u32[]{:S(2)}, u32[]{:S(2)}) collective-permute-start(bf16[128,2048]{1,0:T(8,128)(2,1)S(1)} %collective-permute-done.refs_1_), channel_id=1, source_target_pairs={{0,8},{8,0},{1,9},{9,1},{2,10},{10,2},{3,11},{11,3},{4,12},{12,4},... | collective-permute-start | bytes 1572872 | tf_op jit(solution)/shard_map/ppermute | solution.py:354
  55.7 1.4 collective-permute-done.1.refs_2_
  57.1 1.9 %collective-permute-start.5 = (bf16[128,2048]{1,0:T(8,128)(2,1)S(1)}, bf16[128,2048]{1,0:T(8,128)(2,1)}, u32[]{:S(2)}, u32[]{:S(2)}) collective-permute-start(bf16[128,2048]{1,0:T(8,128)(2,1)S(1)} %collective-permute-done.1.refs_2_), channel_id=1, source_target_pairs={{0,8},{8,0},{1,9},{9,1},{2,10},{10,2},{3,11},{11,3},{4,12},{12,4},... | collective-permute-start | bytes 1572872 | tf_op jit(solution)/shard_map/ppermute | solution.py:354
  59.0 0.0 collective-permute-done.2.refs_3_
  59.0 2.4 %collective-permute-start.6 = (bf16[128,2048]{1,0:T(8,128)(2,1)S(1)}, bf16[128,2048]{1,0:T(8,128)(2,1)}, u32[]{:S(2)}, u32[]{:S(2)}) collective-permute-start(bf16[128,2048]{1,0:T(8,128)(2,1)S(1)} %collective-permute-done.2.refs_3_), channel_id=1, source_target_pairs={{0,8},{8,0},{1,9},{9,1},{2,10},{10,2},{3,11},{11,3},{4,12},{12,4},... | collective-permute-start | bytes 1572872 | tf_op jit(solution)/shard_map/ppermute | solution.py:354
  61.5 3.1 %all-to-all-done.1.w_ref = bf16[4,1024,128]{2,1,0:T(8,128)(2,1)S(1)} async-done(((bf16[4,1024,128]{2,1,0:T(8,128)(2,1)}), bf16[4,1024,128]{2,1,0:T(8,128)(2,1)S(1)}, u32[]{:S(2)}, u32[]{:S(2)}) %all-to-all-start.1) | async-done | bytes 1048608 | tf_op jit(solution)/shard_map/all_to_all | solution.py:363
  64.5 1.7 %decode.1 = (bf16[2048,256]{1,0:T(8,128)(2,1)S(1)}, bf16[2048,256]{1,0:T(8,128)(2,1)S(1)}) custom-call(bf16[4,1024,128]{2,1,0:T(8,128)(2,1)S(1)} %all-to-all-done.1.w_ref), custom_call_target="tpu_custom_call" | custom-call | bytes 3145728 | tf_op jit(solution)/shard_map/decode/pallas_call | solution.py:30
  66.2 0.0 collective-permute-done.3.refs_4_
  66.2 0.0 collective-permute-done.4.refs_5_
  66.2 0.0 collective-permute-done.5.refs_6_
  66.2 0.0 collective-permute-done.6.refs_7_
  66.2 0.0 copy-done.3
  66.2 5.2 %forward.1 = (bf16[4,256,256]{2,1,0:T(8,128)(2,1)S(1)}, bf16[4,128,2048]{2,1,0:T(8,128)(2,1)S(1)}) custom-call(bf16[128,2048]{1,0:T(8,128)(2,1)S(1)} %copy-done.1, bf16[128,2048]{1,0:T(8,128)(2,1)S(1)} %collective-permute-done.refs_1_, bf16[128,2048]{1,0:T(8,128)(2,1)S(1)} %collective-permute-done.1.refs_2_, ...), custom_call_target="tpu_custom_call" | custom-call | flops 2147483648 | bytes 8912916 | tf_op jit(solution)/shard_map/forward/pallas_call | solution.py:30
  71.4 14.2 %all_to_all.30.part_ref = bf16[4,256,256]{2,1,0:T(8,128)(2,1)S(1)} all-to-all(bf16[4,256,256]{2,1,0:T(8,128)(2,1)S(1)} %get-tuple-element.25), channel_id=1, replica_groups=mesh['z'=16,'yl'=2,'core'=2,'yh'=2,'x'=4] {'x'}, dimensions={0} | all-to-all | bytes 1048576 | tf_op jit(solution)/shard_map/all_to_all | solution.py:390
  85.6 0.1 slope.1
  85.7 11.0 %all_to_all.31.refs_5_ = bf16[4,256,256]{2,1,0:T(8,128)(2,1)S(1)} all-to-all(bf16[4,256,256]{2,1,0:T(8,128)(2,1)S(1)} %get-tuple-element.26), channel_id=1, replica_groups=mesh['z'=16,'yl'=2,'core'=2,'yh'=2,'x'=4] {'x'}, dimensions={0} | all-to-all | bytes 1048576 | tf_op jit(solution)/shard_map/all_to_all | solution.py:394
  96.7 4.4 %grad.1 = bf16[32,144,128]{2,1,0:T(8,128)(2,1)} custom-call(bf16[128,2048]{1,0:T(8,128)(2,1)S(1)} %copy-done.1, bf16[128,2048]{1,0:T(8,128)(2,1)S(1)} %collective-permute-done.refs_1_, bf16[128,2048]{1,0:T(8,128)(2,1)S(1)} %collective-permute-done.1.refs_2_, bf16[128,2048]{1,0:T(8,128)(2,1)S(1)} %collective-permute-done.2.refs_3_, ...), custom_call_target="tpu_custom_call" | custom-call | flops 1073741824 | bytes 5898772 | tf_op jit(solution)/shard_map/grad/pallas_call | solution.py:30
  101.1 0.0 copy-start
  101.1 5.8 %all-to-all-start.4 = ((bf16[32,144,128]{2,1,0:T(8,128)(2,1)}), bf16[32,144,128]{2,1,0:T(8,128)(2,1)S(1)}, u32[]{:S(2)}, u32[]{:S(2)}) async-start(bf16[32,144,128]{2,1,0:T(8,128)(2,1)} %grad.1), calls=%async_computation.4 | async-start | bytes 2359296 | tf_op jit(solution)/shard_map/all_to_all | solution.py:408
  106.9 0.0 copy-done
  107.0 0.0 copy-start.2
  107.0 1.1 choose.1.pat_ref
  108.1 15.5 %all-to-all-done.4.got_ref = bf16[32,144,128]{2,1,0:T(8,128)(2,1)S(1)} async-done(((bf16[32,144,128]{2,1,0:T(8,128)(2,1)}), bf16[32,144,128]{2,1,0:T(8,128)(2,1)S(1)}, u32[]{:S(2)}, u32[]{:S(2)}) %all-to-all-start.4) | async-done | bytes 1179680 | tf_op jit(solution)/shard_map/all_to_all | solution.py:408
  123.6 1.3 gather.1
  124.9 26.1 %all_to_all.32.got_ref = bf16[16,48,128]{2,1,0:T(8,128)(2,1)S(1)} all-to-all(bf16[16,48,128]{2,1,0:T(8,128)(2,1)S(1)} %gather.1), channel_id=1, replica_groups=mesh['z'=16,'yl'=2,'core'=2,'yh'=2,'x'=4] {'z'}, dimensions={0} | all-to-all | bytes 393216 | tf_op jit(solution)/shard_map/all_to_all | solution.py:417
  151.0 0.0 copy-done.2
  151.0 0.9 final.1
Async XLA Ops:
  4.0 41.5 %all-to-all-start = ((bf16[128,8,128]{2,1,0:T(8,128)(2,1)}), bf16[128,8,128]{2,1,0:T(8,128)(2,1)S(1)}, u32[]{:S(2)}, u32[]{:S(2)}) async-start(bf16[128,8,128]{2,1,0:T(8,128)(2,1)} %bitcast.16), calls=%async_computation | async-start | bytes 524288 | tf_op jit(solution)/shard_map/all_to_all | solution.py:335
  29.0 22.3 %copy-start.1 = (bf16[128,2048]{1,0:T(8,128)(2,1)S(1)}, bf16[128,2048]{1,0:T(8,128)(2,1)}, u32[]{:S(2)}) copy-start(bf16[128,2048]{1,0:T(8,128)(2,1)} %get-tuple-element.17.refs_0_) | copy-start | bytes 1572868
  29.0 24.2 %collective-permute-start = (bf16[128,2048]{1,0:T(8,128)(2,1)}, bf16[128,2048]{1,0:T(8,128)(2,1)S(1)}, u32[]{:S(2)}, u32[]{:S(2)}) collective-permute-start(bf16[128,2048]{1,0:T(8,128)(2,1)} %get-tuple-element.18), channel_id=1, source_target_pairs={{0,2},{1,3},{2,0},{3,1},{4,6},{5,7},{6,4},{7,5},{8,10},{9,11},{10,... | collective-permute-start | bytes 1572872 | tf_op jit(solution)/shard_map/ppermute | solution.py:353
  32.5 24.6 %collective-permute-start.1 = (bf16[128,2048]{1,0:T(8,128)(2,1)}, bf16[128,2048]{1,0:T(8,128)(2,1)S(1)}, u32[]{:S(2)}, u32[]{:S(2)}) collective-permute-start(bf16[128,2048]{1,0:T(8,128)(2,1)} %get-tuple-element.19), channel_id=1, source_target_pairs={{0,1},{1,2},{2,3},{3,0},{4,5},{5,6},{6,7},{7,4},{8,9},{9,10},{10,1... | collective-permute-start | bytes 1572872 | tf_op jit(solution)/shard_map/ppermute | solution.py:353
  36.5 22.5 %collective-permute-start.2 = (bf16[128,2048]{1,0:T(8,128)(2,1)}, bf16[128,2048]{1,0:T(8,128)(2,1)S(1)}, u32[]{:S(2)}, u32[]{:S(2)}) collective-permute-start(bf16[128,2048]{1,0:T(8,128)(2,1)} %get-tuple-element.20), channel_id=1, source_target_pairs={{0,3},{1,0},{2,1},{3,2},{4,7},{5,4},{6,5},{7,6},{8,11},{9,8},{10,9... | collective-permute-start | bytes 1572872 | tf_op jit(solution)/shard_map/ppermute | solution.py:353
  45.5 20.7 %copy-start.3 = (s32[5]{0:T(128)S(1)}, s32[5]{0:T(128)}, u32[]{:S(2)}) copy-start(s32[5]{0:T(128)} %stack.23.at_ref.refs_10_.refs_7_) | copy-start | bytes 64
  46.9 17.7 %all-to-all-start.1 = ((bf16[4,1024,128]{2,1,0:T(8,128)(2,1)}), bf16[4,1024,128]{2,1,0:T(8,128)(2,1)S(1)}, u32[]{:S(2)}, u32[]{:S(2)}) async-start(bf16[4,1024,128]{2,1,0:T(8,128)(2,1)} %spread.1), calls=%async_computation.1 | async-start | bytes 2097152 | tf_op jit(solution)/shard_map/all_to_all | solution.py:363
  51.3 14.9 %collective-permute-start.3 = (bf16[128,2048]{1,0:T(8,128)(2,1)S(1)}, bf16[128,2048]{1,0:T(8,128)(2,1)}, u32[]{:S(2)}, u32[]{:S(2)}) collective-permute-start(bf16[128,2048]{1,0:T(8,128)(2,1)S(1)} %copy-done.1), channel_id=1, source_target_pairs={{0,8},{8,0},{1,9},{9,1},{2,10},{10,2},{3,11},{11,3},{4,12},{12,4},... | collective-permute-start | bytes 1572872 | tf_op jit(solution)/shard_map/ppermute | solution.py:354
  53.3 12.9 %collective-permute-start.4 = (bf16[128,2048]{1,0:T(8,128)(2,1)S(1)}, bf16[128,2048]{1,0:T(8,128)(2,1)}, u32[]{:S(2)}, u32[]{:S(2)}) collective-permute-start(bf16[128,2048]{1,0:T(8,128)(2,1)S(1)} %collective-permute-done.refs_1_), channel_id=1, source_target_pairs={{0,8},{8,0},{1,9},{9,1},{2,10},{10,2},{3,11},{11,3},{4,12},{12,4},... | collective-permute-start | bytes 1572872 | tf_op jit(solution)/shard_map/ppermute | solution.py:354
  57.1 9.1 %collective-permute-start.5 = (bf16[128,2048]{1,0:T(8,128)(2,1)S(1)}, bf16[128,2048]{1,0:T(8,128)(2,1)}, u32[]{:S(2)}, u32[]{:S(2)}) collective-permute-start(bf16[128,2048]{1,0:T(8,128)(2,1)S(1)} %collective-permute-done.1.refs_2_), channel_id=1, source_target_pairs={{0,8},{8,0},{1,9},{9,1},{2,10},{10,2},{3,11},{11,3},{4,12},{12,4},... | collective-permute-start | bytes 1572872 | tf_op jit(solution)/shard_map/ppermute | solution.py:354
  59.0 7.2 %collective-permute-start.6 = (bf16[128,2048]{1,0:T(8,128)(2,1)S(1)}, bf16[128,2048]{1,0:T(8,128)(2,1)}, u32[]{:S(2)}, u32[]{:S(2)}) collective-permute-start(bf16[128,2048]{1,0:T(8,128)(2,1)S(1)} %collective-permute-done.2.refs_3_), channel_id=1, source_target_pairs={{0,8},{8,0},{1,9},{9,1},{2,10},{10,2},{3,11},{11,3},{4,12},{12,4},... | collective-permute-start | bytes 1572872 | tf_op jit(solution)/shard_map/ppermute | solution.py:354
  101.1 5.8 %copy-start = (s32[2048,64]{0,1:T(8,128)S(1)}, s32[2048,64]{0,1:T(8,128)}, u32[]{:S(2)}) copy-start(s32[2048,64]{0,1:T(8,128)} %param.9) | copy-start | bytes 1572868
  101.1 22.5 %all-to-all-start.4 = ((bf16[32,144,128]{2,1,0:T(8,128)(2,1)}), bf16[32,144,128]{2,1,0:T(8,128)(2,1)S(1)}, u32[]{:S(2)}, u32[]{:S(2)}) async-start(bf16[32,144,128]{2,1,0:T(8,128)(2,1)} %grad.1), calls=%async_computation.4 | async-start | bytes 2359296 | tf_op jit(solution)/shard_map/all_to_all | solution.py:408
  107.0 44.1 %copy-start.2 = (f32[64,128]{1,0:T(8,128)S(1)}, f32[64,128]{1,0:T(8,128)}, u32[]{:S(2)}) copy-start(f32[64,128]{1,0:T(8,128)} %get-tuple-element.29.pat_ref) | copy-start | bytes 98308

commit v9 on v6

--- a/solution.py
+++ b/solution.py
@@ -11,6 +11,7 @@
 AXES = ("z", "yl", "core", "yh", "x")
 Y = ("yl", "yh")
 ZCX = ("z", "core", "x")
+PLANE = ("yl", "core", "yh", "x")
 D, KVW, TOKENS = 8192, 512, 65536
 SHIFT = 34
 VMEM = pl.BlockSpec(memory_space=pltpu.VMEM)
@@ -44,6 +45,10 @@
 
 def lane_group(dims):
     return lax.broadcasted_iota(jnp.int32, dims, len(dims) - 1) // 32
+
+
+def place_in_plane(yl, c, yh, x):
+    return ((yl * NC + c) * NYH + yh) * NX + x
 
 
 def swap_groups(parts, place):
@@ -204,13 +209,18 @@
         out_ref[x, 256:320] = own_pat[x]
         out_ref[x, 320:] = other_pat[x]
     for row in (0, 128):
+        if row:
+            for load in loads:
+                load.wait()
+            rows = held_ref[...].reshape(512, 2048)
+        else:
+            rows = jnp.concatenate([ref[...] for ref in own], axis=0)
+        part = jnp.dot(rows, high_ref[...], preferred_element_type=F32)
+        part += jnp.dot(rows, low_ref[...], preferred_element_type=F32)
+        part = part.astype(BF16)
         for i in range(NX):
-            if row:
-                loads[i].wait()
-            rows = held_ref[i] if row else own[i][...]
-            part = jnp.dot(rows, high_ref[...], preferred_element_type=F32)
-            part += jnp.dot(rows, low_ref[...], preferred_element_type=F32)
-            out_ref[(at_ref[0] + BACK[i]) % NX, row : row + 128] = part.astype(BF16)
+            x = (at_ref[0] + BACK[i]) % NX
+            out_ref[x, row : row + 128] = part[i * 128 : (i + 1) * 128]
 
 
 def thirds(value, rows):
@@ -240,7 +250,7 @@
                 sent = sent.astype(F32)
                 sent = pltpu.roll(sent, shift, 1) if shift else sent
                 total = jnp.where(group == x, sent, total)
-            pat_ref[part, b * 32 : (b + 1) * 32, :] = total.astype(BF16)
+            pat_ref[part, b * 32 : (b + 1) * 32, :] = total
 
 
 def grad_kernel(*refs):
@@ -262,47 +272,59 @@
                 :, yh * 128 : (yh + 1) * 128
             ].reshape(8, 4, 8, 128)
     loss = thirds(loss_ref[...], 16).astype(BF16)
-    for i in range(4):
-        y = i % 2 * 2 + jnp.where(i < 2, at_ref[4], 1 - at_ref[4])
-        first, second = kept_rows(pat_ref[i].astype(F32).reshape(32, 8, 128))
-        for row, which in ((0, first), (256, second)):
-            kept = jnp.zeros_like(which)
-            for k in range(4):
-                kept += jnp.where(which == k, term_ref[y, :, k], 0.0)
-            out_ref[y, row : row + 256] = kept.reshape(256, 128).astype(BF16)
-        out_ref[y, 512:] = loss
+    for part in range(4):
+        yl = part % 2
+        yh = at_ref[4] if part < 2 else 1 - at_ref[4]
+        y = yl * NYH + yh
+        which = kept_rows(pat_ref[part].reshape(32, 8, 128))
+        kept = [jnp.zeros((32, 8, 128), F32) for _ in which]
+        for k in range(4):
+            for i in range(2):
+                kept[i] += jnp.where(which[i] == k, term_ref[y, :, k], 0.0)
+        kept = [rows.reshape(2, 8, NC, 8, 128) for rows in kept]
+        for c in range(NC):
+            parts = [kept[i][half, :, c] for half in range(2) for i in range(2)]
+            for x in range(NX):
+                at = place_in_plane(yl, c, yh, x)
+                out_ref[at, :64, :] = swap_groups(parts, x).reshape(64, 128).astype(BF16)
+                out_ref[at, 64:, :] = loss
 
 
 def gather_kernel(got_ref, out_ref, mid_ref):
-    total = got_ref[0].astype(F32)
-    for y in range(1, 4):
-        total = total + got_ref[y].astype(F32)
-    loss = jnp.sum(total[512:], axis=0, keepdims=True)
-    loss = thirds(jnp.broadcast_to(jnp.sum(loss, axis=1, keepdims=True), (1, 128)), 8)
-    row = lax.broadcasted_iota(jnp.int32, (8, 128), 0)
-    lane = lax.broadcasted_iota(jnp.int32, (8, 128), 1)
-    loss = jnp.where(lane == 64 + row, loss, 0.0)
-    kept = [total[:256].reshape(32, 8, 128), total[256:512].reshape(32, 8, 128)]
-    group = lane_group((32, 8, 128))
+    loss = got_ref[0, 64:, :].astype(F32)
+    for i in range(1, 32):
+        loss = loss + got_ref[i, 64:, :].astype(F32)
+    loss = jnp.sum(jnp.sum(loss, axis=0, keepdims=True), axis=1, keepdims=True)
+    loss = thirds(jnp.broadcast_to(loss, (1, 128)), 16)
+    lane = lax.broadcasted_iota(jnp.int32, (16, 128), 1)
+    mid_ref[:, 32:, :] = jnp.broadcast_to(jnp.where(lane == 0, loss, 0.0), (NZ, 16, 128))
+    group = lane_group((8, 8, 128))
     for x in range(NX):
-        one = pltpu.roll(kept[0], (4 - x) % 4 * 32, 2)
-        two = pltpu.roll(kept[1], (5 - x) % 4 * 32, 2)
-        mid_ref[:, x] = jnp.where(group == 0, one, jnp.where(group == 1, two, loss[None]))
-    out_ref[...] = mid_ref[...].reshape(1024, 128).astype(BF16)
+        sums = []
+        for c in range(NC):
+            total = jnp.zeros((64, 128), F32)
+            for y in range(4):
+                total += got_ref[place_in_plane(y // 2, c, y % 2, x), :64, :].astype(F32)
+            sums.append(total.reshape(8, 8, 128))
+        for half in range(2):
+            rows = jnp.zeros((8, 8, 128), F32)
+            for kept in range(2):
+                for c in range(NC):
+                    goal = kept * 2 + c
+                    shift = (goal - half * 2 - kept) % 4 * 32
+                    moved = pltpu.roll(sums[c], shift, 2) if shift else sums[c]
+                    rows = jnp.where(group == goal, moved, rows)
+            mid_ref[half * 8 : (half + 1) * 8, x * 8 : (x + 1) * 8, :] = rows
+    out_ref[...] = mid_ref[...].astype(BF16)
 
 
 def final_kernel(got_ref, pat_ref, out_ref, loss_ref):
     total = got_ref[0].astype(F32)
     for z in range(1, NZ):
         total = total + got_ref[z].astype(F32)
-    loss = jnp.where(lane_group(total.shape) == 2, total, 0.0)
-    loss = jnp.sum(jnp.sum(loss, axis=0, keepdims=True), axis=1, keepdims=True)
+    loss = jnp.sum(jnp.sum(total[32:], axis=0, keepdims=True), axis=1, keepdims=True)
     loss_ref[...] = loss / (TOKENS * KVW)
-    one, two = total[:32], total[32:]
-    group = lane_group((32, 128))
-    near = jnp.where(group == 0, one, pltpu.roll(two, 32, 1))
-    far = jnp.where(group == 2, pltpu.roll(one, 32, 1), pltpu.roll(two, 64, 1))
-    kept = jnp.where(group < 2, near, far)
+    kept = total[:32]
     row = lax.broadcasted_iota(jnp.int32, (32, 128), 0)
     col = lax.broadcasted_iota(jnp.int32, (32, 128), 1)
     spread = jnp.where(col // 4 == row, 1.0, 0.0).astype(BF16)
@@ -365,8 +387,6 @@
         name="norm",
     )
     own = [split[0]] + [lax.ppermute(split[i], "x", ring(STEP[i])) for i in range(1, NX)]
-    pair = [lax.ppermute(piece, "core", [(0, 1), (1, 0)]) for piece in own]
-
     rows_w = call(
         spread_kernel,
         shape((4, 1024, 128), BF16),
@@ -375,7 +395,6 @@
         name="spread",
     )
     all_w = lax.all_to_all(rows_w, Y, 0, 0, tiled=True)
-    high, low = call(decode_kernel, (shape((2048, 256), BF16),) * 2, all_w, name="decode")
 
     late, _ = lax.optimization_barrier((patterns, rows_w))
     own_pat = call(
@@ -387,6 +406,10 @@
         name="choose",
     )
     other_pat = lax.ppermute(own_pat, "yh", [(0, 1), (1, 0)])
+    own[2], own[3], other_pat = lax.optimization_barrier((own[2], own[3], other_pat))
+    pair = [lax.ppermute(piece, "core", [(0, 1), (1, 0)]) for piece in own]
+
+    high, low = call(decode_kernel, (shape((2048, 256), BF16),) * 2, all_w, name="decode")
 
     flops = 2 * 1024 * 2048 * 256
     part, held = call(
@@ -407,7 +430,7 @@
     got_part = lax.all_to_all(part, "x", 0, 0, tiled=True)
     slope, loss_part, pats = call(
         slope_kernel,
-        (shape((NX, 256, 256), BF16), shape((1, 128), F32), shape((4, 256, 128), BF16)),
+        (shape((NX, 256, 256), BF16), shape((1, 128), F32), shape((4, 256, 128), F32)),
         got_part,
         name="slope",
     )
@@ -415,7 +438,7 @@
 
     term = call(
         grad_kernel,
-        shape((4, 528, 128), BF16),
+        shape((32, 80, 128), BF16),
         *own,
         held,
         pats,
@@ -426,19 +449,19 @@
         flops=flops,
         name="grad",
     )
-    got_term = lax.all_to_all(term, Y, 0, 0, tiled=True)
+    got_term = lax.all_to_all(term, PLANE, 0, 0, tiled=True)
     packed_term = call(
         gather_kernel,
-        shape((1024, 128), BF16),
+        shape((NZ, 48, 128), BF16),
         got_term,
-        scratch=[pltpu.VMEM((32, 4, 8, 128), F32)],
+        scratch=[pltpu.VMEM((NZ, 48, 128), F32)],
         name="gather",
     )
-    got_sum = lax.all_to_all(packed_term.reshape(128, 8, 128), ZCX, 0, 0, tiled=True)
+    got_sum = lax.all_to_all(packed_term, "z", 0, 0, tiled=True)
     grad, loss = call(
         final_kernel,
         (shape((64, 128), F32), shape((1, 1), F32)),
-        got_sum.reshape(NZ, 64, 128),
+        got_sum,
         pat,
         name="final",
     )

time: 160 us -> 155 us (0.969)
  the two profiles are of different devices: /device:TPU:1 before, /device:TPU:32 now
where the time goes in v9:
time: 155 us; the launch traced here: 154 us
  blocking collectives  67 us (43%)
  starting transfers between devices  49.9 us (32%)
  Pallas kernels  24 us (15%)
  waiting for transfers between devices  11.8 us (8%)
    pallas_call x10, Pallas kernels, call(): pl.pallas_call(kernel, out_shape=out_shape, in_specs=specs, out_specs=jax...  24 us
    all_to_all x1, blocking collectives, shards(): got_sum = lax.all_to_all(packed_term, 'z', 0, 0, tiled=True)  22.3 us
    all_to_all x1, starting transfers between devices, shards(): got_w = lax.all_to_all(packed.reshape(128, 8, 128), ZCX, 0, 0, tiled=True)  19 us
    all_to_all x1, blocking collectives, shards(): got_term = lax.all_to_all(term, PLANE, 0, 0, tiled=True)  16.8 us
    all_to_all x1, blocking collectives, shards(): got_part = lax.all_to_all(part, 'x', 0, 0, tiled=True)  16.3 us
    ppermute x3, starting transfers between devices, shards(): lax.ppermute(split[i], 'x', ring(STEP[i]))  12.1 us
    all_to_all x1, blocking collectives, shards(): slopes = lax.all_to_all(slope, 'x', 0, 0, tiled=True)  11.6 us
    ppermute x4, starting transfers between devices, shards(): pair = [lax.ppermute(piece, 'core', [(0, 1), (1, 0)]) for piece in own]  8.9 us
  transfers between devices with their start and end apart: 10, of which 3 were waited for; matrix products, arithmetic and copies ran while one was open for 0% of the time, Pallas kernels for 6%

profile of v9, /device:TPU:32, one launch (start us, length us, event | category | flops | bytes accessed | tf_op | source)
XLA Modules:
  0.0 154.1 jit_solution(11990015067204209047)
XLA Ops:
  0.6 0.7 stack.23.at_ref.refs_12_.refs_8_
  1.3 2.7 %pack.1 = (bf16[16,64,128]{2,1,0:T(8,128)(2,1)}, f32[64,128]{1,0:T(8,128)}) custom-call(bf16[64,128]{1,0:T(8,128)(2,1)} %bitcast.17, bf16[64,128]{1,0:T(8,128)(2,1)} %bitcast.18, s32[64,2048]{1,0:T(8,128)} %bitcast.13, s32[5]{0:T(128)} %stack.23.at_ref.refs_12_.refs_8_), custom_call_target="tpu_custom_call" | custom-call | bytes 851988 | tf_op jit(solution)/shard_map/pack/pallas_call | solution.py:30
  4.0 19.0 %all-to-all-start = ((bf16[128,8,128]{2,1,0:T(8,128)(2,1)}), bf16[128,8,128]{2,1,0:T(8,128)(2,1)S(1)}, u32[]{:S(2)}, u32[]{:S(2)}) async-start(bf16[128,8,128]{2,1,0:T(8,128)(2,1)} %bitcast.16), calls=%async_computation | async-start | bytes 524288 | tf_op jit(solution)/shard_map/all_to_all | solution.py:371
  23.1 5.6 %norm.1 = (bf16[128,2048]{1,0:T(8,128)(2,1)}, bf16[128,2048]{1,0:T(8,128)(2,1)}, bf16[128,2048]{1,0:T(8,128)(2,1)}, bf16[128,2048]{1,0:T(8,128)(2,1)}) custom-call(bf16[128,8192]{1,0:T(8,128)(2,1)} %x_hbm.1, bf16[64,128]{1,0:T(8,128)(2,1)} %bitcast.20, s32[5]{0:T(128)} %stack.23.at_ref.refs_12_.refs_8_), custom_call_target="tpu_custom_call" | custom-call | flops 1073741824 | bytes 4210708 | tf_op jit(solution)/shard_map/norm/pallas_call | solution.py:30
  28.6 0.0 copy-start
  28.7 0.0 copy-start.3
  28.7 0.0 copy-start.1
  28.7 5.0 %collective-permute-start = (bf16[128,2048]{1,0:T(8,128)(2,1)}, bf16[128,2048]{1,0:T(8,128)(2,1)S(1)}, u32[]{:S(2)}, u32[]{:S(2)}) collective-permute-start(bf16[128,2048]{1,0:T(8,128)(2,1)} %get-tuple-element.22), channel_id=1, source_target_pairs={{0,2},{1,3},{2,0},{3,1},{4,6},{5,7},{6,4},{7,5},{8,10},{9,11},{10,... | collective-permute-start | bytes 1572872 | tf_op jit(solution)/shard_map/ppermute | solution.py:389
  33.7 2.5 %collective-permute-start.1 = (bf16[128,2048]{1,0:T(8,128)(2,1)}, bf16[128,2048]{1,0:T(8,128)(2,1)S(1)}, u32[]{:S(2)}, u32[]{:S(2)}) collective-permute-start(bf16[128,2048]{1,0:T(8,128)(2,1)} %get-tuple-element.23), channel_id=1, source_target_pairs={{0,1},{1,2},{2,3},{3,0},{4,5},{5,6},{6,7},{7,4},{8,9},{9,10},{10,1... | collective-permute-start | bytes 1572872 | tf_op jit(solution)/shard_map/ppermute | solution.py:389
  36.2 4.6 %collective-permute-start.2 = (bf16[128,2048]{1,0:T(8,128)(2,1)}, bf16[128,2048]{1,0:T(8,128)(2,1)}, u32[]{:S(2)}, u32[]{:S(2)}) collective-permute-start(bf16[128,2048]{1,0:T(8,128)(2,1)} %get-tuple-element.24), channel_id=1, source_target_pairs={{0,3},{1,0},{2,1},{3,2},{4,7},{5,4},{6,5},{7,6},{8,11},{9,8},{10,9... | collective-permute-start | bytes 1572872 | tf_op jit(solution)/shard_map/ppermute | solution.py:389
  40.8 3.5 %all-to-all-done = bf16[128,8,128]{2,1,0:T(8,128)(2,1)S(1)} async-done(((bf16[128,8,128]{2,1,0:T(8,128)(2,1)}), bf16[128,8,128]{2,1,0:T(8,128)(2,1)S(1)}, u32[]{:S(2)}, u32[]{:S(2)}) %all-to-all-start) | async-done | bytes 262176 | tf_op jit(solution)/shard_map/all_to_all | solution.py:371
  44.3 1.3 spread.1
  45.6 4.5 %all-to-all-start.1 = ((bf16[4,1024,128]{2,1,0:T(8,128)(2,1)}), bf16[4,1024,128]{2,1,0:T(8,128)(2,1)S(1)}, u32[]{:S(2)}, u32[]{:S(2)}) async-start(bf16[4,1024,128]{2,1,0:T(8,128)(2,1)} %spread.1), calls=%async_computation.1 | async-start | bytes 2097152 | tf_op jit(solution)/shard_map/all_to_all | solution.py:397
  50.1 0.0 copy-done
  50.1 0.0 copy-done.3
  50.1 0.9 choose.1.refs_10_
  51.0 5.4 %collective-permute-start.3 = (bf16[4,64,256]{2,1,0:T(8,128)(2,1)S(1)}, bf16[4,64,256]{2,1,0:T(8,128)(2,1)S(1)}, u32[]{:S(2)}, u32[]{:S(2)}) collective-permute-start(bf16[4,64,256]{2,1,0:T(8,128)(2,1)S(1)} %choose.1.refs_10_), channel_id=1, source_target_pairs={{0,4},{4,0},{1,5},{5,1},{2,6},{6,2},{3,7},{7,3},{8,12},{12,8},{9,1... | collective-permute-start | bytes 393224 | tf_op jit(solution)/shard_map/ppermute | solution.py:408
  56.4 0.0 copy-done.1
  56.4 2.7 %collective-permute-start.4 = (bf16[128,2048]{1,0:T(8,128)(2,1)S(1)}, bf16[128,2048]{1,0:T(8,128)(2,1)S(1)}, u32[]{:S(2)}, u32[]{:S(2)}) collective-permute-start(bf16[128,2048]{1,0:T(8,128)(2,1)S(1)} %copy-done.1), channel_id=1, source_target_pairs={{0,8},{8,0},{1,9},{9,1},{2,10},{10,2},{3,11},{11,3},{4,12},{12,4},... | collective-permute-start | bytes 1572872 | tf_op jit(solution)/shard_map/ppermute | solution.py:410
  59.1 0.0 collective-permute-done.refs_1_
  59.1 1.9 %collective-permute-start.5 = (bf16[128,2048]{1,0:T(8,128)(2,1)S(1)}, bf16[128,2048]{1,0:T(8,128)(2,1)}, u32[]{:S(2)}, u32[]{:S(2)}) collective-permute-start(bf16[128,2048]{1,0:T(8,128)(2,1)S(1)} %collective-permute-done.refs_1_), channel_id=1, source_target_pairs={{0,8},{8,0},{1,9},{9,1},{2,10},{10,2},{3,11},{11,3},{4,12},{12,4},... | collective-permute-start | bytes 1572872 | tf_op jit(solution)/shard_map/ppermute | solution.py:410
  61.0 0.0 collective-permute-done.1.refs_2_
  61.0 0.0 collective-permute-done.2.refs_3_
  61.1 8.0 %collective-permute-done.3.refs_11_ = bf16[4,64,256]{2,1,0:T(8,128)(2,1)S(1)} collective-permute-done((bf16[4,64,256]{2,1,0:T(8,128)(2,1)S(1)}, bf16[4,64,256]{2,1,0:T(8,128)(2,1)S(1)}, u32[]{:S(2)}, u32[]{:S(2)}) %collective-permute-start.3) | collective-permute-done | bytes 131104 | tf_op jit(solution)/shard_map/ppermute | solution.py:408
  69.1 2.1 %collective-permute-start.6 = (bf16[128,2048]{1,0:T(8,128)(2,1)S(1)}, bf16[128,2048]{1,0:T(8,128)(2,1)}, u32[]{:S(2)}, u32[]{:S(2)}) collective-permute-start(bf16[128,2048]{1,0:T(8,128)(2,1)S(1)} %collective-permute-done.1.refs_2_), channel_id=1, source_target_pairs={{0,8},{8,0},{1,9},{9,1},{2,10},{10,2},{3,11},{11,3},{4,12},{12,4},... | collective-permute-start | bytes 1572872 | tf_op jit(solution)/shard_map/ppermute | solution.py:410
  71.2 2.3 %collective-permute-start.7 = (bf16[128,2048]{1,0:T(8,128)(2,1)}, bf16[128,2048]{1,0:T(8,128)(2,1)}, u32[]{:S(2)}, u32[]{:S(2)}) collective-permute-start(bf16[128,2048]{1,0:T(8,128)(2,1)} %collective-permute-done.2.refs_3_), channel_id=1, source_target_pairs={{0,8},{8,0},{1,9},{9,1},{2,10},{10,2},{3,11},{11,3},{4,12},{12,4},... | collective-permute-start | bytes 1572872 | tf_op jit(solution)/shard_map/ppermute | solution.py:410
  73.4 0.0 all-to-all-done.1.w_ref
  73.4 1.7 %decode.1 = (bf16[2048,256]{1,0:T(8,128)(2,1)S(1)}, bf16[2048,256]{1,0:T(8,128)(2,1)S(1)}) custom-call(bf16[4,1024,128]{2,1,0:T(8,128)(2,1)S(1)} %all-to-all-done.1.w_ref), custom_call_target="tpu_custom_call" | custom-call | bytes 3145728 | tf_op jit(solution)/shard_map/decode/pallas_call | solution.py:30
  75.1 0.0 collective-permute-done.4.refs_4_
  75.1 0.0 collective-permute-done.5.refs_5_
  75.1 0.0 collective-permute-done.6.refs_6_
  75.2 0.2 collective-permute-done.7.refs_7_
  75.3 6.9 %forward.1 = (bf16[4,384,256]{2,1,0:T(8,128)(2,1)S(1)}, bf16[4,128,2048]{2,1,0:T(8,128)(2,1)S(1)}) custom-call(bf16[128,2048]{1,0:T(8,128)(2,1)S(1)} %copy-done.1, bf16[128,2048]{1,0:T(8,128)(2,1)S(1)} %collective-permute-done.refs_1_, bf16[128,2048]{1,0:T(8,128)(2,1)S(1)} %collective-permute-done.1.refs_2_, ...), custom_call_target="tpu_custom_call" | custom-call | flops 2147483648 | bytes 9437204 | tf_op jit(solution)/shard_map/forward/pallas_call | solution.py:30
  82.2 16.3 %all_to_all.30.part_ref = bf16[4,384,256]{2,1,0:T(8,128)(2,1)S(1)} all-to-all(bf16[4,384,256]{2,1,0:T(8,128)(2,1)S(1)} %get-tuple-element.33), channel_id=1, replica_groups=mesh['z'=16,'yl'=2,'core'=2,'yh'=2,'x'=4] {'x'}, dimensions={0} | all-to-all | bytes 1572864 | tf_op jit(solution)/shard_map/all_to_all | solution.py:430
  98.5 0.4 slope.1
  98.9 11.6 %all_to_all.31.refs_6_ = bf16[4,256,256]{2,1,0:T(8,128)(2,1)S(1)} all-to-all(bf16[4,256,256]{2,1,0:T(8,128)(2,1)S(1)} %get-tuple-element.35), channel_id=1, replica_groups=mesh['z'=16,'yl'=2,'core'=2,'yh'=2,'x'=4] {'x'}, dimensions={0} | all-to-all | bytes 1048576 | tf_op jit(solution)/shard_map/all_to_all | solution.py:437
  110.4 3.5 %grad.1 = bf16[32,80,128]{2,1,0:T(8,128)(2,1)S(1)} custom-call(bf16[128,2048]{1,0:T(8,128)(2,1)S(1)} %copy-done.1, bf16[128,2048]{1,0:T(8,128)(2,1)S(1)} %collective-permute-done.refs_1_, bf16[128,2048]{1,0:T(8,128)(2,1)S(1)} %collective-permute-done.1.refs_2_, bf16[128,2048]{1,0:T(8,128)(2,1)} %collective-permute-done.2.refs_3_, ...), custom_call_target="tpu_custom_call" | custom-call | flops 1073741824 | bytes 5898772 | tf_op jit(solution)/shard_map/grad/pallas_call | solution.py:30
  113.9 0.0 copy-start.2
  113.9 16.8 %all_to_all.32.got_ref = bf16[32,80,128]{2,1,0:T(8,128)(2,1)S(1)} all-to-all(bf16[32,80,128]{2,1,0:T(8,128)(2,1)S(1)} %grad.1), channel_id=1, replica_groups=mesh['z'=16,'yl'=2,'core'=2,'yh'=2,'x'=4] {'yl','core','yh','x'}, dimensions={0} | all-to-all | bytes 1310720 | tf_op jit(solution)/shard_map/all_to_all | solution.py:452
  130.7 0.2 gather.1
  131.0 22.3 %all_to_all.33.got_ref = bf16[16,48,128]{2,1,0:T(8,128)(2,1)S(1)} all-to-all(bf16[16,48,128]{2,1,0:T(8,128)(2,1)S(1)} %gather.1), channel_id=1, replica_groups=mesh['z'=16,'yl'=2,'core'=2,'yh'=2,'x'=4] {'z'}, dimensions={0} | all-to-all | bytes 393216 | tf_op jit(solution)/shard_map/all_to_all | solution.py:460
  153.3 0.0 copy-done.2
  153.3 0.9 final.1
Async XLA Ops:
  4.0 40.3 %all-to-all-start = ((bf16[128,8,128]{2,1,0:T(8,128)(2,1)}), bf16[128,8,128]{2,1,0:T(8,128)(2,1)S(1)}, u32[]{:S(2)}, u32[]{:S(2)}) async-start(bf16[128,8,128]{2,1,0:T(8,128)(2,1)} %bitcast.16), calls=%async_computation | async-start | bytes 524288 | tf_op jit(solution)/shard_map/all_to_all | solution.py:371
  28.6 21.4 %copy-start = (s32[2048,64]{0,1:T(8,128)S(1)}, s32[2048,64]{0,1:T(8,128)}, u32[]{:S(2)}) copy-start(s32[2048,64]{0,1:T(8,128)} %param.9) | copy-start | bytes 1572868
  28.7 21.4 %copy-start.3 = (s32[5]{0:T(128)S(1)}, s32[5]{0:T(128)}, u32[]{:S(2)}) copy-start(s32[5]{0:T(128)} %stack.23.at_ref.refs_12_.refs_8_) | copy-start | bytes 64
  28.7 27.7 %copy-start.1 = (bf16[128,2048]{1,0:T(8,128)(2,1)S(1)}, bf16[128,2048]{1,0:T(8,128)(2,1)}, u32[]{:S(2)}) copy-start(bf16[128,2048]{1,0:T(8,128)(2,1)} %get-tuple-element.21.refs_0_) | copy-start | bytes 1572868
  28.7 30.4 %collective-permute-start = (bf16[128,2048]{1,0:T(8,128)(2,1)}, bf16[128,2048]{1,0:T(8,128)(2,1)S(1)}, u32[]{:S(2)}, u32[]{:S(2)}) collective-permute-start(bf16[128,2048]{1,0:T(8,128)(2,1)} %get-tuple-element.22), channel_id=1, source_target_pairs={{0,2},{1,3},{2,0},{3,1},{4,6},{5,7},{6,4},{7,5},{8,10},{9,11},{10,... | collective-permute-start | bytes 1572872 | tf_op jit(solution)/shard_map/ppermute | solution.py:389
  33.7 27.3 %collective-permute-start.1 = (bf16[128,2048]{1,0:T(8,128)(2,1)}, bf16[128,2048]{1,0:T(8,128)(2,1)S(1)}, u32[]{:S(2)}, u32[]{:S(2)}) collective-permute-start(bf16[128,2048]{1,0:T(8,128)(2,1)} %get-tuple-element.23), channel_id=1, source_target_pairs={{0,1},{1,2},{2,3},{3,0},{4,5},{5,6},{6,7},{7,4},{8,9},{9,10},{10,1... | collective-permute-start | bytes 1572872 | tf_op jit(solution)/shard_map/ppermute | solution.py:389
  36.2 24.9 %collective-permute-start.2 = (bf16[128,2048]{1,0:T(8,128)(2,1)}, bf16[128,2048]{1,0:T(8,128)(2,1)}, u32[]{:S(2)}, u32[]{:S(2)}) collective-permute-start(bf16[128,2048]{1,0:T(8,128)(2,1)} %get-tuple-element.24), channel_id=1, source_target_pairs={{0,3},{1,0},{2,1},{3,2},{4,7},{5,4},{6,5},{7,6},{8,11},{9,8},{10,9... | collective-permute-start | bytes 1572872 | tf_op jit(solution)/shard_map/ppermute | solution.py:389
  45.6 27.8 %all-to-all-start.1 = ((bf16[4,1024,128]{2,1,0:T(8,128)(2,1)}), bf16[4,1024,128]{2,1,0:T(8,128)(2,1)S(1)}, u32[]{:S(2)}, u32[]{:S(2)}) async-start(bf16[4,1024,128]{2,1,0:T(8,128)(2,1)} %spread.1), calls=%async_computation.1 | async-start | bytes 2097152 | tf_op jit(solution)/shard_map/all_to_all | solution.py:397
  51.0 18.1 %collective-permute-start.3 = (bf16[4,64,256]{2,1,0:T(8,128)(2,1)S(1)}, bf16[4,64,256]{2,1,0:T(8,128)(2,1)S(1)}, u32[]{:S(2)}, u32[]{:S(2)}) collective-permute-start(bf16[4,64,256]{2,1,0:T(8,128)(2,1)S(1)} %choose.1.refs_10_), channel_id=1, source_target_pairs={{0,4},{4,0},{1,5},{5,1},{2,6},{6,2},{3,7},{7,3},{8,12},{12,8},{9,1... | collective-permute-start | bytes 393224 | tf_op jit(solution)/shard_map/ppermute | solution.py:408
  56.4 18.7 %collective-permute-start.4 = (bf16[128,2048]{1,0:T(8,128)(2,1)S(1)}, bf16[128,2048]{1,0:T(8,128)(2,1)S(1)}, u32[]{:S(2)}, u32[]{:S(2)}) collective-permute-start(bf16[128,2048]{1,0:T(8,128)(2,1)S(1)} %copy-done.1), channel_id=1, source_target_pairs={{0,8},{8,0},{1,9},{9,1},{2,10},{10,2},{3,11},{11,3},{4,12},{12,4},... | collective-permute-start | bytes 1572872 | tf_op jit(solution)/shard_map/ppermute | solution.py:410
  59.1 16.0 %collective-permute-start.5 = (bf16[128,2048]{1,0:T(8,128)(2,1)S(1)}, bf16[128,2048]{1,0:T(8,128)(2,1)}, u32[]{:S(2)}, u32[]{:S(2)}) collective-permute-start(bf16[128,2048]{1,0:T(8,128)(2,1)S(1)} %collective-permute-done.refs_1_), channel_id=1, source_target_pairs={{0,8},{8,0},{1,9},{9,1},{2,10},{10,2},{3,11},{11,3},{4,12},{12,4},... | collective-permute-start | bytes 1572872 | tf_op jit(solution)/shard_map/ppermute | solution.py:410
  69.1 6.0 %collective-permute-start.6 = (bf16[128,2048]{1,0:T(8,128)(2,1)S(1)}, bf16[128,2048]{1,0:T(8,128)(2,1)}, u32[]{:S(2)}, u32[]{:S(2)}) collective-permute-start(bf16[128,2048]{1,0:T(8,128)(2,1)S(1)} %collective-permute-done.1.refs_2_), channel_id=1, source_target_pairs={{0,8},{8,0},{1,9},{9,1},{2,10},{10,2},{3,11},{11,3},{4,12},{12,4},... | collective-permute-start | bytes 1572872 | tf_op jit(solution)/shard_map/ppermute | solution.py:410
  71.2 4.1 %collective-permute-start.7 = (bf16[128,2048]{1,0:T(8,128)(2,1)}, bf16[128,2048]{1,0:T(8,128)(2,1)}, u32[]{:S(2)}, u32[]{:S(2)}) collective-permute-start(bf16[128,2048]{1,0:T(8,128)(2,1)} %collective-permute-done.2.refs_3_), channel_id=1, source_target_pairs={{0,8},{8,0},{1,9},{9,1},{2,10},{10,2},{3,11},{11,3},{4,12},{12,4},... | collective-permute-start | bytes 1572872 | tf_op jit(solution)/shard_map/ppermute | solution.py:410
  113.9 39.4 %copy-start.2 = (f32[64,128]{1,0:T(8,128)S(1)}, f32[64,128]{1,0:T(8,128)}, u32[]{:S(2)}) copy-start(f32[64,128]{1,0:T(8,128)} %get-tuple-element.37.pat_ref) | copy-start | bytes 98308

commit v10 on v8

--- a/solution.py
+++ b/solution.py
@@ -20,7 +20,7 @@
 BACK = (0, 2, 3, 1)
 
 
-def call(kernel, out_shape, *args, scratch=(), flops=0, name=None, far=(), grant=24):
+def call(kernel, out_shape, *args, scratch=(), flops=0, name=None, far=(), out_far=False, grant=24):
     size = sum(a.size * a.dtype.itemsize for a in args)
     for o in jax.tree.leaves(out_shape):
         size += o.size * o.dtype.itemsize
@@ -31,7 +31,9 @@
         kernel,
         out_shape=out_shape,
         in_specs=specs,
-        out_specs=jax.tree.map(lambda _: VMEM, out_shape),
+        out_specs=jax.tree.map(
+            lambda _: pl.BlockSpec(memory_space=pl.ANY) if out_far else VMEM, out_shape
+        ),
         scratch_shapes=list(scratch),
         name=name,
         cost_estimate=pl.CostEstimate(flops=flops, bytes_accessed=size, transcendentals=0),
@@ -61,6 +63,21 @@
     return total
 
 
+def swap_all(parts):
+    axis = parts[0].ndim - 1
+    group = lane_group(parts[0].shape)
+    low, even = group < 2, group % 2 == 0
+    half = []
+    for a, b in ((0, 2), (1, 3)):
+        half.append(jnp.where(low, parts[a], pltpu.roll(parts[b], 64, axis)))
+        half.append(jnp.where(low, pltpu.roll(parts[a], 64, axis), parts[b]))
+    out = []
+    for a, b in ((half[0], half[2]), (half[1], half[3])):
+        out.append(jnp.where(even, a, pltpu.roll(b, 32, axis)))
+        out.append(jnp.where(even, pltpu.roll(a, 96, axis), b))
+    return out
+
+
 def kept_rows(pat):
     first = jnp.where(pat > 2.5, 1.0, 0.0) + jnp.where(pat > 4.5, 1.0, 0.0)
     second = jnp.where(pat < 2.5, pat + 1.0, jnp.where(pat < 3.5, 2.0, 3.0))
@@ -76,43 +93,49 @@
 
 
 def norm_kernel(x_hbm, gain_ref, at_ref, *rest):
-    outs, (rows_ref, x_ref, sems) = rest[:NX], rest[NX:]
-    me = at_ref[0]
-    cuts = [pl.ds(i * 2048, 2048) for i in range(4)]
+    outs, (x_ref, move_ref, split_ref, sems, out_sems) = rest[:NX], rest[NX:]
     loads = [
         pltpu.make_async_copy(x_hbm.at[:, cut], x_ref.at[:, cut], sems.at[i])
-        for i, cut in enumerate(cuts)
+        for i, cut in enumerate(pl.ds(i * 1024, 1024) for i in range(8))
     ]
     for load in loads:
         load.start()
-    total = jnp.zeros((128, 512), F32)
-    for g in range(16):
-        if g % 4 == 0:
-            loads[g // 4].wait()
-        part = x_ref[:, g * 512 : (g + 1) * 512].astype(F32)
+    src = lax.broadcasted_iota(jnp.int32, (512, 128), 0)
+    dst = lax.broadcasted_iota(jnp.int32, (512, 128), 1)
+    goal = ((src >> 5 & 3) << 7) + (src >> 7 << 5) + ((src & 3) << 3) + (src >> 2 & 7)
+    for x in range(NX):
+        move_ref[:, x * 128 : (x + 1) * 128] = jnp.where(goal == dst + x * 128, 1.0, 0.0).astype(BF16)
+    total = jnp.zeros((128, 128), F32)
+    for g in range(64):
+        if g % 8 == 0:
+            loads[g // 8].wait()
+        part = x_ref[:, g * 128 : (g + 1) * 128].astype(F32)
         total += part * part
     factor = lax.rsqrt(jnp.sum(total, axis=1, keepdims=True) / D + 1e-05)
+    factor = jnp.broadcast_to(factor, (128, 128))
     gain = gain_ref[...].astype(F32)
+    stores = []
     for yl in range(2):
         for m in range(8):
             tile = yl * 8 + m
+            parts = []
             for b in range(4):
                 block = 8 * m + 4 * (b // 2) + 2 * yl + b % 2
                 part = x_ref[:, block * 128 : (block + 1) * 128].astype(F32)
-                rows_ref[tile * 128 : (tile + 1) * 128, b * 128 : (b + 1) * 128] = (
-                    part * factor * gain[block : block + 1, :]
-                ).astype(BF16)
-    src = lax.broadcasted_iota(jnp.int32, (512, 512), 0)
-    dst = lax.broadcasted_iota(jnp.int32, (512, 512), 1)
-    ahead = (src // 32 + NX - me) % NX
-    goal = ahead * 128 + src // 128 * 32 + shuffled(src % 32)
-    move = jnp.where(goal == dst, 1.0, 0.0).astype(BF16)
-    for tile in range(16):
-        seg = jnp.dot(
-            rows_ref[tile * 128 : (tile + 1) * 128, :], move, preferred_element_type=F32
-        ).astype(BF16)
-        for i, x in enumerate(STEP):
-            outs[i][:, tile * 128 : (tile + 1) * 128] = seg[:, x * 128 : (x + 1) * 128]
+                parts.append((part * factor * gain[block : block + 1, :]).astype(BF16))
+            parts = jnp.concatenate(parts, axis=1)
+            seg = jnp.dot(parts, move_ref[...], preferred_element_type=F32).astype(BF16)
+            for x in range(NX):
+                split_ref[x, :, tile * 128 : (tile + 1) * 128] = seg[:, x * 128 : (x + 1) * 128]
+        for i in range(NX):
+            cut = pl.ds(yl * 1024, 1024)
+            piece = split_ref.at[(at_ref[0] + STEP[i]) % NX]
+            stores.append(
+                pltpu.make_async_copy(piece.at[:, cut], outs[i].at[:, cut], out_sems.at[yl * NX + i])
+            )
+            stores[-1].start()
+    for store in stores:
+        store.wait()
 
 
 def choose_kernel(pat_ref, at_ref, out_ref, pick_ref):
@@ -150,16 +173,13 @@
     delta = student_ref[...].astype(F32) * keep - teacher_ref[...].astype(F32)
     delta = delta * 2.0**SHIFT
     delta = ((delta * jnp.abs(delta)) * (delta * delta)).astype(BF16)
-    row = lax.broadcasted_iota(jnp.int32, (64, 128), 0)
-    col = lax.broadcasted_iota(jnp.int32, (64, 128), 1)
-    widen = jnp.where(row == col, 1.0, 0.0).astype(BF16)
-    rows = lax.dot_general(
-        delta, widen, (((0,), (0,)), ((), ())), preferred_element_type=F32
-    ).astype(BF16)
     dst = lax.broadcasted_iota(jnp.int32, (128, 128), 0)
     src = lax.broadcasted_iota(jnp.int32, (128, 128), 1)
     move = jnp.where(src // 32 * 32 + shuffled(src % 32) == dst, 1.0, 0.0).astype(BF16)
-    wide = jnp.dot(move, rows, preferred_element_type=F32).reshape(4, 4, 8, 128)
+    delta = jnp.concatenate([delta, jnp.zeros_like(delta)], axis=0)
+    wide = lax.dot_general(
+        move, delta, (((1,), (1,)), ((), ())), preferred_element_type=F32
+    ).reshape(4, 4, 8, 128)
     for c in range(NC):
         piece = swap_groups([wide[:, q] for q in range(4)], c).reshape(32, 128).astype(BF16)
         for z in range(NZ):
@@ -168,8 +188,8 @@
 
 def spread_kernel(got_ref, out_ref, mid_ref):
     got = got_ref[...].astype(F32).reshape(32, 4, 8, 128)
-    for q in range(4):
-        mid_ref[:, q] = swap_groups([got[:, x] for x in range(NX)], q)
+    for q, rows in enumerate(swap_all([got[:, x] for x in range(NX)])):
+        mid_ref[:, q] = rows
     rows = mid_ref[...].reshape(1024, 128).astype(BF16)
     for y in range(4):
         out_ref[y] = rows
@@ -179,7 +199,7 @@
     for y in range(4):
         for k in range(4):
             sent = w_ref[y, k * 256 : (k + 1) * 256, :].astype(F32)
-            size = jnp.sqrt(jnp.sqrt(jnp.abs(sent))) * 2.0**-SHIFT
+            size = lax.rsqrt(lax.rsqrt(jnp.abs(sent))) * 2.0**-SHIFT
             delta = jnp.where(sent < 0, -size, size)
             high = delta.astype(BF16)
             at = (y // 2) * 1024 + k * 256
@@ -195,18 +215,13 @@
     for load in loads:
         load.start()
     for row in (0, 128):
-        if row:
-            for load in loads:
-                load.wait()
-            rows = held_ref[...].reshape(512, 2048)
-        else:
-            rows = jnp.concatenate([ref[...] for ref in own], axis=0)
-        part = jnp.dot(rows, high_ref[...], preferred_element_type=F32)
-        part += jnp.dot(rows, low_ref[...], preferred_element_type=F32)
-        part = part.astype(BF16)
         for i in range(NX):
-            x = (at_ref[0] + BACK[i]) % NX
-            out_ref[x, row : row + 128] = part[i * 128 : (i + 1) * 128]
+            if row:
+                loads[i].wait()
+            rows = held_ref[i] if row else own[i][...]
+            part = jnp.dot(rows, high_ref[...], preferred_element_type=F32)
+            part += jnp.dot(rows, low_ref[...], preferred_element_type=F32)
+            out_ref[(at_ref[0] + BACK[i]) % NX, row : row + 128] = part.astype(BF16)
 
 
 def thirds(value, rows):
@@ -250,10 +265,9 @@
     for y in range(4):
         term = term_ref[y].reshape(NZ, NC, 4, 8, 128)
         for c in range(NC):
-            parts = [term[:, c, q] for q in range(4)]
-            for x in range(NX):
+            for x, rows in enumerate(swap_all([term[:, c, q] for q in range(4)])):
                 at = place_in_plane(y // 2, c, y % 2, x)
-                out_ref[at, :128, :] = swap_groups(parts, x).reshape(128, 128).astype(BF16)
+                out_ref[at, :128, :] = rows.reshape(128, 128).astype(BF16)
                 out_ref[at, 128:, :] = loss
 
 
@@ -341,18 +355,19 @@
         norm_gain.reshape(64, 128),
         at,
         scratch=[
-            pltpu.VMEM((2048, 512), BF16),
             pltpu.VMEM((128, D), BF16),
-            pltpu.SemaphoreType.DMA((4,)),
+            pltpu.VMEM((512, 512), BF16),
+            pltpu.VMEM((NX, 128, 2048), BF16),
+            pltpu.SemaphoreType.DMA((8,)),
+            pltpu.SemaphoreType.DMA((2 * NX,)),
         ],
         flops=2 * 2048 * 512 * 512,
         far=(0,),
+        out_far=True,
         grant=60,
         name="norm",
     )
     own = [split[0]] + [lax.ppermute(split[i], "x", ring(STEP[i])) for i in range(1, NX)]
-    pair = [lax.ppermute(piece, "core", [(0, 1), (1, 0)]) for piece in own]
-
     rows_w = call(
         spread_kernel,
         shape((4, 1024, 128), BF16),
@@ -361,7 +376,6 @@
         name="spread",
     )
     all_w = lax.all_to_all(rows_w, Y, 0, 0, tiled=True)
-    high, low = call(decode_kernel, (shape((2048, 256), BF16),) * 2, all_w, name="decode")
 
     late, _ = lax.optimization_barrier((patterns, rows_w))
     own_pat = call(
@@ -372,6 +386,10 @@
         scratch=[pltpu.VMEM((NZ, NYL, NC, NX, 8, 128), F32)],
         name="choose",
     )
+    own[2], own_pat = lax.optimization_barrier((own[2], own_pat))
+    pair = [lax.ppermute(piece, "core", [(0, 1), (1, 0)]) for piece in own]
+
+    high, low = call(decode_kernel, (shape((2048, 256), BF16),) * 2, all_w, name="decode")
 
     flops = 2 * 1024 * 2048 * 256
     part, held = call(

time: 155 us -> 154 us (level)
  blocking collectives: 51.2 us -> 75.4 us
  waiting for transfers between devices: 27.1 us -> 10.3 us
  starting transfers between devices: 47.7 us -> 43 us
  Pallas kernels: 24.3 us -> 21.7 us
    all_to_all x0 -> x1, blocking collectives: none -> 23.1 us  [shards(): got_term = lax.all_to_all(term, PLANE, 0, 0, tiled=True)]
    all_to_all x1 -> x0, waiting for transfers between devices: 15.5 us -> none  [shards(): got_term = lax.all_to_all(term, PLANE, 0, 0, tiled=True)]
    all_to_all x1 -> x0, starting transfers between devices: 5.81 us -> none  [shards(): got_term = lax.all_to_all(term, PLANE, 0, 0, tiled=True)]
    pallas_call x10, Pallas kernels: 24.3 us -> 21.7 us  [call(): pl.pallas_call(kernel, out_shape=out_shape, in_specs=specs, out_specs=jax...]
    all_to_all x1, waiting for transfers between devices: 3.06 us -> 0.51 us  [shards(): all_w = lax.all_to_all(rows_w, Y, 0, 0, tiled=True)]
  transfers between devices with their start and end apart: 10 -> 9, of which waited for: 4 -> 4; matrix products, arithmetic and copies ran while one was open for 0% -> 0% of each run, Pallas kernels for 6% -> 5%
where the time goes in v10:
time: 154 us; the launch traced here: 152 us
  blocking collectives  75.4 us (49%)
  starting transfers between devices  43 us (28%)
  Pallas kernels  21.7 us (14%)
  waiting for transfers between devices  10.3 us (7%)
    all_to_all x1, blocking collectives, shards(): got_sum = lax.all_to_all(packed_term, 'z', 0, 0, tiled=True)  27.5 us
    all_to_all x1, blocking collectives, shards(): got_term = lax.all_to_all(term, PLANE, 0, 0, tiled=True)  23.1 us
    pallas_call x10, Pallas kernels, call(): pl.pallas_call(kernel, out_shape=out_shape, in_specs=specs, out_specs=jax...  21.7 us
    all_to_all x1, starting transfers between devices, shards(): got_w = lax.all_to_all(packed.reshape(128, 8, 128), ZCX, 0, 0, tiled=True)  19.4 us
    all_to_all x1, blocking collectives, shards(): got_part = lax.all_to_all(part, 'x', 0, 0, tiled=True)  13.8 us
    all_to_all x1, blocking collectives, shards(): slopes = lax.all_to_all(slope, 'x', 0, 0, tiled=True)  11 us
    ppermute x3, starting transfers between devices, shards(): lax.ppermute(split[i], 'x', ring(STEP[i]))  10.6 us
    ppermute x4, starting transfers between devices, shards(): pair = [lax.ppermute(piece, 'core', [(0, 1), (1, 0)]) for piece in own]  8.62 us
  transfers between devices with their start and end apart: 9, of which 4 were waited for; matrix products, arithmetic and copies ran while one was open for 0% of the time, Pallas kernels for 5%

profile of v10, /device:TPU:6, one launch (start us, length us, event | category | flops | bytes accessed | tf_op | source)
XLA Modules:
  0.0 152.0 jit_solution(17192017094767115818)
XLA Ops:
  0.6 0.7 stack.23.at_ref.refs_10_.refs_7_
  1.3 2.6 %pack.1 = (bf16[16,64,128]{2,1,0:T(8,128)(2,1)}, f32[64,128]{1,0:T(8,128)}) custom-call(bf16[64,128]{1,0:T(8,128)(2,1)} %bitcast.17, bf16[64,128]{1,0:T(8,128)(2,1)} %bitcast.18, s32[64,2048]{1,0:T(8,128)} %bitcast.13, s32[5]{0:T(128)} %stack.23.at_ref.refs_10_.refs_7_), custom_call_target="tpu_custom_call" | custom-call | bytes 851988 | tf_op jit(solution)/shard_map/pack/pallas_call | solution.py:30
  3.9 19.4 %all-to-all-start = ((bf16[128,8,128]{2,1,0:T(8,128)(2,1)}), bf16[128,8,128]{2,1,0:T(8,128)(2,1)S(1)}, u32[]{:S(2)}, u32[]{:S(2)}) async-start(bf16[128,8,128]{2,1,0:T(8,128)(2,1)} %bitcast.16), calls=%async_computation | async-start | bytes 524288 | tf_op jit(solution)/shard_map/all_to_all | solution.py:349
  23.3 4.9 %norm.1 = (bf16[128,2048]{1,0:T(8,128)(2,1)}, bf16[128,2048]{1,0:T(8,128)(2,1)}, bf16[128,2048]{1,0:T(8,128)(2,1)}, bf16[128,2048]{1,0:T(8,128)(2,1)}) custom-call(bf16[128,8192]{1,0:T(8,128)(2,1)} %x_hbm.1, bf16[64,128]{1,0:T(8,128)(2,1)} %bitcast.20, s32[5]{0:T(128)} %stack.23.at_ref.refs_10_.refs_7_), custom_call_target="tpu_custom_call" | custom-call | flops 1073741824 | bytes 4210708 | tf_op jit(solution)/shard_map/norm/pallas_call | solution.py:30
  28.2 0.0 copy-start.1
  28.2 0.0 copy-start
  28.2 0.0 copy-start.3
  28.2 3.5 %collective-permute-start = (bf16[128,2048]{1,0:T(8,128)(2,1)}, bf16[128,2048]{1,0:T(8,128)(2,1)S(1)}, u32[]{:S(2)}, u32[]{:S(2)}) collective-permute-start(bf16[128,2048]{1,0:T(8,128)(2,1)} %get-tuple-element.20), channel_id=1, source_target_pairs={{0,2},{1,3},{2,0},{3,1},{4,6},{5,7},{6,4},{7,5},{8,10},{9,11},{10,... | collective-permute-start | bytes 1572872 | tf_op jit(solution)/shard_map/ppermute | solution.py:370
  31.7 2.2 %collective-permute-start.2 = (bf16[128,2048]{1,0:T(8,128)(2,1)}, bf16[128,2048]{1,0:T(8,128)(2,1)}, u32[]{:S(2)}, u32[]{:S(2)}) collective-permute-start(bf16[128,2048]{1,0:T(8,128)(2,1)} %get-tuple-element.25), channel_id=1, source_target_pairs={{0,3},{1,0},{2,1},{3,2},{4,7},{5,4},{6,5},{7,6},{8,11},{9,8},{10,9... | collective-permute-start | bytes 1572872 | tf_op jit(solution)/shard_map/ppermute | solution.py:370
  33.9 4.9 %collective-permute-start.1 = (bf16[128,2048]{1,0:T(8,128)(2,1)}, bf16[128,2048]{1,0:T(8,128)(2,1)}, u32[]{:S(2)}, u32[]{:S(2)}) collective-permute-start(bf16[128,2048]{1,0:T(8,128)(2,1)} %get-tuple-element.21), channel_id=1, source_target_pairs={{0,1},{1,2},{2,3},{3,0},{4,5},{5,6},{6,7},{7,4},{8,9},{9,10},{10,1... | collective-permute-start | bytes 1572872 | tf_op jit(solution)/shard_map/ppermute | solution.py:370
  38.8 6.6 %all-to-all-done = bf16[128,8,128]{2,1,0:T(8,128)(2,1)S(1)} async-done(((bf16[128,8,128]{2,1,0:T(8,128)(2,1)}), bf16[128,8,128]{2,1,0:T(8,128)(2,1)S(1)}, u32[]{:S(2)}, u32[]{:S(2)}) %all-to-all-start) | async-done | bytes 262176 | tf_op jit(solution)/shard_map/all_to_all | solution.py:349
  45.4 1.3 spread.1
  46.7 4.5 %all-to-all-start.1 = ((bf16[4,1024,128]{2,1,0:T(8,128)(2,1)}), bf16[4,1024,128]{2,1,0:T(8,128)(2,1)S(1)}, u32[]{:S(2)}, u32[]{:S(2)}) async-start(bf16[4,1024,128]{2,1,0:T(8,128)(2,1)} %spread.1), calls=%async_computation.1 | async-start | bytes 2097152 | tf_op jit(solution)/shard_map/all_to_all | solution.py:378
  51.1 0.0 copy-done.1
  51.2 1.9 %collective-permute-start.3 = (bf16[128,2048]{1,0:T(8,128)(2,1)S(1)}, bf16[128,2048]{1,0:T(8,128)(2,1)}, u32[]{:S(2)}, u32[]{:S(2)}) collective-permute-start(bf16[128,2048]{1,0:T(8,128)(2,1)S(1)} %copy-done.1), channel_id=1, source_target_pairs={{0,8},{8,0},{1,9},{9,1},{2,10},{10,2},{3,11},{11,3},{4,12},{12,4},... | collective-permute-start | bytes 1572872 | tf_op jit(solution)/shard_map/ppermute | solution.py:390
  53.1 0.0 collective-permute-done.refs_1_
  53.1 2.4 %collective-permute-start.4 = (bf16[128,2048]{1,0:T(8,128)(2,1)S(1)}, bf16[128,2048]{1,0:T(8,128)(2,1)}, u32[]{:S(2)}, u32[]{:S(2)}) collective-permute-start(bf16[128,2048]{1,0:T(8,128)(2,1)S(1)} %collective-permute-done.refs_1_), channel_id=1, source_target_pairs={{0,8},{8,0},{1,9},{9,1},{2,10},{10,2},{3,11},{11,3},{4,12},{12,4},... | collective-permute-start | bytes 1572872 | tf_op jit(solution)/shard_map/ppermute | solution.py:390
  55.5 2.9 %collective-permute-done.2.refs_3_ = bf16[128,2048]{1,0:T(8,128)(2,1)} collective-permute-done((bf16[128,2048]{1,0:T(8,128)(2,1)}, bf16[128,2048]{1,0:T(8,128)(2,1)}, u32[]{:S(2)}, u32[]{:S(2)}) %collective-permute-start.2) | collective-permute-done | bytes 524320 | tf_op jit(solution)/shard_map/ppermute | solution.py:370
  58.4 2.0 %collective-permute-start.6 = (bf16[128,2048]{1,0:T(8,128)(2,1)}, bf16[128,2048]{1,0:T(8,128)(2,1)}, u32[]{:S(2)}, u32[]{:S(2)}) collective-permute-start(bf16[128,2048]{1,0:T(8,128)(2,1)} %collective-permute-done.2.refs_3_), channel_id=1, source_target_pairs={{0,8},{8,0},{1,9},{9,1},{2,10},{10,2},{3,11},{11,3},{4,12},{12,4},... | collective-permute-start | bytes 1572872 | tf_op jit(solution)/shard_map/ppermute | solution.py:390
  60.3 0.0 copy-done
  60.3 0.0 copy-done.3
  60.3 1.1 choose.1.pat_ref
  61.5 0.0 collective-permute-done.1.refs_2_
  61.5 2.3 %collective-permute-start.5 = (bf16[128,2048]{1,0:T(8,128)(2,1)}, bf16[128,2048]{1,0:T(8,128)(2,1)S(1)}, u32[]{:S(2)}, u32[]{:S(2)}) collective-permute-start(bf16[128,2048]{1,0:T(8,128)(2,1)} %collective-permute-done.1.refs_2_), channel_id=1, source_target_pairs={{0,8},{8,0},{1,9},{9,1},{2,10},{10,2},{3,11},{11,3},{4,12},{12,4},... | collective-permute-start | bytes 1572872 | tf_op jit(solution)/shard_map/ppermute | solution.py:390
  63.8 0.5 all-to-all-done.1.w_ref
  64.3 0.9 decode.1
  65.2 0.0 collective-permute-done.3.refs_4_
  65.2 0.0 collective-permute-done.4.refs_5_
  65.2 0.0 collective-permute-done.6.refs_7_
  65.3 0.3 collective-permute-done.5.refs_6_
  65.6 5.3 %forward.1 = (bf16[4,256,256]{2,1,0:T(8,128)(2,1)S(1)}, bf16[4,128,2048]{2,1,0:T(8,128)(2,1)S(1)}) custom-call(bf16[128,2048]{1,0:T(8,128)(2,1)S(1)} %copy-done.1, bf16[128,2048]{1,0:T(8,128)(2,1)S(1)} %collective-permute-done.refs_1_, bf16[128,2048]{1,0:T(8,128)(2,1)} %collective-permute-done.1.refs_2_, bf16[128,2048]{1,0:T(8,128)(2,1)} %collective-permute-done.2.refs_3_, ...), custom_call_target="tpu_custom_call" | custom-call | flops 2147483648 | bytes 8912916 | tf_op jit(solution)/shard_map/forward/pallas_call | solution.py:30
  70.9 13.8 %all_to_all.30.part_ref = bf16[4,256,256]{2,1,0:T(8,128)(2,1)S(1)} all-to-all(bf16[4,256,256]{2,1,0:T(8,128)(2,1)S(1)} %get-tuple-element.29), channel_id=1, replica_groups=mesh['z'=16,'yl'=2,'core'=2,'yh'=2,'x'=4] {'x'}, dimensions={0} | all-to-all | bytes 1048576 | tf_op jit(solution)/shard_map/all_to_all | solution.py:408
  84.7 0.1 slope.1
  84.8 11.0 %all_to_all.31.refs_5_ = bf16[4,256,256]{2,1,0:T(8,128)(2,1)S(1)} all-to-all(bf16[4,256,256]{2,1,0:T(8,128)(2,1)S(1)} %get-tuple-element.30), channel_id=1, replica_groups=mesh['z'=16,'yl'=2,'core'=2,'yh'=2,'x'=4] {'x'}, dimensions={0} | all-to-all | bytes 1048576 | tf_op jit(solution)/shard_map/all_to_all | solution.py:412
  95.8 3.4 %grad.1 = bf16[32,144,128]{2,1,0:T(8,128)(2,1)S(1)} custom-call(bf16[128,2048]{1,0:T(8,128)(2,1)S(1)} %copy-done.1, bf16[128,2048]{1,0:T(8,128)(2,1)S(1)} %collective-permute-done.refs_1_, bf16[128,2048]{1,0:T(8,128)(2,1)} %collective-permute-done.1.refs_2_, bf16[128,2048]{1,0:T(8,128)(2,1)} %collective-permute-done.2.refs_3_, ...), custom_call_target="tpu_custom_call" | custom-call | flops 1073741824 | bytes 5898772 | tf_op jit(solution)/shard_map/grad/pallas_call | solution.py:30
  99.2 0.0 copy-start.2
  99.2 23.1 %all_to_all.32.got_ref = bf16[32,144,128]{2,1,0:T(8,128)(2,1)S(1)} all-to-all(bf16[32,144,128]{2,1,0:T(8,128)(2,1)S(1)} %grad.1), channel_id=1, replica_groups=mesh['z'=16,'yl'=2,'core'=2,'yh'=2,'x'=4] {'yl','core','yh','x'}, dimensions={0} | all-to-all | bytes 2359296 | tf_op jit(solution)/shard_map/all_to_all | solution.py:426
  122.3 1.3 gather.1
  123.6 27.5 %all_to_all.33.got_ref = bf16[16,48,128]{2,1,0:T(8,128)(2,1)S(1)} all-to-all(bf16[16,48,128]{2,1,0:T(8,128)(2,1)S(1)} %gather.1), channel_id=1, replica_groups=mesh['z'=16,'yl'=2,'core'=2,'yh'=2,'x'=4] {'z'}, dimensions={0} | all-to-all | bytes 393216 | tf_op jit(solution)/shard_map/all_to_all | solution.py:435
  151.1 0.0 copy-done.2
  151.1 0.9 final.1
Async XLA Ops:
  3.9 41.5 %all-to-all-start = ((bf16[128,8,128]{2,1,0:T(8,128)(2,1)}), bf16[128,8,128]{2,1,0:T(8,128)(2,1)S(1)}, u32[]{:S(2)}, u32[]{:S(2)}) async-start(bf16[128,8,128]{2,1,0:T(8,128)(2,1)} %bitcast.16), calls=%async_computation | async-start | bytes 524288 | tf_op jit(solution)/shard_map/all_to_all | solution.py:349
  28.2 23.0 %copy-start.1 = (bf16[128,2048]{1,0:T(8,128)(2,1)S(1)}, bf16[128,2048]{1,0:T(8,128)(2,1)}, u32[]{:S(2)}) copy-start(bf16[128,2048]{1,0:T(8,128)(2,1)} %get-tuple-element.19.refs_0_) | copy-start | bytes 1572868
  28.2 32.1 %copy-start = (s32[2048,64]{0,1:T(8,128)S(1)}, s32[2048,64]{0,1:T(8,128)}, u32[]{:S(2)}) copy-start(s32[2048,64]{0,1:T(8,128)} %param.9) | copy-start | bytes 1572868
  28.2 32.1 %copy-start.3 = (s32[5]{0:T(128)S(1)}, s32[5]{0:T(128)}, u32[]{:S(2)}) copy-start(s32[5]{0:T(128)} %stack.23.at_ref.refs_10_.refs_7_) | copy-start | bytes 64
  28.2 24.8 %collective-permute-start = (bf16[128,2048]{1,0:T(8,128)(2,1)}, bf16[128,2048]{1,0:T(8,128)(2,1)S(1)}, u32[]{:S(2)}, u32[]{:S(2)}) collective-permute-start(bf16[128,2048]{1,0:T(8,128)(2,1)} %get-tuple-element.20), channel_id=1, source_target_pairs={{0,2},{1,3},{2,0},{3,1},{4,6},{5,7},{6,4},{7,5},{8,10},{9,11},{10,... | collective-permute-start | bytes 1572872 | tf_op jit(solution)/shard_map/ppermute | solution.py:370
  31.7 26.6 %collective-permute-start.2 = (bf16[128,2048]{1,0:T(8,128)(2,1)}, bf16[128,2048]{1,0:T(8,128)(2,1)}, u32[]{:S(2)}, u32[]{:S(2)}) collective-permute-start(bf16[128,2048]{1,0:T(8,128)(2,1)} %get-tuple-element.25), channel_id=1, source_target_pairs={{0,3},{1,0},{2,1},{3,2},{4,7},{5,4},{6,5},{7,6},{8,11},{9,8},{10,9... | collective-permute-start | bytes 1572872 | tf_op jit(solution)/shard_map/ppermute | solution.py:370
  33.9 27.5 %collective-permute-start.1 = (bf16[128,2048]{1,0:T(8,128)(2,1)}, bf16[128,2048]{1,0:T(8,128)(2,1)}, u32[]{:S(2)}, u32[]{:S(2)}) collective-permute-start(bf16[128,2048]{1,0:T(8,128)(2,1)} %get-tuple-element.21), channel_id=1, source_target_pairs={{0,1},{1,2},{2,3},{3,0},{4,5},{5,6},{6,7},{7,4},{8,9},{9,10},{10,1... | collective-permute-start | bytes 1572872 | tf_op jit(solution)/shard_map/ppermute | solution.py:370
  46.7 17.7 %all-to-all-start.1 = ((bf16[4,1024,128]{2,1,0:T(8,128)(2,1)}), bf16[4,1024,128]{2,1,0:T(8,128)(2,1)S(1)}, u32[]{:S(2)}, u32[]{:S(2)}) async-start(bf16[4,1024,128]{2,1,0:T(8,128)(2,1)} %spread.1), calls=%async_computation.1 | async-start | bytes 2097152 | tf_op jit(solution)/shard_map/all_to_all | solution.py:378
  51.2 14.1 %collective-permute-start.3 = (bf16[128,2048]{1,0:T(8,128)(2,1)S(1)}, bf16[128,2048]{1,0:T(8,128)(2,1)}, u32[]{:S(2)}, u32[]{:S(2)}) collective-permute-start(bf16[128,2048]{1,0:T(8,128)(2,1)S(1)} %copy-done.1), channel_id=1, source_target_pairs={{0,8},{8,0},{1,9},{9,1},{2,10},{10,2},{3,11},{11,3},{4,12},{12,4},... | collective-permute-start | bytes 1572872 | tf_op jit(solution)/shard_map/ppermute | solution.py:390
  53.1 12.2 %collective-permute-start.4 = (bf16[128,2048]{1,0:T(8,128)(2,1)S(1)}, bf16[128,2048]{1,0:T(8,128)(2,1)}, u32[]{:S(2)}, u32[]{:S(2)}) collective-permute-start(bf16[128,2048]{1,0:T(8,128)(2,1)S(1)} %collective-permute-done.refs_1_), channel_id=1, source_target_pairs={{0,8},{8,0},{1,9},{9,1},{2,10},{10,2},{3,11},{11,3},{4,12},{12,4},... | collective-permute-start | bytes 1572872 | tf_op jit(solution)/shard_map/ppermute | solution.py:390
  58.4 6.9 %collective-permute-start.6 = (bf16[128,2048]{1,0:T(8,128)(2,1)}, bf16[128,2048]{1,0:T(8,128)(2,1)}, u32[]{:S(2)}, u32[]{:S(2)}) collective-permute-start(bf16[128,2048]{1,0:T(8,128)(2,1)} %collective-permute-done.2.refs_3_), channel_id=1, source_target_pairs={{0,8},{8,0},{1,9},{9,1},{2,10},{10,2},{3,11},{11,3},{4,12},{12,4},... | collective-permute-start | bytes 1572872 | tf_op jit(solution)/shard_map/ppermute | solution.py:390
  61.5 4.1 %collective-permute-start.5 = (bf16[128,2048]{1,0:T(8,128)(2,1)}, bf16[128,2048]{1,0:T(8,128)(2,1)S(1)}, u32[]{:S(2)}, u32[]{:S(2)}) collective-permute-start(bf16[128,2048]{1,0:T(8,128)(2,1)} %collective-permute-done.1.refs_2_), channel_id=1, source_target_pairs={{0,8},{8,0},{1,9},{9,1},{2,10},{10,2},{3,11},{11,3},{4,12},{12,4},... | collective-permute-start | bytes 1572872 | tf_op jit(solution)/shard_map/ppermute | solution.py:390
  99.2 51.9 %copy-start.2 = (f32[64,128]{1,0:T(8,128)S(1)}, f32[64,128]{1,0:T(8,128)}, u32[]{:S(2)}) copy-start(f32[64,128]{1,0:T(8,128)} %get-tuple-element.33.pat_ref) | copy-start | bytes 98308

commit v11 on v10

--- a/solution.py
+++ b/solution.py
@@ -9,10 +9,9 @@
 BF16 = jnp.bfloat16
 NZ, NYL, NC, NYH, NX = 16, 2, 2, 2, 4
 AXES = ("z", "yl", "core", "yh", "x")
-Y = ("yl", "yh")
-ZCX = ("z", "core", "x")
 PLANE = ("yl", "core", "yh", "x")
 D, KVW, TOKENS = 8192, 512, 65536
+FLOPS = 2 * 10**9
 SHIFT = 34
 VMEM = pl.BlockSpec(memory_space=pltpu.VMEM)
 SMEM = pl.BlockSpec(memory_space=pltpu.SMEM)
@@ -186,42 +185,61 @@
             out_ref[z, c * 32 : (c + 1) * 32, :] = piece
 
 
-def spread_kernel(got_ref, out_ref, mid_ref):
-    got = got_ref[...].astype(F32).reshape(32, 4, 8, 128)
-    for q, rows in enumerate(swap_all([got[:, x] for x in range(NX)])):
-        mid_ref[:, q] = rows
-    rows = mid_ref[...].reshape(1024, 128).astype(BF16)
-    for y in range(4):
-        out_ref[y] = rows
-
-
-def decode_kernel(w_ref, high_ref, low_ref):
-    for y in range(4):
+def spread_kernel(got_ref, out_ref):
+    got = got_ref[...].astype(F32).reshape(NZ, 8, 8, 128)
+    for c in range(NC):
+        for x in range(NX):
+            rows = got[:, c * NX + x].reshape(128, 128).astype(BF16)
+            for y in range(4):
+                out_ref[place_in_plane(y // 2, c, y % 2, x)] = rows
+
+
+def decode_kernel(got_ref, high_ref, low_ref, w_ref):
+    for yl in range(NYL):
+        for c in range(NC):
+            for yh in range(NYH):
+                at = [place_in_plane(yl, c, yh, x) for x in range(NX)]
+                parts = [got_ref[i].astype(F32).reshape(NZ, 8, 128) for i in at]
+                for q, sent in enumerate(swap_all(parts)):
+                    size = lax.rsqrt(lax.rsqrt(jnp.abs(sent))) * 2.0**-SHIFT
+                    delta = jnp.where(sent < 0, -size, size)
+                    w_ref[yl, :, c, q, :, yh * 128 : (yh + 1) * 128] = delta
+    for yl in range(NYL):
         for k in range(4):
-            sent = w_ref[y, k * 256 : (k + 1) * 256, :].astype(F32)
-            size = lax.rsqrt(lax.rsqrt(jnp.abs(sent))) * 2.0**-SHIFT
-            delta = jnp.where(sent < 0, -size, size)
+            delta = w_ref[yl, k * 4 : (k + 1) * 4].reshape(256, 256)
             high = delta.astype(BF16)
-            at = (y // 2) * 1024 + k * 256
-            lane = (y % 2) * 128
-            high_ref[at : at + 256, lane : lane + 128] = high
-            low_ref[at : at + 256, lane : lane + 128] = (delta - high.astype(F32)).astype(BF16)
-
-
-def forward_kernel(*refs):
-    own, pair, rest = refs[:NX], refs[NX : 2 * NX], refs[2 * NX :]
-    high_ref, low_ref, at_ref, out_ref, held_ref, sems = rest
+            at = yl * 1024 + k * 256
+            high_ref[at : at + 256, :] = high
+            low_ref[at : at + 256, :] = (delta - high.astype(F32)).astype(BF16)
+
+
+def forward(rows, high_ref, low_ref):
+    part = jnp.dot(rows, high_ref[...], preferred_element_type=F32)
+    part += jnp.dot(rows, low_ref[...], preferred_element_type=F32)
+    return part.astype(BF16)
+
+
+def forward_own_kernel(*refs):
+    own, (high_ref, low_ref, at_ref, out_ref) = refs[:NX], refs[NX:]
+    for i in range(NX):
+        out_ref[(at_ref[0] + BACK[i]) % NX] = forward(own[i][...], high_ref, low_ref)
+
+
+def forward_pair_kernel(*refs):
+    pair, rest = refs[:NX], refs[NX:]
+    part_ref, high_ref, low_ref, at_ref, out_ref, held_ref, sems = rest[NX - 1 :]
     loads = [pltpu.make_async_copy(pair[i], held_ref.at[i], sems.at[i]) for i in range(NX)]
     for load in loads:
         load.start()
-    for row in (0, 128):
-        for i in range(NX):
-            if row:
-                loads[i].wait()
-            rows = held_ref[i] if row else own[i][...]
-            part = jnp.dot(rows, high_ref[...], preferred_element_type=F32)
-            part += jnp.dot(rows, low_ref[...], preferred_element_type=F32)
-            out_ref[(at_ref[0] + BACK[i]) % NX, row : row + 128] = part.astype(BF16)
+    for x in range(NX):
+        out_ref[x, :128] = part_ref[x]
+    for i in range(NX):
+        loads[i].wait()
+        out_ref[(at_ref[0] + BACK[i]) % NX, 128:] = forward(held_ref[i], high_ref, low_ref)
+
+
+def mark_kernel(piece_hbm, out_ref):
+    out_ref[...] = jnp.zeros_like(out_ref)
 
 
 def thirds(value, rows):
@@ -346,7 +364,7 @@
         grant=60,
         name="pack",
     )
-    got_w = lax.all_to_all(packed.reshape(128, 8, 128), ZCX, 0, 0, tiled=True)
+    got_w = lax.all_to_all(packed, "z", 0, 0, tiled=True)
 
     split = call(
         norm_kernel,
@@ -368,14 +386,8 @@
         name="norm",
     )
     own = [split[0]] + [lax.ppermute(split[i], "x", ring(STEP[i])) for i in range(1, NX)]
-    rows_w = call(
-        spread_kernel,
-        shape((4, 1024, 128), BF16),
-        got_w.reshape(1024, 128),
-        scratch=[pltpu.VMEM((32, 4, 8, 128), F32)],
-        name="spread",
-    )
-    all_w = lax.all_to_all(rows_w, Y, 0, 0, tiled=True)
+    rows_w = call(spread_kernel, shape((32, 128, 128), BF16), got_w, name="spread")
+    all_w = lax.all_to_all(rows_w, PLANE, 0, 0, tiled=True)
 
     late, _ = lax.optimization_barrier((patterns, rows_w))
     own_pat = call(
@@ -387,23 +399,47 @@
         name="choose",
     )
     own[2], own_pat = lax.optimization_barrier((own[2], own_pat))
+    marks = []
+    for i in range(1, NX):
+        mark = call(
+            mark_kernel, shape((8, 128), F32), own[i], far=(0,), flops=FLOPS, name="mark"
+        )
+        own[i], mark = lax.optimization_barrier((own[i], mark))
+        marks.append(mark)
     pair = [lax.ppermute(piece, "core", [(0, 1), (1, 0)]) for piece in own]
 
-    high, low = call(decode_kernel, (shape((2048, 256), BF16),) * 2, all_w, name="decode")
-
+
+    high, low = call(
+        decode_kernel,
+        (shape((2048, 256), BF16),) * 2,
+        all_w,
+        scratch=[pltpu.VMEM((NYL, NZ, NC, 4, 8, 256), F32)],
+        name="decode",
+    )
     flops = 2 * 1024 * 2048 * 256
-    part, held = call(
-        forward_kernel,
-        (shape((NX, 256, 256), BF16), shape((NX, 128, 2048), BF16)),
+    part = call(
+        forward_own_kernel,
+        shape((NX, 128, 256), BF16),
         *own,
-        *pair,
         high,
         low,
         at,
+        flops=flops,
+        name="forward_own",
+    )
+    part, held = call(
+        forward_pair_kernel,
+        (shape((NX, 256, 256), BF16), shape((NX, 128, 2048), BF16)),
+        *pair,
+        *marks,
+        part,
+        high,
+        low,
+        at,
         scratch=[pltpu.SemaphoreType.DMA((NX,))],
-        flops=2 * flops,
-        far=range(NX, 2 * NX),
-        name="forward",
+        flops=flops,
+        far=range(NX),
+        name="forward_pair",
     )
     got_part = lax.all_to_all(part, "x", 0, 0, tiled=True)
     slope, loss_part = call(

time: 154 us -> 155 us (level)
    all_to_all x2, waiting for transfers between devices: 7.12 us -> 9.1 us  [the longest x1 6.21 us: shards(): all_w = lax.all_to_all(rows_w, PLANE, 0, 0, tiled=True)]
    pallas_call x10 -> x14, Pallas kernels: 21.7 us -> 22.4 us  [call(): pl.pallas_call(kernel, out_shape=out_shape, in_specs=specs, out_specs=jax...]
  transfers between devices with their start and end apart: 9 -> 9, of which waited for: 4 -> 3; matrix products, arithmetic and copies ran while one was open for 0% -> 0% of each run, Pallas kernels for 5% -> 7%
where the time goes in v11:
time: 155 us; the launch traced here: 153 us
  blocking collectives  74.9 us (48%)
  starting transfers between devices  42 us (27%)
  Pallas kernels  22.4 us (14%)
  waiting for transfers between devices  11.3 us (7%)
    all_to_all x1, blocking collectives, shards(): got_sum = lax.all_to_all(packed_term, 'z', 0, 0, tiled=True)  28 us
    all_to_all x1, blocking collectives, shards(): got_term = lax.all_to_all(term, PLANE, 0, 0, tiled=True)  22.9 us
    pallas_call x14, Pallas kernels, call(): pl.pallas_call(kernel, out_shape=out_shape, in_specs=specs, out_specs=jax...  22.4 us
    all_to_all x1, starting transfers between devices, shards(): got_w = lax.all_to_all(packed, 'z', 0, 0, tiled=True)  15.2 us
    all_to_all x1, blocking collectives, shards(): got_part = lax.all_to_all(part, 'x', 0, 0, tiled=True)  13 us
    all_to_all x1, blocking collectives, shards(): slopes = lax.all_to_all(slope, 'x', 0, 0, tiled=True)  11 us
    ppermute x3, starting transfers between devices, shards(): lax.ppermute(split[i], 'x', ring(STEP[i]))  10.5 us
    ppermute x4, starting transfers between devices, shards(): pair = [lax.ppermute(piece, 'core', [(0, 1), (1, 0)]) for piece in own]  8.76 us
  transfers between devices with their start and end apart: 9, of which 3 were waited for; matrix products, arithmetic and copies ran while one was open for 0% of the time, Pallas kernels for 7%

profile of v11, /device:TPU:6, one launch (start us, length us, event | category | flops | bytes accessed | tf_op | source)
XLA Modules:
  0.0 153.0 jit_solution(10423750828144491362)
XLA Ops:
  0.6 0.6 stack.23.at_ref.refs_6_.refs_10_.refs_7_
  1.3 2.6 %pack.1 = (bf16[16,64,128]{2,1,0:T(8,128)(2,1)}, f32[64,128]{1,0:T(8,128)}) custom-call(bf16[64,128]{1,0:T(8,128)(2,1)} %bitcast.13, bf16[64,128]{1,0:T(8,128)(2,1)} %bitcast.14, s32[64,2048]{1,0:T(8,128)} %bitcast.11, s32[5]{0:T(128)} %stack.23.at_ref.refs_6_.refs_10_.refs_7_), custom_call_target="tpu_custom_call" | custom-call | bytes 851988 | tf_op jit(solution)/shard_map/pack/pallas_call | solution.py:29
  3.8 15.2 %all-to-all-start = ((bf16[16,64,128]{2,1,0:T(8,128)(2,1)}), bf16[16,64,128]{2,1,0:T(8,128)(2,1)S(1)}, u32[]{:S(2)}, u32[]{:S(2)}) async-start(bf16[16,64,128]{2,1,0:T(8,128)(2,1)} %get-tuple-element.29), calls=%async_computation | async-start | bytes 524288 | tf_op jit(solution)/shard_map/all_to_all | solution.py:367
  19.0 4.9 %norm.1 = (bf16[128,2048]{1,0:T(8,128)(2,1)}, bf16[128,2048]{1,0:T(8,128)(2,1)}, bf16[128,2048]{1,0:T(8,128)(2,1)}, bf16[128,2048]{1,0:T(8,128)(2,1)}) custom-call(bf16[128,8192]{1,0:T(8,128)(2,1)} %x_hbm.1, bf16[64,128]{1,0:T(8,128)(2,1)} %bitcast.16, s32[5]{0:T(128)} %stack.23.at_ref.refs_6_.refs_10_.refs_7_), custom_call_target="tpu_custom_call" | custom-call | flops 1073741824 | bytes 4210708 | tf_op jit(solution)/shard_map/norm/pallas_call | solution.py:29
  24.0 0.0 copy-start
  24.0 3.5 %collective-permute-start = (bf16[128,2048]{1,0:T(8,128)(2,1)}, bf16[128,2048]{1,0:T(8,128)(2,1)S(1)}, u32[]{:S(2)}, u32[]{:S(2)}) collective-permute-start(bf16[128,2048]{1,0:T(8,128)(2,1)} %get-tuple-element.26), channel_id=1, source_target_pairs={{0,2},{1,3},{2,0},{3,1},{4,6},{5,7},{6,4},{7,5},{8,10},{9,11},{10,... | collective-permute-start | bytes 1572872 | tf_op jit(solution)/shard_map/ppermute | solution.py:388
  27.4 1.9 %collective-permute-start.2 = (bf16[128,2048]{1,0:T(8,128)(2,1)}, bf16[128,2048]{1,0:T(8,128)(2,1)S(1)}, u32[]{:S(2)}, u32[]{:S(2)}) collective-permute-start(bf16[128,2048]{1,0:T(8,128)(2,1)} %get-tuple-element.33), channel_id=1, source_target_pairs={{0,3},{1,0},{2,1},{3,2},{4,7},{5,4},{6,5},{7,6},{8,11},{9,8},{10,9... | collective-permute-start | bytes 1572872 | tf_op jit(solution)/shard_map/ppermute | solution.py:388
  29.4 5.1 %collective-permute-start.1 = (bf16[128,2048]{1,0:T(8,128)(2,1)}, bf16[128,2048]{1,0:T(8,128)(2,1)S(1)}, u32[]{:S(2)}, u32[]{:S(2)}) collective-permute-start(bf16[128,2048]{1,0:T(8,128)(2,1)} %get-tuple-element.28), channel_id=1, source_target_pairs={{0,1},{1,2},{2,3},{3,0},{4,5},{5,6},{6,7},{7,4},{8,9},{9,10},{10,1... | collective-permute-start | bytes 1572872 | tf_op jit(solution)/shard_map/ppermute | solution.py:388
  34.5 2.9 %all-to-all-done.got_ref = bf16[16,64,128]{2,1,0:T(8,128)(2,1)S(1)} async-done(((bf16[16,64,128]{2,1,0:T(8,128)(2,1)}), bf16[16,64,128]{2,1,0:T(8,128)(2,1)S(1)}, u32[]{:S(2)}, u32[]{:S(2)}) %all-to-all-start) | async-done | bytes 262176 | tf_op jit(solution)/shard_map/all_to_all | solution.py:367
  37.4 1.1 spread.1
  38.5 7.6 %all-to-all-start.1 = ((bf16[32,128,128]{2,1,0:T(8,128)(2,1)}), bf16[32,128,128]{2,1,0:T(8,128)(2,1)S(1)}, u32[]{:S(2)}, u32[]{:S(2)}) async-start(bf16[32,128,128]{2,1,0:T(8,128)(2,1)} %spread.1), calls=%async_computation.1 | async-start | bytes 2097152 | tf_op jit(solution)/shard_map/all_to_all | solution.py:390
  46.1 0.0 copy-done
  46.1 2.1 %collective-permute-start.3 = (bf16[128,2048]{1,0:T(8,128)(2,1)S(1)}, bf16[128,2048]{1,0:T(8,128)(2,1)}, u32[]{:S(2)}, u32[]{:S(2)}) collective-permute-start(bf16[128,2048]{1,0:T(8,128)(2,1)S(1)} %copy-done), channel_id=1, source_target_pairs={{0,8},{8,0},{1,9},{9,1},{2,10},{10,2},{3,11},{11,3},{4,12},{12,4},... | collective-permute-start | bytes 1572872 | tf_op jit(solution)/shard_map/ppermute | solution.py:409
  48.2 0.0 collective-permute-done.piece_hbm.refs_1_
  48.2 0.0 copy-start.1
  48.2 0.0 copy-start.5
  48.2 2.4 %collective-permute-start.4 = (bf16[128,2048]{1,0:T(8,128)(2,1)S(1)}, bf16[128,2048]{1,0:T(8,128)(2,1)}, u32[]{:S(2)}, u32[]{:S(2)}) collective-permute-start(bf16[128,2048]{1,0:T(8,128)(2,1)S(1)} %collective-permute-done.piece_hbm.refs_1_), channel_id=1, source_target_pairs={{0,8},{8,0},{1,9},{9,1},{2,10},{10,2},{3,11},{11,3},{4,12},{12,4},... | collective-permute-start | bytes 1572872 | tf_op jit(solution)/shard_map/ppermute | solution.py:409
  50.6 2.1 %collective-permute-done.2.piece_hbm.refs_3_ = bf16[128,2048]{1,0:T(8,128)(2,1)S(1)} collective-permute-done((bf16[128,2048]{1,0:T(8,128)(2,1)}, bf16[128,2048]{1,0:T(8,128)(2,1)S(1)}, u32[]{:S(2)}, u32[]{:S(2)}) %collective-permute-start.2) | collective-permute-done | bytes 524320 | tf_op jit(solution)/shard_map/ppermute | solution.py:388
  52.8 1.9 %collective-permute-start.6 = (bf16[128,2048]{1,0:T(8,128)(2,1)S(1)}, bf16[128,2048]{1,0:T(8,128)(2,1)}, u32[]{:S(2)}, u32[]{:S(2)}) collective-permute-start(bf16[128,2048]{1,0:T(8,128)(2,1)S(1)} %collective-permute-done.2.piece_hbm.refs_3_), channel_id=1, source_target_pairs={{0,8},{8,0},{1,9},{9,1},{2,10},{10,2},{3,11},{11,3},{4,12},{12,4},... | collective-permute-start | bytes 1572872 | tf_op jit(solution)/shard_map/ppermute | solution.py:409
  54.7 0.0 copy-done.1
  54.7 0.0 copy-done.5
  54.7 1.1 choose.1.pat_ref
  55.8 0.0 copy-start.2
  55.9 0.8 copy-done.2
  56.6 0.0 collective-permute-done.1.piece_hbm.refs_2_
  56.6 2.4 %collective-permute-start.5 = (bf16[128,2048]{1,0:T(8,128)(2,1)S(1)}, bf16[128,2048]{1,0:T(8,128)(2,1)}, u32[]{:S(2)}, u32[]{:S(2)}) collective-permute-start(bf16[128,2048]{1,0:T(8,128)(2,1)S(1)} %collective-permute-done.1.piece_hbm.refs_2_), channel_id=1, source_target_pairs={{0,8},{8,0},{1,9},{9,1},{2,10},{10,2},{3,11},{11,3},{4,12},{12,4},... | collective-permute-start | bytes 1572872 | tf_op jit(solution)/shard_map/ppermute | solution.py:409
  59.0 6.2 %all-to-all-done.1.got_ref = bf16[32,128,128]{2,1,0:T(8,128)(2,1)S(1)} async-done(((bf16[32,128,128]{2,1,0:T(8,128)(2,1)}), bf16[32,128,128]{2,1,0:T(8,128)(2,1)S(1)}, u32[]{:S(2)}, u32[]{:S(2)}) %all-to-all-start.1) | async-done | bytes 1048608 | tf_op jit(solution)/shard_map/all_to_all | solution.py:390
  65.3 1.5 decode.1
  66.7 1.8 %forward_own.1.refs_7_ = bf16[4,128,256]{2,1,0:T(8,128)(2,1)S(1)} custom-call(bf16[128,2048]{1,0:T(8,128)(2,1)S(1)} %copy-done, bf16[128,2048]{1,0:T(8,128)(2,1)S(1)} %collective-permute-done.piece_hbm.refs_1_, bf16[128,2048]{1,0:T(8,128)(2,1)S(1)} %collective-permute-done.1.piece_hbm.refs_2_, ...), custom_call_target="tpu_custom_call" | custom-call | flops 1073741824 | bytes 4456468 | tf_op jit(solution)/shard_map/forward_own/pallas_call | solution.py:29
  68.6 0.0 collective-permute-done.3.refs_0_
  68.6 0.0 collective-permute-done.4.refs_1_
  68.6 0.0 collective-permute-done.6.refs_3_
  68.6 0.0 collective-permute-done.5.refs_2_
  68.6 4.4 %forward_pair.1 = (bf16[4,256,256]{2,1,0:T(8,128)(2,1)S(1)}, bf16[4,128,2048]{2,1,0:T(8,128)(2,1)S(1)}) custom-call(bf16[128,2048]{1,0:T(8,128)(2,1)} %collective-permute-done.3.refs_0_, bf16[128,2048]{1,0:T(8,128)(2,1)} %collective-permute-done.4.refs_1_, bf16[128,2048]{1,0:T(8,128)(2,1)} %collective-permute-done.5.refs_2_, ...), custom_call_target="tpu_custom_call" | custom-call | flops 1073741824 | bytes 7090196 | tf_op jit(solution)/shard_map/forward_pair/pallas_call | solution.py:29
  73.0 13.0 %all_to_all.30.part_ref = bf16[4,256,256]{2,1,0:T(8,128)(2,1)S(1)} all-to-all(bf16[4,256,256]{2,1,0:T(8,128)(2,1)S(1)} %get-tuple-element.41), channel_id=1, replica_groups=mesh['z'=16,'yl'=2,'core'=2,'yh'=2,'x'=4] {'x'}, dimensions={0} | all-to-all | bytes 1048576 | tf_op jit(solution)/shard_map/all_to_all | solution.py:444
  86.0 0.1 slope.1
  86.1 11.0 %all_to_all.31.refs_5_ = bf16[4,256,256]{2,1,0:T(8,128)(2,1)S(1)} all-to-all(bf16[4,256,256]{2,1,0:T(8,128)(2,1)S(1)} %get-tuple-element.42), channel_id=1, replica_groups=mesh['z'=16,'yl'=2,'core'=2,'yh'=2,'x'=4] {'x'}, dimensions={0} | all-to-all | bytes 1048576 | tf_op jit(solution)/shard_map/all_to_all | solution.py:448
  97.1 2.7 %grad.1 = bf16[32,144,128]{2,1,0:T(8,128)(2,1)S(1)} custom-call(bf16[128,2048]{1,0:T(8,128)(2,1)S(1)} %copy-done, bf16[128,2048]{1,0:T(8,128)(2,1)S(1)} %collective-permute-done.piece_hbm.refs_1_, bf16[128,2048]{1,0:T(8,128)(2,1)S(1)} %collective-permute-done.1.piece_hbm.refs_2_, bf16[128,2048]{1,0:T(8,128)(2,1)S(1)} %collective-permute-done.2.piece_hbm.refs_3_, ...), custom_call_target="tpu_custom_call" | custom-call | flops 1073741824 | bytes 5898772 | tf_op jit(solution)/shard_map/grad/pallas_call | solution.py:29
  99.8 0.0 copy-start.3
  99.8 0.0 copy-start.4
  99.9 22.9 %all_to_all.32.got_ref = bf16[32,144,128]{2,1,0:T(8,128)(2,1)S(1)} all-to-all(bf16[32,144,128]{2,1,0:T(8,128)(2,1)S(1)} %grad.1), channel_id=1, replica_groups=mesh['z'=16,'yl'=2,'core'=2,'yh'=2,'x'=4] {'yl','core','yh','x'}, dimensions={0} | all-to-all | bytes 2359296 | tf_op jit(solution)/shard_map/all_to_all | solution.py:462
  122.7 0.0 copy-done.3
  122.7 1.3 gather.1
  124.1 28.0 %all_to_all.33.got_ref = bf16[16,48,128]{2,1,0:T(8,128)(2,1)S(1)} all-to-all(bf16[16,48,128]{2,1,0:T(8,128)(2,1)S(1)} %gather.1), channel_id=1, replica_groups=mesh['z'=16,'yl'=2,'core'=2,'yh'=2,'x'=4] {'z'}, dimensions={0} | all-to-all | bytes 393216 | tf_op jit(solution)/shard_map/all_to_all | solution.py:471
  152.1 0.0 copy-done.4
  152.1 0.9 final.1
  (3 shorter events, 0.0 us)
Async XLA Ops:
  3.8 33.6 %all-to-all-start = ((bf16[16,64,128]{2,1,0:T(8,128)(2,1)}), bf16[16,64,128]{2,1,0:T(8,128)(2,1)S(1)}, u32[]{:S(2)}, u32[]{:S(2)}) async-start(bf16[16,64,128]{2,1,0:T(8,128)(2,1)} %get-tuple-element.29), calls=%async_computation | async-start | bytes 524288 | tf_op jit(solution)/shard_map/all_to_all | solution.py:367
  24.0 22.1 %copy-start = (bf16[128,2048]{1,0:T(8,128)(2,1)S(1)}, bf16[128,2048]{1,0:T(8,128)(2,1)}, u32[]{:S(2)}) copy-start(bf16[128,2048]{1,0:T(8,128)(2,1)} %get-tuple-element.25.refs_0_) | copy-start | bytes 1572868
  24.0 24.2 %collective-permute-start = (bf16[128,2048]{1,0:T(8,128)(2,1)}, bf16[128,2048]{1,0:T(8,128)(2,1)S(1)}, u32[]{:S(2)}, u32[]{:S(2)}) collective-permute-start(bf16[128,2048]{1,0:T(8,128)(2,1)} %get-tuple-element.26), channel_id=1, source_target_pairs={{0,2},{1,3},{2,0},{3,1},{4,6},{5,7},{6,4},{7,5},{8,10},{9,11},{10,... | collective-permute-start | bytes 1572872 | tf_op jit(solution)/shard_map/ppermute | solution.py:388
  27.4 25.3 %collective-permute-start.2 = (bf16[128,2048]{1,0:T(8,128)(2,1)}, bf16[128,2048]{1,0:T(8,128)(2,1)S(1)}, u32[]{:S(2)}, u32[]{:S(2)}) collective-permute-start(bf16[128,2048]{1,0:T(8,128)(2,1)} %get-tuple-element.33), channel_id=1, source_target_pairs={{0,3},{1,0},{2,1},{3,2},{4,7},{5,4},{6,5},{7,6},{8,11},{9,8},{10,9... | collective-permute-start | bytes 1572872 | tf_op jit(solution)/shard_map/ppermute | solution.py:388
  29.4 27.3 %collective-permute-start.1 = (bf16[128,2048]{1,0:T(8,128)(2,1)}, bf16[128,2048]{1,0:T(8,128)(2,1)S(1)}, u32[]{:S(2)}, u32[]{:S(2)}) collective-permute-start(bf16[128,2048]{1,0:T(8,128)(2,1)} %get-tuple-element.28), channel_id=1, source_target_pairs={{0,1},{1,2},{2,3},{3,0},{4,5},{5,6},{6,7},{7,4},{8,9},{9,10},{10,1... | collective-permute-start | bytes 1572872 | tf_op jit(solution)/shard_map/ppermute | solution.py:388
  38.5 26.7 %all-to-all-start.1 = ((bf16[32,128,128]{2,1,0:T(8,128)(2,1)}), bf16[32,128,128]{2,1,0:T(8,128)(2,1)S(1)}, u32[]{:S(2)}, u32[]{:S(2)}) async-start(bf16[32,128,128]{2,1,0:T(8,128)(2,1)} %spread.1), calls=%async_computation.1 | async-start | bytes 2097152 | tf_op jit(solution)/shard_map/all_to_all | solution.py:390
  46.1 22.4 %collective-permute-start.3 = (bf16[128,2048]{1,0:T(8,128)(2,1)S(1)}, bf16[128,2048]{1,0:T(8,128)(2,1)}, u32[]{:S(2)}, u32[]{:S(2)}) collective-permute-start(bf16[128,2048]{1,0:T(8,128)(2,1)S(1)} %copy-done), channel_id=1, source_target_pairs={{0,8},{8,0},{1,9},{9,1},{2,10},{10,2},{3,11},{11,3},{4,12},{12,4},... | collective-permute-start | bytes 1572872 | tf_op jit(solution)/shard_map/ppermute | solution.py:409
  48.2 6.5 %copy-start.1 = (s32[2048,64]{0,1:T(8,128)S(1)}, s32[2048,64]{0,1:T(8,128)}, u32[]{:S(2)}) copy-start(s32[2048,64]{0,1:T(8,128)} %param.9) | copy-start | bytes 1572868
  48.2 6.5 %copy-start.5 = (s32[5]{0:T(128)S(1)}, s32[5]{0:T(128)}, u32[]{:S(2)}) copy-start(s32[5]{0:T(128)} %stack.23.at_ref.refs_6_.refs_10_.refs_7_) | copy-start | bytes 64
  48.2 20.3 %collective-permute-start.4 = (bf16[128,2048]{1,0:T(8,128)(2,1)S(1)}, bf16[128,2048]{1,0:T(8,128)(2,1)}, u32[]{:S(2)}, u32[]{:S(2)}) collective-permute-start(bf16[128,2048]{1,0:T(8,128)(2,1)S(1)} %collective-permute-done.piece_hbm.refs_1_), channel_id=1, source_target_pairs={{0,8},{8,0},{1,9},{9,1},{2,10},{10,2},{3,11},{11,3},{4,12},{12,4},... | collective-permute-start | bytes 1572872 | tf_op jit(solution)/shard_map/ppermute | solution.py:409
  52.8 15.8 %collective-permute-start.6 = (bf16[128,2048]{1,0:T(8,128)(2,1)S(1)}, bf16[128,2048]{1,0:T(8,128)(2,1)}, u32[]{:S(2)}, u32[]{:S(2)}) collective-permute-start(bf16[128,2048]{1,0:T(8,128)(2,1)S(1)} %collective-permute-done.2.piece_hbm.refs_3_), channel_id=1, source_target_pairs={{0,8},{8,0},{1,9},{9,1},{2,10},{10,2},{3,11},{11,3},{4,12},{12,4},... | collective-permute-start | bytes 1572872 | tf_op jit(solution)/shard_map/ppermute | solution.py:409
  55.8 0.8 copy-start.2
  56.6 11.9 %collective-permute-start.5 = (bf16[128,2048]{1,0:T(8,128)(2,1)S(1)}, bf16[128,2048]{1,0:T(8,128)(2,1)}, u32[]{:S(2)}, u32[]{:S(2)}) collective-permute-start(bf16[128,2048]{1,0:T(8,128)(2,1)S(1)} %collective-permute-done.1.piece_hbm.refs_2_), channel_id=1, source_target_pairs={{0,8},{8,0},{1,9},{9,1},{2,10},{10,2},{3,11},{11,3},{4,12},{12,4},... | collective-permute-start | bytes 1572872 | tf_op jit(solution)/shard_map/ppermute | solution.py:409
  99.8 22.9 %copy-start.3 = (f32[2,16,4,8,128]{4,3,2,1,0:T(8,128)S(1)}, f32[2,16,4,8,128]{4,3,2,1,0:T(8,128)}, u32[]{:S(2)}) copy-start(f32[2,16,4,8,128]{4,3,2,1,0:T(8,128)} %copy-done.2) | copy-start | bytes 1572868
  99.8 52.3 %copy-start.4 = (f32[64,128]{1,0:T(8,128)S(1)}, f32[64,128]{1,0:T(8,128)}, u32[]{:S(2)}) copy-start(f32[64,128]{1,0:T(8,128)} %get-tuple-element.45.pat_ref) | copy-start | bytes 98308

commit v12 on v11

--- a/solution.py
+++ b/solution.py
@@ -11,12 +11,13 @@
 AXES = ("z", "yl", "core", "yh", "x")
 PLANE = ("yl", "core", "yh", "x")
 D, KVW, TOKENS = 8192, 512, 65536
-FLOPS = 2 * 10**9
+FLOPS = (0, 3 * 10**9, 2 * 10**9, 0)
 SHIFT = 34
 VMEM = pl.BlockSpec(memory_space=pltpu.VMEM)
 SMEM = pl.BlockSpec(memory_space=pltpu.SMEM)
 STEP = (0, 2, 1, 3)
 BACK = (0, 2, 3, 1)
+SOON, LAST = (0, 1, 2), 3
 
 
 def call(kernel, out_shape, *args, scratch=(), flops=0, name=None, far=(), out_far=False, grant=24):
@@ -141,11 +142,17 @@
     pats = pat_ref[...].astype(F32).astype(BF16)
     col = lax.broadcasted_iota(jnp.int32, (64, 128), 0)
     lane = lax.broadcasted_iota(jnp.int32, (64, 128), 1)
+    group = lane_group((32, 128))
     for c in range(NC):
         pick = jnp.where(col - c * 32 == lane % 32, 1.0, 0.0).astype(BF16)
         chosen = lax.dot_general(pats, pick, (((0,), (0,)), ((), ())), preferred_element_type=F32)
         pick_ref[...] = chosen.reshape(NZ, NYL, NC, NX, 8, 128)
-        out_ref[c] = pick_ref[:, at_ref[2], at_ref[1]]
+        for x in range(NX):
+            rows = pick_ref[:, at_ref[2], at_ref[1], x].reshape(4, 32, 128)
+            total = rows[0]
+            for b in range(1, 4):
+                total = jnp.where(group == b, rows[b], total)
+            out_ref[c * NX + x] = total.astype(BF16)
 
 
 def pack_kernel(teacher_hbm, student_hbm, pat_hbm, at_ref, out_ref, rows_ref, *scratch):
@@ -185,25 +192,30 @@
             out_ref[z, c * 32 : (c + 1) * 32, :] = piece
 
 
-def spread_kernel(got_ref, out_ref):
+def spread_kernel(got_ref, pat_ref, out_ref):
     got = got_ref[...].astype(F32).reshape(NZ, 8, 8, 128)
     for c in range(NC):
         for x in range(NX):
             rows = got[:, c * NX + x].reshape(128, 128).astype(BF16)
             for y in range(4):
-                out_ref[place_in_plane(y // 2, c, y % 2, x)] = rows
-
-
-def decode_kernel(got_ref, high_ref, low_ref, w_ref):
+                at = place_in_plane(y // 2, c, y % 2, x)
+                out_ref[at, :128, :] = rows
+                out_ref[at, 128:, :] = pat_ref[c * NX + x]
+
+
+def decode_kernel(got_ref, high_ref, low_ref, pat_ref, w_ref):
     for yl in range(NYL):
         for c in range(NC):
             for yh in range(NYH):
                 at = [place_in_plane(yl, c, yh, x) for x in range(NX)]
-                parts = [got_ref[i].astype(F32).reshape(NZ, 8, 128) for i in at]
+                parts = [got_ref[i, :128, :].astype(F32).reshape(NZ, 8, 128) for i in at]
                 for q, sent in enumerate(swap_all(parts)):
                     size = lax.rsqrt(lax.rsqrt(jnp.abs(sent))) * 2.0**-SHIFT
                     delta = jnp.where(sent < 0, -size, size)
                     w_ref[yl, :, c, q, :, yh * 128 : (yh + 1) * 128] = delta
+                parts = [got_ref[i, 128:, :].astype(F32) for i in at]
+                for b, rows in enumerate(swap_all(parts)):
+                    pat_ref[yl * NYH + yh, b * 4 : (b + 1) * 4, c] = rows.reshape(4, 8, 128)
     for yl in range(NYL):
         for k in range(4):
             delta = w_ref[yl, k * 4 : (k + 1) * 4].reshape(256, 256)
@@ -219,23 +231,28 @@
     return part.astype(BF16)
 
 
-def forward_own_kernel(*refs):
-    own, (high_ref, low_ref, at_ref, out_ref) = refs[:NX], refs[NX:]
-    for i in range(NX):
-        out_ref[(at_ref[0] + BACK[i]) % NX] = forward(own[i][...], high_ref, low_ref)
-
-
-def forward_pair_kernel(*refs):
-    pair, rest = refs[:NX], refs[NX:]
-    part_ref, high_ref, low_ref, at_ref, out_ref, held_ref, sems = rest[NX - 1 :]
-    loads = [pltpu.make_async_copy(pair[i], held_ref.at[i], sems.at[i]) for i in range(NX)]
+def forward_most_kernel(*refs):
+    own, pair, rest = refs[:NX], refs[NX : NX + 3], refs[NX + 3 :]
+    high_ref, low_ref, at_ref, out_ref, held_ref, sems = rest
+    loads = [pltpu.make_async_copy(pair[i], held_ref.at[i], sems.at[i]) for i in range(3)]
     for load in loads:
         load.start()
-    for x in range(NX):
-        out_ref[x, :128] = part_ref[x]
     for i in range(NX):
+        out_ref[(at_ref[0] + BACK[i]) % NX, :128] = forward(own[i][...], high_ref, low_ref)
+    for i in range(3):
         loads[i].wait()
-        out_ref[(at_ref[0] + BACK[i]) % NX, 128:] = forward(held_ref[i], high_ref, low_ref)
+        x = (at_ref[0] + BACK[SOON[i]]) % NX
+        out_ref[x, 128:] = forward(held_ref[i], high_ref, low_ref)
+    out_ref[(at_ref[0] + BACK[LAST]) % NX, 128:] = jnp.zeros((128, 256), BF16)
+
+
+def forward_last_kernel(pair_hbm, part_ref, high_ref, low_ref, at_ref, *rest):
+    out_ref, held_ref, sem = rest[NX - 1 :]
+    load = pltpu.make_async_copy(pair_hbm, held_ref, sem)
+    load.start()
+    out_ref[...] = part_ref[...]
+    load.wait()
+    out_ref[(at_ref[0] + BACK[LAST]) % NX, 128:] = forward(held_ref[...], high_ref, low_ref)
 
 
 def mark_kernel(piece_hbm, out_ref):
@@ -262,8 +279,8 @@
 
 
 def grad_kernel(*refs):
-    own, (held_ref, *rest) = refs[:NX], refs[NX:]
-    slope_ref, loss_ref, at_ref, out_ref, s_ref, term_ref = rest
+    own, (soon_ref, last_ref, *rest) = refs[:NX], refs[NX:]
+    pat_ref, slope_ref, loss_ref, at_ref, out_ref, s_ref, term_ref = rest
     contract = (((0,), (0,)), ((), ()))
     for i in range(NX):
         x = (at_ref[0] + BACK[i]) % NX
@@ -272,7 +289,9 @@
     for k in range(8):
         at = k * 256
         rows = [ref[:, at : at + 256] for ref in own]
-        rows += [held_ref[i, :, at : at + 256] for i in range(NX)]
+        pair = [soon_ref[i, :, at : at + 256] for i in range(3)]
+        pair.insert(LAST, last_ref[:, at : at + 256])
+        rows += pair
         rows = jnp.concatenate(rows, axis=0)
         term = lax.dot_general(rows, s_ref[...], contract, preferred_element_type=F32)
         for yh in range(2):
@@ -281,36 +300,45 @@
             ].reshape(8, 4, 8, 128)
     loss = thirds(loss_ref[...], 16).astype(BF16)
     for y in range(4):
-        term = term_ref[y].reshape(NZ, NC, 4, 8, 128)
+        which = kept_rows(pat_ref[y].reshape(32, 8, 128))
+        kept = [jnp.zeros((32, 8, 128), F32) for _ in which]
+        for k in range(4):
+            for i in range(2):
+                kept[i] += jnp.where(which[i] == k, term_ref[y, :, k], 0.0)
+        kept = [part.reshape(2, 8, NC, 8, 128) for part in kept]
         for c in range(NC):
-            for x, rows in enumerate(swap_all([term[:, c, q] for q in range(4)])):
+            parts = [kept[i][half, :, c] for half in range(2) for i in range(2)]
+            for x, rows in enumerate(swap_all(parts)):
                 at = place_in_plane(y // 2, c, y % 2, x)
-                out_ref[at, :128, :] = rows.reshape(128, 128).astype(BF16)
-                out_ref[at, 128:, :] = loss
-
-
-def gather_kernel(got_ref, pat_ref, out_ref, mid_ref):
-    loss = got_ref[0, 128:, :].astype(F32)
+                out_ref[at, :64, :] = rows.reshape(64, 128).astype(BF16)
+                out_ref[at, 64:, :] = loss
+
+
+def gather_kernel(got_ref, out_ref, mid_ref):
+    loss = got_ref[0, 64:, :].astype(F32)
     for i in range(1, 32):
-        loss = loss + got_ref[i, 128:, :].astype(F32)
+        loss = loss + got_ref[i, 64:, :].astype(F32)
     loss = jnp.sum(jnp.sum(loss, axis=0, keepdims=True), axis=1, keepdims=True)
     loss = thirds(jnp.broadcast_to(loss, (1, 128)), 16)
     lane = lax.broadcasted_iota(jnp.int32, (16, 128), 1)
     mid_ref[:, 32:, :] = jnp.broadcast_to(jnp.where(lane == 0, loss, 0.0), (NZ, 16, 128))
-    group = lane_group((NZ, 8, 128))
+    group = lane_group((8, 8, 128))
     for x in range(NX):
-        rows = jnp.zeros((NZ, 8, 128), F32)
+        sums = []
         for c in range(NC):
-            total = jnp.zeros((128, 128), F32)
+            total = jnp.zeros((64, 128), F32)
             for y in range(4):
-                total += got_ref[place_in_plane(y // 2, c, y % 2, x), :128, :].astype(F32)
-            total = total.reshape(NZ, 8, 128)
-            for i, which in enumerate(kept_rows(pat_ref[c, :, x])):
-                kept = jnp.where(which == group.astype(F32), total, 0.0)
-                kept += pltpu.roll(kept, 64, 2)
-                kept += pltpu.roll(kept, 32, 2)
-                rows = jnp.where(group == i * 2 + c, kept, rows)
-        mid_ref[:, x * 8 : (x + 1) * 8, :] = rows
+                total += got_ref[place_in_plane(y // 2, c, y % 2, x), :64, :].astype(F32)
+            sums.append(total.reshape(8, 8, 128))
+        for half in range(2):
+            rows = jnp.zeros((8, 8, 128), F32)
+            for kept in range(2):
+                for c in range(NC):
+                    goal = kept * 2 + c
+                    shift = (goal - half * 2 - kept) % 4 * 32
+                    moved = pltpu.roll(sums[c], shift, 2) if shift else sums[c]
+                    rows = jnp.where(group == goal, moved, rows)
+            mid_ref[half * 8 : (half + 1) * 8, x * 8 : (x + 1) * 8, :] = rows
     out_ref[...] = mid_ref[...].astype(BF16)
 
 
@@ -386,60 +414,62 @@
         name="norm",
     )
     own = [split[0]] + [lax.ppermute(split[i], "x", ring(STEP[i])) for i in range(1, NX)]
-    rows_w = call(spread_kernel, shape((32, 128, 128), BF16), got_w, name="spread")
-    all_w = lax.all_to_all(rows_w, PLANE, 0, 0, tiled=True)
-
-    late, _ = lax.optimization_barrier((patterns, rows_w))
+    late, got_w = lax.optimization_barrier((patterns, got_w))
     own_pat = call(
         choose_kernel,
-        shape((NC, NZ, NX, 8, 128), F32),
+        shape((8, 32, 128), BF16),
         late,
         at,
         scratch=[pltpu.VMEM((NZ, NYL, NC, NX, 8, 128), F32)],
         name="choose",
     )
-    own[2], own_pat = lax.optimization_barrier((own[2], own_pat))
+    rows_w = call(spread_kernel, shape((32, 160, 128), BF16), got_w, own_pat, name="spread")
+    all_w = lax.all_to_all(rows_w, PLANE, 0, 0, tiled=True)
+
     marks = []
     for i in range(1, NX):
         mark = call(
-            mark_kernel, shape((8, 128), F32), own[i], far=(0,), flops=FLOPS, name="mark"
+            mark_kernel, shape((8, 128), F32), own[i], far=(0,), flops=FLOPS[i], name="mark"
         )
         own[i], mark = lax.optimization_barrier((own[i], mark))
         marks.append(mark)
     pair = [lax.ppermute(piece, "core", [(0, 1), (1, 0)]) for piece in own]
 
 
-    high, low = call(
+    high, low, pats = call(
         decode_kernel,
-        (shape((2048, 256), BF16),) * 2,
+        (shape((2048, 256), BF16),) * 2 + (shape((4, NZ, NC, 8, 128), F32),),
         all_w,
         scratch=[pltpu.VMEM((NYL, NZ, NC, 4, 8, 256), F32)],
         name="decode",
     )
     flops = 2 * 1024 * 2048 * 256
-    part = call(
-        forward_own_kernel,
-        shape((NX, 128, 256), BF16),
+    part, soon = call(
+        forward_most_kernel,
+        (shape((NX, 256, 256), BF16), shape((3, 128, 2048), BF16)),
         *own,
+        *(pair[i] for i in SOON),
         high,
         low,
         at,
-        flops=flops,
-        name="forward_own",
-    )
-    part, held = call(
-        forward_pair_kernel,
-        (shape((NX, 256, 256), BF16), shape((NX, 128, 2048), BF16)),
-        *pair,
-        *marks,
+        scratch=[pltpu.SemaphoreType.DMA((3,))],
+        flops=2 * flops * 7 // 8,
+        far=range(NX, NX + 3),
+        name="forward_most",
+    )
+    part, last = call(
+        forward_last_kernel,
+        (shape((NX, 256, 256), BF16), shape((128, 2048), BF16)),
+        pair[LAST],
         part,
         high,
         low,
         at,
-        scratch=[pltpu.SemaphoreType.DMA((NX,))],
-        flops=flops,
-        far=range(NX),
-        name="forward_pair",
+        *marks,
+        scratch=[pltpu.SemaphoreType.DMA],
+        flops=flops // 4,
+        far=(0,),
+        name="forward_last",
     )
     got_part = lax.all_to_all(part, "x", 0, 0, tiled=True)
     slope, loss_part = call(
@@ -449,9 +479,11 @@
 
     term = call(
         grad_kernel,
-        shape((32, 144, 128), BF16),
+        shape((32, 80, 128), BF16),
         *own,
-        held,
+        soon,
+        last,
+        pats,
         slopes,
         loss_part,
         at,
@@ -464,7 +496,6 @@
         gather_kernel,
         shape((NZ, 48, 128), BF16),
         got_term,
-        own_pat,
         scratch=[pltpu.VMEM((NZ, 48, 128), F32)],
         name="gather",
     )

time: 155 us -> 156 us (level)
  the two profiles are of different devices: /device:TPU:6 before, /device:TPU:32 now
where the time goes in v12:
time: 156 us; the launch traced here: 155 us
  blocking collectives  66.3 us (42%)
  starting transfers between devices  43.8 us (28%)
  Pallas kernels  21.9 us (14%)
  waiting for transfers between devices  21.8 us (14%)
    all_to_all x1, blocking collectives, shards(): got_sum = lax.all_to_all(packed_term, 'z', 0, 0, tiled=True)  22.1 us
    pallas_call x14, Pallas kernels, call(): pl.pallas_call(kernel, out_shape=out_shape, in_specs=specs, out_specs=jax...  21.9 us
    all_to_all x1, blocking collectives, shards(): got_term = lax.all_to_all(term, PLANE, 0, 0, tiled=True)  18.6 us
    ppermute x3, waiting for transfers between devices, shards(): lax.ppermute(split[i], 'x', ring(STEP[i]))  16.9 us
    all_to_all x1, starting transfers between devices, shards(): got_w = lax.all_to_all(packed, 'z', 0, 0, tiled=True)  15.2 us
    all_to_all x1, blocking collectives, shards(): got_part = lax.all_to_all(part, 'x', 0, 0, tiled=True)  13.9 us
    ppermute x3, starting transfers between devices, shards(): lax.ppermute(split[i], 'x', ring(STEP[i]))  12.9 us
    all_to_all x1, blocking collectives, shards(): slopes = lax.all_to_all(slope, 'x', 0, 0, tiled=True)  11.7 us
  transfers between devices with their start and end apart: 9, of which 2 were waited for; matrix products, arithmetic and copies ran while one was open for 0% of the time, Pallas kernels for 9%

profile of v12, /device:TPU:32, one launch (start us, length us, event | category | flops | bytes accessed | tf_op | source)
XLA Modules:
  0.0 155.4 jit_solution(2821353295267026203)
XLA Ops:
  0.6 0.7 stack.23.at_ref.refs_9_
  1.3 2.6 %pack.1 = (bf16[16,64,128]{2,1,0:T(8,128)(2,1)}, f32[64,128]{1,0:T(8,128)}) custom-call(bf16[64,128]{1,0:T(8,128)(2,1)} %bitcast.13, bf16[64,128]{1,0:T(8,128)(2,1)} %bitcast.14, s32[64,2048]{1,0:T(8,128)} %bitcast.11, s32[5]{0:T(128)} %stack.23.at_ref.refs_9_), custom_call_target="tpu_custom_call" | custom-call | bytes 851988 | tf_op jit(solution)/shard_map/pack/pallas_call | solution.py:30
  3.9 15.2 %all-to-all-start = ((bf16[16,64,128]{2,1,0:T(8,128)(2,1)}), bf16[16,64,128]{2,1,0:T(8,128)(2,1)S(1)}, u32[]{:S(2)}, u32[]{:S(2)}) async-start(bf16[16,64,128]{2,1,0:T(8,128)(2,1)} %get-tuple-element.34), calls=%async_computation | async-start | bytes 524288 | tf_op jit(solution)/shard_map/all_to_all | solution.py:395
  19.1 0.0 copy-start
  19.1 0.0 copy-start.3
  19.1 4.9 %norm.1 = (bf16[128,2048]{1,0:T(8,128)(2,1)}, bf16[128,2048]{1,0:T(8,128)(2,1)}, bf16[128,2048]{1,0:T(8,128)(2,1)}, bf16[128,2048]{1,0:T(8,128)(2,1)}) custom-call(bf16[128,8192]{1,0:T(8,128)(2,1)} %x_hbm.1, bf16[64,128]{1,0:T(8,128)(2,1)} %bitcast.16, s32[5]{0:T(128)} %stack.23.at_ref.refs_9_), custom_call_target="tpu_custom_call" | custom-call | flops 1073741824 | bytes 4210708 | tf_op jit(solution)/shard_map/norm/pallas_call | solution.py:30
  24.1 3.4 %collective-permute-start.1 = (bf16[128,2048]{1,0:T(8,128)(2,1)}, bf16[128,2048]{1,0:T(8,128)(2,1)S(1)}, u32[]{:S(2)}, u32[]{:S(2)}) collective-permute-start(bf16[128,2048]{1,0:T(8,128)(2,1)} %get-tuple-element.30), channel_id=1, source_target_pairs={{0,1},{1,2},{2,3},{3,0},{4,5},{5,6},{6,7},{7,4},{8,9},{9,10},{10,1... | collective-permute-start | bytes 1572872 | tf_op jit(solution)/shard_map/ppermute | solution.py:416
  27.5 4.6 %collective-permute-start = (bf16[128,2048]{1,0:T(8,128)(2,1)}, bf16[128,2048]{1,0:T(8,128)(2,1)S(1)}, u32[]{:S(2)}, u32[]{:S(2)}) collective-permute-start(bf16[128,2048]{1,0:T(8,128)(2,1)} %get-tuple-element.28), channel_id=1, source_target_pairs={{0,2},{1,3},{2,0},{3,1},{4,6},{5,7},{6,4},{7,5},{8,10},{9,11},{10,... | collective-permute-start | bytes 1572872 | tf_op jit(solution)/shard_map/ppermute | solution.py:416
  32.1 4.9 %all-to-all-done.got_ref = bf16[16,64,128]{2,1,0:T(8,128)(2,1)S(1)} async-done(((bf16[16,64,128]{2,1,0:T(8,128)(2,1)}), bf16[16,64,128]{2,1,0:T(8,128)(2,1)S(1)}, u32[]{:S(2)}, u32[]{:S(2)}) %all-to-all-start) | async-done | bytes 262176 | tf_op jit(solution)/shard_map/all_to_all | solution.py:395
  37.0 0.0 copy-done
  37.0 0.0 copy-done.3
  37.0 1.1 choose.1.pat_ref
  38.1 1.2 spread.1
  39.4 0.0 copy-start.1
  39.4 7.5 %all-to-all-start.1 = ((bf16[32,160,128]{2,1,0:T(8,128)(2,1)}), bf16[32,160,128]{2,1,0:T(8,128)(2,1)S(1)}, u32[]{:S(2)}, u32[]{:S(2)}) async-start(bf16[32,160,128]{2,1,0:T(8,128)(2,1)} %spread.1), calls=%async_computation.1 | async-start | bytes 2621440 | tf_op jit(solution)/shard_map/all_to_all | solution.py:427
  46.8 4.9 %collective-permute-start.2 = (bf16[128,2048]{1,0:T(8,128)(2,1)}, bf16[128,2048]{1,0:T(8,128)(2,1)S(1)}, u32[]{:S(2)}, u32[]{:S(2)}) collective-permute-start(bf16[128,2048]{1,0:T(8,128)(2,1)} %get-tuple-element.32), channel_id=1, source_target_pairs={{0,3},{1,0},{2,1},{3,2},{4,7},{5,4},{6,5},{7,6},{8,11},{9,8},{10,9... | collective-permute-start | bytes 1572872 | tf_op jit(solution)/shard_map/ppermute | solution.py:416
  51.8 0.0 copy-done.1
  51.8 1.9 %collective-permute-start.3 = (bf16[128,2048]{1,0:T(8,128)(2,1)S(1)}, bf16[128,2048]{1,0:T(8,128)(2,1)}, u32[]{:S(2)}, u32[]{:S(2)}) collective-permute-start(bf16[128,2048]{1,0:T(8,128)(2,1)S(1)} %copy-done.1), channel_id=1, source_target_pairs={{0,8},{8,0},{1,9},{9,1},{2,10},{10,2},{3,11},{11,3},{4,12},{12,4},... | collective-permute-start | bytes 1572872 | tf_op jit(solution)/shard_map/ppermute | solution.py:436
  53.7 0.0 collective-permute-done.1.piece_hbm.refs_2_
  53.7 2.4 %collective-permute-start.5 = (bf16[128,2048]{1,0:T(8,128)(2,1)S(1)}, bf16[128,2048]{1,0:T(8,128)(2,1)}, u32[]{:S(2)}, u32[]{:S(2)}) collective-permute-start(bf16[128,2048]{1,0:T(8,128)(2,1)S(1)} %collective-permute-done.1.piece_hbm.refs_2_), channel_id=1, source_target_pairs={{0,8},{8,0},{1,9},{9,1},{2,10},{10,2},{3,11},{11,3},{4,12},{12,4},... | collective-permute-start | bytes 1572872 | tf_op jit(solution)/shard_map/ppermute | solution.py:436
  56.1 0.0 collective-permute-done.piece_hbm.refs_1_
  56.2 1.9 %collective-permute-start.4 = (bf16[128,2048]{1,0:T(8,128)(2,1)S(1)}, bf16[128,2048]{1,0:T(8,128)(2,1)}, u32[]{:S(2)}, u32[]{:S(2)}) collective-permute-start(bf16[128,2048]{1,0:T(8,128)(2,1)S(1)} %collective-permute-done.piece_hbm.refs_1_), channel_id=1, source_target_pairs={{0,8},{8,0},{1,9},{9,1},{2,10},{10,2},{3,11},{11,3},{4,12},{12,4},... | collective-permute-start | bytes 1572872 | tf_op jit(solution)/shard_map/ppermute | solution.py:436
  58.1 16.9 %collective-permute-done.2.piece_hbm.refs_3_ = bf16[128,2048]{1,0:T(8,128)(2,1)S(1)} collective-permute-done((bf16[128,2048]{1,0:T(8,128)(2,1)}, bf16[128,2048]{1,0:T(8,128)(2,1)S(1)}, u32[]{:S(2)}, u32[]{:S(2)}) %collective-permute-start.2) | collective-permute-done | bytes 524320 | tf_op jit(solution)/shard_map/ppermute | solution.py:416
  75.0 1.9 %collective-permute-start.6 = (bf16[128,2048]{1,0:T(8,128)(2,1)S(1)}, bf16[128,2048]{1,0:T(8,128)(2,1)}, u32[]{:S(2)}, u32[]{:S(2)}) collective-permute-start(bf16[128,2048]{1,0:T(8,128)(2,1)S(1)} %collective-permute-done.2.piece_hbm.refs_3_), channel_id=1, source_target_pairs={{0,8},{8,0},{1,9},{9,1},{2,10},{10,2},{3,11},{11,3},{4,12},{12,4},... | collective-permute-start | bytes 1572872 | tf_op jit(solution)/shard_map/ppermute | solution.py:436
  76.9 0.0 all-to-all-done.1.got_ref
  76.9 2.0 %decode.1 = (bf16[2048,256]{1,0:T(8,128)(2,1)S(1)}, bf16[2048,256]{1,0:T(8,128)(2,1)S(1)}, f32[4,16,2,8,128]{4,3,2,1,0:T(8,128)S(1)}) custom-call(bf16[32,160,128]{2,1,0:T(8,128)(2,1)S(1)} %all-to-all-done.1.got_ref), custom_call_target="tpu_custom_call" | custom-call | bytes 3932160 | tf_op jit(solution)/shard_map/decode/pallas_call | solution.py:30
  79.0 0.0 collective-permute-done.3.refs_4_
  79.0 0.0 collective-permute-done.5.refs_6_
  79.0 0.0 collective-permute-done.4.refs_5_
  79.0 4.2 %forward_most.1 = (bf16[4,256,256]{2,1,0:T(8,128)(2,1)S(1)}, bf16[3,128,2048]{2,1,0:T(8,128)(2,1)S(1)}) custom-call(bf16[128,2048]{1,0:T(8,128)(2,1)S(1)} %copy-done.1, bf16[128,2048]{1,0:T(8,128)(2,1)S(1)} %collective-permute-done.piece_hbm.refs_1_, bf16[128,2048]{1,0:T(8,128)(2,1)S(1)} %collective-permute-done.1.piece_hbm.refs_2_, ...), custom_call_target="tpu_custom_call" | custom-call | flops 1879048192 | bytes 7864340 | tf_op jit(solution)/shard_map/forward_most/pallas_call | solution.py:30
  83.2 0.0 collective-permute-done.6.pair_hbm
  83.2 2.1 %forward_last.1 = (bf16[4,256,256]{2,1,0:T(8,128)(2,1)S(1)}, bf16[128,2048]{1,0:T(8,128)(2,1)S(1)}) custom-call(bf16[128,2048]{1,0:T(8,128)(2,1)} %collective-permute-done.6.pair_hbm, bf16[4,256,256]{2,1,0:T(8,128)(2,1)S(1)} %get-tuple-element.40.part_ref, bf16[2048,256]{1,0:T(8,128)(2,1)S(1)} %get-tuple-element.37.refs_7_.high_ref, ...), custom_call_target="tpu_custom_call" | custom-call | flops 268435456 | bytes 4206612 | tf_op jit(solution)/shard_map/forward_last/pallas_call | solution.py:30
  85.3 13.9 %all_to_all.30.part_ref = bf16[4,256,256]{2,1,0:T(8,128)(2,1)S(1)} all-to-all(bf16[4,256,256]{2,1,0:T(8,128)(2,1)S(1)} %get-tuple-element.46), channel_id=1, replica_groups=mesh['z'=16,'yl'=2,'core'=2,'yh'=2,'x'=4] {'x'}, dimensions={0} | all-to-all | bytes 1048576 | tf_op jit(solution)/shard_map/all_to_all | solution.py:474
  99.2 0.1 slope.1
  99.3 11.7 %all_to_all.31.refs_7_ = bf16[4,256,256]{2,1,0:T(8,128)(2,1)S(1)} all-to-all(bf16[4,256,256]{2,1,0:T(8,128)(2,1)S(1)} %get-tuple-element.47), channel_id=1, replica_groups=mesh['z'=16,'yl'=2,'core'=2,'yh'=2,'x'=4] {'x'}, dimensions={0} | all-to-all | bytes 1048576 | tf_op jit(solution)/shard_map/all_to_all | solution.py:478
  111.0 2.6 %grad.1 = bf16[32,80,128]{2,1,0:T(8,128)(2,1)S(1)} custom-call(bf16[128,2048]{1,0:T(8,128)(2,1)S(1)} %copy-done.1, bf16[128,2048]{1,0:T(8,128)(2,1)S(1)} %collective-permute-done.piece_hbm.refs_1_, bf16[128,2048]{1,0:T(8,128)(2,1)S(1)} %collective-permute-done.1.piece_hbm.refs_2_, bf16[128,2048]{1,0:T(8,128)(2,1)S(1)} %collective-permute-done.2.piece_hbm.refs_3_, ...), custom_call_target="tpu_custom_call" | custom-call | flops 1073741824 | bytes 5898772 | tf_op jit(solution)/shard_map/grad/pallas_call | solution.py:30
  113.6 0.0 copy-start.2
  113.6 18.6 %all_to_all.32.got_ref = bf16[32,80,128]{2,1,0:T(8,128)(2,1)S(1)} all-to-all(bf16[32,80,128]{2,1,0:T(8,128)(2,1)S(1)} %grad.1), channel_id=1, replica_groups=mesh['z'=16,'yl'=2,'core'=2,'yh'=2,'x'=4] {'yl','core','yh','x'}, dimensions={0} | all-to-all | bytes 1310720 | tf_op jit(solution)/shard_map/all_to_all | solution.py:494
  132.2 0.2 gather.1
  132.4 22.1 %all_to_all.33.got_ref = bf16[16,48,128]{2,1,0:T(8,128)(2,1)S(1)} all-to-all(bf16[16,48,128]{2,1,0:T(8,128)(2,1)S(1)} %gather.1), channel_id=1, replica_groups=mesh['z'=16,'yl'=2,'core'=2,'yh'=2,'x'=4] {'z'}, dimensions={0} | all-to-all | bytes 393216 | tf_op jit(solution)/shard_map/all_to_all | solution.py:502
  154.6 0.0 copy-done.2
  154.6 0.9 final.1
  (3 shorter events, 0.0 us)
Async XLA Ops:
  3.9 33.1 %all-to-all-start = ((bf16[16,64,128]{2,1,0:T(8,128)(2,1)}), bf16[16,64,128]{2,1,0:T(8,128)(2,1)S(1)}, u32[]{:S(2)}, u32[]{:S(2)}) async-start(bf16[16,64,128]{2,1,0:T(8,128)(2,1)} %get-tuple-element.34), calls=%async_computation | async-start | bytes 524288 | tf_op jit(solution)/shard_map/all_to_all | solution.py:395
  19.1 17.9 %copy-start = (s32[2048,64]{0,1:T(8,128)S(1)}, s32[2048,64]{0,1:T(8,128)}, u32[]{:S(2)}) copy-start(s32[2048,64]{0,1:T(8,128)} %param.9) | copy-start | bytes 1572868
  19.1 17.9 %copy-start.3 = (s32[5]{0:T(128)S(1)}, s32[5]{0:T(128)}, u32[]{:S(2)}) copy-start(s32[5]{0:T(128)} %stack.23.at_ref.refs_9_) | copy-start | bytes 64
  24.1 29.6 %collective-permute-start.1 = (bf16[128,2048]{1,0:T(8,128)(2,1)}, bf16[128,2048]{1,0:T(8,128)(2,1)S(1)}, u32[]{:S(2)}, u32[]{:S(2)}) collective-permute-start(bf16[128,2048]{1,0:T(8,128)(2,1)} %get-tuple-element.30), channel_id=1, source_target_pairs={{0,1},{1,2},{2,3},{3,0},{4,5},{5,6},{6,7},{7,4},{8,9},{9,10},{10,1... | collective-permute-start | bytes 1572872 | tf_op jit(solution)/shard_map/ppermute | solution.py:416
  27.5 28.7 %collective-permute-start = (bf16[128,2048]{1,0:T(8,128)(2,1)}, bf16[128,2048]{1,0:T(8,128)(2,1)S(1)}, u32[]{:S(2)}, u32[]{:S(2)}) collective-permute-start(bf16[128,2048]{1,0:T(8,128)(2,1)} %get-tuple-element.28), channel_id=1, source_target_pairs={{0,2},{1,3},{2,0},{3,1},{4,6},{5,7},{6,4},{7,5},{8,10},{9,11},{10,... | collective-permute-start | bytes 1572872 | tf_op jit(solution)/shard_map/ppermute | solution.py:416
  39.4 12.4 %copy-start.1 = (bf16[128,2048]{1,0:T(8,128)(2,1)S(1)}, bf16[128,2048]{1,0:T(8,128)(2,1)}, u32[]{:S(2)}) copy-start(bf16[128,2048]{1,0:T(8,128)(2,1)} %get-tuple-element.27.refs_0_) | copy-start | bytes 1572868
  39.4 37.6 %all-to-all-start.1 = ((bf16[32,160,128]{2,1,0:T(8,128)(2,1)}), bf16[32,160,128]{2,1,0:T(8,128)(2,1)S(1)}, u32[]{:S(2)}, u32[]{:S(2)}) async-start(bf16[32,160,128]{2,1,0:T(8,128)(2,1)} %spread.1), calls=%async_computation.1 | async-start | bytes 2621440 | tf_op jit(solution)/shard_map/all_to_all | solution.py:427
  46.8 28.2 %collective-permute-start.2 = (bf16[128,2048]{1,0:T(8,128)(2,1)}, bf16[128,2048]{1,0:T(8,128)(2,1)S(1)}, u32[]{:S(2)}, u32[]{:S(2)}) collective-permute-start(bf16[128,2048]{1,0:T(8,128)(2,1)} %get-tuple-element.32), channel_id=1, source_target_pairs={{0,3},{1,0},{2,1},{3,2},{4,7},{5,4},{6,5},{7,6},{8,11},{9,8},{10,9... | collective-permute-start | bytes 1572872 | tf_op jit(solution)/shard_map/ppermute | solution.py:416
  51.8 27.2 %collective-permute-start.3 = (bf16[128,2048]{1,0:T(8,128)(2,1)S(1)}, bf16[128,2048]{1,0:T(8,128)(2,1)}, u32[]{:S(2)}, u32[]{:S(2)}) collective-permute-start(bf16[128,2048]{1,0:T(8,128)(2,1)S(1)} %copy-done.1), channel_id=1, source_target_pairs={{0,8},{8,0},{1,9},{9,1},{2,10},{10,2},{3,11},{11,3},{4,12},{12,4},... | collective-permute-start | bytes 1572872 | tf_op jit(solution)/shard_map/ppermute | solution.py:436
  53.7 25.3 %collective-permute-start.5 = (bf16[128,2048]{1,0:T(8,128)(2,1)S(1)}, bf16[128,2048]{1,0:T(8,128)(2,1)}, u32[]{:S(2)}, u32[]{:S(2)}) collective-permute-start(bf16[128,2048]{1,0:T(8,128)(2,1)S(1)} %collective-permute-done.1.piece_hbm.refs_2_), channel_id=1, source_target_pairs={{0,8},{8,0},{1,9},{9,1},{2,10},{10,2},{3,11},{11,3},{4,12},{12,4},... | collective-permute-start | bytes 1572872 | tf_op jit(solution)/shard_map/ppermute | solution.py:436
  56.2 22.8 %collective-permute-start.4 = (bf16[128,2048]{1,0:T(8,128)(2,1)S(1)}, bf16[128,2048]{1,0:T(8,128)(2,1)}, u32[]{:S(2)}, u32[]{:S(2)}) collective-permute-start(bf16[128,2048]{1,0:T(8,128)(2,1)S(1)} %collective-permute-done.piece_hbm.refs_1_), channel_id=1, source_target_pairs={{0,8},{8,0},{1,9},{9,1},{2,10},{10,2},{3,11},{11,3},{4,12},{12,4},... | collective-permute-start | bytes 1572872 | tf_op jit(solution)/shard_map/ppermute | solution.py:436
  75.0 8.2 %collective-permute-start.6 = (bf16[128,2048]{1,0:T(8,128)(2,1)S(1)}, bf16[128,2048]{1,0:T(8,128)(2,1)}, u32[]{:S(2)}, u32[]{:S(2)}) collective-permute-start(bf16[128,2048]{1,0:T(8,128)(2,1)S(1)} %collective-permute-done.2.piece_hbm.refs_3_), channel_id=1, source_target_pairs={{0,8},{8,0},{1,9},{9,1},{2,10},{10,2},{3,11},{11,3},{4,12},{12,4},... | collective-permute-start | bytes 1572872 | tf_op jit(solution)/shard_map/ppermute | solution.py:436
  113.6 41.0 %copy-start.2 = (f32[64,128]{1,0:T(8,128)S(1)}, f32[64,128]{1,0:T(8,128)}, u32[]{:S(2)}) copy-start(f32[64,128]{1,0:T(8,128)} %get-tuple-element.49.pat_ref) | copy-start | bytes 98308

commit v13 on v10

--- a/solution.py
+++ b/solution.py
@@ -18,6 +18,7 @@
 SMEM = pl.BlockSpec(memory_space=pltpu.SMEM)
 STEP = (0, 2, 1, 3)
 BACK = (0, 2, 3, 1)
+SOON, LAST = (0, 1, 3), 2
 
 
 def call(kernel, out_shape, *args, scratch=(), flops=0, name=None, far=(), out_far=False, grant=24):
@@ -208,20 +209,34 @@
             low_ref[at : at + 256, lane : lane + 128] = (delta - high.astype(F32)).astype(BF16)
 
 
-def forward_kernel(*refs):
-    own, pair, rest = refs[:NX], refs[NX : 2 * NX], refs[2 * NX :]
+def forward(rows, high_ref, low_ref):
+    part = jnp.dot(rows, high_ref[...], preferred_element_type=F32)
+    part += jnp.dot(rows, low_ref[...], preferred_element_type=F32)
+    return part.astype(BF16)
+
+
+def forward_most_kernel(*refs):
+    own, pair, rest = refs[:NX], refs[NX : NX + 3], refs[NX + 3 :]
     high_ref, low_ref, at_ref, out_ref, held_ref, sems = rest
-    loads = [pltpu.make_async_copy(pair[i], held_ref.at[i], sems.at[i]) for i in range(NX)]
+    loads = [pltpu.make_async_copy(pair[i], held_ref.at[i], sems.at[i]) for i in range(3)]
     for load in loads:
         load.start()
-    for row in (0, 128):
-        for i in range(NX):
-            if row:
-                loads[i].wait()
-            rows = held_ref[i] if row else own[i][...]
-            part = jnp.dot(rows, high_ref[...], preferred_element_type=F32)
-            part += jnp.dot(rows, low_ref[...], preferred_element_type=F32)
-            out_ref[(at_ref[0] + BACK[i]) % NX, row : row + 128] = part.astype(BF16)
+    for i in range(NX):
+        out_ref[(at_ref[0] + BACK[i]) % NX, :128] = forward(own[i][...], high_ref, low_ref)
+    for i in range(3):
+        loads[i].wait()
+        x = (at_ref[0] + BACK[SOON[i]]) % NX
+        out_ref[x, 128:] = forward(held_ref[i], high_ref, low_ref)
+    out_ref[(at_ref[0] + BACK[LAST]) % NX, 128:] = jnp.zeros((128, 256), BF16)
+
+
+def forward_last_kernel(pair_hbm, part_ref, high_ref, low_ref, at_ref, *rest):
+    out_ref, held_ref, sem = rest
+    load = pltpu.make_async_copy(pair_hbm, held_ref, sem)
+    load.start()
+    out_ref[...] = part_ref[...]
+    load.wait()
+    out_ref[(at_ref[0] + BACK[LAST]) % NX, 128:] = forward(held_ref[...], high_ref, low_ref)
 
 
 def thirds(value, rows):
@@ -244,7 +259,7 @@
 
 
 def grad_kernel(*refs):
-    own, (held_ref, *rest) = refs[:NX], refs[NX:]
+    own, (soon_ref, last_ref, *rest) = refs[:NX], refs[NX:]
     slope_ref, loss_ref, at_ref, out_ref, s_ref, term_ref = rest
     contract = (((0,), (0,)), ((), ()))
     for i in range(NX):
@@ -254,7 +269,9 @@
     for k in range(8):
         at = k * 256
         rows = [ref[:, at : at + 256] for ref in own]
-        rows += [held_ref[i, :, at : at + 256] for i in range(NX)]
+        pair = [soon_ref[i, :, at : at + 256] for i in range(3)]
+        pair.insert(LAST, last_ref[:, at : at + 256])
+        rows += pair
         rows = jnp.concatenate(rows, axis=0)
         term = lax.dot_general(rows, s_ref[...], contract, preferred_element_type=F32)
         for yh in range(2):
@@ -386,24 +403,37 @@
         scratch=[pltpu.VMEM((NZ, NYL, NC, NX, 8, 128), F32)],
         name="choose",
     )
-    own[2], own_pat = lax.optimization_barrier((own[2], own_pat))
+    own[3], own_pat = lax.optimization_barrier((own[3], own_pat))
     pair = [lax.ppermute(piece, "core", [(0, 1), (1, 0)]) for piece in own]
 
     high, low = call(decode_kernel, (shape((2048, 256), BF16),) * 2, all_w, name="decode")
 
     flops = 2 * 1024 * 2048 * 256
-    part, held = call(
-        forward_kernel,
-        (shape((NX, 256, 256), BF16), shape((NX, 128, 2048), BF16)),
+    part, soon = call(
+        forward_most_kernel,
+        (shape((NX, 256, 256), BF16), shape((3, 128, 2048), BF16)),
         *own,
-        *pair,
+        *(pair[i] for i in SOON),
         high,
         low,
         at,
-        scratch=[pltpu.SemaphoreType.DMA((NX,))],
-        flops=2 * flops,
-        far=range(NX, 2 * NX),
-        name="forward",
+        scratch=[pltpu.SemaphoreType.DMA((3,))],
+        flops=2 * flops * 7 // 8,
+        far=range(NX, NX + 3),
+        name="forward_most",
+    )
+    part, last = call(
+        forward_last_kernel,
+        (shape((NX, 256, 256), BF16), shape((128, 2048), BF16)),
+        pair[LAST],
+        part,
+        high,
+        low,
+        at,
+        scratch=[pltpu.SemaphoreType.DMA],
+        flops=flops // 4,
+        far=(0,),
+        name="forward_last",
     )
     got_part = lax.all_to_all(part, "x", 0, 0, tiled=True)
     slope, loss_part = call(
@@ -415,7 +445,8 @@
         grad_kernel,
         shape((32, 144, 128), BF16),
         *own,
-        held,
+        soon,
+        last,
         slopes,
         loss_part,
         at,

time: 154 us -> 152 us (0.987)
  blocking collectives: 75.4 us -> 72.6 us
    all_to_all x1, blocking collectives: 27.5 us -> 24.9 us  [shards(): got_sum = lax.all_to_all(packed_term, 'z', 0, 0, tiled=True)]
    pallas_call x10 -> x11, Pallas kernels: 21.7 us -> 22.3 us  [call(): pl.pallas_call(kernel, out_shape=out_shape, in_specs=specs, out_specs=jax...]
  transfers between devices with their start and end apart: 9 -> 9, of which waited for: 4 -> 3; matrix products, arithmetic and copies ran while one was open for 0% -> 0% of each run, Pallas kernels for 5% -> 9%
where the time goes in v13:
time: 152 us; the launch traced here: 150 us
  blocking collectives  72.6 us (48%)
  starting transfers between devices  42.9 us (28%)
  Pallas kernels  22.3 us (15%)
  waiting for transfers between devices  10.1 us (7%)
    all_to_all x1, blocking collectives, shards(): got_sum = lax.all_to_all(packed_term, 'z', 0, 0, tiled=True)  24.9 us
    all_to_all x1, blocking collectives, shards(): got_term = lax.all_to_all(term, PLANE, 0, 0, tiled=True)  22.6 us
    pallas_call x11, Pallas kernels, call(): pl.pallas_call(kernel, out_shape=out_shape, in_specs=specs, out_specs=jax...  22.3 us
    all_to_all x1, starting transfers between devices, shards(): got_w = lax.all_to_all(packed.reshape(128, 8, 128), ZCX, 0, 0, tiled=True)  19.4 us
    all_to_all x1, blocking collectives, shards(): got_part = lax.all_to_all(part, 'x', 0, 0, tiled=True)  14.1 us
    all_to_all x1, blocking collectives, shards(): slopes = lax.all_to_all(slope, 'x', 0, 0, tiled=True)  11 us
    ppermute x3, starting transfers between devices, shards(): lax.ppermute(split[i], 'x', ring(STEP[i]))  10.4 us
    ppermute x4, starting transfers between devices, shards(): pair = [lax.ppermute(piece, 'core', [(0, 1), (1, 0)]) for piece in own]  8.63 us
  transfers between devices with their start and end apart: 9, of which 3 were waited for; matrix products, arithmetic and copies ran while one was open for 0% of the time, Pallas kernels for 9%

profile of v13, /device:TPU:6, one launch (start us, length us, event | category | flops | bytes accessed | tf_op | source)
XLA Modules:
  0.0 149.5 jit_solution(633953626159849212)
XLA Ops:
  0.6 0.7 stack.23.at_ref.refs_9_.refs_8_
  1.3 2.6 %pack.1 = (bf16[16,64,128]{2,1,0:T(8,128)(2,1)}, f32[64,128]{1,0:T(8,128)}) custom-call(bf16[64,128]{1,0:T(8,128)(2,1)} %bitcast.17, bf16[64,128]{1,0:T(8,128)(2,1)} %bitcast.18, s32[64,2048]{1,0:T(8,128)} %bitcast.13, s32[5]{0:T(128)} %stack.23.at_ref.refs_9_.refs_8_), custom_call_target="tpu_custom_call" | custom-call | bytes 851988 | tf_op jit(solution)/shard_map/pack/pallas_call | solution.py:31
  3.9 19.4 %all-to-all-start = ((bf16[128,8,128]{2,1,0:T(8,128)(2,1)}), bf16[128,8,128]{2,1,0:T(8,128)(2,1)S(1)}, u32[]{:S(2)}, u32[]{:S(2)}) async-start(bf16[128,8,128]{2,1,0:T(8,128)(2,1)} %bitcast.16), calls=%async_computation | async-start | bytes 524288 | tf_op jit(solution)/shard_map/all_to_all | solution.py:366
  23.3 4.9 %norm.1 = (bf16[128,2048]{1,0:T(8,128)(2,1)}, bf16[128,2048]{1,0:T(8,128)(2,1)}, bf16[128,2048]{1,0:T(8,128)(2,1)}, bf16[128,2048]{1,0:T(8,128)(2,1)}) custom-call(bf16[128,8192]{1,0:T(8,128)(2,1)} %x_hbm.1, bf16[64,128]{1,0:T(8,128)(2,1)} %bitcast.20, s32[5]{0:T(128)} %stack.23.at_ref.refs_9_.refs_8_), custom_call_target="tpu_custom_call" | custom-call | flops 1073741824 | bytes 4210708 | tf_op jit(solution)/shard_map/norm/pallas_call | solution.py:31
  28.2 3.4 %collective-permute-start = (bf16[128,2048]{1,0:T(8,128)(2,1)}, bf16[128,2048]{1,0:T(8,128)(2,1)S(1)}, u32[]{:S(2)}, u32[]{:S(2)}) collective-permute-start(bf16[128,2048]{1,0:T(8,128)(2,1)} %get-tuple-element.22), channel_id=1, source_target_pairs={{0,2},{1,3},{2,0},{3,1},{4,6},{5,7},{6,4},{7,5},{8,10},{9,11},{10,... | collective-permute-start | bytes 1572872 | tf_op jit(solution)/shard_map/ppermute | solution.py:387
  31.6 2.2 %collective-permute-start.2 = (bf16[128,2048]{1,0:T(8,128)(2,1)}, bf16[128,2048]{1,0:T(8,128)(2,1)}, u32[]{:S(2)}, u32[]{:S(2)}) collective-permute-start(bf16[128,2048]{1,0:T(8,128)(2,1)} %get-tuple-element.24), channel_id=1, source_target_pairs={{0,3},{1,0},{2,1},{3,2},{4,7},{5,4},{6,5},{7,6},{8,11},{9,8},{10,9... | collective-permute-start | bytes 1572872 | tf_op jit(solution)/shard_map/ppermute | solution.py:387
  33.8 4.8 %collective-permute-start.1 = (bf16[128,2048]{1,0:T(8,128)(2,1)}, bf16[128,2048]{1,0:T(8,128)(2,1)}, u32[]{:S(2)}, u32[]{:S(2)}) collective-permute-start(bf16[128,2048]{1,0:T(8,128)(2,1)} %get-tuple-element.23), channel_id=1, source_target_pairs={{0,1},{1,2},{2,3},{3,0},{4,5},{5,6},{6,7},{7,4},{8,9},{9,10},{10,1... | collective-permute-start | bytes 1572872 | tf_op jit(solution)/shard_map/ppermute | solution.py:387
  38.6 6.8 %all-to-all-done = bf16[128,8,128]{2,1,0:T(8,128)(2,1)S(1)} async-done(((bf16[128,8,128]{2,1,0:T(8,128)(2,1)}), bf16[128,8,128]{2,1,0:T(8,128)(2,1)S(1)}, u32[]{:S(2)}, u32[]{:S(2)}) %all-to-all-start) | async-done | bytes 262176 | tf_op jit(solution)/shard_map/all_to_all | solution.py:366
  45.4 0.0 copy-start.1
  45.4 0.0 copy-start
  45.4 0.0 copy-start.3
  45.4 1.3 spread.1
  46.7 4.5 %all-to-all-start.1 = ((bf16[4,1024,128]{2,1,0:T(8,128)(2,1)}), bf16[4,1024,128]{2,1,0:T(8,128)(2,1)S(1)}, u32[]{:S(2)}, u32[]{:S(2)}) async-start(bf16[4,1024,128]{2,1,0:T(8,128)(2,1)} %spread.1), calls=%async_computation.1 | async-start | bytes 2097152 | tf_op jit(solution)/shard_map/all_to_all | solution.py:395
  51.1 0.0 copy-done.1
  51.1 1.9 %collective-permute-start.3 = (bf16[128,2048]{1,0:T(8,128)(2,1)S(1)}, bf16[128,2048]{1,0:T(8,128)(2,1)}, u32[]{:S(2)}, u32[]{:S(2)}) collective-permute-start(bf16[128,2048]{1,0:T(8,128)(2,1)S(1)} %copy-done.1), channel_id=1, source_target_pairs={{0,8},{8,0},{1,9},{9,1},{2,10},{10,2},{3,11},{11,3},{4,12},{12,4},... | collective-permute-start | bytes 1572872 | tf_op jit(solution)/shard_map/ppermute | solution.py:407
  53.1 0.0 collective-permute-done.refs_1_
  53.1 2.4 %collective-permute-start.4 = (bf16[128,2048]{1,0:T(8,128)(2,1)S(1)}, bf16[128,2048]{1,0:T(8,128)(2,1)}, u32[]{:S(2)}, u32[]{:S(2)}) collective-permute-start(bf16[128,2048]{1,0:T(8,128)(2,1)S(1)} %collective-permute-done.refs_1_), channel_id=1, source_target_pairs={{0,8},{8,0},{1,9},{9,1},{2,10},{10,2},{3,11},{11,3},{4,12},{12,4},... | collective-permute-start | bytes 1572872 | tf_op jit(solution)/shard_map/ppermute | solution.py:407
  55.5 0.0 copy-done
  55.5 0.0 copy-done.3
  55.5 1.1 choose.1.pat_ref
  56.6 1.6 %collective-permute-done.2.refs_3_ = bf16[128,2048]{1,0:T(8,128)(2,1)} collective-permute-done((bf16[128,2048]{1,0:T(8,128)(2,1)}, bf16[128,2048]{1,0:T(8,128)(2,1)}, u32[]{:S(2)}, u32[]{:S(2)}) %collective-permute-start.2) | collective-permute-done | bytes 524320 | tf_op jit(solution)/shard_map/ppermute | solution.py:387
  58.2 2.0 %collective-permute-start.5 = (bf16[128,2048]{1,0:T(8,128)(2,1)}, bf16[128,2048]{1,0:T(8,128)(2,1)}, u32[]{:S(2)}, u32[]{:S(2)}) collective-permute-start(bf16[128,2048]{1,0:T(8,128)(2,1)} %collective-permute-done.2.refs_3_), channel_id=1, source_target_pairs={{0,8},{8,0},{1,9},{9,1},{2,10},{10,2},{3,11},{11,3},{4,12},{12,4},... | collective-permute-start | bytes 1572872 | tf_op jit(solution)/shard_map/ppermute | solution.py:407
  60.2 0.0 collective-permute-done.1.refs_2_
  60.2 2.4 %collective-permute-start.6 = (bf16[128,2048]{1,0:T(8,128)(2,1)}, bf16[128,2048]{1,0:T(8,128)(2,1)S(1)}, u32[]{:S(2)}, u32[]{:S(2)}) collective-permute-start(bf16[128,2048]{1,0:T(8,128)(2,1)} %collective-permute-done.1.refs_2_), channel_id=1, source_target_pairs={{0,8},{8,0},{1,9},{9,1},{2,10},{10,2},{3,11},{11,3},{4,12},{12,4},... | collective-permute-start | bytes 1572872 | tf_op jit(solution)/shard_map/ppermute | solution.py:407
  62.6 1.8 %all-to-all-done.1.w_ref = bf16[4,1024,128]{2,1,0:T(8,128)(2,1)S(1)} async-done(((bf16[4,1024,128]{2,1,0:T(8,128)(2,1)}), bf16[4,1024,128]{2,1,0:T(8,128)(2,1)S(1)}, u32[]{:S(2)}, u32[]{:S(2)}) %all-to-all-start.1) | async-done | bytes 1048608 | tf_op jit(solution)/shard_map/all_to_all | solution.py:395
  64.3 0.9 decode.1
  65.2 0.0 collective-permute-done.3.refs_4_
  65.2 0.0 collective-permute-done.4.refs_5_
  65.2 0.0 collective-permute-done.5.refs_6_
  65.3 4.8 %forward_most.1 = (bf16[4,256,256]{2,1,0:T(8,128)(2,1)S(1)}, bf16[3,128,2048]{2,1,0:T(8,128)(2,1)S(1)}) custom-call(bf16[128,2048]{1,0:T(8,128)(2,1)S(1)} %copy-done.1, bf16[128,2048]{1,0:T(8,128)(2,1)S(1)} %collective-permute-done.refs_1_, bf16[128,2048]{1,0:T(8,128)(2,1)} %collective-permute-done.1.refs_2_, ...), custom_call_target="tpu_custom_call" | custom-call | flops 1879048192 | bytes 7864340 | tf_op jit(solution)/shard_map/forward_most/pallas_call | solution.py:31
  70.1 0.0 collective-permute-done.6.pair_hbm
  70.1 1.1 forward_last.1
  71.2 14.1 %all_to_all.30.part_ref = bf16[4,256,256]{2,1,0:T(8,128)(2,1)S(1)} all-to-all(bf16[4,256,256]{2,1,0:T(8,128)(2,1)S(1)} %get-tuple-element.33), channel_id=1, replica_groups=mesh['z'=16,'yl'=2,'core'=2,'yh'=2,'x'=4] {'x'}, dimensions={0} | all-to-all | bytes 1048576 | tf_op jit(solution)/shard_map/all_to_all | solution.py:438
  85.3 0.1 slope.1
  85.4 11.0 %all_to_all.31.refs_6_ = bf16[4,256,256]{2,1,0:T(8,128)(2,1)S(1)} all-to-all(bf16[4,256,256]{2,1,0:T(8,128)(2,1)S(1)} %get-tuple-element.34), channel_id=1, replica_groups=mesh['z'=16,'yl'=2,'core'=2,'yh'=2,'x'=4] {'x'}, dimensions={0} | all-to-all | bytes 1048576 | tf_op jit(solution)/shard_map/all_to_all | solution.py:442
  96.5 3.4 %grad.1 = bf16[32,144,128]{2,1,0:T(8,128)(2,1)S(1)} custom-call(bf16[128,2048]{1,0:T(8,128)(2,1)S(1)} %copy-done.1, bf16[128,2048]{1,0:T(8,128)(2,1)S(1)} %collective-permute-done.refs_1_, bf16[128,2048]{1,0:T(8,128)(2,1)} %collective-permute-done.1.refs_2_, bf16[128,2048]{1,0:T(8,128)(2,1)} %collective-permute-done.2.refs_3_, ...), custom_call_target="tpu_custom_call" | custom-call | flops 1073741824 | bytes 5898772 | tf_op jit(solution)/shard_map/grad/pallas_call | solution.py:31
  99.8 22.6 %all_to_all.32.got_ref = bf16[32,144,128]{2,1,0:T(8,128)(2,1)S(1)} all-to-all(bf16[32,144,128]{2,1,0:T(8,128)(2,1)S(1)} %grad.1), channel_id=1, replica_groups=mesh['z'=16,'yl'=2,'core'=2,'yh'=2,'x'=4] {'yl','core','yh','x'}, dimensions={0} | all-to-all | bytes 2359296 | tf_op jit(solution)/shard_map/all_to_all | solution.py:457
  122.5 0.0 copy-start.2
  122.5 1.3 gather.1
  123.8 24.9 %all_to_all.33.got_ref = bf16[16,48,128]{2,1,0:T(8,128)(2,1)S(1)} all-to-all(bf16[16,48,128]{2,1,0:T(8,128)(2,1)S(1)} %gather.1), channel_id=1, replica_groups=mesh['z'=16,'yl'=2,'core'=2,'yh'=2,'x'=4] {'z'}, dimensions={0} | all-to-all | bytes 393216 | tf_op jit(solution)/shard_map/all_to_all | solution.py:466
  148.7 0.0 copy-done.2
  148.7 0.9 final.1
Async XLA Ops:
  3.9 41.5 %all-to-all-start = ((bf16[128,8,128]{2,1,0:T(8,128)(2,1)}), bf16[128,8,128]{2,1,0:T(8,128)(2,1)S(1)}, u32[]{:S(2)}, u32[]{:S(2)}) async-start(bf16[128,8,128]{2,1,0:T(8,128)(2,1)} %bitcast.16), calls=%async_computation | async-start | bytes 524288 | tf_op jit(solution)/shard_map/all_to_all | solution.py:366
  28.2 24.9 %collective-permute-start = (bf16[128,2048]{1,0:T(8,128)(2,1)}, bf16[128,2048]{1,0:T(8,128)(2,1)S(1)}, u32[]{:S(2)}, u32[]{:S(2)}) collective-permute-start(bf16[128,2048]{1,0:T(8,128)(2,1)} %get-tuple-element.22), channel_id=1, source_target_pairs={{0,2},{1,3},{2,0},{3,1},{4,6},{5,7},{6,4},{7,5},{8,10},{9,11},{10,... | collective-permute-start | bytes 1572872 | tf_op jit(solution)/shard_map/ppermute | solution.py:387
  31.6 26.7 %collective-permute-start.2 = (bf16[128,2048]{1,0:T(8,128)(2,1)}, bf16[128,2048]{1,0:T(8,128)(2,1)}, u32[]{:S(2)}, u32[]{:S(2)}) collective-permute-start(bf16[128,2048]{1,0:T(8,128)(2,1)} %get-tuple-element.24), channel_id=1, source_target_pairs={{0,3},{1,0},{2,1},{3,2},{4,7},{5,4},{6,5},{7,6},{8,11},{9,8},{10,9... | collective-permute-start | bytes 1572872 | tf_op jit(solution)/shard_map/ppermute | solution.py:387
  33.8 26.4 %collective-permute-start.1 = (bf16[128,2048]{1,0:T(8,128)(2,1)}, bf16[128,2048]{1,0:T(8,128)(2,1)}, u32[]{:S(2)}, u32[]{:S(2)}) collective-permute-start(bf16[128,2048]{1,0:T(8,128)(2,1)} %get-tuple-element.23), channel_id=1, source_target_pairs={{0,1},{1,2},{2,3},{3,0},{4,5},{5,6},{6,7},{7,4},{8,9},{9,10},{10,1... | collective-permute-start | bytes 1572872 | tf_op jit(solution)/shard_map/ppermute | solution.py:387
  45.4 5.7 %copy-start.1 = (bf16[128,2048]{1,0:T(8,128)(2,1)S(1)}, bf16[128,2048]{1,0:T(8,128)(2,1)}, u32[]{:S(2)}) copy-start(bf16[128,2048]{1,0:T(8,128)(2,1)} %get-tuple-element.21.refs_0_) | copy-start | bytes 1572868
  45.4 10.1 %copy-start = (s32[2048,64]{0,1:T(8,128)S(1)}, s32[2048,64]{0,1:T(8,128)}, u32[]{:S(2)}) copy-start(s32[2048,64]{0,1:T(8,128)} %param.9) | copy-start | bytes 1572868
  45.4 10.1 %copy-start.3 = (s32[5]{0:T(128)S(1)}, s32[5]{0:T(128)}, u32[]{:S(2)}) copy-start(s32[5]{0:T(128)} %stack.23.at_ref.refs_9_.refs_8_) | copy-start | bytes 64
  46.7 17.7 %all-to-all-start.1 = ((bf16[4,1024,128]{2,1,0:T(8,128)(2,1)}), bf16[4,1024,128]{2,1,0:T(8,128)(2,1)S(1)}, u32[]{:S(2)}, u32[]{:S(2)}) async-start(bf16[4,1024,128]{2,1,0:T(8,128)(2,1)} %spread.1), calls=%async_computation.1 | async-start | bytes 2097152 | tf_op jit(solution)/shard_map/all_to_all | solution.py:395
  51.1 14.1 %collective-permute-start.3 = (bf16[128,2048]{1,0:T(8,128)(2,1)S(1)}, bf16[128,2048]{1,0:T(8,128)(2,1)}, u32[]{:S(2)}, u32[]{:S(2)}) collective-permute-start(bf16[128,2048]{1,0:T(8,128)(2,1)S(1)} %copy-done.1), channel_id=1, source_target_pairs={{0,8},{8,0},{1,9},{9,1},{2,10},{10,2},{3,11},{11,3},{4,12},{12,4},... | collective-permute-start | bytes 1572872 | tf_op jit(solution)/shard_map/ppermute | solution.py:407
  53.1 12.2 %collective-permute-start.4 = (bf16[128,2048]{1,0:T(8,128)(2,1)S(1)}, bf16[128,2048]{1,0:T(8,128)(2,1)}, u32[]{:S(2)}, u32[]{:S(2)}) collective-permute-start(bf16[128,2048]{1,0:T(8,128)(2,1)S(1)} %collective-permute-done.refs_1_), channel_id=1, source_target_pairs={{0,8},{8,0},{1,9},{9,1},{2,10},{10,2},{3,11},{11,3},{4,12},{12,4},... | collective-permute-start | bytes 1572872 | tf_op jit(solution)/shard_map/ppermute | solution.py:407
  58.2 7.0 %collective-permute-start.5 = (bf16[128,2048]{1,0:T(8,128)(2,1)}, bf16[128,2048]{1,0:T(8,128)(2,1)}, u32[]{:S(2)}, u32[]{:S(2)}) collective-permute-start(bf16[128,2048]{1,0:T(8,128)(2,1)} %collective-permute-done.2.refs_3_), channel_id=1, source_target_pairs={{0,8},{8,0},{1,9},{9,1},{2,10},{10,2},{3,11},{11,3},{4,12},{12,4},... | collective-permute-start | bytes 1572872 | tf_op jit(solution)/shard_map/ppermute | solution.py:407
  60.2 9.9 %collective-permute-start.6 = (bf16[128,2048]{1,0:T(8,128)(2,1)}, bf16[128,2048]{1,0:T(8,128)(2,1)S(1)}, u32[]{:S(2)}, u32[]{:S(2)}) collective-permute-start(bf16[128,2048]{1,0:T(8,128)(2,1)} %collective-permute-done.1.refs_2_), channel_id=1, source_target_pairs={{0,8},{8,0},{1,9},{9,1},{2,10},{10,2},{3,11},{11,3},{4,12},{12,4},... | collective-permute-start | bytes 1572872 | tf_op jit(solution)/shard_map/ppermute | solution.py:407
  122.5 26.2 %copy-start.2 = (f32[64,128]{1,0:T(8,128)S(1)}, f32[64,128]{1,0:T(8,128)}, u32[]{:S(2)}) copy-start(f32[64,128]{1,0:T(8,128)} %get-tuple-element.37.pat_ref) | copy-start | bytes 98308

commit v14 on v13

--- a/solution.py
+++ b/solution.py
@@ -216,17 +216,17 @@
 
 
 def forward_most_kernel(*refs):
-    own, pair, rest = refs[:NX], refs[NX : NX + 3], refs[NX + 3 :]
-    high_ref, low_ref, at_ref, out_ref, held_ref, sems = rest
-    loads = [pltpu.make_async_copy(pair[i], held_ref.at[i], sems.at[i]) for i in range(3)]
+    pieces, (high_ref, low_ref, at_ref, out_ref, held_ref, sems) = refs[: NX + 3], refs[NX + 3 :]
+    loads = [
+        pltpu.make_async_copy(piece, held_ref.at[i], sems.at[i]) for i, piece in enumerate(pieces)
+    ]
     for load in loads:
         load.start()
-    for i in range(NX):
-        out_ref[(at_ref[0] + BACK[i]) % NX, :128] = forward(own[i][...], high_ref, low_ref)
-    for i in range(3):
-        loads[i].wait()
-        x = (at_ref[0] + BACK[SOON[i]]) % NX
-        out_ref[x, 128:] = forward(held_ref[i], high_ref, low_ref)
+    for i, load in enumerate(loads):
+        load.wait()
+        back, row = (BACK[i], 0) if i < NX else (BACK[SOON[i - NX]], 128)
+        x = (at_ref[0] + back) % NX
+        out_ref[x, row : row + 128] = forward(held_ref[i], high_ref, low_ref)
     out_ref[(at_ref[0] + BACK[LAST]) % NX, 128:] = jnp.zeros((128, 256), BF16)
 
 
@@ -259,8 +259,7 @@
 
 
 def grad_kernel(*refs):
-    own, (soon_ref, last_ref, *rest) = refs[:NX], refs[NX:]
-    slope_ref, loss_ref, at_ref, out_ref, s_ref, term_ref = rest
+    held_ref, last_ref, slope_ref, loss_ref, at_ref, out_ref, s_ref, term_ref = refs
     contract = (((0,), (0,)), ((), ()))
     for i in range(NX):
         x = (at_ref[0] + BACK[i]) % NX
@@ -268,10 +267,8 @@
         s_ref[512 + i * 128 : 512 + (i + 1) * 128] = slope_ref[x, 128:]
     for k in range(8):
         at = k * 256
-        rows = [ref[:, at : at + 256] for ref in own]
-        pair = [soon_ref[i, :, at : at + 256] for i in range(3)]
-        pair.insert(LAST, last_ref[:, at : at + 256])
-        rows += pair
+        rows = [held_ref[i, :, at : at + 256] for i in range(NX + 3)]
+        rows.insert(NX + LAST, last_ref[:, at : at + 256])
         rows = jnp.concatenate(rows, axis=0)
         term = lax.dot_general(rows, s_ref[...], contract, preferred_element_type=F32)
         for yh in range(2):
@@ -409,17 +406,17 @@
     high, low = call(decode_kernel, (shape((2048, 256), BF16),) * 2, all_w, name="decode")
 
     flops = 2 * 1024 * 2048 * 256
-    part, soon = call(
+    part, held = call(
         forward_most_kernel,
-        (shape((NX, 256, 256), BF16), shape((3, 128, 2048), BF16)),
+        (shape((NX, 256, 256), BF16), shape((NX + 3, 128, 2048), BF16)),
         *own,
         *(pair[i] for i in SOON),
         high,
         low,
         at,
-        scratch=[pltpu.SemaphoreType.DMA((3,))],
+        scratch=[pltpu.SemaphoreType.DMA((NX + 3,))],
         flops=2 * flops * 7 // 8,
-        far=range(NX, NX + 3),
+        far=range(NX + 3),
         name="forward_most",
     )
     part, last = call(
@@ -444,8 +441,7 @@
     term = call(
         grad_kernel,
         shape((32, 144, 128), BF16),
-        *own,
-        soon,
+        held,
         last,
         slopes,
         loss_part,

time: 152 us -> 151 us (level)
  no operation moved by 1% of the time
where the time goes in v14:
time: 151 us; the launch traced here: 149 us
  blocking collectives  72.8 us (48%)
  starting transfers between devices  43 us (28%)
  Pallas kernels  22.1 us (15%)
  waiting for transfers between devices  9.97 us (7%)
    all_to_all x1, blocking collectives, shards(): got_sum = lax.all_to_all(packed_term, 'z', 0, 0, tiled=True)  25 us
    all_to_all x1, blocking collectives, shards(): got_term = lax.all_to_all(term, PLANE, 0, 0, tiled=True)  22.6 us
    pallas_call x11, Pallas kernels, call(): pl.pallas_call(kernel, out_shape=out_shape, in_specs=specs, out_specs=jax...  22.1 us
    all_to_all x1, starting transfers between devices, shards(): got_w = lax.all_to_all(packed.reshape(128, 8, 128), ZCX, 0, 0, tiled=True)  19.4 us
    all_to_all x1, blocking collectives, shards(): got_part = lax.all_to_all(part, 'x', 0, 0, tiled=True)  14.1 us
    all_to_all x1, blocking collectives, shards(): slopes = lax.all_to_all(slope, 'x', 0, 0, tiled=True)  11 us
    ppermute x3, starting transfers between devices, shards(): lax.ppermute(split[i], 'x', ring(STEP[i]))  10.6 us
    ppermute x4, starting transfers between devices, shards(): pair = [lax.ppermute(piece, 'core', [(0, 1), (1, 0)]) for piece in own]  8.63 us
  transfers between devices with their start and end apart: 9, of which 3 were waited for; matrix products, arithmetic and copies ran while one was open for 0% of the time, Pallas kernels for 9%

profile of v14, /device:TPU:6, one launch (start us, length us, event | category | flops | bytes accessed | tf_op | source)
XLA Modules:
  0.0 149.4 jit_solution(2817018460852081025)
XLA Ops:
  0.6 0.7 stack.23.at_ref.refs_9_.refs_4_
  1.3 2.6 %pack.1 = (bf16[16,64,128]{2,1,0:T(8,128)(2,1)}, f32[64,128]{1,0:T(8,128)}) custom-call(bf16[64,128]{1,0:T(8,128)(2,1)} %bitcast.17, bf16[64,128]{1,0:T(8,128)(2,1)} %bitcast.18, s32[64,2048]{1,0:T(8,128)} %bitcast.13, s32[5]{0:T(128)} %stack.23.at_ref.refs_9_.refs_4_), custom_call_target="tpu_custom_call" | custom-call | bytes 851988 | tf_op jit(solution)/shard_map/pack/pallas_call | solution.py:31
  3.9 19.4 %all-to-all-start = ((bf16[128,8,128]{2,1,0:T(8,128)(2,1)}), bf16[128,8,128]{2,1,0:T(8,128)(2,1)S(1)}, u32[]{:S(2)}, u32[]{:S(2)}) async-start(bf16[128,8,128]{2,1,0:T(8,128)(2,1)} %bitcast.16), calls=%async_computation | async-start | bytes 524288 | tf_op jit(solution)/shard_map/all_to_all | solution.py:363
  23.3 4.9 %norm.1 = (bf16[128,2048]{1,0:T(8,128)(2,1)}, bf16[128,2048]{1,0:T(8,128)(2,1)}, bf16[128,2048]{1,0:T(8,128)(2,1)}, bf16[128,2048]{1,0:T(8,128)(2,1)}) custom-call(bf16[128,8192]{1,0:T(8,128)(2,1)} %x_hbm.1, bf16[64,128]{1,0:T(8,128)(2,1)} %bitcast.20, s32[5]{0:T(128)} %stack.23.at_ref.refs_9_.refs_4_), custom_call_target="tpu_custom_call" | custom-call | flops 1073741824 | bytes 4210708 | tf_op jit(solution)/shard_map/norm/pallas_call | solution.py:31
  28.2 0.0 copy-start.3
  28.2 0.0 copy-start
  28.2 0.0 copy-start.2
  28.2 3.5 %collective-permute-start = (bf16[128,2048]{1,0:T(8,128)(2,1)}, bf16[128,2048]{1,0:T(8,128)(2,1)S(1)}, u32[]{:S(2)}, u32[]{:S(2)}) collective-permute-start(bf16[128,2048]{1,0:T(8,128)(2,1)} %get-tuple-element.22), channel_id=1, source_target_pairs={{0,2},{1,3},{2,0},{3,1},{4,6},{5,7},{6,4},{7,5},{8,10},{9,11},{10,... | collective-permute-start | bytes 1572872 | tf_op jit(solution)/shard_map/ppermute | solution.py:384
  31.7 2.2 %collective-permute-start.2 = (bf16[128,2048]{1,0:T(8,128)(2,1)}, bf16[128,2048]{1,0:T(8,128)(2,1)}, u32[]{:S(2)}, u32[]{:S(2)}) collective-permute-start(bf16[128,2048]{1,0:T(8,128)(2,1)} %get-tuple-element.24), channel_id=1, source_target_pairs={{0,3},{1,0},{2,1},{3,2},{4,7},{5,4},{6,5},{7,6},{8,11},{9,8},{10,9... | collective-permute-start | bytes 1572872 | tf_op jit(solution)/shard_map/ppermute | solution.py:384
  33.9 4.9 %collective-permute-start.1 = (bf16[128,2048]{1,0:T(8,128)(2,1)}, bf16[128,2048]{1,0:T(8,128)(2,1)}, u32[]{:S(2)}, u32[]{:S(2)}) collective-permute-start(bf16[128,2048]{1,0:T(8,128)(2,1)} %get-tuple-element.23), channel_id=1, source_target_pairs={{0,1},{1,2},{2,3},{3,0},{4,5},{5,6},{6,7},{7,4},{8,9},{9,10},{10,1... | collective-permute-start | bytes 1572872 | tf_op jit(solution)/shard_map/ppermute | solution.py:384
  38.8 6.6 %all-to-all-done = bf16[128,8,128]{2,1,0:T(8,128)(2,1)S(1)} async-done(((bf16[128,8,128]{2,1,0:T(8,128)(2,1)}), bf16[128,8,128]{2,1,0:T(8,128)(2,1)S(1)}, u32[]{:S(2)}, u32[]{:S(2)}) %all-to-all-start) | async-done | bytes 262176 | tf_op jit(solution)/shard_map/all_to_all | solution.py:363
  45.4 1.3 spread.1
  46.7 4.5 %all-to-all-start.1 = ((bf16[4,1024,128]{2,1,0:T(8,128)(2,1)}), bf16[4,1024,128]{2,1,0:T(8,128)(2,1)S(1)}, u32[]{:S(2)}, u32[]{:S(2)}) async-start(bf16[4,1024,128]{2,1,0:T(8,128)(2,1)} %spread.1), calls=%async_computation.1 | async-start | bytes 2097152 | tf_op jit(solution)/shard_map/all_to_all | solution.py:392
  51.1 0.0 copy-done.3
  51.1 1.9 %collective-permute-start.3 = (bf16[128,2048]{1,0:T(8,128)(2,1)S(1)}, bf16[128,2048]{1,0:T(8,128)(2,1)}, u32[]{:S(2)}, u32[]{:S(2)}) collective-permute-start(bf16[128,2048]{1,0:T(8,128)(2,1)S(1)} %copy-done.3), channel_id=1, source_target_pairs={{0,8},{8,0},{1,9},{9,1},{2,10},{10,2},{3,11},{11,3},{4,12},{12,4},... | collective-permute-start | bytes 1572872 | tf_op jit(solution)/shard_map/ppermute | solution.py:404
  53.1 0.0 collective-permute-done.refs_1_
  53.1 2.4 %collective-permute-start.4 = (bf16[128,2048]{1,0:T(8,128)(2,1)S(1)}, bf16[128,2048]{1,0:T(8,128)(2,1)}, u32[]{:S(2)}, u32[]{:S(2)}) collective-permute-start(bf16[128,2048]{1,0:T(8,128)(2,1)S(1)} %collective-permute-done.refs_1_), channel_id=1, source_target_pairs={{0,8},{8,0},{1,9},{9,1},{2,10},{10,2},{3,11},{11,3},{4,12},{12,4},... | collective-permute-start | bytes 1572872 | tf_op jit(solution)/shard_map/ppermute | solution.py:404
  55.5 0.0 copy-done
  55.5 0.0 copy-done.2
  55.5 1.1 choose.1.pat_ref
  56.6 1.7 %collective-permute-done.2.refs_3_ = bf16[128,2048]{1,0:T(8,128)(2,1)} collective-permute-done((bf16[128,2048]{1,0:T(8,128)(2,1)}, bf16[128,2048]{1,0:T(8,128)(2,1)}, u32[]{:S(2)}, u32[]{:S(2)}) %collective-permute-start.2) | collective-permute-done | bytes 524320 | tf_op jit(solution)/shard_map/ppermute | solution.py:384
  58.3 2.0 %collective-permute-start.5 = (bf16[128,2048]{1,0:T(8,128)(2,1)}, bf16[128,2048]{1,0:T(8,128)(2,1)}, u32[]{:S(2)}, u32[]{:S(2)}) collective-permute-start(bf16[128,2048]{1,0:T(8,128)(2,1)} %collective-permute-done.2.refs_3_), channel_id=1, source_target_pairs={{0,8},{8,0},{1,9},{9,1},{2,10},{10,2},{3,11},{11,3},{4,12},{12,4},... | collective-permute-start | bytes 1572872 | tf_op jit(solution)/shard_map/ppermute | solution.py:404
  60.3 0.0 collective-permute-done.1.refs_2_
  60.3 2.4 %collective-permute-start.6 = (bf16[128,2048]{1,0:T(8,128)(2,1)}, bf16[128,2048]{1,0:T(8,128)(2,1)S(1)}, u32[]{:S(2)}, u32[]{:S(2)}) collective-permute-start(bf16[128,2048]{1,0:T(8,128)(2,1)} %collective-permute-done.1.refs_2_), channel_id=1, source_target_pairs={{0,8},{8,0},{1,9},{9,1},{2,10},{10,2},{3,11},{11,3},{4,12},{12,4},... | collective-permute-start | bytes 1572872 | tf_op jit(solution)/shard_map/ppermute | solution.py:404
  62.7 1.6 %all-to-all-done.1.w_ref = bf16[4,1024,128]{2,1,0:T(8,128)(2,1)S(1)} async-done(((bf16[4,1024,128]{2,1,0:T(8,128)(2,1)}), bf16[4,1024,128]{2,1,0:T(8,128)(2,1)S(1)}, u32[]{:S(2)}, u32[]{:S(2)}) %all-to-all-start.1) | async-done | bytes 1048608 | tf_op jit(solution)/shard_map/all_to_all | solution.py:392
  64.3 0.9 decode.1
  65.2 0.0 collective-permute-done.3.refs_4_
  65.2 0.0 collective-permute-done.4.refs_5_
  65.2 0.0 collective-permute-done.5.refs_6_
  65.2 5.3 %forward_most.1 = (bf16[4,256,256]{2,1,0:T(8,128)(2,1)S(1)}, bf16[7,128,2048]{2,1,0:T(8,128)(2,1)S(1)}) custom-call(bf16[128,2048]{1,0:T(8,128)(2,1)S(1)} %copy-done.3, bf16[128,2048]{1,0:T(8,128)(2,1)S(1)} %collective-permute-done.refs_1_, bf16[128,2048]{1,0:T(8,128)(2,1)} %collective-permute-done.1.refs_2_, ...), custom_call_target="tpu_custom_call" | custom-call | flops 1879048192 | bytes 9961492 | tf_op jit(solution)/shard_map/forward_most/pallas_call | solution.py:31
  70.5 0.0 collective-permute-done.6.pair_hbm
  70.5 1.1 forward_last.1
  71.6 14.1 %all_to_all.30.part_ref = bf16[4,256,256]{2,1,0:T(8,128)(2,1)S(1)} all-to-all(bf16[4,256,256]{2,1,0:T(8,128)(2,1)S(1)} %get-tuple-element.33), channel_id=1, replica_groups=mesh['z'=16,'yl'=2,'core'=2,'yh'=2,'x'=4] {'x'}, dimensions={0} | all-to-all | bytes 1048576 | tf_op jit(solution)/shard_map/all_to_all | solution.py:435
  85.8 0.1 slope.1
  85.9 11.0 %all_to_all.31.refs_2_ = bf16[4,256,256]{2,1,0:T(8,128)(2,1)S(1)} all-to-all(bf16[4,256,256]{2,1,0:T(8,128)(2,1)S(1)} %get-tuple-element.34), channel_id=1, replica_groups=mesh['z'=16,'yl'=2,'core'=2,'yh'=2,'x'=4] {'x'}, dimensions={0} | all-to-all | bytes 1048576 | tf_op jit(solution)/shard_map/all_to_all | solution.py:439
  96.9 2.7 %grad.1 = bf16[32,144,128]{2,1,0:T(8,128)(2,1)S(1)} custom-call(bf16[7,128,2048]{2,1,0:T(8,128)(2,1)S(1)} %get-tuple-element.30.refs_0_, bf16[128,2048]{1,0:T(8,128)(2,1)S(1)} %get-tuple-element.32.refs_1_, bf16[4,256,256]{2,1,0:T(8,128)(2,1)S(1)} %all_to_all.31.refs_2_, f32[1,128]{1,0:T(1,128)S(1)} %get-tuple-element.35.refs_3_, s32[5]{0:T(128)S(1)} %copy-done.2), custom_call_target="tpu_custom_call" | custom-call | flops 1073741824 | bytes 5898772 | tf_op jit(solution)/shard_map/grad/pallas_call | solution.py:31
  99.6 0.0 copy-start.1
  99.6 22.6 %all_to_all.32.got_ref = bf16[32,144,128]{2,1,0:T(8,128)(2,1)S(1)} all-to-all(bf16[32,144,128]{2,1,0:T(8,128)(2,1)S(1)} %grad.1), channel_id=1, replica_groups=mesh['z'=16,'yl'=2,'core'=2,'yh'=2,'x'=4] {'yl','core','yh','x'}, dimensions={0} | all-to-all | bytes 2359296 | tf_op jit(solution)/shard_map/all_to_all | solution.py:453
  122.2 1.3 gather.1
  123.5 25.0 %all_to_all.33.got_ref = bf16[16,48,128]{2,1,0:T(8,128)(2,1)S(1)} all-to-all(bf16[16,48,128]{2,1,0:T(8,128)(2,1)S(1)} %gather.1), channel_id=1, replica_groups=mesh['z'=16,'yl'=2,'core'=2,'yh'=2,'x'=4] {'z'}, dimensions={0} | all-to-all | bytes 393216 | tf_op jit(solution)/shard_map/all_to_all | solution.py:462
  148.6 0.0 copy-done.1
  148.6 0.9 final.1
Async XLA Ops:
  3.9 41.5 %all-to-all-start = ((bf16[128,8,128]{2,1,0:T(8,128)(2,1)}), bf16[128,8,128]{2,1,0:T(8,128)(2,1)S(1)}, u32[]{:S(2)}, u32[]{:S(2)}) async-start(bf16[128,8,128]{2,1,0:T(8,128)(2,1)} %bitcast.16), calls=%async_computation | async-start | bytes 524288 | tf_op jit(solution)/shard_map/all_to_all | solution.py:363
  28.2 22.9 %copy-start.3 = (bf16[128,2048]{1,0:T(8,128)(2,1)S(1)}, bf16[128,2048]{1,0:T(8,128)(2,1)}, u32[]{:S(2)}) copy-start(bf16[128,2048]{1,0:T(8,128)(2,1)} %get-tuple-element.21.refs_0_) | copy-start | bytes 1572868
  28.2 27.3 %copy-start = (s32[2048,64]{0,1:T(8,128)S(1)}, s32[2048,64]{0,1:T(8,128)}, u32[]{:S(2)}) copy-start(s32[2048,64]{0,1:T(8,128)} %param.9) | copy-start | bytes 1572868
  28.2 27.3 %copy-start.2 = (s32[5]{0:T(128)S(1)}, s32[5]{0:T(128)}, u32[]{:S(2)}) copy-start(s32[5]{0:T(128)} %stack.23.at_ref.refs_9_.refs_4_) | copy-start | bytes 64
  28.2 24.8 %collective-permute-start = (bf16[128,2048]{1,0:T(8,128)(2,1)}, bf16[128,2048]{1,0:T(8,128)(2,1)S(1)}, u32[]{:S(2)}, u32[]{:S(2)}) collective-permute-start(bf16[128,2048]{1,0:T(8,128)(2,1)} %get-tuple-element.22), channel_id=1, source_target_pairs={{0,2},{1,3},{2,0},{3,1},{4,6},{5,7},{6,4},{7,5},{8,10},{9,11},{10,... | collective-permute-start | bytes 1572872 | tf_op jit(solution)/shard_map/ppermute | solution.py:384
  31.7 26.6 %collective-permute-start.2 = (bf16[128,2048]{1,0:T(8,128)(2,1)}, bf16[128,2048]{1,0:T(8,128)(2,1)}, u32[]{:S(2)}, u32[]{:S(2)}) collective-permute-start(bf16[128,2048]{1,0:T(8,128)(2,1)} %get-tuple-element.24), channel_id=1, source_target_pairs={{0,3},{1,0},{2,1},{3,2},{4,7},{5,4},{6,5},{7,6},{8,11},{9,8},{10,9... | collective-permute-start | bytes 1572872 | tf_op jit(solution)/shard_map/ppermute | solution.py:384
  33.9 26.4 %collective-permute-start.1 = (bf16[128,2048]{1,0:T(8,128)(2,1)}, bf16[128,2048]{1,0:T(8,128)(2,1)}, u32[]{:S(2)}, u32[]{:S(2)}) collective-permute-start(bf16[128,2048]{1,0:T(8,128)(2,1)} %get-tuple-element.23), channel_id=1, source_target_pairs={{0,1},{1,2},{2,3},{3,0},{4,5},{5,6},{6,7},{7,4},{8,9},{9,10},{10,1... | collective-permute-start | bytes 1572872 | tf_op jit(solution)/shard_map/ppermute | solution.py:384
  46.7 17.7 %all-to-all-start.1 = ((bf16[4,1024,128]{2,1,0:T(8,128)(2,1)}), bf16[4,1024,128]{2,1,0:T(8,128)(2,1)S(1)}, u32[]{:S(2)}, u32[]{:S(2)}) async-start(bf16[4,1024,128]{2,1,0:T(8,128)(2,1)} %spread.1), calls=%async_computation.1 | async-start | bytes 2097152 | tf_op jit(solution)/shard_map/all_to_all | solution.py:392
  51.1 14.1 %collective-permute-start.3 = (bf16[128,2048]{1,0:T(8,128)(2,1)S(1)}, bf16[128,2048]{1,0:T(8,128)(2,1)}, u32[]{:S(2)}, u32[]{:S(2)}) collective-permute-start(bf16[128,2048]{1,0:T(8,128)(2,1)S(1)} %copy-done.3), channel_id=1, source_target_pairs={{0,8},{8,0},{1,9},{9,1},{2,10},{10,2},{3,11},{11,3},{4,12},{12,4},... | collective-permute-start | bytes 1572872 | tf_op jit(solution)/shard_map/ppermute | solution.py:404
  53.1 12.2 %collective-permute-start.4 = (bf16[128,2048]{1,0:T(8,128)(2,1)S(1)}, bf16[128,2048]{1,0:T(8,128)(2,1)}, u32[]{:S(2)}, u32[]{:S(2)}) collective-permute-start(bf16[128,2048]{1,0:T(8,128)(2,1)S(1)} %collective-permute-done.refs_1_), channel_id=1, source_target_pairs={{0,8},{8,0},{1,9},{9,1},{2,10},{10,2},{3,11},{11,3},{4,12},{12,4},... | collective-permute-start | bytes 1572872 | tf_op jit(solution)/shard_map/ppermute | solution.py:404
  58.3 6.9 %collective-permute-start.5 = (bf16[128,2048]{1,0:T(8,128)(2,1)}, bf16[128,2048]{1,0:T(8,128)(2,1)}, u32[]{:S(2)}, u32[]{:S(2)}) collective-permute-start(bf16[128,2048]{1,0:T(8,128)(2,1)} %collective-permute-done.2.refs_3_), channel_id=1, source_target_pairs={{0,8},{8,0},{1,9},{9,1},{2,10},{10,2},{3,11},{11,3},{4,12},{12,4},... | collective-permute-start | bytes 1572872 | tf_op jit(solution)/shard_map/ppermute | solution.py:404
  60.3 10.2 %collective-permute-start.6 = (bf16[128,2048]{1,0:T(8,128)(2,1)}, bf16[128,2048]{1,0:T(8,128)(2,1)S(1)}, u32[]{:S(2)}, u32[]{:S(2)}) collective-permute-start(bf16[128,2048]{1,0:T(8,128)(2,1)} %collective-permute-done.1.refs_2_), channel_id=1, source_target_pairs={{0,8},{8,0},{1,9},{9,1},{2,10},{10,2},{3,11},{11,3},{4,12},{12,4},... | collective-permute-start | bytes 1572872 | tf_op jit(solution)/shard_map/ppermute | solution.py:404
  99.6 49.0 %copy-start.1 = (f32[64,128]{1,0:T(8,128)S(1)}, f32[64,128]{1,0:T(8,128)}, u32[]{:S(2)}) copy-start(f32[64,128]{1,0:T(8,128)} %get-tuple-element.37.pat_ref) | copy-start | bytes 98308

commit v15 on v14

--- a/solution.py
+++ b/solution.py
@@ -216,17 +216,20 @@
 
 
 def forward_most_kernel(*refs):
-    pieces, (high_ref, low_ref, at_ref, out_ref, held_ref, sems) = refs[: NX + 3], refs[NX + 3 :]
-    loads = [
-        pltpu.make_async_copy(piece, held_ref.at[i], sems.at[i]) for i, piece in enumerate(pieces)
-    ]
+    near, far, rest = refs[:2], refs[2:7], refs[7:]
+    high_ref, low_ref, at_ref, out_ref, held_ref, sems = rest
+    loads = [pltpu.make_async_copy(piece, held_ref.at[i], sems.at[i]) for i, piece in enumerate(far)]
     for load in loads:
         load.start()
-    for i, load in enumerate(loads):
-        load.wait()
+    for i in range(NX + 3):
+        if i < 2:
+            rows = near[i][...]
+        else:
+            loads[i - 2].wait()
+            rows = held_ref[i - 2]
         back, row = (BACK[i], 0) if i < NX else (BACK[SOON[i - NX]], 128)
         x = (at_ref[0] + back) % NX
-        out_ref[x, row : row + 128] = forward(held_ref[i], high_ref, low_ref)
+        out_ref[x, row : row + 128] = forward(rows, high_ref, low_ref)
     out_ref[(at_ref[0] + BACK[LAST]) % NX, 128:] = jnp.zeros((128, 256), BF16)
 
 
@@ -259,7 +262,8 @@
 
 
 def grad_kernel(*refs):
-    held_ref, last_ref, slope_ref, loss_ref, at_ref, out_ref, s_ref, term_ref = refs
+    near, (held_ref, last_ref, *rest) = refs[:2], refs[2:]
+    slope_ref, loss_ref, at_ref, out_ref, s_ref, term_ref = rest
     contract = (((0,), (0,)), ((), ()))
     for i in range(NX):
         x = (at_ref[0] + BACK[i]) % NX
@@ -267,7 +271,8 @@
         s_ref[512 + i * 128 : 512 + (i + 1) * 128] = slope_ref[x, 128:]
     for k in range(8):
         at = k * 256
-        rows = [held_ref[i, :, at : at + 256] for i in range(NX + 3)]
+        rows = [ref[:, at : at + 256] for ref in near]
+        rows += [held_ref[i, :, at : at + 256] for i in range(NX + 1)]
         rows.insert(NX + LAST, last_ref[:, at : at + 256])
         rows = jnp.concatenate(rows, axis=0)
         term = lax.dot_general(rows, s_ref[...], contract, preferred_element_type=F32)
@@ -408,15 +413,15 @@
     flops = 2 * 1024 * 2048 * 256
     part, held = call(
         forward_most_kernel,
-        (shape((NX, 256, 256), BF16), shape((NX + 3, 128, 2048), BF16)),
+        (shape((NX, 256, 256), BF16), shape((NX + 1, 128, 2048), BF16)),
         *own,
         *(pair[i] for i in SOON),
         high,
         low,
         at,
-        scratch=[pltpu.SemaphoreType.DMA((NX + 3,))],
+        scratch=[pltpu.SemaphoreType.DMA((NX + 1,))],
         flops=2 * flops * 7 // 8,
-        far=range(NX + 3),
+        far=range(2, NX + 3),
         name="forward_most",
     )
     part, last = call(
@@ -441,6 +446,8 @@
     term = call(
         grad_kernel,
         shape((32, 144, 128), BF16),
+        own[0],
+        own[1],
         held,
         last,
         slopes,

time: 151 us -> 151 us (level)
  no operation moved by 1% of the time
where the time goes in v15:
time: 151 us; the launch traced here: 149 us
  blocking collectives  72.8 us (48%)
  starting transfers between devices  43 us (28%)
  Pallas kernels  21.9 us (15%)
  waiting for transfers between devices  9.97 us (7%)
    all_to_all x1, blocking collectives, shards(): got_sum = lax.all_to_all(packed_term, 'z', 0, 0, tiled=True)  25 us
    all_to_all x1, blocking collectives, shards(): got_term = lax.all_to_all(term, PLANE, 0, 0, tiled=True)  22.6 us
    pallas_call x11, Pallas kernels, call(): pl.pallas_call(kernel, out_shape=out_shape, in_specs=specs, out_specs=jax...  21.9 us
    all_to_all x1, starting transfers between devices, shards(): got_w = lax.all_to_all(packed.reshape(128, 8, 128), ZCX, 0, 0, tiled=True)  19.4 us
    all_to_all x1, blocking collectives, shards(): got_part = lax.all_to_all(part, 'x', 0, 0, tiled=True)  14.1 us
    all_to_all x1, blocking collectives, shards(): slopes = lax.all_to_all(slope, 'x', 0, 0, tiled=True)  11 us
    ppermute x3, starting transfers between devices, shards(): lax.ppermute(split[i], 'x', ring(STEP[i]))  10.6 us
    ppermute x4, starting transfers between devices, shards(): pair = [lax.ppermute(piece, 'core', [(0, 1), (1, 0)]) for piece in own]  8.63 us
  transfers between devices with their start and end apart: 9, of which 3 were waited for; matrix products, arithmetic and copies ran while one was open for 0% of the time, Pallas kernels for 9%

profile of v15, /device:TPU:6, one launch (start us, length us, event | category | flops | bytes accessed | tf_op | source)
XLA Modules:
  0.0 149.3 jit_solution(9936556018610038149)
XLA Ops:
  0.6 0.7 stack.23.at_ref.refs_9_.refs_6_
  1.3 2.6 %pack.1 = (bf16[16,64,128]{2,1,0:T(8,128)(2,1)}, f32[64,128]{1,0:T(8,128)}) custom-call(bf16[64,128]{1,0:T(8,128)(2,1)} %bitcast.17, bf16[64,128]{1,0:T(8,128)(2,1)} %bitcast.18, s32[64,2048]{1,0:T(8,128)} %bitcast.13, s32[5]{0:T(128)} %stack.23.at_ref.refs_9_.refs_6_), custom_call_target="tpu_custom_call" | custom-call | bytes 851988 | tf_op jit(solution)/shard_map/pack/pallas_call | solution.py:31
  3.9 19.4 %all-to-all-start = ((bf16[128,8,128]{2,1,0:T(8,128)(2,1)}), bf16[128,8,128]{2,1,0:T(8,128)(2,1)S(1)}, u32[]{:S(2)}, u32[]{:S(2)}) async-start(bf16[128,8,128]{2,1,0:T(8,128)(2,1)} %bitcast.16), calls=%async_computation | async-start | bytes 524288 | tf_op jit(solution)/shard_map/all_to_all | solution.py:368
  23.3 4.9 %norm.1 = (bf16[128,2048]{1,0:T(8,128)(2,1)}, bf16[128,2048]{1,0:T(8,128)(2,1)}, bf16[128,2048]{1,0:T(8,128)(2,1)}, bf16[128,2048]{1,0:T(8,128)(2,1)}) custom-call(bf16[128,8192]{1,0:T(8,128)(2,1)} %x_hbm.1, bf16[64,128]{1,0:T(8,128)(2,1)} %bitcast.20, s32[5]{0:T(128)} %stack.23.at_ref.refs_9_.refs_6_), custom_call_target="tpu_custom_call" | custom-call | flops 1073741824 | bytes 4210708 | tf_op jit(solution)/shard_map/norm/pallas_call | solution.py:31
  28.2 0.0 copy-start.1
  28.2 0.0 copy-start
  28.2 0.0 copy-start.3
  28.2 3.5 %collective-permute-start = (bf16[128,2048]{1,0:T(8,128)(2,1)}, bf16[128,2048]{1,0:T(8,128)(2,1)S(1)}, u32[]{:S(2)}, u32[]{:S(2)}) collective-permute-start(bf16[128,2048]{1,0:T(8,128)(2,1)} %get-tuple-element.22), channel_id=1, source_target_pairs={{0,2},{1,3},{2,0},{3,1},{4,6},{5,7},{6,4},{7,5},{8,10},{9,11},{10,... | collective-permute-start | bytes 1572872 | tf_op jit(solution)/shard_map/ppermute | solution.py:389
  31.7 2.2 %collective-permute-start.2 = (bf16[128,2048]{1,0:T(8,128)(2,1)}, bf16[128,2048]{1,0:T(8,128)(2,1)}, u32[]{:S(2)}, u32[]{:S(2)}) collective-permute-start(bf16[128,2048]{1,0:T(8,128)(2,1)} %get-tuple-element.24), channel_id=1, source_target_pairs={{0,3},{1,0},{2,1},{3,2},{4,7},{5,4},{6,5},{7,6},{8,11},{9,8},{10,9... | collective-permute-start | bytes 1572872 | tf_op jit(solution)/shard_map/ppermute | solution.py:389
  33.9 4.9 %collective-permute-start.1 = (bf16[128,2048]{1,0:T(8,128)(2,1)}, bf16[128,2048]{1,0:T(8,128)(2,1)}, u32[]{:S(2)}, u32[]{:S(2)}) collective-permute-start(bf16[128,2048]{1,0:T(8,128)(2,1)} %get-tuple-element.23), channel_id=1, source_target_pairs={{0,1},{1,2},{2,3},{3,0},{4,5},{5,6},{6,7},{7,4},{8,9},{9,10},{10,1... | collective-permute-start | bytes 1572872 | tf_op jit(solution)/shard_map/ppermute | solution.py:389
  38.8 6.6 %all-to-all-done = bf16[128,8,128]{2,1,0:T(8,128)(2,1)S(1)} async-done(((bf16[128,8,128]{2,1,0:T(8,128)(2,1)}), bf16[128,8,128]{2,1,0:T(8,128)(2,1)S(1)}, u32[]{:S(2)}, u32[]{:S(2)}) %all-to-all-start) | async-done | bytes 262176 | tf_op jit(solution)/shard_map/all_to_all | solution.py:368
  45.4 1.3 spread.1
  46.7 4.5 %all-to-all-start.1 = ((bf16[4,1024,128]{2,1,0:T(8,128)(2,1)}), bf16[4,1024,128]{2,1,0:T(8,128)(2,1)S(1)}, u32[]{:S(2)}, u32[]{:S(2)}) async-start(bf16[4,1024,128]{2,1,0:T(8,128)(2,1)} %spread.1), calls=%async_computation.1 | async-start | bytes 2097152 | tf_op jit(solution)/shard_map/all_to_all | solution.py:397
  51.1 0.0 copy-done.1
  51.1 1.9 %collective-permute-start.3 = (bf16[128,2048]{1,0:T(8,128)(2,1)S(1)}, bf16[128,2048]{1,0:T(8,128)(2,1)}, u32[]{:S(2)}, u32[]{:S(2)}) collective-permute-start(bf16[128,2048]{1,0:T(8,128)(2,1)S(1)} %copy-done.1), channel_id=1, source_target_pairs={{0,8},{8,0},{1,9},{9,1},{2,10},{10,2},{3,11},{11,3},{4,12},{12,4},... | collective-permute-start | bytes 1572872 | tf_op jit(solution)/shard_map/ppermute | solution.py:409
  53.1 0.0 collective-permute-done.refs_1_
  53.1 2.4 %collective-permute-start.4 = (bf16[128,2048]{1,0:T(8,128)(2,1)S(1)}, bf16[128,2048]{1,0:T(8,128)(2,1)}, u32[]{:S(2)}, u32[]{:S(2)}) collective-permute-start(bf16[128,2048]{1,0:T(8,128)(2,1)S(1)} %collective-permute-done.refs_1_), channel_id=1, source_target_pairs={{0,8},{8,0},{1,9},{9,1},{2,10},{10,2},{3,11},{11,3},{4,12},{12,4},... | collective-permute-start | bytes 1572872 | tf_op jit(solution)/shard_map/ppermute | solution.py:409
  55.5 0.0 copy-done
  55.5 0.0 copy-done.3
  55.5 1.1 choose.1.pat_ref
  56.6 1.7 %collective-permute-done.2.refs_3_ = bf16[128,2048]{1,0:T(8,128)(2,1)} collective-permute-done((bf16[128,2048]{1,0:T(8,128)(2,1)}, bf16[128,2048]{1,0:T(8,128)(2,1)}, u32[]{:S(2)}, u32[]{:S(2)}) %collective-permute-start.2) | collective-permute-done | bytes 524320 | tf_op jit(solution)/shard_map/ppermute | solution.py:389
  58.3 2.0 %collective-permute-start.5 = (bf16[128,2048]{1,0:T(8,128)(2,1)}, bf16[128,2048]{1,0:T(8,128)(2,1)}, u32[]{:S(2)}, u32[]{:S(2)}) collective-permute-start(bf16[128,2048]{1,0:T(8,128)(2,1)} %collective-permute-done.2.refs_3_), channel_id=1, source_target_pairs={{0,8},{8,0},{1,9},{9,1},{2,10},{10,2},{3,11},{11,3},{4,12},{12,4},... | collective-permute-start | bytes 1572872 | tf_op jit(solution)/shard_map/ppermute | solution.py:409
  60.3 0.0 collective-permute-done.1.refs_2_
  60.3 2.4 %collective-permute-start.6 = (bf16[128,2048]{1,0:T(8,128)(2,1)}, bf16[128,2048]{1,0:T(8,128)(2,1)S(1)}, u32[]{:S(2)}, u32[]{:S(2)}) collective-permute-start(bf16[128,2048]{1,0:T(8,128)(2,1)} %collective-permute-done.1.refs_2_), channel_id=1, source_target_pairs={{0,8},{8,0},{1,9},{9,1},{2,10},{10,2},{3,11},{11,3},{4,12},{12,4},... | collective-permute-start | bytes 1572872 | tf_op jit(solution)/shard_map/ppermute | solution.py:409
  62.7 1.6 %all-to-all-done.1.w_ref = bf16[4,1024,128]{2,1,0:T(8,128)(2,1)S(1)} async-done(((bf16[4,1024,128]{2,1,0:T(8,128)(2,1)}), bf16[4,1024,128]{2,1,0:T(8,128)(2,1)S(1)}, u32[]{:S(2)}, u32[]{:S(2)}) %all-to-all-start.1) | async-done | bytes 1048608 | tf_op jit(solution)/shard_map/all_to_all | solution.py:397
  64.3 0.9 decode.1
  65.2 0.0 collective-permute-done.3.refs_4_
  65.2 0.0 collective-permute-done.4.refs_5_
  65.2 0.0 collective-permute-done.5.refs_6_
  65.2 5.1 %forward_most.1 = (bf16[4,256,256]{2,1,0:T(8,128)(2,1)S(1)}, bf16[5,128,2048]{2,1,0:T(8,128)(2,1)S(1)}) custom-call(bf16[128,2048]{1,0:T(8,128)(2,1)S(1)} %copy-done.1, bf16[128,2048]{1,0:T(8,128)(2,1)S(1)} %collective-permute-done.refs_1_, bf16[128,2048]{1,0:T(8,128)(2,1)} %collective-permute-done.1.refs_2_, ...), custom_call_target="tpu_custom_call" | custom-call | flops 1879048192 | bytes 8912916 | tf_op jit(solution)/shard_map/forward_most/pallas_call | solution.py:31
  70.3 0.0 collective-permute-done.6.pair_hbm
  70.4 1.1 forward_last.1
  71.4 14.1 %all_to_all.30.part_ref = bf16[4,256,256]{2,1,0:T(8,128)(2,1)S(1)} all-to-all(bf16[4,256,256]{2,1,0:T(8,128)(2,1)S(1)} %get-tuple-element.33), channel_id=1, replica_groups=mesh['z'=16,'yl'=2,'core'=2,'yh'=2,'x'=4] {'x'}, dimensions={0} | all-to-all | bytes 1048576 | tf_op jit(solution)/shard_map/all_to_all | solution.py:440
  85.6 0.1 slope.1
  85.7 11.0 %all_to_all.31.refs_4_ = bf16[4,256,256]{2,1,0:T(8,128)(2,1)S(1)} all-to-all(bf16[4,256,256]{2,1,0:T(8,128)(2,1)S(1)} %get-tuple-element.34), channel_id=1, replica_groups=mesh['z'=16,'yl'=2,'core'=2,'yh'=2,'x'=4] {'x'}, dimensions={0} | all-to-all | bytes 1048576 | tf_op jit(solution)/shard_map/all_to_all | solution.py:444
  96.7 2.7 %grad.1 = bf16[32,144,128]{2,1,0:T(8,128)(2,1)S(1)} custom-call(bf16[128,2048]{1,0:T(8,128)(2,1)S(1)} %copy-done.1, bf16[128,2048]{1,0:T(8,128)(2,1)S(1)} %collective-permute-done.refs_1_, bf16[5,128,2048]{2,1,0:T(8,128)(2,1)S(1)} %get-tuple-element.30.refs_2_, bf16[128,2048]{1,0:T(8,128)(2,1)S(1)} %get-tuple-element.32.refs_3_, ...), custom_call_target="tpu_custom_call" | custom-call | flops 1073741824 | bytes 5898772 | tf_op jit(solution)/shard_map/grad/pallas_call | solution.py:31
  99.4 0.0 copy-start.2
  99.4 22.6 %all_to_all.32.got_ref = bf16[32,144,128]{2,1,0:T(8,128)(2,1)S(1)} all-to-all(bf16[32,144,128]{2,1,0:T(8,128)(2,1)S(1)} %grad.1), channel_id=1, replica_groups=mesh['z'=16,'yl'=2,'core'=2,'yh'=2,'x'=4] {'yl','core','yh','x'}, dimensions={0} | all-to-all | bytes 2359296 | tf_op jit(solution)/shard_map/all_to_all | solution.py:460
  122.1 1.3 gather.1
  123.4 25.0 %all_to_all.33.got_ref = bf16[16,48,128]{2,1,0:T(8,128)(2,1)S(1)} all-to-all(bf16[16,48,128]{2,1,0:T(8,128)(2,1)S(1)} %gather.1), channel_id=1, replica_groups=mesh['z'=16,'yl'=2,'core'=2,'yh'=2,'x'=4] {'z'}, dimensions={0} | all-to-all | bytes 393216 | tf_op jit(solution)/shard_map/all_to_all | solution.py:469
  148.4 0.0 copy-done.2
  148.4 0.9 final.1
Async XLA Ops:
  3.9 41.5 %all-to-all-start = ((bf16[128,8,128]{2,1,0:T(8,128)(2,1)}), bf16[128,8,128]{2,1,0:T(8,128)(2,1)S(1)}, u32[]{:S(2)}, u32[]{:S(2)}) async-start(bf16[128,8,128]{2,1,0:T(8,128)(2,1)} %bitcast.16), calls=%async_computation | async-start | bytes 524288 | tf_op jit(solution)/shard_map/all_to_all | solution.py:368
  28.2 22.9 %copy-start.1 = (bf16[128,2048]{1,0:T(8,128)(2,1)S(1)}, bf16[128,2048]{1,0:T(8,128)(2,1)}, u32[]{:S(2)}) copy-start(bf16[128,2048]{1,0:T(8,128)(2,1)} %get-tuple-element.21.refs_0_) | copy-start | bytes 1572868
  28.2 27.3 %copy-start = (s32[2048,64]{0,1:T(8,128)S(1)}, s32[2048,64]{0,1:T(8,128)}, u32[]{:S(2)}) copy-start(s32[2048,64]{0,1:T(8,128)} %param.9) | copy-start | bytes 1572868
  28.2 27.3 %copy-start.3 = (s32[5]{0:T(128)S(1)}, s32[5]{0:T(128)}, u32[]{:S(2)}) copy-start(s32[5]{0:T(128)} %stack.23.at_ref.refs_9_.refs_6_) | copy-start | bytes 64
  28.2 24.8 %collective-permute-start = (bf16[128,2048]{1,0:T(8,128)(2,1)}, bf16[128,2048]{1,0:T(8,128)(2,1)S(1)}, u32[]{:S(2)}, u32[]{:S(2)}) collective-permute-start(bf16[128,2048]{1,0:T(8,128)(2,1)} %get-tuple-element.22), channel_id=1, source_target_pairs={{0,2},{1,3},{2,0},{3,1},{4,6},{5,7},{6,4},{7,5},{8,10},{9,11},{10,... | collective-permute-start | bytes 1572872 | tf_op jit(solution)/shard_map/ppermute | solution.py:389
  31.7 26.6 %collective-permute-start.2 = (bf16[128,2048]{1,0:T(8,128)(2,1)}, bf16[128,2048]{1,0:T(8,128)(2,1)}, u32[]{:S(2)}, u32[]{:S(2)}) collective-permute-start(bf16[128,2048]{1,0:T(8,128)(2,1)} %get-tuple-element.24), channel_id=1, source_target_pairs={{0,3},{1,0},{2,1},{3,2},{4,7},{5,4},{6,5},{7,6},{8,11},{9,8},{10,9... | collective-permute-start | bytes 1572872 | tf_op jit(solution)/shard_map/ppermute | solution.py:389
  33.9 26.4 %collective-permute-start.1 = (bf16[128,2048]{1,0:T(8,128)(2,1)}, bf16[128,2048]{1,0:T(8,128)(2,1)}, u32[]{:S(2)}, u32[]{:S(2)}) collective-permute-start(bf16[128,2048]{1,0:T(8,128)(2,1)} %get-tuple-element.23), channel_id=1, source_target_pairs={{0,1},{1,2},{2,3},{3,0},{4,5},{5,6},{6,7},{7,4},{8,9},{9,10},{10,1... | collective-permute-start | bytes 1572872 | tf_op jit(solution)/shard_map/ppermute | solution.py:389
  46.7 17.7 %all-to-all-start.1 = ((bf16[4,1024,128]{2,1,0:T(8,128)(2,1)}), bf16[4,1024,128]{2,1,0:T(8,128)(2,1)S(1)}, u32[]{:S(2)}, u32[]{:S(2)}) async-start(bf16[4,1024,128]{2,1,0:T(8,128)(2,1)} %spread.1), calls=%async_computation.1 | async-start | bytes 2097152 | tf_op jit(solution)/shard_map/all_to_all | solution.py:397
  51.1 14.1 %collective-permute-start.3 = (bf16[128,2048]{1,0:T(8,128)(2,1)S(1)}, bf16[128,2048]{1,0:T(8,128)(2,1)}, u32[]{:S(2)}, u32[]{:S(2)}) collective-permute-start(bf16[128,2048]{1,0:T(8,128)(2,1)S(1)} %copy-done.1), channel_id=1, source_target_pairs={{0,8},{8,0},{1,9},{9,1},{2,10},{10,2},{3,11},{11,3},{4,12},{12,4},... | collective-permute-start | bytes 1572872 | tf_op jit(solution)/shard_map/ppermute | solution.py:409
  53.1 12.2 %collective-permute-start.4 = (bf16[128,2048]{1,0:T(8,128)(2,1)S(1)}, bf16[128,2048]{1,0:T(8,128)(2,1)}, u32[]{:S(2)}, u32[]{:S(2)}) collective-permute-start(bf16[128,2048]{1,0:T(8,128)(2,1)S(1)} %collective-permute-done.refs_1_), channel_id=1, source_target_pairs={{0,8},{8,0},{1,9},{9,1},{2,10},{10,2},{3,11},{11,3},{4,12},{12,4},... | collective-permute-start | bytes 1572872 | tf_op jit(solution)/shard_map/ppermute | solution.py:409
  58.3 6.9 %collective-permute-start.5 = (bf16[128,2048]{1,0:T(8,128)(2,1)}, bf16[128,2048]{1,0:T(8,128)(2,1)}, u32[]{:S(2)}, u32[]{:S(2)}) collective-permute-start(bf16[128,2048]{1,0:T(8,128)(2,1)} %collective-permute-done.2.refs_3_), channel_id=1, source_target_pairs={{0,8},{8,0},{1,9},{9,1},{2,10},{10,2},{3,11},{11,3},{4,12},{12,4},... | collective-permute-start | bytes 1572872 | tf_op jit(solution)/shard_map/ppermute | solution.py:409
  60.3 10.0 %collective-permute-start.6 = (bf16[128,2048]{1,0:T(8,128)(2,1)}, bf16[128,2048]{1,0:T(8,128)(2,1)S(1)}, u32[]{:S(2)}, u32[]{:S(2)}) collective-permute-start(bf16[128,2048]{1,0:T(8,128)(2,1)} %collective-permute-done.1.refs_2_), channel_id=1, source_target_pairs={{0,8},{8,0},{1,9},{9,1},{2,10},{10,2},{3,11},{11,3},{4,12},{12,4},... | collective-permute-start | bytes 1572872 | tf_op jit(solution)/shard_map/ppermute | solution.py:409
  99.4 49.0 %copy-start.2 = (f32[64,128]{1,0:T(8,128)S(1)}, f32[64,128]{1,0:T(8,128)}, u32[]{:S(2)}) copy-start(f32[64,128]{1,0:T(8,128)} %get-tuple-element.37.pat_ref) | copy-start | bytes 98308

commit v16 on v14

--- a/solution.py
+++ b/solution.py
@@ -25,7 +25,7 @@
     size = sum(a.size * a.dtype.itemsize for a in args)
     for o in jax.tree.leaves(out_shape):
         size += o.size * o.dtype.itemsize
-    specs = [SMEM if a.shape == (5,) else VMEM for a in args]
+    specs = [SMEM if a.shape in ((1,), (5,)) else VMEM for a in args]
     for i in far:
         specs[i] = pl.BlockSpec(memory_space=pl.ANY)
     return pl.pallas_call(
@@ -152,7 +152,7 @@
 
 def pack_kernel(teacher_hbm, student_hbm, pat_hbm, at_ref, out_ref, rows_ref, *scratch):
     teacher_ref, student_ref, pat_ref, sems = scratch
-    place = at_ref[3]
+    place = at_ref[0]
     window = pl.ds(pl.multiple_of(place // 4 * 128, 128), 128)
     loads = [
         pltpu.make_async_copy(pat_hbm.at[:, window], pat_ref, sems.at[0]),
@@ -349,7 +349,7 @@
         teacher_k.T,
         student_k.T,
         patterns,
-        at,
+        place.reshape(1).astype(jnp.int32),
         scratch=[
             pltpu.VMEM((64, 128), BF16),
             pltpu.VMEM((64, 128), BF16),
@@ -367,7 +367,7 @@
         (shape((128, 2048), BF16),) * NX,
         hidden,
         norm_gain.reshape(64, 128),
-        at,
+        x.reshape(1).astype(jnp.int32),
         scratch=[
             pltpu.VMEM((128, D), BF16),
             pltpu.VMEM((512, 512), BF16),

time: 151 us -> 150 us (level)
  no operation moved by 1% of the time
where the time goes in v16:
time: 150 us; the launch traced here: 148 us
  blocking collectives  72.7 us (48%)
  starting transfers between devices  43 us (29%)
  Pallas kernels  21.4 us (14%)
  waiting for transfers between devices  10 us (7%)
    all_to_all x1, blocking collectives, shards(): got_sum = lax.all_to_all(packed_term, 'z', 0, 0, tiled=True)  24.9 us
    all_to_all x1, blocking collectives, shards(): got_term = lax.all_to_all(term, PLANE, 0, 0, tiled=True)  22.6 us
    pallas_call x11, Pallas kernels, call(): pl.pallas_call(kernel, out_shape=out_shape, in_specs=specs, out_specs=jax...  21.4 us
    all_to_all x1, starting transfers between devices, shards(): got_w = lax.all_to_all(packed.reshape(128, 8, 128), ZCX, 0, 0, tiled=True)  19.4 us
    all_to_all x1, blocking collectives, shards(): got_part = lax.all_to_all(part, 'x', 0, 0, tiled=True)  14.1 us
    all_to_all x1, blocking collectives, shards(): slopes = lax.all_to_all(slope, 'x', 0, 0, tiled=True)  11 us
    ppermute x3, starting transfers between devices, shards(): lax.ppermute(split[i], 'x', ring(STEP[i]))  10.6 us
    ppermute x4, starting transfers between devices, shards(): pair = [lax.ppermute(piece, 'core', [(0, 1), (1, 0)]) for piece in own]  8.62 us
  transfers between devices with their start and end apart: 9, of which 3 were waited for; matrix products, arithmetic and copies ran while one was open for 0% of the time, Pallas kernels for 9%

profile of v16, /device:TPU:6, one launch (start us, length us, event | category | flops | bytes accessed | tf_op | source)
XLA Modules:
  0.0 148.0 jit_solution(6956370301741354502)
XLA Ops:
  0.6 1.9 %pack.1 = (bf16[16,64,128]{2,1,0:T(8,128)(2,1)}, f32[64,128]{1,0:T(8,128)}) custom-call(bf16[64,128]{1,0:T(8,128)(2,1)} %bitcast.17, bf16[64,128]{1,0:T(8,128)(2,1)} %bitcast.18, s32[64,2048]{1,0:T(8,128)} %bitcast.13, s32[1]{0:T(128)} %bitcast.5.at_ref), custom_call_target="tpu_custom_call" | custom-call | bytes 851972 | tf_op jit(solution)/shard_map/pack/pallas_call | solution.py:31
  2.5 19.4 %all-to-all-start = ((bf16[128,8,128]{2,1,0:T(8,128)(2,1)}), bf16[128,8,128]{2,1,0:T(8,128)(2,1)S(1)}, u32[]{:S(2)}, u32[]{:S(2)}) async-start(bf16[128,8,128]{2,1,0:T(8,128)(2,1)} %bitcast.16), calls=%async_computation | async-start | bytes 524288 | tf_op jit(solution)/shard_map/all_to_all | solution.py:363
  21.9 4.9 %norm.1 = (bf16[128,2048]{1,0:T(8,128)(2,1)}, bf16[128,2048]{1,0:T(8,128)(2,1)}, bf16[128,2048]{1,0:T(8,128)(2,1)}, bf16[128,2048]{1,0:T(8,128)(2,1)}) custom-call(bf16[128,8192]{1,0:T(8,128)(2,1)} %x_hbm.1, bf16[64,128]{1,0:T(8,128)(2,1)} %bitcast.20, s32[1]{0:T(128)} %bitcast.1.at_ref), custom_call_target="tpu_custom_call" | custom-call | flops 1073741824 | bytes 4210692 | tf_op jit(solution)/shard_map/norm/pallas_call | solution.py:31
  26.8 0.0 copy-start.2
  26.8 0.0 copy-start
  26.8 3.5 %collective-permute-start = (bf16[128,2048]{1,0:T(8,128)(2,1)}, bf16[128,2048]{1,0:T(8,128)(2,1)S(1)}, u32[]{:S(2)}, u32[]{:S(2)}) collective-permute-start(bf16[128,2048]{1,0:T(8,128)(2,1)} %get-tuple-element.22), channel_id=1, source_target_pairs={{0,2},{1,3},{2,0},{3,1},{4,6},{5,7},{6,4},{7,5},{8,10},{9,11},{10,... | collective-permute-start | bytes 1572872 | tf_op jit(solution)/shard_map/ppermute | solution.py:384
  30.3 2.2 %collective-permute-start.2 = (bf16[128,2048]{1,0:T(8,128)(2,1)}, bf16[128,2048]{1,0:T(8,128)(2,1)}, u32[]{:S(2)}, u32[]{:S(2)}) collective-permute-start(bf16[128,2048]{1,0:T(8,128)(2,1)} %get-tuple-element.24), channel_id=1, source_target_pairs={{0,3},{1,0},{2,1},{3,2},{4,7},{5,4},{6,5},{7,6},{8,11},{9,8},{10,9... | collective-permute-start | bytes 1572872 | tf_op jit(solution)/shard_map/ppermute | solution.py:384
  32.5 4.9 %collective-permute-start.1 = (bf16[128,2048]{1,0:T(8,128)(2,1)}, bf16[128,2048]{1,0:T(8,128)(2,1)}, u32[]{:S(2)}, u32[]{:S(2)}) collective-permute-start(bf16[128,2048]{1,0:T(8,128)(2,1)} %get-tuple-element.23), channel_id=1, source_target_pairs={{0,1},{1,2},{2,3},{3,0},{4,5},{5,6},{6,7},{7,4},{8,9},{9,10},{10,1... | collective-permute-start | bytes 1572872 | tf_op jit(solution)/shard_map/ppermute | solution.py:384
  37.4 6.7 %all-to-all-done = bf16[128,8,128]{2,1,0:T(8,128)(2,1)S(1)} async-done(((bf16[128,8,128]{2,1,0:T(8,128)(2,1)}), bf16[128,8,128]{2,1,0:T(8,128)(2,1)S(1)}, u32[]{:S(2)}, u32[]{:S(2)}) %all-to-all-start) | async-done | bytes 262176 | tf_op jit(solution)/shard_map/all_to_all | solution.py:363
  44.1 1.3 spread.1
  45.4 4.5 %all-to-all-start.1 = ((bf16[4,1024,128]{2,1,0:T(8,128)(2,1)}), bf16[4,1024,128]{2,1,0:T(8,128)(2,1)S(1)}, u32[]{:S(2)}, u32[]{:S(2)}) async-start(bf16[4,1024,128]{2,1,0:T(8,128)(2,1)} %spread.1), calls=%async_computation.1 | async-start | bytes 2097152 | tf_op jit(solution)/shard_map/all_to_all | solution.py:392
  49.8 0.0 copy-done.2
  49.8 1.9 %collective-permute-start.3 = (bf16[128,2048]{1,0:T(8,128)(2,1)S(1)}, bf16[128,2048]{1,0:T(8,128)(2,1)}, u32[]{:S(2)}, u32[]{:S(2)}) collective-permute-start(bf16[128,2048]{1,0:T(8,128)(2,1)S(1)} %copy-done.2), channel_id=1, source_target_pairs={{0,8},{8,0},{1,9},{9,1},{2,10},{10,2},{3,11},{11,3},{4,12},{12,4},... | collective-permute-start | bytes 1572872 | tf_op jit(solution)/shard_map/ppermute | solution.py:404
  51.7 0.1 stack.17.at_ref.refs_9_.refs_4_
  51.8 0.0 collective-permute-done.refs_1_
  51.8 2.4 %collective-permute-start.4 = (bf16[128,2048]{1,0:T(8,128)(2,1)S(1)}, bf16[128,2048]{1,0:T(8,128)(2,1)}, u32[]{:S(2)}, u32[]{:S(2)}) collective-permute-start(bf16[128,2048]{1,0:T(8,128)(2,1)S(1)} %collective-permute-done.refs_1_), channel_id=1, source_target_pairs={{0,8},{8,0},{1,9},{9,1},{2,10},{10,2},{3,11},{11,3},{4,12},{12,4},... | collective-permute-start | bytes 1572872 | tf_op jit(solution)/shard_map/ppermute | solution.py:404
  54.2 0.0 copy-done
  54.2 1.1 choose.1.pat_ref
  55.4 1.6 %collective-permute-done.2.refs_3_ = bf16[128,2048]{1,0:T(8,128)(2,1)} collective-permute-done((bf16[128,2048]{1,0:T(8,128)(2,1)}, bf16[128,2048]{1,0:T(8,128)(2,1)}, u32[]{:S(2)}, u32[]{:S(2)}) %collective-permute-start.2) | collective-permute-done | bytes 524320 | tf_op jit(solution)/shard_map/ppermute | solution.py:384
  57.0 2.0 %collective-permute-start.5 = (bf16[128,2048]{1,0:T(8,128)(2,1)}, bf16[128,2048]{1,0:T(8,128)(2,1)}, u32[]{:S(2)}, u32[]{:S(2)}) collective-permute-start(bf16[128,2048]{1,0:T(8,128)(2,1)} %collective-permute-done.2.refs_3_), channel_id=1, source_target_pairs={{0,8},{8,0},{1,9},{9,1},{2,10},{10,2},{3,11},{11,3},{4,12},{12,4},... | collective-permute-start | bytes 1572872 | tf_op jit(solution)/shard_map/ppermute | solution.py:404
  58.9 0.0 collective-permute-done.1.refs_2_
  59.0 2.4 %collective-permute-start.6 = (bf16[128,2048]{1,0:T(8,128)(2,1)}, bf16[128,2048]{1,0:T(8,128)(2,1)S(1)}, u32[]{:S(2)}, u32[]{:S(2)}) collective-permute-start(bf16[128,2048]{1,0:T(8,128)(2,1)} %collective-permute-done.1.refs_2_), channel_id=1, source_target_pairs={{0,8},{8,0},{1,9},{9,1},{2,10},{10,2},{3,11},{11,3},{4,12},{12,4},... | collective-permute-start | bytes 1572872 | tf_op jit(solution)/shard_map/ppermute | solution.py:404
  61.3 1.7 %all-to-all-done.1.w_ref = bf16[4,1024,128]{2,1,0:T(8,128)(2,1)S(1)} async-done(((bf16[4,1024,128]{2,1,0:T(8,128)(2,1)}), bf16[4,1024,128]{2,1,0:T(8,128)(2,1)S(1)}, u32[]{:S(2)}, u32[]{:S(2)}) %all-to-all-start.1) | async-done | bytes 1048608 | tf_op jit(solution)/shard_map/all_to_all | solution.py:392
  63.0 0.9 decode.1
  63.9 0.0 collective-permute-done.3.refs_4_
  63.9 0.0 collective-permute-done.4.refs_5_
  63.9 0.0 collective-permute-done.5.refs_6_
  63.9 5.3 %forward_most.1 = (bf16[4,256,256]{2,1,0:T(8,128)(2,1)S(1)}, bf16[7,128,2048]{2,1,0:T(8,128)(2,1)S(1)}) custom-call(bf16[128,2048]{1,0:T(8,128)(2,1)S(1)} %copy-done.2, bf16[128,2048]{1,0:T(8,128)(2,1)S(1)} %collective-permute-done.refs_1_, bf16[128,2048]{1,0:T(8,128)(2,1)} %collective-permute-done.1.refs_2_, ...), custom_call_target="tpu_custom_call" | custom-call | flops 1879048192 | bytes 9961492 | tf_op jit(solution)/shard_map/forward_most/pallas_call | solution.py:31
  69.2 0.0 collective-permute-done.6.pair_hbm
  69.2 1.1 forward_last.1
  70.3 14.1 %all_to_all.30.part_ref = bf16[4,256,256]{2,1,0:T(8,128)(2,1)S(1)} all-to-all(bf16[4,256,256]{2,1,0:T(8,128)(2,1)S(1)} %get-tuple-element.33), channel_id=1, replica_groups=mesh['z'=16,'yl'=2,'core'=2,'yh'=2,'x'=4] {'x'}, dimensions={0} | all-to-all | bytes 1048576 | tf_op jit(solution)/shard_map/all_to_all | solution.py:435
  84.4 0.1 slope.1
  84.5 11.0 %all_to_all.31.refs_2_ = bf16[4,256,256]{2,1,0:T(8,128)(2,1)S(1)} all-to-all(bf16[4,256,256]{2,1,0:T(8,128)(2,1)S(1)} %get-tuple-element.34), channel_id=1, replica_groups=mesh['z'=16,'yl'=2,'core'=2,'yh'=2,'x'=4] {'x'}, dimensions={0} | all-to-all | bytes 1048576 | tf_op jit(solution)/shard_map/all_to_all | solution.py:439
  95.6 2.7 %grad.1 = bf16[32,144,128]{2,1,0:T(8,128)(2,1)S(1)} custom-call(bf16[7,128,2048]{2,1,0:T(8,128)(2,1)S(1)} %get-tuple-element.30.refs_0_, bf16[128,2048]{1,0:T(8,128)(2,1)S(1)} %get-tuple-element.32.refs_1_, bf16[4,256,256]{2,1,0:T(8,128)(2,1)S(1)} %all_to_all.31.refs_2_, f32[1,128]{1,0:T(1,128)S(1)} %get-tuple-element.35.refs_3_, ...), custom_call_target="tpu_custom_call" | custom-call | flops 1073741824 | bytes 5898772 | tf_op jit(solution)/shard_map/grad/pallas_call | solution.py:31
  98.3 0.0 copy-start.1
  98.3 22.6 %all_to_all.32.got_ref = bf16[32,144,128]{2,1,0:T(8,128)(2,1)S(1)} all-to-all(bf16[32,144,128]{2,1,0:T(8,128)(2,1)S(1)} %grad.1), channel_id=1, replica_groups=mesh['z'=16,'yl'=2,'core'=2,'yh'=2,'x'=4] {'yl','core','yh','x'}, dimensions={0} | all-to-all | bytes 2359296 | tf_op jit(solution)/shard_map/all_to_all | solution.py:453
  120.9 1.3 gather.1
  122.3 24.9 %all_to_all.33.got_ref = bf16[16,48,128]{2,1,0:T(8,128)(2,1)S(1)} all-to-all(bf16[16,48,128]{2,1,0:T(8,128)(2,1)S(1)} %gather.1), channel_id=1, replica_groups=mesh['z'=16,'yl'=2,'core'=2,'yh'=2,'x'=4] {'z'}, dimensions={0} | all-to-all | bytes 393216 | tf_op jit(solution)/shard_map/all_to_all | solution.py:462
  147.2 0.0 copy-done.1
  147.2 0.9 final.1
Async XLA Ops:
  2.5 41.5 %all-to-all-start = ((bf16[128,8,128]{2,1,0:T(8,128)(2,1)}), bf16[128,8,128]{2,1,0:T(8,128)(2,1)S(1)}, u32[]{:S(2)}, u32[]{:S(2)}) async-start(bf16[128,8,128]{2,1,0:T(8,128)(2,1)} %bitcast.16), calls=%async_computation | async-start | bytes 524288 | tf_op jit(solution)/shard_map/all_to_all | solution.py:363
  26.8 23.0 %copy-start.2 = (bf16[128,2048]{1,0:T(8,128)(2,1)S(1)}, bf16[128,2048]{1,0:T(8,128)(2,1)}, u32[]{:S(2)}) copy-start(bf16[128,2048]{1,0:T(8,128)(2,1)} %get-tuple-element.21.refs_0_) | copy-start | bytes 1572868
  26.8 27.4 %copy-start = (s32[2048,64]{0,1:T(8,128)S(1)}, s32[2048,64]{0,1:T(8,128)}, u32[]{:S(2)}) copy-start(s32[2048,64]{0,1:T(8,128)} %param.9) | copy-start | bytes 1572868
  26.8 25.0 %collective-permute-start = (bf16[128,2048]{1,0:T(8,128)(2,1)}, bf16[128,2048]{1,0:T(8,128)(2,1)S(1)}, u32[]{:S(2)}, u32[]{:S(2)}) collective-permute-start(bf16[128,2048]{1,0:T(8,128)(2,1)} %get-tuple-element.22), channel_id=1, source_target_pairs={{0,2},{1,3},{2,0},{3,1},{4,6},{5,7},{6,4},{7,5},{8,10},{9,11},{10,... | collective-permute-start | bytes 1572872 | tf_op jit(solution)/shard_map/ppermute | solution.py:384
  30.3 26.6 %collective-permute-start.2 = (bf16[128,2048]{1,0:T(8,128)(2,1)}, bf16[128,2048]{1,0:T(8,128)(2,1)}, u32[]{:S(2)}, u32[]{:S(2)}) collective-permute-start(bf16[128,2048]{1,0:T(8,128)(2,1)} %get-tuple-element.24), channel_id=1, source_target_pairs={{0,3},{1,0},{2,1},{3,2},{4,7},{5,4},{6,5},{7,6},{8,11},{9,8},{10,9... | collective-permute-start | bytes 1572872 | tf_op jit(solution)/shard_map/ppermute | solution.py:384
  32.5 26.4 %collective-permute-start.1 = (bf16[128,2048]{1,0:T(8,128)(2,1)}, bf16[128,2048]{1,0:T(8,128)(2,1)}, u32[]{:S(2)}, u32[]{:S(2)}) collective-permute-start(bf16[128,2048]{1,0:T(8,128)(2,1)} %get-tuple-element.23), channel_id=1, source_target_pairs={{0,1},{1,2},{2,3},{3,0},{4,5},{5,6},{6,7},{7,4},{8,9},{9,10},{10,1... | collective-permute-start | bytes 1572872 | tf_op jit(solution)/shard_map/ppermute | solution.py:384
  45.4 17.7 %all-to-all-start.1 = ((bf16[4,1024,128]{2,1,0:T(8,128)(2,1)}), bf16[4,1024,128]{2,1,0:T(8,128)(2,1)S(1)}, u32[]{:S(2)}, u32[]{:S(2)}) async-start(bf16[4,1024,128]{2,1,0:T(8,128)(2,1)} %spread.1), calls=%async_computation.1 | async-start | bytes 2097152 | tf_op jit(solution)/shard_map/all_to_all | solution.py:392
  49.8 14.1 %collective-permute-start.3 = (bf16[128,2048]{1,0:T(8,128)(2,1)S(1)}, bf16[128,2048]{1,0:T(8,128)(2,1)}, u32[]{:S(2)}, u32[]{:S(2)}) collective-permute-start(bf16[128,2048]{1,0:T(8,128)(2,1)S(1)} %copy-done.2), channel_id=1, source_target_pairs={{0,8},{8,0},{1,9},{9,1},{2,10},{10,2},{3,11},{11,3},{4,12},{12,4},... | collective-permute-start | bytes 1572872 | tf_op jit(solution)/shard_map/ppermute | solution.py:404
  51.8 12.1 %collective-permute-start.4 = (bf16[128,2048]{1,0:T(8,128)(2,1)S(1)}, bf16[128,2048]{1,0:T(8,128)(2,1)}, u32[]{:S(2)}, u32[]{:S(2)}) collective-permute-start(bf16[128,2048]{1,0:T(8,128)(2,1)S(1)} %collective-permute-done.refs_1_), channel_id=1, source_target_pairs={{0,8},{8,0},{1,9},{9,1},{2,10},{10,2},{3,11},{11,3},{4,12},{12,4},... | collective-permute-start | bytes 1572872 | tf_op jit(solution)/shard_map/ppermute | solution.py:404
  57.0 6.9 %collective-permute-start.5 = (bf16[128,2048]{1,0:T(8,128)(2,1)}, bf16[128,2048]{1,0:T(8,128)(2,1)}, u32[]{:S(2)}, u32[]{:S(2)}) collective-permute-start(bf16[128,2048]{1,0:T(8,128)(2,1)} %collective-permute-done.2.refs_3_), channel_id=1, source_target_pairs={{0,8},{8,0},{1,9},{9,1},{2,10},{10,2},{3,11},{11,3},{4,12},{12,4},... | collective-permute-start | bytes 1572872 | tf_op jit(solution)/shard_map/ppermute | solution.py:404
  59.0 10.3 %collective-permute-start.6 = (bf16[128,2048]{1,0:T(8,128)(2,1)}, bf16[128,2048]{1,0:T(8,128)(2,1)S(1)}, u32[]{:S(2)}, u32[]{:S(2)}) collective-permute-start(bf16[128,2048]{1,0:T(8,128)(2,1)} %collective-permute-done.1.refs_2_), channel_id=1, source_target_pairs={{0,8},{8,0},{1,9},{9,1},{2,10},{10,2},{3,11},{11,3},{4,12},{12,4},... | collective-permute-start | bytes 1572872 | tf_op jit(solution)/shard_map/ppermute | solution.py:404
  98.3 48.9 %copy-start.1 = (f32[64,128]{1,0:T(8,128)S(1)}, f32[64,128]{1,0:T(8,128)}, u32[]{:S(2)}) copy-start(f32[64,128]{1,0:T(8,128)} %get-tuple-element.37.pat_ref) | copy-start | bytes 98308
